TPU v7x, 32 devices: a whole 2x2x4 slice. The times are simulated.
32 devices in a mesh: dp: 4 (over y, x), group: 8 (over z, core).
Axes of the slice: x: 2, y: 2, z: 4, core: 2. Of those that a mesh axis runs over, the one named last changes fastest.
Arguments:
- source: bfloat16 [512, 9, 9, 2048], P('dp', None, None, 'group'), may hold values from -32 to 32
- offsets: int32 [512, 2], P('dp'), may hold values from 0 to 2
- cotangent: bfloat16 [512, 7, 7, 2048], P('dp', None, None, 'group'), may hold values from -6 to 6
- reduce_weight: float32 [2048, 1024], P('group'), may hold values from -0.125 to 0.125
- reduce_first: float32 [2048, 1024], P('group'), may hold values from -0.0068359375 to 0.0068359375
- reduce_second: float32 [2048, 1024], P('group'), may hold values from 2.223503e-07 to 8.894012e-07
- group_weight: float32 [3, 3, 32, 1024], P(None, None, None, 'group'), may hold values from -0.375 to 0.375
- group_first: float32 [3, 3, 32, 1024], P(None, None, None, 'group'), may hold values from -0.0068359375 to 0.0068359375
- group_second: float32 [3, 3, 32, 1024], P(None, None, None, 'group'), may hold values from 2.223503e-07 to 8.894012e-07
- expand_weight: float32 [1024, 2048], P(None, 'group'), may hold values from -0.1875 to 0.1875
- expand_first: float32 [1024, 2048], P(None, 'group'), may hold values from -0.0068359375 to 0.0068359375
- expand_second: float32 [1024, 2048], P(None, 'group'), may hold values from 2.223503e-07 to 8.894012e-07
- mid_norms: float32 [4, 1024], P(None, 'group'), may hold values from -1 to 3
- mid_first: float32 [4, 1024], P(None, 'group'), may hold values from -0.0068359375 to 0.0068359375
- mid_second: float32 [4, 1024], P(None, 'group'), may hold values from 2.223503e-07 to 8.894012e-07
- out_norms: float32 [2, 2048], P(None, 'group'), may hold values from -1 to 3
- out_first: float32 [2, 2048], P(None, 'group'), may hold values from -0.0068359375 to 0.0068359375
- out_second: float32 [2, 2048], P(None, 'group'), may hold values from 2.223503e-07 to 8.894012e-07
Outputs:
- output: bfloat16 [512, 7, 7, 2048], P('dp', None, None, 'group')
- input_grad: bfloat16 [512, 7, 7, 2048], P('dp', None, None, 'group')
- grad_norm: float32 [], replicated
- reduce_master: float32 [2048, 1024], P('group')
- reduce_momentum: float32 [2048, 1024], P('group')
- reduce_variance: float32 [2048, 1024], P('group')
- reduce_copy: bfloat16 [2048, 1024], P('group')
- group_master: float32 [3, 3, 32, 1024], P(None, None, None, 'group')
- group_momentum: float32 [3, 3, 32, 1024], P(None, None, None, 'group')
- group_variance: float32 [3, 3, 32, 1024], P(None, None, None, 'group')
- group_copy: bfloat16 [3, 3, 32, 1024], P(None, None, None, 'group')
- expand_master: float32 [1024, 2048], P(None, 'group')
- expand_momentum: float32 [1024, 2048], P(None, 'group')
- expand_variance: float32 [1024, 2048], P(None, 'group')
- expand_copy: bfloat16 [1024, 2048], P(None, 'group')
- mid_master: float32 [4, 1024], P(None, 'group')
- mid_momentum: float32 [4, 1024], P(None, 'group')
- mid_variance: float32 [4, 1024], P(None, 'group')
- mid_copy: bfloat16 [4, 1024], P(None, 'group')
- out_master: float32 [2, 2048], P(None, 'group')
- out_momentum: float32 [2, 2048], P(None, 'group')
- out_variance: float32 [2, 2048], P(None, 'group')
- out_copy: bfloat16 [2, 2048], P(None, 'group')
All inputs are finite; a program needn't handle non-finite values.
Results may differ from a plain program's by a relative error of at most 0.023.
Values may be sent and summed in bfloat16 or wider, within the bound.
No kernel may reach another device: no remote copies, remote signals or barrier semaphores. Data moves between devices by JAX's collectives and lax.ppermute only.
A program may use at most 256 MiB of HBM per device.

v0:
```python
import jax
import jax.numpy as jnp
from jax import lax
from jax.sharding import PartitionSpec as P

CIN = 2048
GW = 32
HW = 7
STEP = 10
MID = 1024
SRC = 9


norm_eps = 1e-05
adam_eps = 1e-08
clip_norm = 1.0
moment_decay = 0.5


def crop_images(images, offsets):

    def crop_one(one_image, offset):
        return lax.dynamic_slice(
            one_image,
            (offset[0], offset[1], jnp.zeros((), jnp.int32)),
            (HW, HW, one_image.shape[2]),
        )

    return jax.vmap(crop_one)(images, offsets)


def channel_sums(sum_values, sum_squares):
    return lax.psum((sum_values, sum_squares), "dp")


def rows_everywhere(local_rows):
    return local_rows * lax.axis_size("dp")


def norm_forward(values, gain_row, shifts, row_axis):
    totals = channel_sums(jnp.sum(values, row_axis), jnp.sum(values * values, row_axis))
    row_total = rows_everywhere(values.shape[row_axis])
    center = totals[0] / row_total
    spread = totals[1] / row_total - center * center
    inverse = lax.rsqrt(spread + norm_eps)
    normed = (values - jnp.expand_dims(center, row_axis)) * jnp.expand_dims(inverse, row_axis)
    result = normed * jnp.expand_dims(gain_row, row_axis) + jnp.expand_dims(shifts, row_axis)
    return (result, normed, inverse)


def norm_backward(incoming, normed, inverse, gain_row, row_axis):
    totals = channel_sums(jnp.sum(incoming, row_axis), jnp.sum(incoming * normed, row_axis))
    row_total = rows_everywhere(incoming.shape[row_axis])
    mean_grad = jnp.expand_dims(totals[0] / row_total, row_axis)
    mean_cross = jnp.expand_dims(totals[1] / row_total, row_axis)
    factor = jnp.expand_dims(inverse * gain_row, row_axis)
    return (factor * (incoming - mean_grad - normed * mean_cross), totals[1], totals[0])


def gelu_back(location, incoming):
    return jax.vjp(jax.nn.gelu, location)[1](incoming)[0]


def to_grid(values, images):
    channels = values.shape[0]
    padded_grid = values.reshape(channels, images, HW, HW)
    padded_grid = jnp.pad(padded_grid, ((0, 0), (0, 0), (1, 1), (1, 1)))
    flat_grid = padded_grid.reshape(channels, images * SRC * SRC)
    return jnp.pad(flat_grid, ((0, 0), (SRC + 1, SRC + 1)))


def from_grid(flat_grid, images):
    channels = flat_grid.shape[0]
    inner = flat_grid.reshape(channels, images, SRC, SRC)[:, :, 1 : HW + 1, 1 : HW + 1]
    return inner.reshape(channels, images * HW * HW)


def tap_kernels(kernel):
    group_count = kernel.shape[3] // GW
    return (
        kernel.reshape(3, 3, GW, group_count, GW)
        .transpose(0, 1, 3, 2, 4)
        .reshape(9, group_count, GW, GW)
    )


def tap_offset(tap_index):
    return (tap_index // 3 - 1) * SRC + (tap_index % 3 - 1)


def conv_forward(act_grid, kernel_taps, length):
    group_count = kernel_taps.shape[1]
    grouped = act_grid.reshape(group_count, GW, act_grid.shape[1])
    running = jnp.zeros((group_count, GW, length), jnp.float32)
    for tap_index in range(9):
        start_at = SRC + 1 + tap_offset(tap_index)
        window = lax.slice_in_dim(grouped, start_at, start_at + length, axis=2)
        running = running + jnp.einsum(
            "gik,gio->gok", window, kernel_taps[tap_index], preferred_element_type=jnp.float32
        )
    return running.reshape(group_count * GW, length)


def conv_backward(act_grid, grad_grid, kernel_taps, length):
    group_count = kernel_taps.shape[1]
    act_grouped = act_grid.reshape(group_count, GW, act_grid.shape[1])
    grad_grouped = grad_grid.reshape(group_count, GW, grad_grid.shape[1])
    grad_middle = lax.slice_in_dim(grad_grouped, SRC + 1, SRC + 1 + length, axis=2)
    running = jnp.zeros((group_count, GW, length), jnp.float32)
    kernel_parts = []
    for tap_index in range(9):
        offset_flat = tap_offset(tap_index)
        grad_window = lax.slice_in_dim(
            grad_grouped, SRC + 1 - offset_flat, SRC + 1 - offset_flat + length, axis=2
        )
        running = running + jnp.einsum(
            "gok,gio->gik", grad_window, kernel_taps[tap_index], preferred_element_type=jnp.float32
        )
        act_window = lax.slice_in_dim(
            act_grouped, SRC + 1 + offset_flat, SRC + 1 + offset_flat + length, axis=2
        )
        kernel_parts.append(
            jnp.einsum("gik,gok->gio", act_window, grad_middle, preferred_element_type=jnp.float32)
        )
    kernel_grad = (
        jnp.stack(kernel_parts)
        .reshape(3, 3, group_count, GW, GW)
        .transpose(0, 1, 3, 2, 4)
        .reshape(3, 3, GW, group_count * GW)
    )
    return (running.reshape(group_count * GW, length), kernel_grad)


def adam_step(weight, gradient, momentum, variance, learn_rate, decay_rate):
    momentum_new = moment_decay * momentum + (1.0 - moment_decay) * gradient
    variance_new = moment_decay * variance + (1.0 - moment_decay) * gradient * gradient
    correction = 1.0 - moment_decay**STEP
    direction = momentum_new / correction / (jnp.sqrt(variance_new / correction) + adam_eps)
    weight_new = weight - learn_rate * (direction + decay_rate * weight)
    return (weight_new, momentum_new, variance_new, weight_new.astype(jnp.bfloat16))


def shards(
    source,
    offsets,
    cotangent,
    reduce_weight,
    reduce_first,
    reduce_second,
    group_weight,
    group_first,
    group_second,
    expand_weight,
    expand_first,
    expand_second,
    mid_norms,
    mid_first,
    mid_second,
    out_norms,
    out_first,
    out_second,
):
    reduce_low = reduce_weight.astype(jnp.bfloat16)
    expand_low = expand_weight.astype(jnp.bfloat16)
    kernel_low = group_weight.astype(jnp.bfloat16)
    cropped = crop_images(source, offsets)
    images = cropped.shape[0]
    width_in = cropped.shape[3]
    row_count = images * HW * HW
    length = images * SRC * SRC
    pixels = cropped.reshape(row_count, width_in)
    weight_block = reduce_low
    first_pre = lax.psum_scatter(
        lax.dot_general(
            weight_block, pixels, (((0,), (1,)), ((), ())), preferred_element_type=jnp.float32
        ),
        "group",
        scatter_dimension=0,
        tiled=True,
    )
    first_norm, first_hat, first_inv = norm_forward(first_pre, mid_norms[0], mid_norms[1], 1)
    first_act = jax.nn.gelu(first_norm).astype(jnp.bfloat16)
    kernel_taps = tap_kernels(kernel_low)
    act_grid = to_grid(first_act, images)
    second_pre = from_grid(conv_forward(act_grid, kernel_taps, length), images)
    second_norm, second_hat, second_inv = norm_forward(second_pre, mid_norms[2], mid_norms[3], 1)
    second_act = jax.nn.gelu(second_norm).astype(jnp.bfloat16)
    mid_full = lax.all_gather(second_act, "group", axis=0, tiled=True)
    expanded = lax.dot_general(
        mid_full, expand_low, (((0,), (0,)), ((), ())), preferred_element_type=jnp.float32
    )
    third_norm, third_hat, third_inv = norm_forward(expanded, out_norms[0], out_norms[1], 0)
    summed = third_norm + pixels.astype(jnp.float32)
    output = jax.nn.gelu(summed).astype(jnp.bfloat16).reshape(images, HW, HW, width_in)
    upstream = gelu_back(summed, cotangent.reshape(row_count, width_in).astype(jnp.float32))
    expand_full, out_gain_grad, out_shift_grad = norm_backward(
        upstream, third_hat, third_inv, out_norms[0], 0
    )
    expand_grad = expand_full.astype(jnp.bfloat16)
    expand_wgrad = lax.dot_general(
        mid_full, expand_grad, (((1,), (0,)), ((), ())), preferred_element_type=jnp.float32
    )
    weight_block = expand_low
    second_grad = lax.psum_scatter(
        lax.dot_general(
            weight_block, expand_grad, (((1,), (1,)), ((), ())), preferred_element_type=jnp.float32
        ).astype(jnp.bfloat16),
        "group",
        scatter_dimension=0,
        tiled=True,
    ).astype(jnp.float32)
    second_up = gelu_back(second_norm, second_grad)
    conv_full, second_gain_grad, second_shift_grad = norm_backward(
        second_up, second_hat, second_inv, mid_norms[2], 1
    )
    conv_grad = conv_full.astype(jnp.bfloat16)
    act_flat, group_wgrad = conv_backward(act_grid, to_grid(conv_grad, images), kernel_taps, length)
    act_grad = from_grid(act_flat, images)
    first_up = gelu_back(first_norm, act_grad)
    first_full, first_gain_grad, first_shift_grad = norm_backward(
        first_up, first_hat, first_inv, mid_norms[0], 1
    )
    first_grad = first_full.astype(jnp.bfloat16)
    gathered = lax.all_gather(first_grad, "group", axis=0, tiled=True)
    weight_block = reduce_low
    input_acc = lax.dot_general(
        gathered, weight_block, (((0,), (1,)), ((), ())), preferred_element_type=jnp.float32
    )
    column_part = lax.dot_general(
        pixels, gathered, (((0,), (1,)), ((), ())), preferred_element_type=jnp.float32
    )
    reduce_wgrad = column_part
    input_grad = (upstream + input_acc).astype(jnp.bfloat16).reshape(images, HW, HW, width_in)
    reduce_wgrad, group_wgrad, expand_wgrad = (
        lax.psum(reduce_wgrad.astype(jnp.bfloat16), "dp").astype(jnp.float32),
        lax.psum(group_wgrad.astype(jnp.bfloat16), "dp").astype(jnp.float32),
        lax.psum(expand_wgrad.astype(jnp.bfloat16), "dp").astype(jnp.float32),
    )
    mid_grads = jnp.stack([first_gain_grad, first_shift_grad, second_gain_grad, second_shift_grad])
    out_grads = jnp.stack([out_gain_grad, out_shift_grad])
    local_sq = jnp.zeros((), jnp.float32)
    for grad_item in (reduce_wgrad, group_wgrad, expand_wgrad, mid_grads, out_grads):
        local_sq = local_sq + jnp.sum(grad_item * grad_item)
    total_sq = lax.psum(local_sq, "group")
    grad_norm = jnp.sqrt(total_sq)
    clip_scale = jnp.minimum(1.0, clip_norm / (grad_norm + 1e-06))
    reduce_out = adam_step(
        reduce_weight,
        reduce_wgrad * clip_scale,
        reduce_first,
        reduce_second,
        1.0 / jnp.sqrt(1.0 * CIN),
        0.1,
    )
    group_out = adam_step(
        group_weight,
        group_wgrad * clip_scale,
        group_first,
        group_second,
        1.0 / jnp.sqrt(9.0 * GW),
        0.1,
    )
    expand_out = adam_step(
        expand_weight,
        expand_wgrad * clip_scale,
        expand_first,
        expand_second,
        1.0 / jnp.sqrt(1.0 * MID),
        0.1,
    )
    mid_out = adam_step(mid_norms, mid_grads * clip_scale, mid_first, mid_second, 0.5, 0.0)
    out_out = adam_step(out_norms, out_grads * clip_scale, out_first, out_second, 0.5, 0.0)
    return (
        output,
        input_grad,
        grad_norm,
        reduce_out[0],
        reduce_out[1],
        reduce_out[2],
        reduce_out[3],
        group_out[0],
        group_out[1],
        group_out[2],
        group_out[3],
        expand_out[0],
        expand_out[1],
        expand_out[2],
        expand_out[3],
        mid_out[0],
        mid_out[1],
        mid_out[2],
        mid_out[3],
        out_out[0],
        out_out[1],
        out_out[2],
        out_out[3],
    )


def solution(mesh):
    in_specs = (
        P("dp", None, None, "group"),
        P("dp", None),
        P("dp", None, None, "group"),
        P("group", None),
        P("group", None),
        P("group", None),
        P(None, None, None, "group"),
        P(None, None, None, "group"),
        P(None, None, None, "group"),
        P(None, "group"),
        P(None, "group"),
        P(None, "group"),
        P(None, "group"),
        P(None, "group"),
        P(None, "group"),
        P(None, "group"),
        P(None, "group"),
        P(None, "group"),
    )
    out_specs = (
        P("dp", None, None, "group"),
        P("dp", None, None, "group"),
        P(),
        P("group", None),
        P("group", None),
        P("group", None),
        P("group", None),
        P(None, None, None, "group"),
        P(None, None, None, "group"),
        P(None, None, None, "group"),
        P(None, None, None, "group"),
        P(None, "group"),
        P(None, "group"),
        P(None, "group"),
        P(None, "group"),
        P(None, "group"),
        P(None, "group"),
        P(None, "group"),
        P(None, "group"),
        P(None, "group"),
        P(None, "group"),
        P(None, "group"),
        P(None, "group"),
    )
    return jax.shard_map(shards, mesh=mesh, in_specs=in_specs, out_specs=out_specs, check_vma=False)
```

profile of v0, /device:TPU:0, one launch (start us, length us, event | category | flops | bytes accessed | tf_op | source)
XLA Modules:
  0.0 1069.4 jit_solution(2544628786702086974)
XLA Ops:
  8.0 10.3 gather_fusion
  18.3 5.5 copy.79
  23.9 6.2 reshape.112
  30.1 12.2 %convolution_bitcast_fusion = f32[1024,6272]{0,1:T(8,128)} fusion(bf16[6272,256]{1,0:T(8,128)(2,1)} %reshape.112, f32[256,1024]{1,0:T(8,128)S(1)} %copy-done.4), kind=kOutput, calls=%fused_computation.1 | convolution fusion | flops 3288596480 | bytes 29949952 | tf_op jit(solution)/shard_map/dot_general | solution.py:174
  43.5 253.8 %reduce-scatter.5.cloned.1.call-done = f32[128,6272]{0,1:T(8,128)} async-done(((f32[1024,6272]{0,1:T(8,128)}), f32[128,6272]{0,1:T(8,128)}) %reduce-scatter.5.cloned.1.call-update) | async-done | bytes 3211280 | tf_op jit(solution)/shard_map/reduce_scatter | solution.py:173
  300.0 10.2 all-reduce.9
  310.8 4.5 multiply_convert_fusion.5
  321.1 5.1 reshape.114
  344.2 15.9 %copy.82 = f32[4,32,10368]{1,0,2:T(4,128)} copy(f32[4,32,10368]{2,1,0:T(8,128)} %fusion.1) | data formatting | bytes 10616832 | tf_op jit(solution)/shard_map/add | solution.py:98
  360.1 19.0 %reshape_reshape.6 = f32[128,128,9,9]{0,3,2,1:T(8,128)} reshape(f32[4,32,10368]{1,0,2:T(4,128)} %copy.82) | data formatting | bytes 10616832 | tf_op jit(solution)/shard_map/reshape;reshape | solution.py:74
  379.1 4.8 slice_reduce_fusion
  383.9 4.5 reshape.118
  388.4 7.9 all-reduce.8
  396.4 4.6 multiply_convert_fusion.4
  401.0 7.3 copy.83
  408.3 8.2 reshape.125
  416.5 101.4 %all-gather.3.cloned.1.call-done = bf16[1024,6272]{0,1:T(8,128)(2,1)} async-done(((bf16[128,6272]{0,1:T(8,128)(2,1)}), bf16[1024,6272]{0,1:T(8,128)(2,1)}) %all-gather.3.cloned.1.call-update) | async-done | bytes 12845072 | tf_op jit(solution)/shard_map/all_gather | solution.py:188
  517.9 11.1 %fusion.178 = (f32[256]{0:T(256)S(1)}, f32[256]{0:T(256)S(1)}, f32[6272,256]{1,0:T(8,128)}) fusion(bf16[1024,6272]{0,1:T(8,128)(2,1)} %all-gather.3.cloned.1.call-done, f32[1024,256]{1,0:T(8,128)} %param.27), kind=kOutput, calls=%fused_computation.225 | convolution fusion | flops 3293412864 | bytes 20318208 | tf_op jit(solution)/shard_map/dot_general | solution.py:189
  529.1 10.0 all-reduce.7
  539.1 13.5 %fusion.177 = (f32[256]{0:T(256)S(1)}, f32[256]{0:T(256)S(1)}, f32[6272,256]{1,0:T(8,128)}, bf16[6272,256]{1,0:T(8,128)(2,1)}) fusion(f32[256]{0:T(256)S(1)} %get-tuple-element.146, f32[6272,256]{1,0:T(8,128)} %get-tuple-element.158, f32[256]{0:T(256)S(1)} %get-tuple-element.154, f32[6272,256]{1,0:T(8,128)} %reshape.125, bf16[6272,256]{1,0:T(8,128)(2,1)} %reshape.112, ...), kind=kLoop, calls=%fused_computation.224 | loop fusion | flops 48168448 | bytes 25696256 | tf_op jit(solution)/shard_map/reduce_sum | solution.py:52
  552.6 7.9 all-reduce.6
  560.6 6.1 multiply_convert_fusion
  568.4 6.5 fusion.2
  574.9 16.4 %copy.108 = bf16[1024,6272]{1,0:T(8,128)(2,1)} copy(bf16[1024,6272]{0,1:T(8,128)(2,1)} %fusion.2) | data formatting | bytes 25690112
  591.4 129.2 %reduce-scatter.7.cloned.1.call-done = bf16[128,6272]{1,0:T(8,128)(2,1)} async-done(((bf16[1024,6272]{1,0:T(8,128)(2,1)}), bf16[128,6272]{1,0:T(8,128)(2,1)}) %reduce-scatter.7.cloned.1.call-update) | async-done | bytes 1605648
  724.2 4.6 fusion.176
  728.8 9.8 all-reduce.5
  738.6 5.7 multiply_convert_fusion.3
  748.0 4.7 pad.16
  752.7 6.5 reshape.121
  759.2 4.9 copy.111
  779.0 15.9 %copy.94 = f32[4,32,10368]{1,0,2:T(4,128)} copy(f32[4,32,10368]{2,1,0:T(8,128)} %fusion) | data formatting | bytes 10616832 | tf_op jit(solution)/shard_map/add | solution.py:116
  794.9 19.0 %reshape_reshape.7 = f32[128,128,9,9]{0,3,2,1:T(8,128)} reshape(f32[4,32,10368]{1,0,2:T(4,128)} %copy.94) | data formatting | bytes 10616832 | tf_op jit(solution)/shard_map/reshape;reshape | solution.py:74
  814.0 4.2 slice.202
  818.2 4.6 reshape.123
  822.8 5.9 fusion.179
  828.7 7.9 all-reduce.4
  836.6 4.8 multiply_convert_fusion.2
  841.4 6.1 reshape.119
  847.5 5.4 copy.96
  853.6 8.1 convolution_convert_fusion.1
  880.6 77.8 %all-gather.5.cloned.1.call-done = bf16[1024,6272]{0,1:T(8,128)(2,1)} async-done(((bf16[128,6272]{0,1:T(8,128)(2,1)}), bf16[1024,6272]{0,1:T(8,128)(2,1)}) %all-gather.5.cloned.1.call-update) | async-done | bytes 12845072 | tf_op jit(solution)/shard_map/all_gather | solution.py:224
  958.3 10.0 convolution_convert_fusion.2
  968.4 12.1 %fusion.3 = bf16[6272,256]{1,0:T(8,128)(2,1)} fusion(f32[6272,256]{1,0:T(8,128)} %get-tuple-element.140, bf16[1024,6272]{0,1:T(8,128)(2,1)} %all-gather.5.cloned.1.call-done, f32[256,1024]{1,0:T(8,128)S(1)} %copy-done.5), kind=kOutput, calls=%fused_computation.25 | convolution fusion | flops 3291807744 | bytes 23527424 | tf_op jit(solution)/shard_map/dot_general | solution.py:226
  980.5 6.1 reshape.124
  986.6 34.4 %all-reduce.13.cloned.1.call-done = (bf16[256,1024]{1,0:T(8,128)(2,1)}, bf16[3,3,32,128]{3,2,1,0:T(8,128)(2,1)}, bf16[1024,256]{1,0:T(8,128)(2,1)}) async-done(((bf16[256,1024]{1,0:T(8,128)(2,1)}, bf16[3,3,32,128]{3,2,1,0:T(8,128)(2,1)}, bf16[1024,256]{1,0:T(8,128)(2,1)}), (bf16[256,1024]{1,0:T(8,128)(2,1)}, bf16[3,3,32,128]{3,2,1,0:T(8,128)(2,1)}, ...) | async-done | bytes 1122320 | tf_op jit(solution)/shard_map/psum | solution.py:235
  1029.7 4.7 copy.97
  1034.4 17.1 %psum.127 = f32[]{:T(128)} all-reduce(f32[]{:T(128)S(6)} %add.321), channel_id=1, replica_groups=mesh['dp'=4,'group'=8] {'group'}, use_global_device_ids=true, to_apply=%region_34.35 | all-reduce | flops 1 | bytes 8 | tf_op jit(solution)/shard_map/psum | solution.py:244
  (136 shorter events, 86.7 us)
Async XLA Ops:
  7.2 290.1 %reduce-scatter.5.cloned.1.call-start = ((), (), s32[]{:S(2)}) async-start(), calls=%async_computation.2 | async-start | bytes 28901376 | tf_op jit(solution)/shard_map/reduce_scatter | solution.py:173
  23.9 6.2 copy-start.4
  42.3 0.9 copy-start.12
  42.3 1.2 copy-start.17
  42.3 475.6 %all-gather.3.cloned.1.call-start = ((), (), s32[]{:S(2)}) async-start(), calls=%async_computation.3 | async-start | bytes 14450688 | tf_op jit(solution)/shard_map/all_gather | solution.py:188
  43.5 271.8 %copy-start.25 = (f32[128]{0:T(128)}, f32[128]{0:T(128)S(1)}, u32[]{:S(2)}) copy-start(f32[128]{0:T(128)S(1)} %get-tuple-element.148) | copy-start | bytes 1540
  43.5 271.8 %copy-start.27 = (f32[128]{0:T(128)}, f32[128]{0:T(128)S(1)}, u32[]{:S(2)}) copy-start(f32[128]{0:T(128)S(1)} %get-tuple-element.149) | copy-start | bytes 1540
  310.2 0.5 copy-start.19
  310.2 0.5 copy-start.21
  401.0 319.6 %reduce-scatter.7.cloned.1.call-start = ((), (), s32[]{:S(2)}) async-start(), calls=%async_computation.5 | async-start | bytes 14450688
  408.3 8.2 copy-start.23
  560.6 7.8 copy-start.6
  566.7 1.7 copy-start.2
  591.3 367.0 %all-gather.5.cloned.1.call-start = ((), (), s32[]{:S(2)}) async-start(), calls=%async_computation.4 | async-start | bytes 14450688 | tf_op jit(solution)/shard_map/all_gather | solution.py:224
  766.7 9.2 copy-start
  818.1 4.6 copy-start.20
  818.1 4.6 copy-start.22
  818.1 4.6 copy-start.26
  818.2 4.6 copy-start.28
  841.4 179.6 %all-reduce.13.cloned.1.call-start = ((), (), s32[]{:S(2)}) async-start(), calls=%async_computation.6 | async-start | bytes 2244608 | tf_op jit(solution)/shard_map/psum | solution.py:235
  847.5 6.0 copy-start.3
  853.6 8.1 copy-start.1
  880.6 87.8 %copy-start.5 = (f32[256,1024]{1,0:T(8,128)S(1)}, f32[256,1024]{1,0:T(8,128)}, u32[]{:S(2)}) copy-start(f32[256,1024]{1,0:T(8,128)} %param.21) | copy-start | bytes 3145732
  1029.6 22.7 %copy-start.24 = (f32[2,256]{1,0:T(2,128)S(1)}, f32[2,256]{1,0:T(2,128)}, u32[]{:S(2)}) copy-start(f32[2,256]{1,0:T(2,128)} %param.33) | copy-start | bytes 6148
  1029.6 22.7 %copy-start.29 = (f32[2,256]{1,0:T(2,128)S(1)}, f32[2,256]{1,0:T(2,128)}, u32[]{:S(2)}) copy-start(f32[2,256]{1,0:T(2,128)} %param.34) | copy-start | bytes 6148
  1029.6 22.7 %copy-start.30 = (f32[2,256]{1,0:T(2,128)S(1)}, f32[2,256]{1,0:T(2,128)}, u32[]{:S(2)}) copy-start(f32[2,256]{1,0:T(2,128)} %param.35) | copy-start | bytes 6148
  1029.6 23.3 %copy-start.18 = (f32[4,128]{1,0:T(4,128)S(1)}, f32[4,128]{1,0:T(4,128)}, u32[]{:S(2)}) copy-start(f32[4,128]{1,0:T(4,128)} %param.30) | copy-start | bytes 6148
  1029.6 23.3 %copy-start.31 = (f32[4,128]{1,0:T(4,128)S(1)}, f32[4,128]{1,0:T(4,128)}, u32[]{:S(2)}) copy-start(f32[4,128]{1,0:T(4,128)} %param.31) | copy-start | bytes 6148
  1029.6 23.3 %copy-start.32 = (f32[4,128]{1,0:T(4,128)S(1)}, f32[4,128]{1,0:T(4,128)}, u32[]{:S(2)}) copy-start(f32[4,128]{1,0:T(4,128)} %param.32) | copy-start | bytes 6148
  1029.7 23.9 %copy-start.13 = (f32[3,3,32,128]{3,2,1,0:T(8,128)S(1)}, f32[3,3,32,128]{3,2,1,0:T(8,128)}, u32[]{:S(2)}) copy-start(f32[3,3,32,128]{3,2,1,0:T(8,128)} %param.24) | copy-start | bytes 442372
  1029.7 23.9 %copy-start.14 = (bf16[3,3,32,128]{3,2,1,0:T(8,128)(2,1)S(1)}, bf16[3,3,32,128]{3,2,1,0:T(8,128)(2,1)}, u32[]{:S(2)}) copy-start(bf16[3,3,32,128]{3,2,1,0:T(8,128)(2,1)} %get-tuple-element.117) | copy-start | bytes 221188
  1029.7 23.9 %copy-start.15 = (f32[3,3,32,128]{3,2,1,0:T(8,128)S(1)}, f32[3,3,32,128]{3,2,1,0:T(8,128)}, u32[]{:S(2)}) copy-start(f32[3,3,32,128]{3,2,1,0:T(8,128)} %param.25) | copy-start | bytes 442372
  1029.7 23.9 %copy-start.16 = (f32[3,3,32,128]{3,2,1,0:T(8,128)S(1)}, f32[3,3,32,128]{3,2,1,0:T(8,128)}, u32[]{:S(2)}) copy-start(f32[3,3,32,128]{3,2,1,0:T(8,128)} %param.26) | copy-start | bytes 442372
  1029.7 24.8 %copy-start.7 = (f32[1024,256]{1,0:T(8,128)S(1)}, f32[1024,256]{1,0:T(8,128)}, u32[]{:S(2)}) copy-start(f32[1024,256]{1,0:T(8,128)} %param.27) | copy-start | bytes 3145732
  1029.7 24.8 %copy-start.9 = (bf16[1024,256]{1,0:T(8,128)(2,1)S(1)}, bf16[1024,256]{1,0:T(8,128)(2,1)}, u32[]{:S(2)}) copy-start(bf16[1024,256]{1,0:T(8,128)(2,1)} %get-tuple-element.118) | copy-start | bytes 1572868
  1054.5 4.2 copy-start.8
  1054.5 4.2 copy-start.10
  1054.5 4.2 copy-start.11
Sparse Core Ops, SparseCore 0:
  42.4 254.7 reduce-scatter.4
  401.1 116.8 all-gather.2
  591.4 129.0 reduce-scatter.6
  841.5 116.8 all-gather.4
  968.5 52.4 all-reduce.12
where the time goes:
time: 1080 us; the launch traced here: 1070 us
  waiting for transfers between devices  597 us (55%)
  local copies, waits for them, and re-layouts  207 us (19%)
  matrix products  101 us (9%)
  other arithmetic  73.4 us (7%)
  blocking collectives  71 us (7%)
  between operations  20 us (2%)
    reduce_scatter x1, waiting for transfers between devices, shards(): lax.psum_scatter(lax.dot_general(weight_block, pixels, (((0,), (1,)), (()...  254 us
    unnamed x6, waiting for transfers between devices  129 us
    all_gather x1, waiting for transfers between devices, shards(): mid_full = lax.all_gather(second_act, 'group', axis=0, tiled=True)  101 us
    all_gather x1, waiting for transfers between devices, shards(): gathered = lax.all_gather(first_grad, 'group', axis=0, tiled=True)  77.8 us
    psum x6, blocking collectives, channel_sums(): return lax.psum((sum_values, sum_squares), 'dp')  53.9 us
    unnamed x72, local copies, waits for them, and re-layouts  41.5 us
    another operation x2, local copies, waits for them, and re-layouts, from_grid(): flat_grid.reshape(channels, images, SRC, SRC)[:, :, 1:HW + 1, 1:HW + 1]  38 us
    psum x1, waiting for transfers between devices, shards(): lax.psum(reduce_wgrad.astype(jnp.bfloat16), 'dp').astype(jnp.float32)  34.4 us
  transfers between devices with their start and end apart: 5, of which 5 were waited for; matrix products, arithmetic and copies ran while one was open for 7% of the time, Pallas kernels for 0%

commit v1 on v0

v1 whole, which is shorter than its diff:
```python
import functools

import jax
import jax.numpy as jnp
from jax import lax
from jax.experimental import pallas as pl
from jax.experimental.pallas import tpu as pltpu
from jax.sharding import PartitionSpec as P

CIN = 2048
GW = 32
HW = 7
STEP = 10
MID = 1024
SRC = 9
NQ = 4
QW = MID // NQ
SPOTS = HW * HW

norm_eps = 1e-05
adam_eps = 1e-08
clip_norm = 1.0
moment_decay = 0.5

GELU_K = 0.7978845608028654
GELU_C = 0.044715
VMEM_MB = 56
BF = jnp.bfloat16
F32 = jnp.float32


def dot(a, b):
    return jnp.dot(a, b, preferred_element_type=F32)


def dot_t(a, b):
    return lax.dot_general(a, b, (((1,), (1,)), ((), ())), preferred_element_type=F32)


def dot_rows(a, b):
    return lax.dot_general(a, b, (((0,), (0,)), ((), ())), preferred_element_type=F32)


def gelu(u):
    t = jnp.tanh(GELU_K * (u + GELU_C * (u * u * u)))
    return 0.5 * u * (1.0 + t)


def gelu_both(u):
    u2 = u * u
    t = jnp.tanh(GELU_K * (u + GELU_C * (u2 * u)))
    half = 0.5 * (1.0 + t)
    slope = half + (0.5 * GELU_K) * u * (1.0 - t * t) * (1.0 + (3.0 * GELU_C) * u2)
    return u * half, slope


def norm_rows(total, squares, count):
    center = total / count
    spread = squares / count - center * center
    return center, lax.rsqrt(spread + norm_eps)


def whole(shape):
    return pl.BlockSpec(shape, lambda *_: (0,) * len(shape))


def call(body, name, grid, in_specs, out_specs, out_shape, scratch=(), flops=0, aliases=None):
    nbytes = sum(s.size * s.dtype.itemsize for s in jax.tree.leaves(out_shape))
    return pl.pallas_call(
        body,
        grid_spec=pltpu.PrefetchScalarGridSpec(
            num_scalar_prefetch=1,
            grid=grid,
            in_specs=in_specs,
            out_specs=out_specs,
            scratch_shapes=list(scratch),
        ),
        out_shape=out_shape,
        compiler_params=pltpu.CompilerParams(vmem_limit_bytes=VMEM_MB * 1024 * 1024),
        cost_estimate=pl.CostEstimate(flops=flops, bytes_accessed=3 * nbytes, transcendentals=0),
        input_output_aliases=aliases or {},
        name=name,
    )


def sds(shape, dtype):
    return jax.ShapeDtypeStruct(shape, dtype)


def crop_kernel(sc, src, off, out):
    images = src.shape[2]
    lanes = src.shape[3]
    row = jnp.broadcast_to(off[:, 0:1], (images, lanes))
    col = jnp.broadcast_to(off[:, 1:2], (images, lanes))
    r0, r1 = row == 0, row == 1
    c0, c1 = col == 0, col == 1

    def step(i, carry):
        for j in range(HW):
            picks = []
            for a in range(SRC - HW + 1):
                x0 = src[i + a, j].astype(F32)
                x1 = src[i + a, j + 1].astype(F32)
                x2 = src[i + a, j + 2].astype(F32)
                picks.append(jnp.where(c0, x0, jnp.where(c1, x1, x2)))
            best = jnp.where(r0, picks[0], jnp.where(r1, picks[1], picks[2]))
            out[i * HW + j] = best.astype(out.dtype)
        return carry

    lax.fori_loop(0, HW, step, 0)


def split_store(sc, k, value, own, other):
    q = sc[0] ^ k
    mine = (q // 2) == sc[1]

    @pl.when(mine)
    def _():
        own[pl.ds(q % 2, 1)] = value[None]

    @pl.when(jnp.logical_not(mine))
    def _():
        other[pl.ds(q % 2, 1)] = value.astype(other.dtype)[None]


def fill_quarters(sc, own, rec, quarters):
    for h in range(2):
        quarters[pl.ds(2 * sc[1] + h, 1)] = own[h : h + 1]
        quarters[pl.ds(2 * (1 - sc[1]) + h, 1)] = rec[h : h + 1]


def quarter(sc, quarters, k):
    return quarters[pl.ds(sc[0] ^ k, 1)][0]


def reduce_kernel(nz, sc, *refs):
    xs, ws, (own, other) = refs[:nz], refs[nz : nz + NQ], refs[nz + NQ :]
    x = jnp.concatenate([r[...] for r in xs], axis=1)
    for k in range(NQ):
        split_store(sc, k, dot(x, ws[k][...].reshape(x.shape[1], QW)), own, other)


def add_sums(sums, index, first, second):
    rows = jnp.concatenate(
        [jnp.sum(first, axis=0, keepdims=True), jnp.sum(second, axis=0, keepdims=True)], axis=0
    )
    sums[pl.ds(index, 1)] += rows[None]


def start_sums(sums):
    @pl.when(pl.program_id(0) == 0)
    def _():
        sums[...] = jnp.zeros_like(sums)


def first_sums_kernel(sc, own, rec, sums):
    start_sums(sums)
    for h in range(2):
        v = own[h] + rec[h].astype(F32)
        add_sums(sums, h, v, v * v)


def zero_border(pad, images):
    span = pad.shape[1]
    pad[0] = jnp.zeros_like(pad[0])
    pad[SRC - 1] = jnp.zeros_like(pad[0])
    edge = jnp.zeros((HW, images, pad.shape[2]), pad.dtype)
    pad[1 : HW + 1, 0:images] = edge
    pad[1 : HW + 1, span - images : span] = edge


def conv_kernel(count, images, sc, own, rec, tot, par, diag, act, v2, sums, pad):
    rows = HW * images
    center, inv = norm_rows(tot[0, 0:1], tot[0, 1:2], count)
    gain, shift = par[0, 0:1], par[0, 1:2]
    zero_border(pad, images)

    def fill(i, carry):
        at = pl.ds(pl.multiple_of(i * rows, rows), rows)
        v = own[0, at] + rec[0, at].astype(F32)
        a = gelu((v - center) * inv * gain + shift).astype(BF)
        act[0, at] = a
        pad[pl.ds(i + 1, 1), images : images + rows] = a[None]
        return carry

    lax.fori_loop(0, HW, fill, 0)
    sums[...] = jnp.zeros_like(sums)

    def taps(i, carry):
        acc = jnp.zeros((rows, QW), F32)
        for di in range(3):
            line = pad[pl.ds(i + di, 1)][0]
            for dj in range(3):
                acc = acc + dot(line[dj * images : dj * images + rows], diag[0, di * 3 + dj])
        v2[0, pl.ds(pl.multiple_of(i * rows, rows), rows)] = acc
        add_sums(sums, 0, acc, acc * acc)
        return carry

    lax.fori_loop(0, HW, taps, 0)


def second_act_kernel(count, sc, v2, tot, par, out):
    for h in range(2):
        center, inv = norm_rows(tot[h, 0:1], tot[h, 1:2], count)
        u = (v2[h] - center) * inv * par[h, 2:3] + par[h, 3:4]
        out[h] = gelu(u).astype(BF)


def expand_kernel(nz, sc, own, rec, *refs):
    ws, (e, sums, quarters) = refs[:NQ], refs[NQ:]
    start_sums(sums)
    fill_quarters(sc, own, rec, quarters)
    for d in range(nz):
        acc = dot(quarter(sc, quarters, 0), ws[0][d])
        for k in range(1, NQ):
            acc = acc + dot(quarter(sc, quarters, k), ws[k][d])
        e[d] = acc
        add_sums(sums, (sc[2] + (nz - d)) % nz, acc, acc * acc)


def out_kernel(nz, count, sc, e, tot, par, *refs):
    xs, cots, outs, (up, sums) = (
        refs[:nz],
        refs[nz : 2 * nz],
        refs[2 * nz : 3 * nz],
        refs[3 * nz :],
    )
    start_sums(sums)
    for d in range(nz):
        zs = (sc[2] + (nz - d)) % nz
        t = tot[pl.ds(zs, 1)][0]
        center, inv = norm_rows(t[0:1], t[1:2], count)
        hat = (e[d] - center) * inv
        value, slope = gelu_both(hat * par[d, 0:1] + par[d, 1:2] + xs[d][...].astype(F32))
        outs[d][...] = value.astype(BF)
        u = cots[d][...].astype(F32) * slope
        up[d] = u
        add_sums(sums, zs, u, u * hat)


def expand_back_kernel(nz, count, sc, e, up, tot, tot_b, par, *refs):
    ws, (eg, own, other) = refs[:NQ], refs[NQ:]
    grads = []
    for d in range(nz):
        zs = (sc[2] + (nz - d)) % nz
        t, b = tot[pl.ds(zs, 1)][0], tot_b[pl.ds(zs, 1)][0]
        center, inv = norm_rows(t[0:1], t[1:2], count)
        hat = (e[d] - center) * inv
        g = (inv * par[d, 0:1]) * (up[d] - b[0:1] / count - hat * (b[1:2] / count))
        grads.append(g.astype(BF))
        eg[d] = grads[d]
    for k in range(NQ):
        acc = dot_t(grads[0], ws[k][0])
        for d in range(1, nz):
            acc = acc + dot_t(grads[d], ws[k][d])
        split_store(sc, k, acc, own, other)


def second_up_kernel(count, sc, own, rec, v2, tot, par, up, sums):
    start_sums(sums)
    for h in range(2):
        center, inv = norm_rows(tot[h, 0:1], tot[h, 1:2], count)
        hat = (v2[h] - center) * inv
        slope = gelu_both(hat * par[h, 2:3] + par[h, 3:4])[1]
        u = (own[h] + rec[h].astype(F32)) * slope
        up[h] = u
        add_sums(sums, h, u, u * hat)


def conv_back_kernel(
    count, images, sc, up2, v2, tot2, tot2b, par, diag, own, rec, tot1, cg, up1, sums, pad
):
    rows = HW * images
    center2, inv2 = norm_rows(tot2[0, 0:1], tot2[0, 1:2], count)
    factor = inv2 * par[0, 2:3]
    mean_d, mean_x = tot2b[0, 0:1] / count, tot2b[0, 1:2] / count
    zero_border(pad, images)

    def fill(i, carry):
        at = pl.ds(pl.multiple_of(i * rows, rows), rows)
        hat = (v2[0, at] - center2) * inv2
        g = (factor * (up2[0, at] - mean_d - hat * mean_x)).astype(BF)
        cg[0, at] = g
        pad[pl.ds(i + 1, 1), images : images + rows] = g[None]
        return carry

    lax.fori_loop(0, HW, fill, 0)
    center, inv = norm_rows(tot1[0, 0:1], tot1[0, 1:2], count)
    sums[...] = jnp.zeros_like(sums)

    def taps(i, carry):
        at = pl.ds(pl.multiple_of(i * rows, rows), rows)
        acc = jnp.zeros((rows, QW), F32)
        for di in range(3):
            line = pad[pl.ds(i + 2 - di, 1)][0]
            for dj in range(3):
                start = (2 - dj) * images
                acc = acc + dot_t(line[start : start + rows], diag[0, di * 3 + dj])
        hat = (own[0, at] + rec[0, at].astype(F32) - center) * inv
        u = acc * gelu_both(hat * par[0, 0:1] + par[0, 1:2])[1]
        up1[0, at] = u
        add_sums(sums, 0, u, u * hat)
        return carry

    lax.fori_loop(0, HW, taps, 0)


def first_grad_kernel(count, sc, up1, own, rec, tot, tot_b, par, out):
    for h in range(2):
        center, inv = norm_rows(tot[h, 0:1], tot[h, 1:2], count)
        hat = (own[h] + rec[h].astype(F32) - center) * inv
        g = (inv * par[h, 0:1]) * (up1[h] - tot_b[h, 0:1] / count - hat * (tot_b[h, 1:2] / count))
        out[h] = g.astype(BF)


def input_grad_kernel(sc, own, rec, up, *refs):
    ws, (out, quarters) = refs[:NQ], refs[NQ:]
    fill_quarters(sc, own, rec, quarters)
    acc = up[0]
    for k in range(NQ):
        acc = acc + dot_t(quarter(sc, quarters, k), ws[k][0])
    out[...] = acc.astype(BF)


def reduce_wgrad_kernel(nz, sc, own, rec, *refs):
    xs, outs, quarters = refs[:nz], refs[nz : nz + NQ], refs[nz + NQ]
    fill_quarters(sc, own, rec, quarters)
    grads = jnp.concatenate([quarter(sc, quarters, k) for k in range(NQ)], axis=1)
    for d in range(nz):
        g = dot_rows(xs[d][...], grads)
        for k in range(NQ):
            outs[k][d] = g[:, k * QW : (k + 1) * QW].astype(BF)


def expand_wgrad_kernel(nz, sc, own, rec, eg, *refs):
    outs, quarters = refs[:NQ], refs[NQ]
    fill_quarters(sc, own, rec, quarters)
    width = eg.shape[2]
    grads = jnp.concatenate([eg[d] for d in range(nz)], axis=1)
    for k in range(NQ):
        g = dot_rows(quarter(sc, quarters, k), grads)
        for d in range(nz):
            outs[k][d] = g[:, d * width : (d + 1) * width].astype(BF)


def conv_wgrad_kernel(images, sc, act, cg, out, pad):
    rows = HW * images
    zero_border(pad, images)
    for i in range(HW):
        pad[i + 1, images : images + rows] = act[0, i * rows : (i + 1) * rows]
    grad = cg[0]
    group_row = lax.broadcasted_iota(jnp.int32, (QW, QW), 0) // GW
    group_col = lax.broadcasted_iota(jnp.int32, (QW, QW), 1) // GW
    keep = group_row == group_col
    for di in range(3):
        for dj in range(3):
            window = pad[di : di + HW, dj * images : dj * images + rows].reshape(HW * rows, QW)
            full = jnp.where(keep, dot_rows(window, grad), 0.0)
            out[0, di * 3 + dj] = jnp.sum(full.reshape(QW // GW, GW, QW), axis=0)


def place_kernel(sc, *refs):
    refs[-1][...] = refs[0][...].reshape(refs[-1].shape)


def adam_step(weight, gradient, momentum, variance, learn_rate, decay_rate):
    momentum_new = moment_decay * momentum + (1.0 - moment_decay) * gradient
    variance_new = moment_decay * variance + (1.0 - moment_decay) * gradient * gradient
    correction = 1.0 - moment_decay**STEP
    direction = momentum_new / correction / (jnp.sqrt(variance_new / correction) + adam_eps)
    weight_new = weight - learn_rate * (direction + decay_rate * weight)
    return (weight_new, momentum_new, variance_new, weight_new.astype(BF))


def shards(
    source,
    offsets,
    cotangent,
    reduce_weight,
    reduce_first,
    reduce_second,
    group_weight,
    group_first,
    group_second,
    expand_weight,
    expand_first,
    expand_second,
    mid_norms,
    mid_first,
    mid_second,
    out_norms,
    out_first,
    out_second,
):
    nd, ng = lax.axis_size("dp"), lax.axis_size("group")
    nz = ng // 2
    gi = lax.axis_index("group")
    z, core = gi // 2, gi % 2
    p = lax.axis_index("dp") % NQ
    sc = jnp.stack([p, core, z]).astype(jnp.int32)
    n = source.shape[0]
    images = n // nz
    rows = SPOTS * images
    step = HW * images
    cb = source.shape[3]
    mb = group_weight.shape[3]
    zh = nz // 2
    count = float(SPOTS * n * nd)

    def over_z(value, d):
        pairs = [(2 * a + c, 2 * ((a + d) % nz) + c) for a in range(nz) for c in range(2)]
        return lax.ppermute(value, "group", pairs)

    def over_core(value):
        return lax.ppermute(value, "group", [(a, a ^ 1) for a in range(ng)])

    def over_dp(value, k):
        return lax.ppermute(value, "dp", [(a, a ^ k) for a in range(nd)])

    def everywhere(value):
        k = 1
        while k < nd:
            value = value + over_dp(value, k)
            k *= 2
        k = 2
        while k < ng:
            value = value + lax.ppermute(value, "group", [(a, a ^ k) for a in range(ng)])
            k *= 2
        return value

    col_starts = [((p % 2) * zh + j) * 2 * mb + (p // 2) * mb for j in range(zh)]
    reduce_piece = jnp.concatenate(
        [lax.dynamic_slice_in_dim(reduce_weight, s, mb, 1) for s in col_starts], axis=1
    ).astype(BF)
    expand_piece = (
        lax.dynamic_slice(
            expand_weight.reshape(nz, 2, mb, cb),
            ((p % 2) * zh, p // 2, 0, 0),
            (zh, 1, mb, cb),
        )
        .reshape(QW, cb)
        .astype(BF)
    )

    def spread_weight(piece):
        mine = jnp.stack([piece] + [over_z(piece, d) for d in range(1, nz)])
        return [mine] + [over_dp(mine, k) for k in range(1, NQ)]

    reduce_q = spread_weight(reduce_piece)
    taps_rows = 9 * GW
    pack = jnp.concatenate(
        [group_weight.reshape(taps_rows, mb), mid_norms, out_norms.reshape(-1, mb)], axis=0
    )
    packs = [pack] + [over_z(pack, d) for d in range(1, nz)]
    by_z = jnp.zeros((nz,) + pack.shape, F32)
    for d in range(nz):
        by_z = lax.dynamic_update_slice(by_z, packs[d][None], ((z + nz - d) % nz, 0, 0))
    half = by_z.transpose(1, 0, 2).reshape(pack.shape[0], 2, QW)
    mid_par = half[taps_rows : taps_rows + 4].transpose(1, 0, 2)
    out_par = jnp.stack([v[taps_rows + 4 :].reshape(2, cb) for v in packs])
    conv_low = half[:taps_rows].astype(BF).reshape(9, 1, GW, 2, QW).transpose(3, 0, 1, 2, 4)
    own_group = (jnp.arange(QW) // GW)[None, :] == jnp.arange(QW // GW)[:, None]
    diag = jnp.where(own_group[:, None, :], conv_low, jnp.zeros((), BF)).reshape(2, 9, QW, QW)

    src = source.transpose(1, 2, 0, 3)
    pixels = []
    lane = 128 if cb % 128 == 0 else cb
    for d in range(nz):
        crop = call(
            crop_kernel,
            "crop",
            (cb // lane,),
            [
                pl.BlockSpec(
                    (SRC, SRC, images, lane), lambda i, s, d=d: (0, 0, (s[2] + d) % nz, i)
                ),
                pl.BlockSpec((images, 2), lambda i, s, d=d: ((s[2] + d) % nz, 0)),
            ],
            pl.BlockSpec((SPOTS, images, lane), lambda i, s: (0, 0, i)),
            sds((SPOTS, images, cb), BF),
        )(sc, src, offsets)
        crop = crop.reshape(rows, cb)
        pixels.append(over_z(crop, d) if d else crop)
    cot = cotangent.transpose(1, 2, 0, 3).reshape(SPOTS, n, cb)
    cots = []
    for d in range(nz):
        piece = lax.dynamic_slice_in_dim(cot, ((z + d) % nz) * images, images, 1)
        piece = piece.reshape(rows, cb)
        cots.append(over_z(piece, d) if d else piece)
    expand_q = spread_weight(expand_piece)

    grid = (HW,)
    block2 = pl.BlockSpec((2, step, QW), lambda i, s: (0, i, 0))
    blockz = pl.BlockSpec((nz, step, cb), lambda i, s: (0, i, 0))
    rowc = pl.BlockSpec((step, cb), lambda i, s: (i, 0))
    sum2, sumz = whole((2, 2, QW)), whole((nz, 2, cb))
    par2 = whole((2, 4, QW))
    wr, we = whole((nz, cb, QW)), whole((nz, QW, cb))
    half_f, half_b = sds((2, rows, QW), F32), sds((2, rows, QW), BF)
    sum2_s, sumz_s = sds((2, 2, QW), F32), sds((nz, 2, cb), F32)
    per_h = pl.BlockSpec((1, rows, QW), lambda i, s: (i, 0, 0))
    sum_h = pl.BlockSpec((1, 2, QW), lambda i, s: (i, 0, 0))
    par_h = pl.BlockSpec((1, 4, QW), lambda i, s: (i, 0, 0))
    diag_h = pl.BlockSpec((1, 9, QW, QW), lambda i, s: (i, 0, 0, 0))
    pad_s = pltpu.VMEM((SRC, SRC * images, QW), BF)
    quarters_s = pltpu.VMEM((NQ, step, QW), BF)
    big = 2 * rows * MID * MID

    own1, oth1 = call(
        functools.partial(reduce_kernel, nz),
        "reduce",
        grid,
        [rowc] * nz + [wr] * NQ,
        [block2, block2],
        [half_f, half_b],
        flops=big,
    )(sc, *pixels, *reduce_q)
    rec1 = over_core(oth1)
    tot1 = everywhere(
        call(first_sums_kernel, "first_sums", grid, [block2, block2], sum2, sum2_s)(sc, own1, rec1)
    )
    act, v2, sums2 = call(
        functools.partial(conv_kernel, count, images),
        "conv",
        (2,),
        [per_h, per_h, sum_h, par_h, diag_h],
        [per_h, per_h, sum_h],
        [half_b, half_f, sum2_s],
        [pad_s],
        flops=big,
    )(sc, own1, rec1, tot1, mid_par, diag)
    tot2 = everywhere(sums2)
    sa = call(
        functools.partial(second_act_kernel, count),
        "second_act",
        grid,
        [block2, sum2, par2],
        block2,
        half_b,
    )(sc, v2, tot2, mid_par)
    sa_rec = over_core(sa)
    e, sums3 = call(
        functools.partial(expand_kernel, nz),
        "expand",
        grid,
        [block2, block2] + [we] * NQ,
        [blockz, sumz],
        [sds((nz, rows, cb), F32), sumz_s],
        [quarters_s],
        flops=big,
    )(sc, sa, sa_rec, *expand_q)
    tot3 = everywhere(sums3)
    res = call(
        functools.partial(out_kernel, nz, count),
        "out",
        grid,
        [blockz, sumz, whole((nz, 2, cb))] + [rowc] * (2 * nz),
        [rowc] * nz + [blockz, sumz],
        [sds((rows, cb), BF)] * nz + [sds((nz, rows, cb), F32), sumz_s],
    )(sc, e, tot3, out_par, *pixels, *cots)
    outs, up3, sums3b = res[:nz], res[nz], res[nz + 1]
    tot3b = everywhere(sums3b)

    def place(blocks):
        shape = sds((SPOTS, n, cb), BF)
        result = None
        for d in range(nz):
            spec = pl.BlockSpec((SPOTS, images, cb), lambda i, s, d=d: (0, (s[2] + d) % nz, 0))
            inputs = [blocks[d]]
            in_specs = [whole((rows, cb))]
            aliases = {}
            if result is not None:
                inputs.append(result)
                in_specs.append(pl.BlockSpec(memory_space=pl.ANY))
                aliases = {2: 0}
            result = call(place_kernel, "place", (1,), in_specs, spec, shape, aliases=aliases)(
                sc, *inputs
            )
        return result.reshape(HW, HW, n, cb).transpose(2, 0, 1, 3)

    output = place([over_z(outs[d], -d) if d else outs[0] for d in range(nz)])

    eg, own2, oth2 = call(
        functools.partial(expand_back_kernel, nz, count),
        "expand_back",
        grid,
        [blockz, blockz, sumz, sumz, whole((nz, 2, cb))] + [we] * NQ,
        [blockz, block2, block2],
        [sds((nz, rows, cb), BF), half_f, half_b],
        flops=big,
    )(sc, e, up3, tot3, tot3b, out_par, *expand_q)
    rec2 = over_core(oth2)
    up2, sums2b = call(
        functools.partial(second_up_kernel, count),
        "second_up",
        grid,
        [block2, block2, block2, sum2, par2],
        [block2, sum2],
        [half_f, sum2_s],
    )(sc, own2, rec2, v2, tot2, mid_par)
    tot2b = everywhere(sums2b)
    cg, up1, sums1b = call(
        functools.partial(conv_back_kernel, count, images),
        "conv_back",
        (2,),
        [per_h, per_h, sum_h, sum_h, par_h, diag_h, per_h, per_h, sum_h],
        [per_h, per_h, sum_h],
        [half_b, half_f, sum2_s],
        [pad_s],
        flops=big,
    )(sc, up2, v2, tot2, tot2b, mid_par, diag, own1, rec1, tot1)
    tot1b = everywhere(sums1b)
    fg = call(
        functools.partial(first_grad_kernel, count),
        "first_grad",
        grid,
        [block2, block2, block2, sum2, sum2, par2],
        block2,
        half_b,
    )(sc, up1, own1, rec1, tot1, tot1b, mid_par)
    fg_rec = over_core(fg)
    input_blocks = [None] * nz
    for d in list(range(1, nz)) + [0]:
        block = call(
            input_grad_kernel,
            "input_grad",
            grid,
            [
                block2,
                block2,
                pl.BlockSpec((1, step, cb), lambda i, s, d=d: (d, i, 0)),
            ]
            + [pl.BlockSpec((1, cb, QW), lambda i, s, d=d: (d, 0, 0))] * NQ,
            rowc,
            sds((rows, cb), BF),
            [quarters_s],
            flops=big // nz,
        )(sc, fg, fg_rec, up3, *reduce_q)
        input_blocks[d] = over_z(block, -d) if d else block
    input_grad = place(input_blocks)

    full2 = whole((2, rows, QW))
    quarters_full = pltpu.VMEM((NQ, rows, QW), BF)
    expand_parts = call(
        functools.partial(expand_wgrad_kernel, nz),
        "expand_wgrad",
        (1,),
        [full2, full2, whole((nz, rows, cb))],
        [we] * NQ,
        [sds((nz, QW, cb), BF)] * NQ,
        [quarters_full],
        flops=big,
    )(sc, sa, sa_rec, eg)
    reduce_parts = call(
        functools.partial(reduce_wgrad_kernel, nz),
        "reduce_wgrad",
        (1,),
        [full2, full2] + [whole((rows, cb))] * nz,
        [wr] * NQ,
        [sds((nz, cb, QW), BF)] * NQ,
        [quarters_full],
        flops=big,
    )(sc, fg, fg_rec, *pixels)
    conv_part = call(
        functools.partial(conv_wgrad_kernel, images),
        "conv_wgrad",
        (2,),
        [per_h, per_h],
        pl.BlockSpec((1, 9, GW, QW), lambda i, s: (i, 0, 0, 0)),
        sds((2, 9, GW, QW), F32),
        [pad_s],
        flops=big,
    )(sc, act, cg)

    def low_sum(mine, others):
        total = mine.astype(F32)
        for value in others:
            total = total + value.astype(F32)
        return total

    def home(parts):
        total = low_sum(parts[0], [over_dp(parts[k], k) for k in range(1, NQ)])
        low = total.astype(BF)
        total = low_sum(total[0], [over_z(low[d], -d) for d in range(1, nz)])
        k = NQ
        while k < nd:
            total = low_sum(total, [over_dp(total.astype(BF), k)])
            k *= 2
        low = total.astype(BF)
        pieces = [low] + [over_dp(low, k) for k in range(1, NQ)]
        result = []
        for q in range(NQ):
            k = p ^ q
            value = pieces[NQ - 1]
            for j in range(NQ - 1):
                value = jnp.where(k == j, pieces[j], value)
            result.append(value.astype(F32))
        return result

    blocks = [(a, c, 2 * c + a // zh, (a % zh) * mb) for a in range(nz) for c in range(2)]
    expand_home = home(expand_parts)
    expand_wgrad = jnp.concatenate([expand_home[q][s : s + mb] for _, _, q, s in blocks], axis=0)
    reduce_home = home(reduce_parts)
    reduce_wgrad = jnp.concatenate([reduce_home[q][:, s : s + mb] for _, _, q, s in blocks], axis=1)

    conv_all = conv_part.transpose(1, 2, 0, 3).reshape(taps_rows, nz, mb).transpose(1, 0, 2)
    conv_low_part = conv_all.astype(BF)

    def conv_at(d):
        return lax.dynamic_index_in_dim(conv_low_part, (z + d) % nz, 0, keepdims=False)

    conv_total = low_sum(conv_at(0), [over_z(conv_at(d), d) for d in range(1, nz)])
    k = 1
    while k < nd:
        low = conv_total.astype(BF)
        conv_total = low_sum(low, [over_dp(low, k)])
        k *= 2
    group_wgrad = conv_total.reshape(group_weight.shape)

    def my_mid(total):
        lanes = lax.dynamic_slice_in_dim(total.transpose(1, 0, 2).reshape(2, 2 * QW), z * mb, mb, 1)
        return [lanes[1], lanes[0]]

    mid_grads = jnp.stack(my_mid(tot1b) + my_mid(tot2b))
    mine3 = lax.dynamic_index_in_dim(tot3b, z, 0, keepdims=False)
    out_grads = jnp.stack([mine3[1], mine3[0]])

    local_sq = jnp.zeros((), F32)
    for grad_item in (reduce_wgrad, group_wgrad, expand_wgrad, mid_grads, out_grads):
        local_sq = local_sq + jnp.sum(grad_item * grad_item)
    total_sq = jnp.broadcast_to(local_sq, (8, 128))
    k = 1
    while k < ng:
        total_sq = total_sq + lax.ppermute(total_sq, "group", [(a, a ^ k) for a in range(ng)])
        k *= 2
    grad_norm = jnp.sqrt(total_sq[0, 0])
    clip_scale = jnp.minimum(1.0, clip_norm / (grad_norm + 1e-06))
    reduce_out = adam_step(
        reduce_weight,
        reduce_wgrad * clip_scale,
        reduce_first,
        reduce_second,
        1.0 / jnp.sqrt(1.0 * CIN),
        0.1,
    )
    group_out = adam_step(
        group_weight,
        group_wgrad * clip_scale,
        group_first,
        group_second,
        1.0 / jnp.sqrt(9.0 * GW),
        0.1,
    )
    expand_out = adam_step(
        expand_weight,
        expand_wgrad * clip_scale,
        expand_first,
        expand_second,
        1.0 / jnp.sqrt(1.0 * MID),
        0.1,
    )
    mid_out = adam_step(mid_norms, mid_grads * clip_scale, mid_first, mid_second, 0.5, 0.0)
    out_out = adam_step(out_norms, out_grads * clip_scale, out_first, out_second, 0.5, 0.0)
    return (
        output,
        input_grad,
        grad_norm,
        *reduce_out,
        *group_out,
        *expand_out,
        *mid_out,
        *out_out,
    )


def solution(mesh):
    images = P("dp", None, None, "group")
    rows, cols = P("group", None), P(None, "group")
    kernel = P(None, None, None, "group")
    in_specs = (
        (images, P("dp", None), images) + (rows,) * 3 + (kernel,) * 3 + (cols,) * 3 + (cols,) * 6
    )
    out_specs = (images, images, P()) + (rows,) * 4 + (kernel,) * 4 + (cols,) * 4 + (cols,) * 8
    return jax.shard_map(shards, mesh=mesh, in_specs=in_specs, out_specs=out_specs, check_vma=False)
```

time: 1080 us -> 677 us (0.63)
  waiting for transfers between devices: 597 us -> 277 us
  Pallas kernels: 0 us -> 204 us
  local copies, waits for them, and re-layouts: 207 us -> 36.3 us
  starting transfers between devices: 0.21 us -> 121 us
  matrix products: 101 us -> 0 us
  blocking collectives: 71 us -> 0 us
  other arithmetic: 73.4 us -> 29 us
  between operations: 20 us -> 6.54 us
    ppermute x0 -> x81, waiting for transfers between devices: none -> 277 us  [the longest x32 95.6 us: over_dp(): return lax.ppermute(value, 'dp', [(a, a ^ k) for a in range(nd)])]
    reduce_scatter x1 -> x0, waiting for transfers between devices: 254 us -> none  [shards(): lax.psum_scatter(lax.dot_general(weight_block, pixels, (((0,), (1,)), (()...]
    pallas_call x0 -> x29, Pallas kernels: none -> 204 us  [the longest x4 30.5 us: shards(): call(input_grad_kernel, 'input_grad', grid, [block2, block2, pl.BlockSpec...]
    all_gather x2 -> x0, waiting for transfers between devices: 179 us -> none  [the longest x1 101 us: shards(): mid_full = lax.all_gather(second_act, 'group', axis=0, tiled=True)]
    unnamed x6 -> x0, waiting for transfers between devices: 129 us -> none
    ppermute x0 -> x81, starting transfers between devices: none -> 121 us  [the longest x30 69.5 us: over_z(): return lax.ppermute(value, 'group', pairs)]
    dot_general x33 -> x0, matrix products: 101 us -> none  [the longest x9 17.2 us: conv_backward(): jnp.einsum('gik,gok->gio', act_window, grad_middle, preferred_element_typ...]
    psum x7 -> x0, blocking collectives: 71 us -> none  [the longest x6 53.9 us: channel_sums(): return lax.psum((sum_values, sum_squares), 'dp')]
  transfers between devices with their start and end apart: 5 -> 81, of which waited for: 5 -> 41; matrix products, arithmetic and copies ran while one was open for 7% -> 8% of each run, Pallas kernels for 0% -> 16%
where the time goes in v1:
time: 677 us; the launch traced here: 674 us
  waiting for transfers between devices  277 us (41%)
  Pallas kernels  204 us (30%)
  starting transfers between devices  121 us (18%)
  local copies, waits for them, and re-layouts  36.3 us (5%)
  other arithmetic  29 us (4%)
    ppermute x32, waiting for transfers between devices, over_dp(): return lax.ppermute(value, 'dp', [(a, a ^ k) for a in range(nd)])  95.6 us
    ppermute x30, waiting for transfers between devices, over_z(): return lax.ppermute(value, 'group', pairs)  86.7 us
    ppermute x30, starting transfers between devices, over_z(): return lax.ppermute(value, 'group', pairs)  69.5 us
    ppermute x12, waiting for transfers between devices, everywhere(): lax.ppermute(value, 'group', [(a, a ^ k) for a in range(ng)])  59.1 us
    ppermute x32, starting transfers between devices, over_dp(): return lax.ppermute(value, 'dp', [(a, a ^ k) for a in range(nd)])  38.9 us
    ppermute x3, waiting for transfers between devices, shards(): lax.ppermute(total_sq, 'group', [(a, a ^ k) for a in range(ng)])  32.1 us
    pallas_call x4, Pallas kernels, shards(): call(input_grad_kernel, 'input_grad', grid, [block2, block2, pl.BlockSpec...  30.5 us
    pallas_call x8, Pallas kernels, place(): call(place_kernel, 'place', (1,), in_specs, spec, shape, aliases=aliases)  22.1 us
  transfers between devices with their start and end apart: 81, of which 41 were waited for; matrix products, arithmetic and copies ran while one was open for 8% of the time, Pallas kernels for 16%

profile of v1, /device:TPU:0, one launch (start us, length us, event | category | flops | bytes accessed | tf_op | source)
XLA Modules:
  0.0 673.8 jit_solution(6679044978231168144)
XLA Ops:
  1.7 5.1 collective-permute-start.5
  10.7 7.3 %collective-permute-done.4 = bf16[256,256]{1,0:T(8,128)(2,1)S(1)} collective-permute-done((bf16[256,256]{1,0:T(8,128)(2,1)S(1)}, bf16[256,256]{1,0:T(8,128)(2,1)S(1)}, u32[]{:S(2)}, u32[]{:S(2)}) %collective-permute-start.4) | collective-permute-done | bytes 131104 | tf_op jit(solution)/shard_map/ppermute | solution.py:412
  43.0 17.7 %collective-permute-done.7.refs_6_.refs_2_ = bf16[4,256,256]{2,1,0:T(8,128)(2,1)S(1)} collective-permute-done((bf16[4,256,256]{2,1,0:T(8,128)(2,1)S(1)}, bf16[4,256,256]{2,1,0:T(8,128)(2,1)S(1)}, u32[]{:S(2)}, u32[]{:S(2)}) %collective-permute-start.7) | collective-permute-done | bytes 524320 | tf_op jit(solution)/shard_map/ppermute | solution.py:418
  60.8 19.8 %collective-permute-done.1.refs_2_ = bf16[1568,256]{1,0:T(8,128)(2,1)S(1)} collective-permute-done((bf16[1568,256]{1,0:T(8,128)(2,1)}, bf16[1568,256]{1,0:T(8,128)(2,1)S(1)}, u32[]{:S(2)}, u32[]{:S(2)}) %collective-permute-start.1) | collective-permute-done | bytes 802848 | tf_op jit(solution)/shard_map/ppermute | solution.py:412
  81.7 14.9 %reduce.2 = (f32[2,1568,256]{2,1,0:T(8,128)}, bf16[2,1568,256]{2,1,0:T(8,128)(2,1)}) custom-call(s32[3]{0:T(128)} %pad_add_fusion.sc, bf16[1568,256]{1,0:T(8,128)(2,1)} %bitcast.118, bf16[1568,256]{1,0:T(8,128)(2,1)} %copy-done.12, bf16[1568,256]{1,0:T(8,128)(2,1)} %copy-done.13, bf16[1568,256]{1,0:T(8,128)(2,1)} %copy-done.14, ...), custom_call_target="tpu_custom_call" | custom-call | flops 3288334336 | bytes 14450688 | tf_op jit(solution)/shard_map/reduce/pallas_call | solution.py:509
  96.7 3.6 collective-permute-done.9.rec
  101.5 6.1 first_sums.1
  108.2 17.5 %collective-permute-start.14 = (f32[296,128]{1,0:T(8,128)S(1)}, f32[296,128]{1,0:T(8,128)S(1)}, u32[]{:S(2)}, u32[]{:S(2)}) collective-permute-start(f32[296,128]{1,0:T(8,128)S(1)} %pad_maximum_fusion.2), channel_id=1, source_target_pairs={{0,2},{1,3},{2,4},{3,5},{4,6},{5,7},{6,0},{7,1},{8,10},{9,11},{10,... | collective-permute-start | bytes 454664 | tf_op jit(solution)/shard_map/ppermute | solution.py:412
  138.2 4.5 dynamic_update_slice.12
  142.7 4.5 dynamic_update_slice.13
  147.2 4.5 dynamic_update_slice.14
  151.7 4.5 dynamic_update_slice.15
  159.4 12.5 %conv.1 = (bf16[2,1568,256]{2,1,0:T(8,128)(2,1)}, f32[2,1568,256]{2,1,0:T(8,128)}, f32[2,2,256]{2,1,0:T(2,128)}) custom-call(s32[3]{0:T(128)} %pad_add_fusion.sc, f32[2,1568,256]{2,1,0:T(8,128)} %get-tuple-element.52.own, bf16[2,1568,256]{2,1,0:T(8,128)(2,1)} %copy-done.1, f32[2,2,256]{2,1,0:T(2,128)} %add.353.tot.tot1, f32[2,4,256]{2,1,0:T(4,128)} %bitcast.141, ...), custom_call_target="tpu_custom_call" | custom-call | flops 3288334336 | bytes 14462976 | tf_op jit(solution)/shard_map/conv/pallas_call | solution.py:522
  188.8 6.7 second_act.1.own
  202.7 8.5 %collective-permute-done.23 = bf16[256,256]{1,0:T(8,128)(2,1)S(1)} collective-permute-done((bf16[256,256]{1,0:T(8,128)(2,1)S(1)}, bf16[256,256]{1,0:T(8,128)(2,1)S(1)}, u32[]{:S(2)}, u32[]{:S(2)}) %collective-permute-start.23) | collective-permute-done | bytes 131104 | tf_op jit(solution)/shard_map/ppermute | solution.py:412
  217.6 9.7 %collective-permute-done.25.refs_1_ = bf16[4,256,256]{2,1,0:T(8,128)(2,1)} collective-permute-done((bf16[4,256,256]{2,1,0:T(8,128)(2,1)}, bf16[4,256,256]{2,1,0:T(8,128)(2,1)}, u32[]{:S(2)}, u32[]{:S(2)}) %collective-permute-start.25) | collective-permute-done | bytes 524320 | tf_op jit(solution)/shard_map/ppermute | solution.py:418
  229.4 8.1 %collective-permute-done.26.refs_2_ = bf16[4,256,256]{2,1,0:T(8,128)(2,1)} collective-permute-done((bf16[4,256,256]{2,1,0:T(8,128)(2,1)}, bf16[4,256,256]{2,1,0:T(8,128)(2,1)}, u32[]{:S(2)}, u32[]{:S(2)}) %collective-permute-start.26) | collective-permute-done | bytes 524320 | tf_op jit(solution)/shard_map/ppermute | solution.py:418
  239.2 10.3 %expand.1 = (f32[4,1568,256]{2,1,0:T(8,128)}, f32[4,2,256]{2,1,0:T(2,128)}) custom-call(s32[3]{0:T(128)} %pad_add_fusion.sc, bf16[2,1568,256]{2,1,0:T(8,128)(2,1)} %second_act.1.own, bf16[2,1568,256]{2,1,0:T(8,128)(2,1)} %collective-permute-done.21.rec, bf16[4,256,256]{2,1,0:T(8,128)(2,1)} %pad_maximum_fusion.1.refs_0_, ...), custom_call_target="tpu_custom_call" | custom-call | flops 3288334336 | bytes 19292160 | tf_op jit(solution)/shard_map/expand/pallas_call | solution.py:542
  260.8 12.0 %collective-permute-done.30 = f32[4,2,256]{2,1,0:T(2,128)S(1)} collective-permute-done((f32[4,2,256]{2,1,0:T(2,128)S(1)}, f32[4,2,256]{2,1,0:T(2,128)S(1)}, u32[]{:S(2)}, u32[]{:S(2)}) %collective-permute-start.30) | collective-permute-done | bytes 8224 | tf_op jit(solution)/shard_map/ppermute | solution.py:427
  274.2 16.1 %collective-permute-done.31 = f32[4,2,256]{2,1,0:T(2,128)S(1)} collective-permute-done((f32[4,2,256]{2,1,0:T(2,128)S(1)}, f32[4,2,256]{2,1,0:T(2,128)S(1)}, u32[]{:S(2)}, u32[]{:S(2)}) %collective-permute-start.31) | collective-permute-done | bytes 8224 | tf_op jit(solution)/shard_map/ppermute | solution.py:427
  292.3 13.7 %out.1 = (bf16[1568,256]{1,0:T(8,128)(2,1)}, bf16[1568,256]{1,0:T(8,128)(2,1)}, bf16[1568,256]{1,0:T(8,128)(2,1)}, bf16[1568,256]{1,0:T(8,128)(2,1)}, f32[4,1568,256]{2,1,0:T(8,128)}, /*index=5*/f32[4,2,256]{2,1,0:T(2,128)}) custom-call(s32[3]{0:T(128)} %pad_add_fusion.sc, f32[4,1568,256]{2,1,0:T(8,128)} %get-tuple-element.56.e, f32[4,2,256]{2,1,0:T(2,128)} %add.372.tot, ...), custom_call_target="tpu_custom_call" | custom-call | bytes 28925952 | tf_op jit(solution)/shard_map/out/pallas_call | solution.py:553
  314.3 3.7 collective-permute-done.40
  318.0 4.5 collective-permute-done.41
  323.1 17.1 %expand_back.1 = (bf16[4,1568,256]{2,1,0:T(8,128)(2,1)}, f32[2,1568,256]{2,1,0:T(8,128)}, bf16[2,1568,256]{2,1,0:T(8,128)(2,1)}) custom-call(s32[3]{0:T(128)} %pad_add_fusion.sc, f32[4,1568,256]{2,1,0:T(8,128)} %get-tuple-element.56.e, f32[4,1568,256]{2,1,0:T(8,128)} %get-tuple-element.62.up, f32[4,2,256]{2,1,0:T(2,128)} %add.372.tot, ...), custom_call_target="tpu_custom_call" | custom-call | flops 3288334336 | bytes 24084480 | tf_op jit(solution)/shard_map/expand_back/pallas_call | solution.py:583
  340.2 8.7 %expand_wgrad.1 = (bf16[4,256,256]{2,1,0:T(8,128)(2,1)}, bf16[4,256,256]{2,1,0:T(8,128)(2,1)}, bf16[4,256,256]{2,1,0:T(8,128)(2,1)}, bf16[4,256,256]{2,1,0:T(8,128)(2,1)}) custom-call(s32[3]{0:T(128)} %pad_add_fusion.sc, bf16[2,1568,256]{2,1,0:T(8,128)(2,1)} %second_act.1.own, bf16[2,1568,256]{2,1,0:T(8,128)(2,1)} %collective-permute-done.21.rec, ...), custom_call_target="tpu_custom_call" | custom-call | flops 3288334336 | bytes 6291456 | tf_op jit(solution)/shard_map/expand_wgrad/pallas_call | solution.py:644
  352.4 12.4 %collective-permute-done.71 = bf16[4,256,256]{2,1,0:T(8,128)(2,1)S(1)} collective-permute-done((bf16[4,256,256]{2,1,0:T(8,128)(2,1)}, bf16[4,256,256]{2,1,0:T(8,128)(2,1)S(1)}, u32[]{:S(2)}, u32[]{:S(2)}) %collective-permute-start.71) | collective-permute-done | bytes 524320 | tf_op jit(solution)/shard_map/ppermute | solution.py:418
  364.8 10.8 %collective-permute-done.70 = bf16[4,256,256]{2,1,0:T(8,128)(2,1)S(1)} collective-permute-done((bf16[4,256,256]{2,1,0:T(8,128)(2,1)}, bf16[4,256,256]{2,1,0:T(8,128)(2,1)S(1)}, u32[]{:S(2)}, u32[]{:S(2)}) %collective-permute-start.70) | collective-permute-done | bytes 524320 | tf_op jit(solution)/shard_map/ppermute | solution.py:418
  379.0 32.3 %collective-permute-done.74 = bf16[256,256]{1,0:T(8,128)(2,1)S(1)} collective-permute-done((bf16[256,256]{1,0:T(8,128)(2,1)S(1)}, bf16[256,256]{1,0:T(8,128)(2,1)S(1)}, u32[]{:S(2)}, u32[]{:S(2)}) %collective-permute-start.74) | collective-permute-done | bytes 131104 | tf_op jit(solution)/shard_map/ppermute | solution.py:412
  411.3 16.0 %collective-permute-start.73 = (bf16[256,256]{1,0:T(8,128)(2,1)S(1)}, bf16[256,256]{1,0:T(8,128)(2,1)S(1)}, u32[]{:S(2)}, u32[]{:S(2)}) collective-permute-start(bf16[256,256]{1,0:T(8,128)(2,1)S(1)} %get-tuple-element.117), channel_id=1, source_target_pairs={{0,4},{1,5},{2,6},{3,7},{4,0},{5,1},{6,2},{7,3},{8,12},{9,13},{10,... | collective-permute-start | bytes 393224 | tf_op jit(solution)/shard_map/ppermute | solution.py:412
  428.4 8.9 %second_up.1 = (f32[2,1568,256]{2,1,0:T(8,128)}, f32[2,2,256]{2,1,0:T(2,128)}) custom-call(s32[3]{0:T(128)} %pad_add_fusion.sc, f32[2,1568,256]{2,1,0:T(8,128)} %get-tuple-element.64.own, bf16[2,1568,256]{2,1,0:T(8,128)(2,1)} %copy-done.7, f32[2,1568,256]{2,1,0:T(8,128)} %get-tuple-element.54.v2, f32[2,2,256]{2,1,0:T(2,128)} %add.366.tot.tot2, ...), custom_call_target="tpu_custom_call" | custom-call | bytes 9646080 | tf_op jit(solution)/shard_map/second_up/pallas_call | solution.py:593
  461.1 4.5 collective-permute-done.46
  466.2 15.0 %conv_back.1 = (bf16[2,1568,256]{2,1,0:T(8,128)(2,1)}, f32[2,1568,256]{2,1,0:T(8,128)}, f32[2,2,256]{2,1,0:T(2,128)}) custom-call(s32[3]{0:T(128)} %pad_add_fusion.sc, f32[2,1568,256]{2,1,0:T(8,128)} %get-tuple-element.66.up2, f32[2,1568,256]{2,1,0:T(8,128)} %get-tuple-element.54.v2, f32[2,2,256]{2,1,0:T(2,128)} %add.366.tot.tot2, f32[2,2,256]{2,1,0:T(2,128)} %add.385.tot2b, ...), custom_call_target="tpu_custom_call" | custom-call | flops 3288334336 | bytes 14462976 | tf_op jit(solution)/shard_map/conv_back/pallas_call | solution.py:602
  493.1 4.5 collective-permute-done.50
  498.2 7.4 %first_grad.1.own = bf16[2,1568,256]{2,1,0:T(8,128)(2,1)} custom-call(s32[3]{0:T(128)} %pad_add_fusion.sc, f32[2,1568,256]{2,1,0:T(8,128)} %get-tuple-element.68.up1, f32[2,1568,256]{2,1,0:T(8,128)} %get-tuple-element.52.own, bf16[2,1568,256]{2,1,0:T(8,128)(2,1)} %copy-done.1, f32[2,2,256]{2,1,0:T(2,128)} %add.353.tot.tot1, f32[2,2,256]{2,1,0:T(2,128)} %add.389.tot_b, ...), custom_call_target="tpu_custom_call" | custom-call | bytes 4816896 | tf_op jit(solution)/shard_map/first_grad/pallas_call | solution.py:613
  506.5 7.5 %conv_wgrad.1 = f32[2,9,32,256]{3,2,1,0:T(8,128)} custom-call(s32[3]{0:T(128)} %pad_add_fusion.sc, bf16[2,1568,256]{2,1,0:T(8,128)(2,1)} %get-tuple-element.74.act, bf16[2,1568,256]{2,1,0:T(8,128)(2,1)} %get-tuple-element.75.cg), custom_call_target="tpu_custom_call" | custom-call | flops 3288334336 | bytes 1769472 | tf_op jit(solution)/shard_map/conv_wgrad/pallas_call | solution.py:664
  520.6 8.7 %reduce_wgrad.1 = (bf16[4,256,256]{2,1,0:T(8,128)(2,1)}, bf16[4,256,256]{2,1,0:T(8,128)(2,1)}, bf16[4,256,256]{2,1,0:T(8,128)(2,1)}, bf16[4,256,256]{2,1,0:T(8,128)(2,1)}) custom-call(s32[3]{0:T(128)} %pad_add_fusion.sc, bf16[2,1568,256]{2,1,0:T(8,128)(2,1)} %first_grad.1.own, bf16[2,1568,256]{2,1,0:T(8,128)(2,1)} %copy-done, bf16[1568,256]{1,0:T(8,128)(2,1)} %bitcast.120, ...), custom_call_target="tpu_custom_call" | custom-call | flops 3288334336 | bytes 6291456 | tf_op jit(solution)/shard_map/reduce_wgrad/pallas_call | solution.py:654
  534.0 5.5 collective-permute-done.64
  540.3 4.9 collective-permute-done.57
  545.2 10.2 %collective-permute-done.56 = bf16[4,256,256]{2,1,0:T(8,128)(2,1)S(1)} collective-permute-done((bf16[4,256,256]{2,1,0:T(8,128)(2,1)}, bf16[4,256,256]{2,1,0:T(8,128)(2,1)S(1)}, u32[]{:S(2)}, u32[]{:S(2)}) %collective-permute-start.56) | collective-permute-done | bytes 524320 | tf_op jit(solution)/shard_map/ppermute | solution.py:418
  562.4 3.6 collective-permute-done.60
  566.0 3.8 collective-permute-done.59
  574.1 7.6 %input_grad.4 = bf16[1568,256]{1,0:T(8,128)(2,1)} custom-call(s32[3]{0:T(128)} %pad_add_fusion.sc, bf16[2,1568,256]{2,1,0:T(8,128)(2,1)} %first_grad.1.own, bf16[2,1568,256]{2,1,0:T(8,128)(2,1)} %copy-done, f32[4,1568,256]{2,1,0:T(8,128)} %get-tuple-element.62.up, bf16[4,256,256]{2,1,0:T(8,128)(2,1)} %copy-done.2, bf16[4,256,256]{2,1,0:T(8,128)(2,1)} %copy-done.3, ...), custom_call_target="tpu_custom_call" | custom-call | flops 822083584 | bytes 2408448 | tf_op jit(solution)/shard_map/input_grad/pallas_call | solution.py:624
  588.6 7.6 %input_grad.5 = bf16[1568,256]{1,0:T(8,128)(2,1)} custom-call(s32[3]{0:T(128)} %pad_add_fusion.sc, bf16[2,1568,256]{2,1,0:T(8,128)(2,1)} %first_grad.1.own, bf16[2,1568,256]{2,1,0:T(8,128)(2,1)} %copy-done, f32[4,1568,256]{2,1,0:T(8,128)} %get-tuple-element.62.up, bf16[4,256,256]{2,1,0:T(8,128)(2,1)} %copy-done.2, bf16[4,256,256]{2,1,0:T(8,128)(2,1)} %copy-done.3, ...), custom_call_target="tpu_custom_call" | custom-call | flops 822083584 | bytes 2408448 | tf_op jit(solution)/shard_map/input_grad/pallas_call | solution.py:624
  598.2 7.6 %input_grad.6 = bf16[1568,256]{1,0:T(8,128)(2,1)} custom-call(s32[3]{0:T(128)} %pad_add_fusion.sc, bf16[2,1568,256]{2,1,0:T(8,128)(2,1)} %first_grad.1.own, bf16[2,1568,256]{2,1,0:T(8,128)(2,1)} %copy-done, f32[4,1568,256]{2,1,0:T(8,128)} %get-tuple-element.62.up, bf16[4,256,256]{2,1,0:T(8,128)(2,1)} %copy-done.2, bf16[4,256,256]{2,1,0:T(8,128)(2,1)} %copy-done.3, ...), custom_call_target="tpu_custom_call" | custom-call | flops 822083584 | bytes 2408448 | tf_op jit(solution)/shard_map/input_grad/pallas_call | solution.py:624
  608.2 10.3 %collective-permute-done.79 = f32[8,128]{1,0:T(8,128)S(1)} collective-permute-done((f32[8,128]{1,0:T(8,128)S(1)}, f32[8,128]{1,0:T(8,128)S(1)}, u32[]{:S(2)}, u32[]{:S(2)}) %collective-permute-start.79) | collective-permute-done | bytes 4128 | tf_op jit(solution)/shard_map/ppermute | solution.py:734
  621.0 7.6 %input_grad.7.refs_0_ = bf16[1568,256]{1,0:T(8,128)(2,1)} custom-call(s32[3]{0:T(128)} %pad_add_fusion.sc, bf16[2,1568,256]{2,1,0:T(8,128)(2,1)} %first_grad.1.own, bf16[2,1568,256]{2,1,0:T(8,128)(2,1)} %copy-done, f32[4,1568,256]{2,1,0:T(8,128)} %get-tuple-element.62.up, bf16[4,256,256]{2,1,0:T(8,128)(2,1)} %copy-done.2, bf16[4,256,256]{2,1,0:T(8,128)(2,1)} %copy-done.3, ...), custom_call_target="tpu_custom_call" | custom-call | flops 822083584 | bytes 2408448 | tf_op jit(solution)/shard_map/input_grad/pallas_call | solution.py:624
  631.6 21.8 %collective-permute-done.80 = f32[8,128]{1,0:T(8,128)S(1)} collective-permute-done((f32[8,128]{1,0:T(8,128)S(1)}, f32[8,128]{1,0:T(8,128)S(1)}, u32[]{:S(2)}, u32[]{:S(2)}) %collective-permute-start.80) | collective-permute-done | bytes 4128 | tf_op jit(solution)/shard_map/ppermute | solution.py:734
  657.8 4.1 fusion.24
  (318 shorter events, 203.0 us)
Async XLA Ops:
  18.1 21.0 %collective-permute-start.6 = (bf16[4,256,256]{2,1,0:T(8,128)(2,1)S(1)}, bf16[4,256,256]{2,1,0:T(8,128)(2,1)S(1)}, u32[]{:S(2)}, u32[]{:S(2)}) collective-permute-start(bf16[4,256,256]{2,1,0:T(8,128)(2,1)S(1)} %pad_maximum_fusion.refs_4_.refs_0_), channel_id=1, source_target_pairs={{0,8},{8,0},{16,24},{24,16},{1,9},{9,1},{17,25},{25,17},{2,10},{10... | collective-permute-start | bytes 1572872 | tf_op jit(solution)/shard_map/ppermute | solution.py:418
  25.1 35.6 %collective-permute-start = (bf16[1568,256]{1,0:T(8,128)(2,1)}, bf16[1568,256]{1,0:T(8,128)(2,1)S(1)}, u32[]{:S(2)}, u32[]{:S(2)}) collective-permute-start(bf16[1568,256]{1,0:T(8,128)(2,1)} %bitcast.127), channel_id=1, source_target_pairs={{0,2},{1,3},{2,4},{3,5},{4,6},{5,7},{6,0},{7,1},{8,10},{9,11},{10,... | collective-permute-start | bytes 2408456 | tf_op jit(solution)/shard_map/ppermute | solution.py:412
  29.3 51.3 %collective-permute-start.1 = (bf16[1568,256]{1,0:T(8,128)(2,1)}, bf16[1568,256]{1,0:T(8,128)(2,1)S(1)}, u32[]{:S(2)}, u32[]{:S(2)}) collective-permute-start(bf16[1568,256]{1,0:T(8,128)(2,1)} %bitcast.128), channel_id=1, source_target_pairs={{0,4},{1,5},{2,6},{3,7},{4,0},{5,1},{6,2},{7,3},{8,12},{9,13},{10,... | collective-permute-start | bytes 2408456 | tf_op jit(solution)/shard_map/ppermute | solution.py:412
  34.6 45.9 %collective-permute-start.2 = (bf16[1568,256]{1,0:T(8,128)(2,1)}, bf16[1568,256]{1,0:T(8,128)(2,1)S(1)}, u32[]{:S(2)}, u32[]{:S(2)}) collective-permute-start(bf16[1568,256]{1,0:T(8,128)(2,1)} %bitcast.129), channel_id=1, source_target_pairs={{0,6},{1,7},{2,0},{3,1},{4,2},{5,3},{6,4},{7,5},{8,14},{9,15},{10,... | collective-permute-start | bytes 2408456 | tf_op jit(solution)/shard_map/ppermute | solution.py:412
  37.5 23.2 %collective-permute-start.7 = (bf16[4,256,256]{2,1,0:T(8,128)(2,1)S(1)}, bf16[4,256,256]{2,1,0:T(8,128)(2,1)S(1)}, u32[]{:S(2)}, u32[]{:S(2)}) collective-permute-start(bf16[4,256,256]{2,1,0:T(8,128)(2,1)S(1)} %pad_maximum_fusion.refs_4_.refs_0_), channel_id=1, source_target_pairs={{0,16},{8,24},{16,0},{24,8},{1,17},{9,25},{17,1},{25,9},{2,18},{10... | collective-permute-start | bytes 1572872 | tf_op jit(solution)/shard_map/ppermute | solution.py:418
  39.1 21.7 %collective-permute-start.8 = (bf16[4,256,256]{2,1,0:T(8,128)(2,1)S(1)}, bf16[4,256,256]{2,1,0:T(8,128)(2,1)S(1)}, u32[]{:S(2)}, u32[]{:S(2)}) collective-permute-start(bf16[4,256,256]{2,1,0:T(8,128)(2,1)S(1)} %pad_maximum_fusion.refs_4_.refs_0_), channel_id=1, source_target_pairs={{0,24},{8,16},{16,8},{24,0},{1,25},{9,17},{17,9},{25,1},{2,26},{10... | collective-permute-start | bytes 1572872 | tf_op jit(solution)/shard_map/ppermute | solution.py:418
  107.6 20.5 %collective-permute-start.10 = (f32[2,2,256]{2,1,0:T(2,128)}, f32[2,2,256]{2,1,0:T(2,128)S(1)}, u32[]{:S(2)}, u32[]{:S(2)}) collective-permute-start(f32[2,2,256]{2,1,0:T(2,128)} %first_sums.1), channel_id=1, source_target_pairs={{0,8},{8,0},{16,24},{24,16},{1,9},{9,1},{17,25},{25,17},{2,10},{10... | collective-permute-start | bytes 12296 | tf_op jit(solution)/shard_map/ppermute | solution.py:418
  108.2 34.4 %collective-permute-start.14 = (f32[296,128]{1,0:T(8,128)S(1)}, f32[296,128]{1,0:T(8,128)S(1)}, u32[]{:S(2)}, u32[]{:S(2)}) collective-permute-start(f32[296,128]{1,0:T(8,128)S(1)} %pad_maximum_fusion.2), channel_id=1, source_target_pairs={{0,2},{1,3},{2,4},{3,5},{4,6},{5,7},{6,0},{7,1},{8,10},{9,11},{10,... | collective-permute-start | bytes 454664 | tf_op jit(solution)/shard_map/ppermute | solution.py:412
  125.7 21.5 %collective-permute-start.15 = (f32[296,128]{1,0:T(8,128)S(1)}, f32[296,128]{1,0:T(8,128)S(1)}, u32[]{:S(2)}, u32[]{:S(2)}) collective-permute-start(f32[296,128]{1,0:T(8,128)S(1)} %pad_maximum_fusion.2), channel_id=1, source_target_pairs={{0,4},{1,5},{2,6},{3,7},{4,0},{5,1},{6,2},{7,3},{8,12},{9,13},{10,... | collective-permute-start | bytes 454664 | tf_op jit(solution)/shard_map/ppermute | solution.py:412
  127.5 24.1 %collective-permute-start.16 = (f32[296,128]{1,0:T(8,128)S(1)}, f32[296,128]{1,0:T(8,128)S(1)}, u32[]{:S(2)}, u32[]{:S(2)}) collective-permute-start(f32[296,128]{1,0:T(8,128)S(1)} %pad_maximum_fusion.2), channel_id=1, source_target_pairs={{0,6},{1,7},{2,0},{3,1},{4,2},{5,3},{6,4},{7,5},{8,14},{9,15},{10,... | collective-permute-start | bytes 454664 | tf_op jit(solution)/shard_map/ppermute | solution.py:412
  136.4 22.4 %collective-permute-start.13 = (f32[2,2,256]{2,1,0:T(2,128)S(1)}, f32[2,2,256]{2,1,0:T(2,128)S(1)}, u32[]{:S(2)}, u32[]{:S(2)}) collective-permute-start(f32[2,2,256]{2,1,0:T(2,128)S(1)} %add.352), channel_id=1, source_target_pairs={{0,4},{1,5},{2,6},{3,7},{4,0},{5,1},{6,2},{7,3},{8,12},{9,13},{10,... | collective-permute-start | bytes 12296 | tf_op jit(solution)/shard_map/ppermute | solution.py:427
  195.5 42.8 %collective-permute-start.21 = (bf16[2,1568,256]{2,1,0:T(8,128)(2,1)}, bf16[2,1568,256]{2,1,0:T(8,128)(2,1)}, u32[]{:S(2)}, u32[]{:S(2)}) collective-permute-start(bf16[2,1568,256]{2,1,0:T(8,128)(2,1)} %second_act.1.own), channel_id=1, source_target_pairs={{0,1},{1,0},{2,3},{3,2},{4,5},{5,4},{6,7},{7,6},{8,9},{9,8},{10,11... | collective-permute-start | bytes 4816904 | tf_op jit(solution)/shard_map/ppermute | solution.py:415
  198.8 12.4 %collective-permute-start.23 = (bf16[256,256]{1,0:T(8,128)(2,1)S(1)}, bf16[256,256]{1,0:T(8,128)(2,1)S(1)}, u32[]{:S(2)}, u32[]{:S(2)}) collective-permute-start(bf16[256,256]{1,0:T(8,128)(2,1)S(1)} %bitcast.137), channel_id=1, source_target_pairs={{0,4},{1,5},{2,6},{3,7},{4,0},{5,1},{6,2},{7,3},{8,12},{9,13},{10,... | collective-permute-start | bytes 393224 | tf_op jit(solution)/shard_map/ppermute | solution.py:412
  199.0 12.3 %collective-permute-start.22 = (bf16[256,256]{1,0:T(8,128)(2,1)S(1)}, bf16[256,256]{1,0:T(8,128)(2,1)S(1)}, u32[]{:S(2)}, u32[]{:S(2)}) collective-permute-start(bf16[256,256]{1,0:T(8,128)(2,1)S(1)} %bitcast.138), channel_id=1, source_target_pairs={{0,2},{1,3},{2,4},{3,5},{4,6},{5,7},{6,0},{7,1},{8,10},{9,11},{10,... | collective-permute-start | bytes 393224 | tf_op jit(solution)/shard_map/ppermute | solution.py:412
  212.2 15.1 %collective-permute-start.25 = (bf16[4,256,256]{2,1,0:T(8,128)(2,1)}, bf16[4,256,256]{2,1,0:T(8,128)(2,1)}, u32[]{:S(2)}, u32[]{:S(2)}) collective-permute-start(bf16[4,256,256]{2,1,0:T(8,128)(2,1)} %pad_maximum_fusion.1.refs_0_), channel_id=1, source_target_pairs={{0,8},{8,0},{16,24},{24,16},{1,9},{9,1},{17,25},{25,17},{2,10},{10... | collective-permute-start | bytes 1572872 | tf_op jit(solution)/shard_map/ppermute | solution.py:418
  213.6 24.0 %collective-permute-start.26 = (bf16[4,256,256]{2,1,0:T(8,128)(2,1)}, bf16[4,256,256]{2,1,0:T(8,128)(2,1)}, u32[]{:S(2)}, u32[]{:S(2)}) collective-permute-start(bf16[4,256,256]{2,1,0:T(8,128)(2,1)} %pad_maximum_fusion.1.refs_0_), channel_id=1, source_target_pairs={{0,16},{8,24},{16,0},{24,8},{1,17},{9,25},{17,1},{25,9},{2,18},{10... | collective-permute-start | bytes 1572872 | tf_op jit(solution)/shard_map/ppermute | solution.py:418
  215.1 23.3 %collective-permute-start.27 = (bf16[4,256,256]{2,1,0:T(8,128)(2,1)}, bf16[4,256,256]{2,1,0:T(8,128)(2,1)S(1)}, u32[]{:S(2)}, u32[]{:S(2)}) collective-permute-start(bf16[4,256,256]{2,1,0:T(8,128)(2,1)} %pad_maximum_fusion.1.refs_0_), channel_id=1, source_target_pairs={{0,24},{8,16},{16,8},{24,0},{1,25},{9,17},{17,9},{25,1},{2,26},{10... | collective-permute-start | bytes 1572872 | tf_op jit(solution)/shard_map/ppermute | solution.py:418
  217.4 73.5 %collective-permute-start.32 = (bf16[1568,256]{1,0:T(8,128)(2,1)}, bf16[1568,256]{1,0:T(8,128)(2,1)S(1)}, u32[]{:S(2)}, u32[]{:S(2)}) collective-permute-start(bf16[1568,256]{1,0:T(8,128)(2,1)} %bitcast.38), channel_id=1, source_target_pairs={{0,2},{1,3},{2,4},{3,5},{4,6},{5,7},{6,0},{7,1},{8,10},{9,11},{10,... | collective-permute-start | bytes 2408456 | tf_op jit(solution)/shard_map/ppermute | solution.py:412
  227.3 63.7 %collective-permute-start.33 = (bf16[1568,256]{1,0:T(8,128)(2,1)}, bf16[1568,256]{1,0:T(8,128)(2,1)S(1)}, u32[]{:S(2)}, u32[]{:S(2)}) collective-permute-start(bf16[1568,256]{1,0:T(8,128)(2,1)} %bitcast.39), channel_id=1, source_target_pairs={{0,4},{1,5},{2,6},{3,7},{4,0},{5,1},{6,2},{7,3},{8,12},{9,13},{10,... | collective-permute-start | bytes 2408456 | tf_op jit(solution)/shard_map/ppermute | solution.py:412
  237.6 53.4 %collective-permute-start.34 = (bf16[1568,256]{1,0:T(8,128)(2,1)}, bf16[1568,256]{1,0:T(8,128)(2,1)S(1)}, u32[]{:S(2)}, u32[]{:S(2)}) collective-permute-start(bf16[1568,256]{1,0:T(8,128)(2,1)} %bitcast.40), channel_id=1, source_target_pairs={{0,6},{1,7},{2,0},{3,1},{4,2},{5,3},{6,4},{7,5},{8,14},{9,15},{10,... | collective-permute-start | bytes 2408456 | tf_op jit(solution)/shard_map/ppermute | solution.py:412
  257.7 15.1 %collective-permute-start.30 = (f32[4,2,256]{2,1,0:T(2,128)S(1)}, f32[4,2,256]{2,1,0:T(2,128)S(1)}, u32[]{:S(2)}, u32[]{:S(2)}) collective-permute-start(f32[4,2,256]{2,1,0:T(2,128)S(1)} %add.370), channel_id=1, source_target_pairs={{0,2},{1,3},{2,0},{3,1},{4,6},{5,7},{6,4},{7,5},{8,10},{9,11},{10,... | collective-permute-start | bytes 24584 | tf_op jit(solution)/shard_map/ppermute | solution.py:427
  272.9 17.5 %collective-permute-start.31 = (f32[4,2,256]{2,1,0:T(2,128)S(1)}, f32[4,2,256]{2,1,0:T(2,128)S(1)}, u32[]{:S(2)}, u32[]{:S(2)}) collective-permute-start(f32[4,2,256]{2,1,0:T(2,128)S(1)} %add.371), channel_id=1, source_target_pairs={{0,4},{1,5},{2,6},{3,7},{4,0},{5,1},{6,2},{7,3},{8,12},{9,13},{10,... | collective-permute-start | bytes 24584 | tf_op jit(solution)/shard_map/ppermute | solution.py:427
  340.2 87.1 %collective-permute-start.42 = (bf16[2,1568,256]{2,1,0:T(8,128)(2,1)}, bf16[2,1568,256]{2,1,0:T(8,128)(2,1)S(1)}, u32[]{:S(2)}, u32[]{:S(2)}) collective-permute-start(bf16[2,1568,256]{2,1,0:T(8,128)(2,1)} %get-tuple-element.65), channel_id=1, source_target_pairs={{0,1},{1,0},{2,3},{3,2},{4,5},{5,4},{6,7},{7,6},{8,9},{9,8},{10,11... | collective-permute-start | bytes 4816904 | tf_op jit(solution)/shard_map/ppermute | solution.py:415
  348.9 15.9 %collective-permute-start.71 = (bf16[4,256,256]{2,1,0:T(8,128)(2,1)}, bf16[4,256,256]{2,1,0:T(8,128)(2,1)S(1)}, u32[]{:S(2)}, u32[]{:S(2)}) collective-permute-start(bf16[4,256,256]{2,1,0:T(8,128)(2,1)} %get-tuple-element.80), channel_id=1, source_target_pairs={{0,24},{8,16},{16,8},{24,0},{1,25},{9,17},{17,9},{25,1},{2,26},{10... | collective-permute-start | bytes 1572872 | tf_op jit(solution)/shard_map/ppermute | solution.py:418
  351.3 24.3 %collective-permute-start.70 = (bf16[4,256,256]{2,1,0:T(8,128)(2,1)}, bf16[4,256,256]{2,1,0:T(8,128)(2,1)S(1)}, u32[]{:S(2)}, u32[]{:S(2)}) collective-permute-start(bf16[4,256,256]{2,1,0:T(8,128)(2,1)} %get-tuple-element.79), channel_id=1, source_target_pairs={{0,16},{8,24},{16,0},{24,8},{1,17},{9,25},{17,1},{25,9},{2,18},{10... | collective-permute-start | bytes 1572872 | tf_op jit(solution)/shard_map/ppermute | solution.py:418
  351.8 24.5 %collective-permute-start.69 = (bf16[4,256,256]{2,1,0:T(8,128)(2,1)}, bf16[4,256,256]{2,1,0:T(8,128)(2,1)S(1)}, u32[]{:S(2)}, u32[]{:S(2)}) collective-permute-start(bf16[4,256,256]{2,1,0:T(8,128)(2,1)} %get-tuple-element.78), channel_id=1, source_target_pairs={{0,8},{8,0},{16,24},{24,16},{1,9},{9,1},{17,25},{25,17},{2,10},{10... | collective-permute-start | bytes 1572872 | tf_op jit(solution)/shard_map/ppermute | solution.py:418
  352.4 101.4 %collective-permute-start.35 = (bf16[1568,256]{1,0:T(8,128)(2,1)}, bf16[1568,256]{1,0:T(8,128)(2,1)S(1)}, u32[]{:S(2)}, u32[]{:S(2)}) collective-permute-start(bf16[1568,256]{1,0:T(8,128)(2,1)} %get-tuple-element.58), channel_id=1, source_target_pairs={{0,2},{1,3},{2,4},{3,5},{4,6},{5,7},{6,0},{7,1},{8,10},{9,11},{10,... | collective-permute-start | bytes 2408456 | tf_op jit(solution)/shard_map/ppermute | solution.py:412
  364.8 75.7 %collective-permute-start.36 = (bf16[1568,256]{1,0:T(8,128)(2,1)S(1)}, bf16[1568,256]{1,0:T(8,128)(2,1)S(1)}, u32[]{:S(2)}, u32[]{:S(2)}) collective-permute-start(bf16[1568,256]{1,0:T(8,128)(2,1)S(1)} %copy-done.32), channel_id=1, source_target_pairs={{0,4},{1,5},{2,6},{3,7},{4,0},{5,1},{6,2},{7,3},{8,12},{9,13},{10,... | collective-permute-start | bytes 2408456 | tf_op jit(solution)/shard_map/ppermute | solution.py:412
  375.6 70.8 %collective-permute-start.37 = (bf16[1568,256]{1,0:T(8,128)(2,1)}, bf16[1568,256]{1,0:T(8,128)(2,1)S(1)}, u32[]{:S(2)}, u32[]{:S(2)}) collective-permute-start(bf16[1568,256]{1,0:T(8,128)(2,1)} %get-tuple-element.60), channel_id=1, source_target_pairs={{0,6},{1,7},{2,0},{3,1},{4,2},{5,3},{6,4},{7,5},{8,14},{9,15},{10,... | collective-permute-start | bytes 2408456 | tf_op jit(solution)/shard_map/ppermute | solution.py:412
  377.6 33.7 %collective-permute-start.74 = (bf16[256,256]{1,0:T(8,128)(2,1)S(1)}, bf16[256,256]{1,0:T(8,128)(2,1)S(1)}, u32[]{:S(2)}, u32[]{:S(2)}) collective-permute-start(bf16[256,256]{1,0:T(8,128)(2,1)S(1)} %get-tuple-element.116), channel_id=1, source_target_pairs={{0,2},{1,3},{2,4},{3,5},{4,6},{5,7},{6,0},{7,1},{8,10},{9,11},{10,... | collective-permute-start | bytes 393224 | tf_op jit(solution)/shard_map/ppermute | solution.py:412
  411.3 26.1 %collective-permute-start.73 = (bf16[256,256]{1,0:T(8,128)(2,1)S(1)}, bf16[256,256]{1,0:T(8,128)(2,1)S(1)}, u32[]{:S(2)}, u32[]{:S(2)}) collective-permute-start(bf16[256,256]{1,0:T(8,128)(2,1)S(1)} %get-tuple-element.117), channel_id=1, source_target_pairs={{0,4},{1,5},{2,6},{3,7},{4,0},{5,1},{6,2},{7,3},{8,12},{9,13},{10,... | collective-permute-start | bytes 393224 | tf_op jit(solution)/shard_map/ppermute | solution.py:412
  438.9 19.5 %collective-permute-start.75 = (bf16[256,256]{1,0:T(8,128)(2,1)S(1)}, bf16[256,256]{1,0:T(8,128)(2,1)S(1)}, u32[]{:S(2)}, u32[]{:S(2)}) collective-permute-start(bf16[256,256]{1,0:T(8,128)(2,1)S(1)} %fusion.5), channel_id=1, source_target_pairs={{0,16},{8,24},{16,0},{24,8},{1,17},{9,25},{17,1},{25,9},{2,18},{10... | collective-permute-start | bytes 393224 | tf_op jit(solution)/shard_map/ppermute | solution.py:418
  440.5 17.9 %collective-permute-start.76 = (bf16[256,256]{1,0:T(8,128)(2,1)S(1)}, bf16[256,256]{1,0:T(8,128)(2,1)S(1)}, u32[]{:S(2)}, u32[]{:S(2)}) collective-permute-start(bf16[256,256]{1,0:T(8,128)(2,1)S(1)} %fusion.5), channel_id=1, source_target_pairs={{0,8},{8,0},{16,24},{24,16},{1,9},{9,1},{17,25},{25,17},{2,10},{10... | collective-permute-start | bytes 393224 | tf_op jit(solution)/shard_map/ppermute | solution.py:418
  441.3 17.1 %collective-permute-start.77 = (bf16[256,256]{1,0:T(8,128)(2,1)S(1)}, bf16[256,256]{1,0:T(8,128)(2,1)S(1)}, u32[]{:S(2)}, u32[]{:S(2)}) collective-permute-start(bf16[256,256]{1,0:T(8,128)(2,1)S(1)} %fusion.5), channel_id=1, source_target_pairs={{0,24},{8,16},{16,8},{24,0},{1,25},{9,17},{17,9},{25,1},{2,26},{10... | collective-permute-start | bytes 393224 | tf_op jit(solution)/shard_map/ppermute | solution.py:418
  505.6 13.8 %collective-permute-start.51 = (bf16[2,1568,256]{2,1,0:T(8,128)(2,1)}, bf16[2,1568,256]{2,1,0:T(8,128)(2,1)S(1)}, u32[]{:S(2)}, u32[]{:S(2)}) collective-permute-start(bf16[2,1568,256]{2,1,0:T(8,128)(2,1)} %first_grad.1.own), channel_id=1, source_target_pairs={{0,1},{1,0},{2,3},{3,2},{4,5},{5,4},{6,7},{7,6},{8,9},{9,8},{10,11... | collective-permute-start | bytes 4816904 | tf_op jit(solution)/shard_map/ppermute | solution.py:415
  516.2 17.2 %collective-permute-start.66 = (bf16[288,128]{1,0:T(8,128)(2,1)S(1)}, bf16[288,128]{1,0:T(8,128)(2,1)S(1)}, u32[]{:S(2)}, u32[]{:S(2)}) collective-permute-start(bf16[288,128]{1,0:T(8,128)(2,1)S(1)} %bitcast.157), channel_id=1, source_target_pairs={{0,6},{1,7},{2,0},{3,1},{4,2},{5,3},{6,4},{7,5},{8,14},{9,15},{10,... | collective-permute-start | bytes 221192 | tf_op jit(solution)/shard_map/ppermute | solution.py:412
  516.9 17.1 %collective-permute-start.65 = (bf16[288,128]{1,0:T(8,128)(2,1)S(1)}, bf16[288,128]{1,0:T(8,128)(2,1)S(1)}, u32[]{:S(2)}, u32[]{:S(2)}) collective-permute-start(bf16[288,128]{1,0:T(8,128)(2,1)S(1)} %bitcast.155), channel_id=1, source_target_pairs={{0,4},{1,5},{2,6},{3,7},{4,0},{5,1},{6,2},{7,3},{8,12},{9,13},{10,... | collective-permute-start | bytes 221192 | tf_op jit(solution)/shard_map/ppermute | solution.py:412
  529.2 15.9 %collective-permute-start.57 = (bf16[4,256,256]{2,1,0:T(8,128)(2,1)}, bf16[4,256,256]{2,1,0:T(8,128)(2,1)S(1)}, u32[]{:S(2)}, u32[]{:S(2)}) collective-permute-start(bf16[4,256,256]{2,1,0:T(8,128)(2,1)} %get-tuple-element.73), channel_id=1, source_target_pairs={{0,24},{8,16},{16,8},{24,0},{1,25},{9,17},{17,9},{25,1},{2,26},{10... | collective-permute-start | bytes 1572872 | tf_op jit(solution)/shard_map/ppermute | solution.py:418
  530.9 24.5 %collective-permute-start.56 = (bf16[4,256,256]{2,1,0:T(8,128)(2,1)}, bf16[4,256,256]{2,1,0:T(8,128)(2,1)S(1)}, u32[]{:S(2)}, u32[]{:S(2)}) collective-permute-start(bf16[4,256,256]{2,1,0:T(8,128)(2,1)} %get-tuple-element.72), channel_id=1, source_target_pairs={{0,16},{8,24},{16,0},{24,8},{1,17},{9,25},{17,1},{25,9},{2,18},{10... | collective-permute-start | bytes 1572872 | tf_op jit(solution)/shard_map/ppermute | solution.py:418
  531.4 24.9 %collective-permute-start.55 = (bf16[4,256,256]{2,1,0:T(8,128)(2,1)}, bf16[4,256,256]{2,1,0:T(8,128)(2,1)S(1)}, u32[]{:S(2)}, u32[]{:S(2)}) collective-permute-start(bf16[4,256,256]{2,1,0:T(8,128)(2,1)} %get-tuple-element.71), channel_id=1, source_target_pairs={{0,8},{8,0},{16,24},{24,16},{1,9},{9,1},{17,25},{25,17},{2,10},{10... | collective-permute-start | bytes 1572872 | tf_op jit(solution)/shard_map/ppermute | solution.py:418
  539.6 22.2 %collective-permute-start.67 = (bf16[288,128]{1,0:T(8,128)(2,1)S(1)}, bf16[288,128]{1,0:T(8,128)(2,1)S(1)}, u32[]{:S(2)}, u32[]{:S(2)}) collective-permute-start(bf16[288,128]{1,0:T(8,128)(2,1)S(1)} %add_convert_fusion.1), channel_id=1, source_target_pairs={{0,8},{8,0},{16,24},{24,16},{1,9},{9,1},{17,25},{25,17},{2,10},{10... | collective-permute-start | bytes 221192 | tf_op jit(solution)/shard_map/ppermute | solution.py:418
  569.9 14.2 %collective-permute-start.61 = (bf16[256,256]{1,0:T(8,128)(2,1)S(1)}, bf16[256,256]{1,0:T(8,128)(2,1)S(1)}, u32[]{:S(2)}, u32[]{:S(2)}) collective-permute-start(bf16[256,256]{1,0:T(8,128)(2,1)S(1)} %fusion.9), channel_id=1, source_target_pairs={{0,16},{8,24},{16,0},{24,8},{1,17},{9,25},{17,1},{25,9},{2,18},{10... | collective-permute-start | bytes 393224 | tf_op jit(solution)/shard_map/ppermute | solution.py:418
  570.3 13.8 %collective-permute-start.62 = (bf16[256,256]{1,0:T(8,128)(2,1)S(1)}, bf16[256,256]{1,0:T(8,128)(2,1)S(1)}, u32[]{:S(2)}, u32[]{:S(2)}) collective-permute-start(bf16[256,256]{1,0:T(8,128)(2,1)S(1)} %fusion.9), channel_id=1, source_target_pairs={{0,8},{8,0},{16,24},{24,16},{1,9},{9,1},{17,25},{25,17},{2,10},{10... | collective-permute-start | bytes 393224 | tf_op jit(solution)/shard_map/ppermute | solution.py:418
  581.7 88.2 %collective-permute-start.52 = (bf16[1568,256]{1,0:T(8,128)(2,1)}, bf16[1568,256]{1,0:T(8,128)(2,1)}, u32[]{:S(2)}, u32[]{:S(2)}) collective-permute-start(bf16[1568,256]{1,0:T(8,128)(2,1)} %input_grad.4), channel_id=1, source_target_pairs={{0,2},{1,3},{2,4},{3,5},{4,6},{5,7},{6,0},{7,1},{8,10},{9,11},{10,... | collective-permute-start | bytes 2408456 | tf_op jit(solution)/shard_map/ppermute | solution.py:412
  596.2 70.9 %collective-permute-start.53 = (bf16[1568,256]{1,0:T(8,128)(2,1)}, bf16[1568,256]{1,0:T(8,128)(2,1)}, u32[]{:S(2)}, u32[]{:S(2)}) collective-permute-start(bf16[1568,256]{1,0:T(8,128)(2,1)} %input_grad.5), channel_id=1, source_target_pairs={{0,4},{1,5},{2,6},{3,7},{4,0},{5,1},{6,2},{7,3},{8,12},{9,13},{10,... | collective-permute-start | bytes 2408456 | tf_op jit(solution)/shard_map/ppermute | solution.py:412
  597.8 20.7 %collective-permute-start.79 = (f32[8,128]{1,0:T(8,128)S(1)}, f32[8,128]{1,0:T(8,128)S(1)}, u32[]{:S(2)}, u32[]{:S(2)}) collective-permute-start(f32[8,128]{1,0:T(8,128)S(1)} %broadcast_add_fusion), channel_id=1, source_target_pairs={{0,2},{1,3},{2,0},{3,1},{4,6},{5,7},{6,4},{7,5},{8,10},{9,11},{10,... | collective-permute-start | bytes 12296 | tf_op jit(solution)/shard_map/ppermute | solution.py:734
  605.8 58.5 %collective-permute-start.54 = (bf16[1568,256]{1,0:T(8,128)(2,1)}, bf16[1568,256]{1,0:T(8,128)(2,1)}, u32[]{:S(2)}, u32[]{:S(2)}) collective-permute-start(bf16[1568,256]{1,0:T(8,128)(2,1)} %input_grad.6), channel_id=1, source_target_pairs={{0,6},{1,7},{2,0},{3,1},{4,2},{5,3},{6,4},{7,5},{8,14},{9,15},{10,... | collective-permute-start | bytes 2408456 | tf_op jit(solution)/shard_map/ppermute | solution.py:412
  618.5 34.8 %collective-permute-start.80 = (f32[8,128]{1,0:T(8,128)S(1)}, f32[8,128]{1,0:T(8,128)S(1)}, u32[]{:S(2)}, u32[]{:S(2)}) collective-permute-start(f32[8,128]{1,0:T(8,128)S(1)} %fusion.30), channel_id=1, source_target_pairs={{0,4},{1,5},{2,6},{3,7},{4,0},{5,1},{6,2},{7,3},{8,12},{9,13},{10,... | collective-permute-start | bytes 12296 | tf_op jit(solution)/shard_map/ppermute | solution.py:734
  (66 other events, 631.0 us)

commit v2 on v0

v2 whole, which is shorter than its diff:
```python
import functools

import jax
import jax.numpy as jnp
from jax import lax
from jax.experimental import pallas as pl
from jax.experimental.pallas import tpu as pltpu
from jax.sharding import PartitionSpec as P

CIN = 2048
GW = 32
HW = 7
STEP = 10
MID = 1024
SRC = 9
NQ = 4
QW = MID // NQ
SPOTS = HW * HW

norm_eps = 1e-05
adam_eps = 1e-08
clip_norm = 1.0
moment_decay = 0.5

GELU_K = 0.7978845608028654
GELU_C = 0.044715
BF = jnp.bfloat16
F32 = jnp.float32


def dot(a, b):
    return jnp.dot(a, b, preferred_element_type=F32)


def dot_t(a, b):
    return lax.dot_general(a, b, (((1,), (1,)), ((), ())), preferred_element_type=F32)


def dot_rows(a, b):
    return lax.dot_general(a, b, (((0,), (0,)), ((), ())), preferred_element_type=F32)


def gelu(u):
    t = jnp.tanh(u * (GELU_K * GELU_C * (u * u) + GELU_K))
    return u * (0.5 * t + 0.5)


def gelu_both(u):
    u2 = u * u
    part = 0.5 * jnp.tanh(u * (GELU_K * GELU_C * u2 + GELU_K)) + 0.5
    bend = u * (6.0 * GELU_K * GELU_C * u2 + 2.0 * GELU_K)
    return u * part, part * (bend * (1.0 - part) + 1.0)


def norm_rows(total, squares, count):
    center = total / count
    spread = squares / count - center * center
    return center, lax.rsqrt(spread + norm_eps)


VMEM = pl.BlockSpec(memory_space=pltpu.VMEM)
SMEM = pl.BlockSpec(memory_space=pltpu.SMEM)
ANY = pl.BlockSpec(memory_space=pl.ANY)


def call(body, name, out_shape, *inputs, scratch=(), limit=8, specs=None, deps=(), **more):
    used, unused = len(inputs), len(deps)

    def inner(*refs):
        body(*refs[:used], *refs[used + unused :])

    return pl.pallas_call(
        inner,
        in_specs=(specs or [SMEM] + [VMEM] * (used - 1)) + [ANY] * unused,
        out_specs=more.pop("out_specs", jax.tree.map(lambda _: VMEM, out_shape)),
        out_shape=out_shape,
        scratch_shapes=list(scratch),
        compiler_params=pltpu.CompilerParams(vmem_limit_bytes=limit << 20),
        cost_estimate=pl.CostEstimate(flops=1024, bytes_accessed=1024, transcendentals=0),
        name=name,
        **more,
    )(*inputs, *deps)


def sds(shape, dtype):
    return jax.ShapeDtypeStruct(shape, dtype)


def tiles(rows, body, carry):
    size = 32 if rows % 32 == 0 else 16

    def step(i, c):
        return body(pl.ds(pl.multiple_of(i * size, size), size), c)

    return lax.fori_loop(0, rows // size, step, carry, unroll=7)


def fold(x):
    return jnp.sum(x.reshape(x.shape[0] // 8, 8, x.shape[1]), axis=0)


def no_sums(width):
    return (jnp.zeros((8, width), F32), jnp.zeros((8, width), F32))


def put_sums(sums, index, pair):
    rows = jnp.concatenate([jnp.sum(v, axis=0, keepdims=True) for v in pair], axis=0)
    sums[pl.ds(index, 1)] = rows[None]


def own_at(sc, h):
    return 2 * sc[1] + h


def other_at(sc, h):
    return 2 * (1 - sc[1]) + h


def source_at(sc, nz, d):
    return lax.rem(sc[2] + (nz - d), nz)


def lanes_of(refs):
    return jnp.concatenate([r[...] for r in refs], axis=1)


def four(sc, own, rec):
    return [own.at[0], own.at[1], rec.at[0], rec.at[1]]


def four_at(sc):
    return [own_at(sc, 0), own_at(sc, 1), other_at(sc, 0), other_at(sc, 1)]


def split3(x):
    high = x.astype(BF)
    rest = x - high.astype(F32)
    middle = rest.astype(BF)
    return high, middle, (rest - middle.astype(F32)).astype(BF)


def tap_spot(t, mb):
    parts = QW // mb
    each = -(-9 // parts)
    return (t % each) * 8, t // each * mb


def tap_lines(mb):
    lines = -(-9 // (QW // mb)) * 8
    return lines + lines % 16


def join_taps(cells, mb):
    each = tap_lines(mb) // 8
    empty = jnp.zeros((8, mb), F32)
    grid = [[empty] * (QW // mb) for _ in range(each)]
    for t, cell in enumerate(cells):
        line, lane = tap_spot(t, mb)
        grid[line // 8][lane // mb] = cell
    rows = [jnp.concatenate(row, axis=1) for row in grid]
    return jnp.concatenate(rows, axis=0).astype(BF)


def bundle_kernel(sc, reduce_piece, expand_piece, taps, norms, out):
    cb, mb = reduce_piece.shape[0], norms.shape[1]
    at = pl.ds(pl.multiple_of(sc[0] * 8, 8), 8)
    tail = cb + tap_lines(mb)
    out[:cb] = reduce_piece[...]
    out[cb:tail] = join_taps([taps[t, at] for t in range(9)], mb)
    parts = [v.astype(F32) for v in split3(norms[...])]
    empty = jnp.zeros((8, mb), F32)
    grid = [[empty] * (QW // mb) for _ in range(2)]
    for t, part in enumerate(parts):
        grid[t * mb // QW][t * mb % QW // mb] = part
    rows = [jnp.concatenate(row, axis=1) for row in grid]
    out[tail : tail + 16] = jnp.concatenate(rows, axis=0).astype(BF)
    for t in range(QW // cb):
        out[tail + 16 :, t * cb : (t + 1) * cb] = expand_piece[t * cb : (t + 1) * cb]


def stack_kernel(lines, *refs):
    reduce_part, expand_part = refs[-2:]
    cb = expand_part.shape[2]
    for d, ref in enumerate(refs[:-2]):
        reduce_part[0, d] = ref[:lines]
        expand_part[0, d] = ref[lines:]


def pair_kernel(a, b, out):
    out[0] = a[0]
    out[1] = b[0]


def spread_kernel(nz, sc, *refs):
    (a0, a1, a2), (b0, b2, b1) = refs[:3], refs[3:6]
    reduce_w, expand_w, diag, mid_par, out_par, taps, norms = refs[6:]
    firsts = [a0.at[0], a1.at[0], a2.at[0], a2.at[1]]
    seconds = [b0.at[0], b1.at[0], b2.at[0], b1.at[1]]
    cb, mb = reduce_w.shape[2], norms.shape[2]
    tail = cb + tap_lines(mb)
    for d in range(nz):
        zs = source_at(sc, nz, d)
        for k in range(NQ):
            q = sc[0] ^ k
            reduce_w[q, d] = firsts[k][d, :cb]
            for t in range(QW // cb):
                expand_w[q, d, t * cb : (t + 1) * cb] = seconds[k][d, :, t * cb : (t + 1) * cb]
            block = firsts[k][d, cb:tail].astype(F32)
            at = pl.ds(pl.multiple_of(q * 8, 8), 8)
            for t in range(9):
                line, lane = tap_spot(t, mb)
                taps[zs, t, at] = block[line : line + 8, lane : lane + mb]
        block = firsts[0][d, tail : tail + 16].astype(F32)
        total = jnp.zeros((8, mb), F32)
        for t in range(3):
            line, lane = t * mb // QW * 8, t * mb % QW
            total = total + block[line : line + 8, lane : lane + mb]
        norms[zs] = total
    keep = group_mask()
    half = nz // 2
    for h in range(2):
        mine = range(h * half, (h + 1) * half)
        mid_par[h] = jnp.concatenate([norms[v][:4] for v in mine], axis=1)
        for t in range(9):
            cell = jnp.concatenate([taps[v, t] for v in mine], axis=1)
            full = jnp.concatenate([cell] * (QW // GW), axis=0)
            diag[h, t] = jnp.where(keep, full, 0.0).astype(BF)
    per = cb // mb
    for v in range(nz):
        lines = norms[v]
        out_par[v] = jnp.concatenate(
            [
                jnp.concatenate([lines[4 + r * per + j : 5 + r * per + j] for j in range(per)], axis=1)
                for r in range(2)
            ],
            axis=0,
        )


def group_mask():
    group_row = lax.broadcasted_iota(jnp.int32, (QW, QW), 0) // GW
    group_col = lax.broadcasted_iota(jnp.int32, (QW, QW), 1) // GW
    return group_row == group_col


def cut_kernel(nz, d, sc, cot, out, sem):
    images = out.shape[1]
    start = pl.multiple_of(lax.rem(sc[2] + d, nz) * images, images)
    copy = pltpu.make_async_copy(cot.at[:, pl.ds(start, images)], out, sem)
    copy.start()
    copy.wait()


def pick_kernel(k, sc, parts, out):
    out[...] = parts[sc[0] ^ k]


def pick_both_kernel(nz, k, sc, parts, taps, out):
    q, cb = sc[0] ^ k, parts.shape[2]
    for d in range(nz):
        out[d, :cb] = parts[q, d]
        out[d, cb:] = taps[q, source_at(sc, nz, d)]


def total_kernel(*refs):
    total = refs[0][...].astype(F32)
    for ref in refs[1:-1]:
        total = total + ref[...].astype(F32)
    refs[-1][...] = total.astype(refs[-1].dtype)


def home_kernel(nz, sc, *refs):
    parts, outs = refs[:NQ], refs[NQ:]
    for d in range(nz):
        total = parts[0][d].astype(F32)
        for k in range(1, NQ):
            total = total + parts[k][d].astype(F32)
        outs[d][...] = total.astype(outs[d].dtype)


def pick3(masks, values):
    return masks[0] * values[0] + masks[1] * values[1] + masks[2] * values[2]


def crop_kernel(nz, d, sc, src, off, out):
    images, lanes = out.shape[1:]
    start = pl.multiple_of(lax.rem(sc[2] + d, nz) * images, images)
    at = pl.ds(start, images)
    row = jnp.broadcast_to(off[at, 0:1], (images, 128))
    col = jnp.broadcast_to(off[at, 1:2], (images, 128))
    row_masks = [(row == a).astype(F32).astype(BF) for a in range(3)]
    col_masks = [(col == a).astype(F32).astype(BF) for a in range(3)]
    for base in range(0, lanes, 128):
        span = slice(base, base + 128)
        lines = []
        for i in range(SRC):
            cells = [src[i, j, at, span] for j in range(SRC)]
            lines.append([pick3(col_masks, cells[j : j + 3]) for j in range(HW)])
            if i >= 2:
                for j in range(HW):
                    cell = pick3(row_masks, [line[j] for line in lines[i - 2 : i + 1]])
                    out[(i - 2) * HW + j, :, span] = cell


def reduce_kernel(nz, sc, *refs):
    xs, (w, own, other) = refs[:nz], refs[nz:]
    x = lanes_of(xs)
    for h in range(2):
        own[h] = dot(x, w[own_at(sc, h)].reshape(x.shape[1], QW))
        other[h] = dot(x, w[other_at(sc, h)].reshape(x.shape[1], QW)).astype(BF)


def first_sums_kernel(sc, own, rec, sums):
    for h in range(2):

        def body(at, c):
            v = own[h, at] + rec[h, at].astype(F32)
            return c[0] + fold(v), c[1] + fold(v * v)

        put_sums(sums, h, tiles(own.shape[1], body, no_sums(QW)))


def zero_border(pad, images):
    span = pad.shape[1]
    pad[0] = jnp.zeros_like(pad[0])
    pad[SRC - 1] = jnp.zeros_like(pad[0])
    edge = jnp.zeros((HW, images, pad.shape[2]), pad.dtype)
    pad[1 : HW + 1, 0:images] = edge
    pad[1 : HW + 1, span - images : span] = edge


def each_cell(images, body, carry):
    def line(i, c):
        for j in range(HW):
            at = pl.ds(pl.multiple_of((i * HW + j) * images, images), images)
            c = body(i, j, at, c)
        return c

    return lax.fori_loop(0, HW, line, carry)


def conv_kernel(count, images, sc, own, rec, tot, par, diag, act, v2, sums, pad):
    rows = HW * images
    zero_border(pad, images)
    for h in range(2):
        center, inv = norm_rows(tot[h, 0:1], tot[h, 1:2], count)
        gain, shift = par[h, 0:1], par[h, 1:2]

        def fill(i, j, at, c):
            v = own[h, at] + rec[h, at].astype(F32)
            a = gelu((v - center) * inv * gain + shift).astype(BF)
            act[h, at] = a
            pad[i + 1, (j + 1) * images : (j + 2) * images] = a
            return c

        each_cell(images, fill, 0)

        def taps(i, c):
            acc = jnp.zeros((rows, QW), F32)
            for di in range(3):
                line = pad.at[i + di]
                for dj in range(3):
                    acc = acc + dot(line[dj * images : dj * images + rows], diag[h, di * 3 + dj])
            v2[h, pl.ds(pl.multiple_of(i * rows, rows), rows)] = acc
            return c[0] + fold(acc), c[1] + fold(acc * acc)

        put_sums(sums, h, lax.fori_loop(0, HW, taps, no_sums(QW)))


def second_act_kernel(count, sc, v2, tot, par, out):
    for h in range(2):
        center, inv = norm_rows(tot[h, 0:1], tot[h, 1:2], count)
        gain, shift = par[h, 2:3], par[h, 3:4]

        def body(at, c):
            out[h, at] = gelu((v2[h, at] - center) * inv * gain + shift).astype(BF)
            return c

        tiles(v2.shape[1], body, 0)


def expand_kernel(nz, sc, own, rec, w, e, sums):
    x = lanes_of(four(sc, own, rec))
    for d in range(nz):
        e[d] = dot(x, jnp.concatenate([w[k, d] for k in four_at(sc)], axis=0))

        def body(at, c):
            v = e[d, at]
            return c[0] + fold(v), c[1] + fold(v * v)

        put_sums(sums, source_at(sc, nz, d), tiles(e.shape[1], body, no_sums(e.shape[2])))


def up_kernel(nz, count, sc, e, tot, par, *refs):
    xs, cots = refs[:nz], refs[nz : 2 * nz]
    outs, (up, sums) = refs[2 * nz : 3 * nz], refs[3 * nz :]
    for d in range(nz):
        zs = source_at(sc, nz, d)
        t = tot[zs]
        center, inv = norm_rows(t[0:1], t[1:2], count)
        gain, shift = par[zs, 0:1], par[zs, 1:2]

        def body(at, c):
            hat = (e[d, at] - center) * inv
            value, slope = gelu_both(hat * gain + shift + xs[d][at].astype(F32))
            outs[d][at] = value.astype(BF)
            u = cots[d][at].astype(F32) * slope
            up[d, at] = u
            return c[0] + fold(u), c[1] + fold(u * hat)

        put_sums(sums, zs, tiles(e.shape[1], body, no_sums(e.shape[2])))


def add_kernel(a, b, out):
    out[...] = a[...] + b[...]


def pass_kernel(value, out):
    out[...] = value[...]


def expand_back_kernel(nz, count, sc, e, up, tot, tot_b, par, w, eg, own, other):
    for d in range(nz):
        zs = source_at(sc, nz, d)
        t, b = tot[zs], tot_b[zs]
        center, inv = norm_rows(t[0:1], t[1:2], count)
        factor, mean_d, mean_x = inv * par[zs, 0:1], b[0:1] / count, b[1:2] / count

        def body(at, c):
            hat = (e[d, at] - center) * inv
            eg[d, at] = (factor * (up[d, at] - mean_d - hat * mean_x)).astype(BF)
            return c

        tiles(e.shape[1], body, 0)
    grads = lanes_of([eg.at[d] for d in range(nz)])
    for h in range(2):
        for index, out in ((own_at(sc, h), own), (other_at(sc, h), other)):
            out[h] = dot_t(grads, lanes_of([w.at[index, d] for d in range(nz)])).astype(out.dtype)


def second_up_kernel(count, sc, own, rec, v2, tot, par, up, sums):
    for h in range(2):
        center, inv = norm_rows(tot[h, 0:1], tot[h, 1:2], count)
        gain, shift = par[h, 2:3], par[h, 3:4]

        def body(at, c):
            hat = (v2[h, at] - center) * inv
            u = (own[h, at] + rec[h, at].astype(F32)) * gelu_both(hat * gain + shift)[1]
            up[h, at] = u
            return c[0] + fold(u), c[1] + fold(u * hat)

        put_sums(sums, h, tiles(v2.shape[1], body, no_sums(QW)))


def conv_back_kernel(
    count, images, sc, up2, v2, tot2, tot2b, par, diag, own, rec, tot1, cg, up1, sums, pad, temp
):
    rows = HW * images
    zero_border(pad, images)
    for h in range(2):
        center2, inv2 = norm_rows(tot2[h, 0:1], tot2[h, 1:2], count)
        factor = inv2 * par[h, 2:3]
        mean_d, mean_x = tot2b[h, 0:1] / count, tot2b[h, 1:2] / count

        def fill(i, j, at, c):
            hat = (v2[h, at] - center2) * inv2
            g = (factor * (up2[h, at] - mean_d - hat * mean_x)).astype(BF)
            cg[h, at] = g
            pad[i + 1, (j + 1) * images : (j + 2) * images] = g
            return c

        each_cell(images, fill, 0)
        center, inv = norm_rows(tot1[h, 0:1], tot1[h, 1:2], count)
        gain, shift = par[h, 0:1], par[h, 1:2]

        def taps(i, c):
            acc = jnp.zeros((rows, QW), F32)
            for di in range(3):
                line = pad.at[i + 2 - di]
                for dj in range(3):
                    start = (2 - dj) * images
                    acc = acc + dot_t(line[start : start + rows], diag[h, di * 3 + dj])
            temp[...] = acc
            for j in range(HW):
                at = pl.ds(pl.multiple_of(i * rows + j * images, images), images)
                hat = (own[h, at] + rec[h, at].astype(F32) - center) * inv
                u = temp[j * images : (j + 1) * images] * gelu_both(hat * gain + shift)[1]
                up1[h, at] = u
                c = (c[0] + fold(u), c[1] + fold(u * hat))
            return c

        put_sums(sums, h, lax.fori_loop(0, HW, taps, no_sums(QW)))


def first_grad_kernel(count, sc, up1, own, rec, tot, tot_b, par, out):
    for h in range(2):
        center, inv = norm_rows(tot[h, 0:1], tot[h, 1:2], count)
        factor = inv * par[h, 0:1]
        mean_d, mean_x = tot_b[h, 0:1] / count, tot_b[h, 1:2] / count

        def body(at, c):
            hat = (own[h, at] + rec[h, at].astype(F32) - center) * inv
            out[h, at] = (factor * (up1[h, at] - mean_d - hat * mean_x)).astype(BF)
            return c

        tiles(up1.shape[1], body, 0)


def input_grad_kernel(d, sc, own, rec, up, w, out):
    weights = lanes_of([w.at[k, d] for k in four_at(sc)])
    out[...] = (up[d] + dot_t(lanes_of(four(sc, own, rec)), weights)).astype(BF)


def reduce_wgrad_kernel(nz, sc, own, rec, *refs):
    xs, out = refs[:nz], refs[nz]
    grads = lanes_of(four(sc, own, rec))
    for d in range(nz):
        g = dot_rows(xs[d][...], grads).astype(BF)
        for j, k in enumerate(four_at(sc)):
            out[k, d] = g[:, j * QW : (j + 1) * QW]


def expand_wgrad_kernel(nz, sc, own, rec, eg, out):
    width = eg.shape[2]
    grads = lanes_of([eg.at[d] for d in range(nz)])
    for ref, k in zip(four(sc, own, rec), four_at(sc)):
        g = dot_rows(ref[...], grads).astype(BF)
        for d in range(nz):
            out[k, d] = g[:, d * width : (d + 1) * width]


def conv_wgrad_kernel(images, mb, sc, act, cg, out, pad):
    rows = HW * images
    keep = group_mask()
    zero_border(pad, images)
    for h in range(2):
        for i in range(HW):
            pad[i + 1, images : images + rows] = act[h, i * rows : (i + 1) * rows]
        grad = cg[h]
        cells = []
        for di in range(3):
            for dj in range(3):
                window = pad[di : di + HW, dj * images : dj * images + rows]
                full = dot_rows(window.reshape(HW * rows, QW), grad)
                full = jnp.where(keep, full, 0.0)
                cells.append(jnp.sum(full.reshape(QW // GW, GW, QW), axis=0))
        for q in range(NQ):
            for a in range(QW // mb):
                pieces = [c[q * 8 : q * 8 + 8, a * mb : (a + 1) * mb] for c in cells]
                out[q, h * (QW // mb) + a] = join_taps(pieces, mb)


def square_sum(x):
    return jnp.sum(x.reshape(x.shape[0] // 8, 8, x.shape[1]), axis=0)


def lane_fold(x):
    return sum(x[:, j : j + 128] for j in range(0, x.shape[1], 128)) if x.shape[1] > 128 else x


def expand_home_kernel(nz, sc, *refs):
    parts, (grad, squares, whole) = refs[:NQ], refs[NQ:]
    rows = grad.shape[0] // (2 * nz)
    half = nz // 2
    for k in range(NQ):
        whole[sc[0] ^ k] = parts[k][...]
    total = jnp.zeros((8, 128), F32)
    for q in range(NQ):
        for a in range(half):
            g = whole[q, a * rows : (a + 1) * rows].astype(F32)
            start = (((q % 2) * half + a) * 2 + q // 2) * rows
            grad[start : start + rows] = g
            total = total + lane_fold(square_sum(g * g))
    squares[...] = total


def reduce_home_kernel(nz, sc, *refs):
    parts, (mid, out, before) = refs[:NQ], refs[NQ : NQ + 3]
    grad, taps, squares, whole = refs[NQ + 3 :]
    cb, mb = grad.shape[0], taps.shape[2]
    half = nz // 2
    for k in range(NQ):
        whole[sc[0] ^ k] = parts[k][...]
    total = before[...]
    for q in range(NQ):
        for a in range(half):
            start = (((q % 2) * half + a) * 2 + q // 2) * mb
            grad[:, start : start + mb] = whole[q, :cb, a * mb : (a + 1) * mb].astype(F32)
        block = whole[q, cb:].astype(F32)
        for t in range(9):
            line, lane = tap_spot(t, mb)
            taps[t, q * 8 : (q + 1) * 8] = block[line : line + 8, lane : lane + mb]
        full = whole[q].astype(F32)
        total = total + lane_fold(square_sum(full * full))
    extra = jnp.sum(mid[...] * mid[...]) + jnp.sum(out[...] * out[...])
    first = lax.broadcasted_iota(jnp.int32, (8, 128), 0) + lax.broadcasted_iota(
        jnp.int32, (8, 128), 1
    )
    total = total + jnp.where(first == 0, extra, 0.0)
    squares[...] = jnp.broadcast_to(jnp.sum(total, keepdims=True), (8, 128))


def place_kernel(nz, d, sc, block, *refs):
    out, sem = refs[-2:]
    images = block.shape[1]
    start = pl.multiple_of(lax.rem(sc[2] + d, nz) * images, images)
    copy = pltpu.make_async_copy(block, out.at[:, pl.ds(start, images)], sem)
    copy.start()
    copy.wait()


def adam_step(weight, gradient, momentum, variance, learn_rate, decay_rate):
    momentum_new = moment_decay * momentum + (1.0 - moment_decay) * gradient
    variance_new = moment_decay * variance + (1.0 - moment_decay) * gradient * gradient
    correction = 1.0 - moment_decay**STEP
    direction = momentum_new / correction / (jnp.sqrt(variance_new / correction) + adam_eps)
    weight_new = weight - learn_rate * (direction + decay_rate * weight)
    return (weight_new, momentum_new, variance_new, weight_new.astype(BF))


def shards(
    source,
    offsets,
    cotangent,
    reduce_weight,
    reduce_first,
    reduce_second,
    group_weight,
    group_first,
    group_second,
    expand_weight,
    expand_first,
    expand_second,
    mid_norms,
    mid_first,
    mid_second,
    out_norms,
    out_first,
    out_second,
):
    nd, ng = lax.axis_size("dp"), lax.axis_size("group")
    nz = ng // 2
    gi = lax.axis_index("group")
    z, core = gi // 2, gi % 2
    p = lax.axis_index("dp") % NQ
    sc = jnp.stack([p, core, z]).astype(jnp.int32)
    n = source.shape[0]
    images = n // nz
    rows = SPOTS * images
    cb = source.shape[3]
    mb = group_weight.shape[3]
    zh = nz // 2
    count = float(SPOTS * n * nd)

    def over_z(value, d):
        pairs = [(2 * a + c, 2 * ((a + d) % nz) + c) for a in range(nz) for c in range(2)]
        return lax.ppermute(value, "group", pairs)

    def over_core(value):
        return lax.ppermute(value, "group", [(a, a ^ 1) for a in range(ng)])

    def over_dp(value, k):
        return lax.ppermute(value, "dp", [(a, a ^ k) for a in range(nd)])

    def over_all_dp(value, *pins):
        k = 1
        while k < nd:
            other = over_dp(value, k)
            k *= 2
            if k < nd or not pins:
                value = value + other
            else:
                value = call(
                    add_kernel,
                    "add",
                    sds(value.shape, F32),
                    value,
                    other,
                    specs=[VMEM] * 2,
                    deps=pins,
                )
        return value

    def over_all_z(value):
        k = 2
        while k < ng:
            value = value + lax.ppermute(value, "group", [(a, a ^ k) for a in range(ng)])
            k *= 2
        return value

    def everywhere(value, *pins):
        return over_all_z(over_all_dp(value, *pins))

    src = source.transpose(1, 2, 0, 3)
    crops = []
    order = [1] + list(range(2, nz))[::-1] + [0]
    for d in order:
        crop = call(
            functools.partial(crop_kernel, nz, d),
            "crop",
            sds((SPOTS, images, cb), BF),
            sc,
            src,
            offsets,
            deps=crops[-1:],
        ).reshape(rows, cb)
        crops.append(crop)
    pixels = [over_z(crops[order.index(d)], d) if d else crops[-1] for d in range(nz)]

    col_starts = [((p % 2) * zh + j) * 2 * mb + (p // 2) * mb for j in range(zh)]
    reduce_piece = jnp.concatenate(
        [lax.dynamic_slice_in_dim(reduce_weight, s, mb, 1) for s in col_starts], axis=1
    ).astype(BF)
    expand_piece = (
        lax.dynamic_slice(
            expand_weight.reshape(nz, 2, mb, cb),
            ((p % 2) * zh, p // 2, 0, 0),
            (zh, 1, mb, cb),
        )
        .reshape(QW, cb)
        .astype(BF)
    )

    pack = jnp.concatenate([mid_norms, out_norms.reshape(-1, mb)], axis=0)
    bundle = call(
        bundle_kernel,
        "bundle",
        sds((2 * cb + tap_lines(mb) + 16, QW), BF),
        sc,
        reduce_piece,
        expand_piece,
        group_weight.reshape(9, GW, mb),
        pack,
        deps=crops[:1],
    )
    bundles = [bundle] + [over_z(bundle, d) for d in range(1, nz)]

    lines = cb + tap_lines(mb) + 16
    first_w, second_w = call(
        functools.partial(stack_kernel, lines),
        "stack",
        [sds((1, nz, lines, QW), BF), sds((1, nz, cb, QW), BF)],
        *bundles,
        specs=[VMEM] * nz,
        deps=[crops[-1], pixels[1]],
    )

    def pair(a, b):
        shape = sds((2,) + a.shape[1:], BF)
        return call(pair_kernel, "pair", shape, a, b, specs=[VMEM] * 2, deps=[pixels[-1]])

    first_x, second_y = over_dp(first_w, 1), over_dp(second_w, 2)
    first_y, second_x = (
        over_dp(pair(first_w, first_x), 2),
        over_dp(pair(second_w, second_y), 1),
    )
    reduce_q, expand_q, diag, mid_par, out_par = call(
        functools.partial(spread_kernel, nz),
        "spread",
        [
            sds((NQ, nz, cb, QW), BF),
            sds((NQ, nz, QW, cb), BF),
            sds((2, 9, QW, QW), BF),
            sds((2, 4, QW), F32),
            sds((nz, 2, cb), F32),
        ],
        sc,
        first_w,
        first_x,
        first_y,
        second_w,
        second_y,
        second_x,
        scratch=[pltpu.VMEM((nz, 9, GW, mb), F32), pltpu.VMEM((nz, 8, mb), F32)],
    )

    cot = cotangent.transpose(1, 2, 0, 3).reshape(SPOTS, n, cb)

    def cut(d, *deps):
        piece = call(
            functools.partial(cut_kernel, nz, d),
            "cut",
            sds((SPOTS, images, cb), BF),
            sc,
            cot,
            specs=[SMEM, ANY],
            scratch=[pltpu.SemaphoreType.DMA],
            deps=deps,
        ).reshape(rows, cb)
        return piece

    def turn(d):
        return 0 if d == 1 else (1 if d == nz - 1 else 2)

    half_f, half_b = sds((2, rows, QW), F32), sds((2, rows, QW), BF)
    sum2_s, sumz_s = sds((2, 2, QW), F32), sds((nz, 2, cb), F32)
    pad_s = pltpu.VMEM((SRC, SRC * images, QW), BF)

    own1, oth1 = call(
        functools.partial(reduce_kernel, nz),
        "reduce",
        [half_f, half_b],
        sc,
        *pixels,
        reduce_q,
        limit=16,
        deps=[diag, mid_par, out_par, expand_q],
    )
    rec1 = over_core(oth1)
    turns = [[d for d in range(1, nz) if turn(d) == t] for t in range(3)]
    cots = [cut(0, diag)] + [None] * (nz - 1)

    def send_cots(t, *deps):
        pieces = [cut(d, *deps) for d in turns[t]]
        for d, piece in zip(turns[t], pieces):
            cots[d] = over_z(piece, d)
        return pieces, [cots[d] for d in turns[t]]

    sent, pins = send_cots(0, oth1)
    sums1 = call(first_sums_kernel, "first_sums", sum2_s, sc, own1, rec1, deps=sent)
    tot1 = everywhere(sums1, *pins)
    sent, pins = send_cots(1, tot1)
    act, v2, sums2 = call(
        functools.partial(conv_kernel, count, images),
        "conv",
        [half_b, half_f, sum2_s],
        sc,
        own1,
        rec1,
        tot1,
        mid_par,
        diag,
        scratch=[pad_s],
        deps=sent,
    )
    tot2 = everywhere(sums2, *pins)
    sent, pins = send_cots(2, tot2)
    sa = call(
        functools.partial(second_act_kernel, count),
        "second_act",
        half_b,
        sc,
        v2,
        tot2,
        mid_par,
        deps=sent,
    )
    sa_rec = over_core(sa)
    e, sums3 = call(
        functools.partial(expand_kernel, nz),
        "expand",
        [sds((nz, rows, cb), F32), sumz_s],
        sc,
        sa,
        sa_rec,
        expand_q,
        limit=12,
    )
    tot3 = everywhere(sums3)
    res = call(
        functools.partial(up_kernel, nz, count),
        "up",
        [sds((rows, cb), BF)] * nz + [sds((nz, rows, cb), F32), sumz_s],
        sc,
        e,
        tot3,
        out_par,
        *pixels,
        *cots,
    )
    values, up3, sums3b = res[:nz], res[nz], res[nz + 1]
    part3b = over_all_z(sums3b)
    tot3b = over_all_dp(part3b)
    outs = list(values)

    def later(value, *deps):
        return call(
            pass_kernel, "pass", sds(value.shape, value.dtype), value, specs=[VMEM], deps=deps
        )

    def place(blocks, *deps):
        result = None
        for d in range(nz):
            extra = () if result is None else (result,)
            result = call(
                functools.partial(place_kernel, nz, d),
                "place",
                sds((SPOTS, n, cb), BF),
                sc,
                blocks[d].reshape(SPOTS, images, cb),
                *extra,
                specs=[SMEM, VMEM] + [ANY] * len(extra),
                out_specs=ANY,
                scratch=[pltpu.SemaphoreType.DMA],
                input_output_aliases={2: 0} if extra else {},
                deps=deps,
            )
        return result.reshape(HW, HW, n, cb).transpose(2, 0, 1, 3)

    def send_outs(t, *deps):
        pieces = [later(values[d], *deps) for d in turns[t]]
        for d, piece in zip(turns[t], pieces):
            outs[d] = over_z(piece, -d)
        return pieces, [outs[d] for d in turns[t]]

    sent, pins = send_outs(0, part3b)
    eg, own2, oth2 = call(
        functools.partial(expand_back_kernel, nz, count),
        "expand_back",
        [sds((nz, rows, cb), BF), half_f, half_b],
        sc,
        e,
        up3,
        tot3,
        tot3b,
        out_par,
        expand_q,
        deps=sent,
    )
    rec2 = over_core(oth2)
    up2, sums2b = call(
        functools.partial(second_up_kernel, count),
        "second_up",
        [half_f, sum2_s],
        sc,
        own2,
        rec2,
        v2,
        tot2,
        mid_par,
    )
    mid2b = over_all_dp(sums2b, *pins)
    tot2b = over_all_z(mid2b)
    sent, pins = send_outs(1, tot2b)
    cg, up1, sums1b = call(
        functools.partial(conv_back_kernel, count, images),
        "conv_back",
        [half_b, half_f, sum2_s],
        sc,
        up2,
        v2,
        tot2,
        tot2b,
        mid_par,
        diag,
        own1,
        rec1,
        tot1,
        scratch=[pad_s, pltpu.VMEM((HW * images, QW), F32)],
        deps=sent,
    )
    tot1b = everywhere(sums1b, *pins)
    sent, _ = send_outs(2, tot1b)
    fg = call(
        functools.partial(first_grad_kernel, count),
        "first_grad",
        half_b,
        sc,
        up1,
        own1,
        rec1,
        tot1,
        tot1b,
        mid_par,
        deps=sent,
    )
    fg_rec = over_core(fg)
    def input_block(d, *deps):
        return call(
            functools.partial(input_grad_kernel, d),
            "input_grad",
            sds((rows, cb), BF),
            sc,
            fg,
            fg_rec,
            up3,
            reduce_q,
            deps=deps,
        )

    expand_parts = call(
        functools.partial(expand_wgrad_kernel, nz),
        "expand_wgrad",
        sds((NQ, nz, QW, cb), BF),
        sc,
        sa,
        sa_rec,
        eg,
        limit=12,
    )
    first = input_block(2)
    conv_parts = call(
        functools.partial(conv_wgrad_kernel, images, mb),
        "conv_wgrad",
        sds((NQ, nz, tap_lines(mb), QW), BF),
        sc,
        act,
        cg,
        scratch=[pad_s],
        deps=[first],
    )
    reduce_parts = call(
        functools.partial(reduce_wgrad_kernel, nz),
        "reduce_wgrad",
        sds((NQ, nz, cb, QW), BF),
        sc,
        fg,
        fg_rec,
        *pixels,
        limit=12,
        deps=[conv_parts],
    )
    reduce_picks = [
        call(
            functools.partial(pick_both_kernel, nz, k),
            "pick_both",
            sds((nz, cb + tap_lines(mb), QW), BF),
            sc,
            reduce_parts,
            conv_parts,
            deps=[outs[d] for d in turns[2]],
        )
        for k in range(NQ)
    ]
    input_blocks = {2: first}
    last = reduce_picks[-1]
    for d in [d for d in range(1, nz) if d != 2] + [0]:
        last = input_block(d, last)
        input_blocks[d] = last
    input_moved = [over_z(input_blocks[d], -d) if d else input_blocks[0] for d in range(nz)]

    def low_sum(mine, others):
        total = mine.astype(F32)
        for value in others:
            total = total + value.astype(F32)
        return total

    def picks(parts, *deps):
        return [
            call(
                functools.partial(pick_kernel, k),
                "pick",
                sds(parts.shape[1:], BF),
                sc,
                parts,
                deps=deps,
            )
            for k in range(NQ)
        ]

    def home(parts, deps, pins):
        shape = parts[0].shape[1:]
        pieces = call(
            functools.partial(home_kernel, nz),
            "home",
            [sds(shape, F32)] + [sds(shape, BF)] * (nz - 1),
            sc,
            parts[0],
            *[over_dp(parts[k], k) for k in range(1, NQ)],
            deps=deps,
        )
        low = call(
            total_kernel,
            "total",
            sds(shape, BF),
            pieces[0],
            *[over_z(pieces[d], -d) for d in range(1, nz)],
            specs=[VMEM] * nz,
            deps=pins,
        )
        k = NQ
        while k < nd:
            low = low_sum(low, [over_dp(low, k)]).astype(BF)
            k *= 2
        return [low] + [over_dp(low, k) for k in range(1, NQ)]

    expand_pieces = home(picks(expand_parts, mid2b), [last], [])
    expand_wgrad, squares = call(
        functools.partial(expand_home_kernel, nz),
        "expand_home",
        [sds((MID, cb), F32), sds((8, 128), F32)],
        sc,
        *expand_pieces,
        scratch=[pltpu.VMEM((NQ, QW, cb), BF)],
    )
    reduce_pieces = home(
        reduce_picks,
        [input_moved[2], last, squares],
        [input_moved[d] for d in range(1, nz) if d not in (2, nz - 1)],
    )
    input_grad = place(input_moved)
    output = place(outs, last)

    def my_mid(total):
        lanes = lax.dynamic_slice_in_dim(total.transpose(1, 0, 2).reshape(2, 2 * QW), z * mb, mb, 1)
        return [lanes[1], lanes[0]]

    mid_grads = jnp.stack(my_mid(tot1b) + my_mid(tot2b))
    mine3 = lax.dynamic_index_in_dim(tot3b, z, 0, keepdims=False)
    out_grads = jnp.stack([mine3[1], mine3[0]])

    reduce_wgrad, tap_grad, total_sq = call(
        functools.partial(reduce_home_kernel, nz),
        "reduce_home",
        [sds((cb, MID), F32), sds((9, GW, mb), F32), sds((8, 128), F32)],
        sc,
        *reduce_pieces,
        mid_grads,
        out_grads,
        squares,
        scratch=[pltpu.VMEM((NQ, cb + tap_lines(mb), QW), BF)],
    )
    group_wgrad = tap_grad.reshape(group_weight.shape)
    k = 1
    while k < ng:
        total_sq = total_sq + lax.ppermute(total_sq, "group", [(a, a ^ k) for a in range(ng)])
        k *= 2
    grad_norm = jnp.sqrt(total_sq[0, 0])
    clip_scale = jnp.minimum(1.0, clip_norm / (grad_norm + 1e-06))
    reduce_out = adam_step(
        reduce_weight,
        reduce_wgrad * clip_scale,
        reduce_first,
        reduce_second,
        1.0 / jnp.sqrt(1.0 * CIN),
        0.1,
    )
    group_out = adam_step(
        group_weight,
        group_wgrad * clip_scale,
        group_first,
        group_second,
        1.0 / jnp.sqrt(9.0 * GW),
        0.1,
    )
    expand_out = adam_step(
        expand_weight,
        expand_wgrad * clip_scale,
        expand_first,
        expand_second,
        1.0 / jnp.sqrt(1.0 * MID),
        0.1,
    )
    mid_out = adam_step(mid_norms, mid_grads * clip_scale, mid_first, mid_second, 0.5, 0.0)
    out_out = adam_step(out_norms, out_grads * clip_scale, out_first, out_second, 0.5, 0.0)
    return (
        output,
        input_grad,
        grad_norm,
        *reduce_out,
        *group_out,
        *expand_out,
        *mid_out,
        *out_out,
    )


def solution(mesh):
    images = P("dp", None, None, "group")
    rows, cols = P("group", None), P(None, "group")
    kernel = P(None, None, None, "group")
    in_specs = (
        (images, P("dp", None), images) + (rows,) * 3 + (kernel,) * 3 + (cols,) * 3 + (cols,) * 6
    )
    out_specs = (images, images, P()) + (rows,) * 4 + (kernel,) * 4 + (cols,) * 4 + (cols,) * 8
    return jax.shard_map(shards, mesh=mesh, in_specs=in_specs, out_specs=out_specs, check_vma=False)
```

time: 1080 us -> 499 us (0.46)
  waiting for transfers between devices: 597 us -> 251 us
  local copies, waits for them, and re-layouts: 207 us -> 13.5 us
  Pallas kernels: 0 us -> 109 us
  starting transfers between devices: 0.21 us -> 107 us
  matrix products: 101 us -> 0 us
  blocking collectives: 71 us -> 0 us
  other arithmetic: 73.4 us -> 9.26 us
  between operations: 20 us -> 3.88 us
    reduce_scatter x1 -> x0, waiting for transfers between devices: 254 us -> none  [shards(): lax.psum_scatter(lax.dot_general(weight_block, pixels, (((0,), (1,)), (()...]
    ppermute x0 -> x68, waiting for transfers between devices: none -> 251 us  [the longest x21 137 us: over_z(): return lax.ppermute(value, 'group', pairs)]
    all_gather x2 -> x0, waiting for transfers between devices: 179 us -> none  [the longest x1 101 us: shards(): mid_full = lax.all_gather(second_act, 'group', axis=0, tiled=True)]
    unnamed x6 -> x0, waiting for transfers between devices: 129 us -> none
    pallas_call x0 -> x59, Pallas kernels: none -> 109 us  [call(): pl.pallas_call(inner, in_specs=(specs or [SMEM] + [VMEM] * (used - 1)) +...]
    ppermute x0 -> x68, starting transfers between devices: none -> 107 us  [the longest x21 52 us: over_z(): return lax.ppermute(value, 'group', pairs)]
    dot_general x33 -> x0, matrix products: 101 us -> none  [the longest x9 17.2 us: conv_backward(): jnp.einsum('gik,gok->gio', act_window, grad_middle, preferred_element_typ...]
    psum x7 -> x0, blocking collectives: 71 us -> none  [the longest x6 53.9 us: channel_sums(): return lax.psum((sum_values, sum_squares), 'dp')]
  transfers between devices with their start and end apart: 5 -> 68, of which waited for: 5 -> 45; matrix products, arithmetic and copies ran while one was open for 7% -> 0% of each run, Pallas kernels for 0% -> 17%
where the time goes in v2:
time: 499 us; the launch traced here: 493 us
  waiting for transfers between devices  251 us (50%)
  Pallas kernels  109 us (22%)
  starting transfers between devices  107 us (21%)
  local copies, waits for them, and re-layouts  13.5 us (3%)
  other arithmetic  9.26 us (2%)
    ppermute x21, waiting for transfers between devices, over_z(): return lax.ppermute(value, 'group', pairs)  137 us
    pallas_call x59, Pallas kernels, call(): pl.pallas_call(inner, in_specs=(specs or [SMEM] + [VMEM] * (used - 1)) +...  109 us
    ppermute x28, waiting for transfers between devices, over_dp(): return lax.ppermute(value, 'dp', [(a, a ^ k) for a in range(nd)])  58.8 us
    ppermute x21, starting transfers between devices, over_z(): return lax.ppermute(value, 'group', pairs)  52 us
    ppermute x12, waiting for transfers between devices, over_all_z(): lax.ppermute(value, 'group', [(a, a ^ k) for a in range(ng)])  48.1 us
    ppermute x28, starting transfers between devices, over_dp(): return lax.ppermute(value, 'dp', [(a, a ^ k) for a in range(nd)])  39.9 us
    ppermute x12, starting transfers between devices, over_all_z(): lax.ppermute(value, 'group', [(a, a ^ k) for a in range(ng)])  11.4 us
    unnamed x85, local copies, waits for them, and re-layouts  11 us
  transfers between devices with their start and end apart: 68, of which 45 were waited for; matrix products, arithmetic and copies ran while one was open for 0% of the time, Pallas kernels for 17%

profile of v2, /device:TPU:0, one launch (start us, length us, event | category | flops | bytes accessed | tf_op | source)
XLA Modules:
  0.0 493.0 jit_solution(15454584562036908996)
XLA Ops:
  5.1 3.1 collective-permute-start
  13.5 2.8 collective-permute-start.5
  22.4 13.0 %collective-permute-done.3.refs_1_ = bf16[576,256]{1,0:T(8,128)(2,1)S(1)} collective-permute-done((bf16[576,256]{1,0:T(8,128)(2,1)S(1)}, bf16[576,256]{1,0:T(8,128)(2,1)S(1)}, u32[]{:S(2)}, u32[]{:S(2)}) %collective-permute-start.3) | collective-permute-done | bytes 294944 | tf_op jit(solution)/shard_map/ppermute | solution.py:657
  35.4 11.8 %collective-permute-done.4.refs_2_ = bf16[576,256]{1,0:T(8,128)(2,1)S(1)} collective-permute-done((bf16[576,256]{1,0:T(8,128)(2,1)S(1)}, bf16[576,256]{1,0:T(8,128)(2,1)S(1)}, u32[]{:S(2)}, u32[]{:S(2)}) %collective-permute-start.4) | collective-permute-done | bytes 294944 | tf_op jit(solution)/shard_map/ppermute | solution.py:657
  50.4 13.9 %collective-permute-done.2.refs_2_.refs_4_.refs_7_.refs_6_ = bf16[1568,256]{1,0:T(8,128)(2,1)S(1)} collective-permute-done((bf16[1568,256]{1,0:T(8,128)(2,1)S(1)}, bf16[1568,256]{1,0:T(8,128)(2,1)S(1)}, u32[]{:S(2)}, u32[]{:S(2)}) %collective-permute-start.2) | collective-permute-done | bytes 802848 | tf_op jit(solution)/shard_map/ppermute | solution.py:657
  67.6 16.1 %collective-permute-start.1 = (bf16[1568,256]{1,0:T(8,128)(2,1)S(1)}, bf16[1568,256]{1,0:T(8,128)(2,1)S(1)}, u32[]{:S(2)}, u32[]{:S(2)}) collective-permute-start(bf16[1568,256]{1,0:T(8,128)(2,1)S(1)} %bitcast.71), channel_id=1, source_target_pairs={{0,4},{1,5},{2,6},{3,7},{4,0},{5,1},{6,2},{7,3},{8,12},{9,13},{10,... | collective-permute-start | bytes 2408456 | tf_op jit(solution)/shard_map/ppermute | solution.py:657
  83.7 7.2 %collective-permute-done.9.refs_6_ = bf16[2,4,256,256]{3,2,1,0:T(8,128)(2,1)S(1)} collective-permute-done((bf16[2,4,256,256]{3,2,1,0:T(8,128)(2,1)S(1)}, bf16[2,4,256,256]{3,2,1,0:T(8,128)(2,1)S(1)}, u32[]{:S(2)}, u32[]{:S(2)}) %collective-permute-start.9) | collective-permute-done | bytes 1048608 | tf_op jit(solution)/shard_map/ppermute | solution.py:663
  90.9 4.2 collective-permute-done.7.refs_3_
  96.3 14.7 %collective-permute-done.1.refs_3_.refs_6_.refs_5_ = bf16[1568,256]{1,0:T(8,128)(2,1)S(1)} collective-permute-done((bf16[1568,256]{1,0:T(8,128)(2,1)S(1)}, bf16[1568,256]{1,0:T(8,128)(2,1)S(1)}, u32[]{:S(2)}, u32[]{:S(2)}) %collective-permute-start.1) | collective-permute-done | bytes 802848 | tf_op jit(solution)/shard_map/ppermute | solution.py:657
  111.0 4.1 reduce.1
  115.9 4.3 collective-permute-start.13
  126.6 15.0 %collective-permute-done.13.refs_2_.refs_9_ = bf16[1568,256]{1,0:T(8,128)(2,1)S(1)} collective-permute-done((bf16[1568,256]{1,0:T(8,128)(2,1)S(1)}, bf16[1568,256]{1,0:T(8,128)(2,1)S(1)}, u32[]{:S(2)}, u32[]{:S(2)}) %collective-permute-start.13) | collective-permute-done | bytes 802848 | tf_op jit(solution)/shard_map/ppermute | solution.py:657
  141.6 3.6 collective-permute-done.14
  145.4 4.2 collective-permute-done.15
  152.3 8.8 %conv.1 = (bf16[2,1568,256]{2,1,0:T(8,128)(2,1)S(1)}, f32[2,1568,256]{2,1,0:T(8,128)S(1)}, f32[2,2,256]{2,1,0:T(2,128)S(1)}) custom-call(s32[3]{0:T(128)S(1)} %pad_add_fusion.refs_0_, f32[2,1568,256]{2,1,0:T(8,128)S(1)} %get-tuple-element.71.refs_1_.refs_7_.refs_2_, bf16[2,1568,256]{2,1,0:T(8,128)(2,1)S(1)} %collective-permute-done.10.refs_2_.refs_8_.refs_3_, ...), custom_call_target="tpu_custom_call" | custom-call | flops 1024 | bytes 1024 | tf_op jit(solution)/shard_map/conv/pallas_call | solution.py:72
  168.6 3.3 collective-permute-done.19
  173.5 2.9 collective-permute-done.20
  182.7 8.6 %expand.1 = (f32[4,1568,256]{2,1,0:T(8,128)S(1)}, f32[4,2,256]{2,1,0:T(2,128)S(1)}) custom-call(s32[3]{0:T(128)S(1)} %pad_add_fusion.refs_0_, bf16[2,1568,256]{2,1,0:T(8,128)(2,1)S(1)} %second_act.1.refs_1_, bf16[2,1568,256]{2,1,0:T(8,128)(2,1)S(1)} %collective-permute-done.21.refs_2_, bf16[4,4,256,256]{3,2,1,0:T(8,128)(2,1)S(1)} %get-tuple-element.70.refs_9_.refs_3_.refs_6_), custom_call_target="tpu_custom_call" | custom-call | flops 1024 | bytes 1024 | tf_op jit(solution)/shard_map/expand/pallas_call | solution.py:72
  199.3 3.8 collective-permute-done.24
  204.5 13.5 %collective-permute-done.25 = f32[4,2,256]{2,1,0:T(2,128)S(1)} collective-permute-done((f32[4,2,256]{2,1,0:T(2,128)S(1)}, f32[4,2,256]{2,1,0:T(2,128)S(1)}, u32[]{:S(2)}, u32[]{:S(2)}) %collective-permute-start.25) | collective-permute-done | bytes 8224 | tf_op jit(solution)/shard_map/ppermute | solution.py:687
  218.0 6.7 %up.1 = (bf16[1568,256]{1,0:T(8,128)(2,1)S(1)}, bf16[1568,256]{1,0:T(8,128)(2,1)S(1)}, bf16[1568,256]{1,0:T(8,128)(2,1)S(1)}, bf16[1568,256]{1,0:T(8,128)(2,1)S(...) custom-call(s32[3]{0:T(128)S(1)} %pad_add_fusion.refs_0_, f32[4,1568,256]{2,1,0:T(8,128)S(1)} %get-tuple-element.75.refs_1_, ...), custom_call_target="tpu_custom_call" | custom-call | flops 1024 | bytes 1024 | tf_op jit(solution)/shard_map/up/pallas_call | solution.py:72
  224.8 3.6 collective-permute-done.27
  229.4 3.6 collective-permute-done.28
  240.3 5.9 %expand_back.1 = (bf16[4,1568,256]{2,1,0:T(8,128)(2,1)S(1)}, f32[2,1568,256]{2,1,0:T(8,128)S(1)}, bf16[2,1568,256]{2,1,0:T(8,128)(2,1)S(1)}) custom-call(s32[3]{0:T(128)S(1)} %pad_add_fusion.refs_0_, f32[4,1568,256]{2,1,0:T(8,128)S(1)} %get-tuple-element.75.refs_1_, f32[4,1568,256]{2,1,0:T(8,128)S(1)} %get-tuple-element.78.refs_2_.refs_3_, ...), custom_call_target="tpu_custom_call" | custom-call | flops 1024 | bytes 1024 | tf_op jit(solution)/shard_map/expand_back/pallas_call | solution.py:72
  249.7 3.3 second_up.1
  258.2 8.4 %collective-permute-done.34.refs_2_ = bf16[1568,256]{1,0:T(8,128)(2,1)S(1)} collective-permute-done((bf16[1568,256]{1,0:T(8,128)(2,1)S(1)}, bf16[1568,256]{1,0:T(8,128)(2,1)S(1)}, u32[]{:S(2)}, u32[]{:S(2)}) %collective-permute-start.34) | collective-permute-done | bytes 802848 | tf_op jit(solution)/shard_map/ppermute | solution.py:657
  266.8 3.5 collective-permute-done.35
  270.3 2.8 collective-permute-start.36
  276.8 10.1 %conv_back.1 = (bf16[2,1568,256]{2,1,0:T(8,128)(2,1)S(1)}, f32[2,1568,256]{2,1,0:T(8,128)S(1)}, f32[2,2,256]{2,1,0:T(2,128)S(1)}) custom-call(s32[3]{0:T(128)S(1)} %pad_add_fusion.refs_0_, f32[2,1568,256]{2,1,0:T(8,128)S(1)} %get-tuple-element.85.refs_1_, f32[2,1568,256]{2,1,0:T(8,128)S(1)} %get-tuple-element.73.refs_1_.refs_3_.refs_2_, ...), custom_call_target="tpu_custom_call" | custom-call | flops 1024 | bytes 1024 | tf_op jit(solution)/shard_map/conv_back/pallas_call | solution.py:72
  298.2 2.6 collective-permute-start.41
  304.7 2.7 collective-permute-start.42
  307.4 4.5 expand_wgrad.1.refs_1_
  319.9 5.1 %conv_wgrad.1.refs_7_.refs_2_ = bf16[4,4,48,256]{3,2,1,0:T(8,128)(2,1)S(1)} custom-call(s32[3]{0:T(128)S(1)} %pad_add_fusion.refs_0_, bf16[2,1568,256]{2,1,0:T(8,128)(2,1)S(1)} %copy-done.15, bf16[2,1568,256]{2,1,0:T(8,128)(2,1)S(1)} %get-tuple-element.90.refs_2_, bf16[1568,256]{1,0:T(8,128)(2,1)} %input_grad.4.refs_3_), custom_call_target="tpu_custom_call" | custom-call | flops 1024 | bytes 1024 | tf_op jit(solution)/shard_map/conv_wgrad/pallas_call | solution.py:72
  325.0 4.6 reduce_wgrad.1.refs_1_
  329.6 13.6 %collective-permute-done.42.refs_3_ = bf16[1568,256]{1,0:T(8,128)(2,1)S(1)} collective-permute-done((bf16[1568,256]{1,0:T(8,128)(2,1)S(1)}, bf16[1568,256]{1,0:T(8,128)(2,1)S(1)}, u32[]{:S(2)}, u32[]{:S(2)}) %collective-permute-start.42) | collective-permute-done | bytes 802848 | tf_op jit(solution)/shard_map/ppermute | solution.py:657
  347.1 2.8 input_grad.6.refs_5_
  360.2 24.0 %collective-permute-done.54.refs_2_ = bf16[256,256]{1,0:T(8,128)(2,1)S(1)} collective-permute-done((bf16[256,256]{1,0:T(8,128)(2,1)S(1)}, bf16[256,256]{1,0:T(8,128)(2,1)S(1)}, u32[]{:S(2)}, u32[]{:S(2)}) %collective-permute-start.54) | collective-permute-done | bytes 131104 | tf_op jit(solution)/shard_map/ppermute | solution.py:657
  401.3 7.2 %collective-permute-done.47.refs_2_ = bf16[4,304,256]{2,1,0:T(8,128)(2,1)} collective-permute-done((bf16[4,304,256]{2,1,0:T(8,128)(2,1)}, bf16[4,304,256]{2,1,0:T(8,128)(2,1)}, u32[]{:S(2)}, u32[]{:S(2)}) %collective-permute-start.47) | collective-permute-done | bytes 622624 | tf_op jit(solution)/shard_map/ppermute | solution.py:663
  408.5 11.2 %collective-permute-done.49.refs_4_ = bf16[4,304,256]{2,1,0:T(8,128)(2,1)} collective-permute-done((bf16[4,304,256]{2,1,0:T(8,128)(2,1)}, bf16[4,304,256]{2,1,0:T(8,128)(2,1)}, u32[]{:S(2)}, u32[]{:S(2)}) %collective-permute-start.49) | collective-permute-done | bytes 622624 | tf_op jit(solution)/shard_map/ppermute | solution.py:663
  421.3 2.7 collective-permute-start.59
  425.8 11.0 %collective-permute-done.46.refs_4_ = bf16[1568,256]{1,0:T(8,128)(2,1)} collective-permute-done((bf16[1568,256]{1,0:T(8,128)(2,1)}, bf16[1568,256]{1,0:T(8,128)(2,1)}, u32[]{:S(2)}, u32[]{:S(2)}) %collective-permute-start.46) | collective-permute-done | bytes 802848 | tf_op jit(solution)/shard_map/ppermute | solution.py:657
  436.8 4.8 collective-permute-done.59.refs_1_
  441.6 6.7 %collective-permute-done.60.refs_2_ = bf16[304,256]{1,0:T(8,128)(2,1)S(1)} collective-permute-done((bf16[304,256]{1,0:T(8,128)(2,1)S(1)}, bf16[304,256]{1,0:T(8,128)(2,1)S(1)}, u32[]{:S(2)}, u32[]{:S(2)}) %collective-permute-start.60) | collective-permute-done | bytes 155680 | tf_op jit(solution)/shard_map/ppermute | solution.py:657
  452.0 2.8 collective-permute-done.62.refs_2_
  454.8 3.7 collective-permute-done.63.refs_3_
  461.9 3.0 collective-permute-done.66
  464.9 2.6 collective-permute-start.67
  483.7 4.5 fusion.11
  (274 shorter events, 162.5 us)
Async XLA Ops:
  5.1 42.1 %collective-permute-start = (bf16[1568,256]{1,0:T(8,128)(2,1)S(1)}, bf16[1568,256]{1,0:T(8,128)(2,1)S(1)}, u32[]{:S(2)}, u32[]{:S(2)}) collective-permute-start(bf16[1568,256]{1,0:T(8,128)(2,1)S(1)} %bitcast.60), channel_id=1, source_target_pairs={{0,2},{1,3},{2,4},{3,5},{4,6},{5,7},{6,0},{7,1},{8,10},{9,11},{10,... | collective-permute-start | bytes 2408456 | tf_op jit(solution)/shard_map/ppermute | solution.py:657
  10.8 24.6 %collective-permute-start.3 = (bf16[576,256]{1,0:T(8,128)(2,1)S(1)}, bf16[576,256]{1,0:T(8,128)(2,1)S(1)}, u32[]{:S(2)}, u32[]{:S(2)}) collective-permute-start(bf16[576,256]{1,0:T(8,128)(2,1)S(1)} %bundle.1.refs_0_), channel_id=1, source_target_pairs={{0,2},{1,3},{2,4},{3,5},{4,6},{5,7},{6,0},{7,1},{8,10},{9,11},{10,... | collective-permute-start | bytes 884744 | tf_op jit(solution)/shard_map/ppermute | solution.py:657
  12.4 34.8 %collective-permute-start.4 = (bf16[576,256]{1,0:T(8,128)(2,1)S(1)}, bf16[576,256]{1,0:T(8,128)(2,1)S(1)}, u32[]{:S(2)}, u32[]{:S(2)}) collective-permute-start(bf16[576,256]{1,0:T(8,128)(2,1)S(1)} %bundle.1.refs_0_), channel_id=1, source_target_pairs={{0,4},{1,5},{2,6},{3,7},{4,0},{5,1},{6,2},{7,3},{8,12},{9,13},{10,... | collective-permute-start | bytes 884744 | tf_op jit(solution)/shard_map/ppermute | solution.py:657
  13.5 33.7 %collective-permute-start.5 = (bf16[576,256]{1,0:T(8,128)(2,1)S(1)}, bf16[576,256]{1,0:T(8,128)(2,1)S(1)}, u32[]{:S(2)}, u32[]{:S(2)}) collective-permute-start(bf16[576,256]{1,0:T(8,128)(2,1)S(1)} %bundle.1.refs_0_), channel_id=1, source_target_pairs={{0,6},{1,7},{2,0},{3,1},{4,2},{5,3},{6,4},{7,5},{8,14},{9,15},{10,... | collective-permute-start | bytes 884744 | tf_op jit(solution)/shard_map/ppermute | solution.py:657
  19.9 44.4 %collective-permute-start.2 = (bf16[1568,256]{1,0:T(8,128)(2,1)S(1)}, bf16[1568,256]{1,0:T(8,128)(2,1)S(1)}, u32[]{:S(2)}, u32[]{:S(2)}) collective-permute-start(bf16[1568,256]{1,0:T(8,128)(2,1)S(1)} %bitcast.72), channel_id=1, source_target_pairs={{0,6},{1,7},{2,0},{3,1},{4,2},{5,3},{6,4},{7,5},{8,14},{9,15},{10,... | collective-permute-start | bytes 2408456 | tf_op jit(solution)/shard_map/ppermute | solution.py:657
  47.3 16.9 %collective-permute-start.6 = (bf16[1,4,320,256]{3,2,1,0:T(8,128)(2,1)S(1)}, bf16[1,4,320,256]{3,2,1,0:T(8,128)(2,1)S(1)}, u32[]{:S(2)}, u32[]{:S(2)}) collective-permute-start(bf16[1,4,320,256]{3,2,1,0:T(8,128)(2,1)S(1)} %get-tuple-element.64.refs_0_.refs_1_), channel_id=1, source_target_pairs={{0,8},{8,0},{16,24},{24,16},{1,9},{9,1},{17,25},{25,17},{2,10},{10... | collective-permute-start | bytes 1966088 | tf_op jit(solution)/shard_map/ppermute | solution.py:663
  48.9 17.1 %collective-permute-start.8 = (bf16[1,4,256,256]{3,2,1,0:T(8,128)(2,1)S(1)}, bf16[1,4,256,256]{3,2,1,0:T(8,128)(2,1)S(1)}, u32[]{:S(2)}, u32[]{:S(2)}) collective-permute-start(bf16[1,4,256,256]{3,2,1,0:T(8,128)(2,1)S(1)} %get-tuple-element.65.refs_0_.refs_4_), channel_id=1, source_target_pairs={{0,16},{8,24},{16,0},{24,8},{1,17},{9,25},{17,1},{25,9},{2,18},{10... | collective-permute-start | bytes 1572872 | tf_op jit(solution)/shard_map/ppermute | solution.py:663
  64.4 30.8 %collective-permute-start.7 = (bf16[2,4,320,256]{3,2,1,0:T(8,128)(2,1)S(1)}, bf16[2,4,320,256]{3,2,1,0:T(8,128)(2,1)S(1)}, u32[]{:S(2)}, u32[]{:S(2)}) collective-permute-start(bf16[2,4,320,256]{3,2,1,0:T(8,128)(2,1)S(1)} %pair.2), channel_id=1, source_target_pairs={{0,16},{8,24},{16,0},{24,8},{1,17},{9,25},{17,1},{25,9},{2,18},{10... | collective-permute-start | bytes 3932168 | tf_op jit(solution)/shard_map/ppermute | solution.py:663
  66.0 24.9 %collective-permute-start.9 = (bf16[2,4,256,256]{3,2,1,0:T(8,128)(2,1)S(1)}, bf16[2,4,256,256]{3,2,1,0:T(8,128)(2,1)S(1)}, u32[]{:S(2)}, u32[]{:S(2)}) collective-permute-start(bf16[2,4,256,256]{3,2,1,0:T(8,128)(2,1)S(1)} %pair.3), channel_id=1, source_target_pairs={{0,8},{8,0},{16,24},{24,16},{1,9},{9,1},{17,25},{25,17},{2,10},{10... | collective-permute-start | bytes 3145736 | tf_op jit(solution)/shard_map/ppermute | solution.py:663
  67.6 43.4 %collective-permute-start.1 = (bf16[1568,256]{1,0:T(8,128)(2,1)S(1)}, bf16[1568,256]{1,0:T(8,128)(2,1)S(1)}, u32[]{:S(2)}, u32[]{:S(2)}) collective-permute-start(bf16[1568,256]{1,0:T(8,128)(2,1)S(1)} %bitcast.71), channel_id=1, source_target_pairs={{0,4},{1,5},{2,6},{3,7},{4,0},{5,1},{6,2},{7,3},{8,12},{9,13},{10,... | collective-permute-start | bytes 2408456 | tf_op jit(solution)/shard_map/ppermute | solution.py:657
  115.1 5.1 %collective-permute-start.10 = (bf16[2,1568,256]{2,1,0:T(8,128)(2,1)S(1)}, bf16[2,1568,256]{2,1,0:T(8,128)(2,1)S(1)}, u32[]{:S(2)}, u32[]{:S(2)}) collective-permute-start(bf16[2,1568,256]{2,1,0:T(8,128)(2,1)S(1)} %get-tuple-element.72.refs_2_), channel_id=1, source_target_pairs={{0,1},{1,0},{2,3},{3,2},{4,5},{5,4},{6,7},{7,6},{8,9},{9,8},{10,11... | collective-permute-start | bytes 4816904 | tf_op jit(solution)/shard_map/ppermute | solution.py:660
  115.9 25.7 %collective-permute-start.13 = (bf16[1568,256]{1,0:T(8,128)(2,1)S(1)}, bf16[1568,256]{1,0:T(8,128)(2,1)S(1)}, u32[]{:S(2)}, u32[]{:S(2)}) collective-permute-start(bf16[1568,256]{1,0:T(8,128)(2,1)S(1)} %bitcast.68), channel_id=1, source_target_pairs={{0,2},{1,3},{2,4},{3,5},{4,6},{5,7},{6,0},{7,1},{8,10},{9,11},{10,... | collective-permute-start | bytes 2408456 | tf_op jit(solution)/shard_map/ppermute | solution.py:657
  125.0 16.5 %collective-permute-start.12 = (f32[2,2,256]{2,1,0:T(2,128)S(1)}, f32[2,2,256]{2,1,0:T(2,128)S(1)}, u32[]{:S(2)}, u32[]{:S(2)}) collective-permute-start(f32[2,2,256]{2,1,0:T(2,128)S(1)} %add.204.refs_0_), channel_id=1, source_target_pairs={{0,16},{8,24},{16,0},{24,8},{1,17},{9,25},{17,1},{25,9},{2,18},{10... | collective-permute-start | bytes 12296 | tf_op jit(solution)/shard_map/ppermute | solution.py:663
  145.2 4.5 collective-permute-start.15
  150.3 18.0 %collective-permute-start.18 = (bf16[1568,256]{1,0:T(8,128)(2,1)S(1)}, bf16[1568,256]{1,0:T(8,128)(2,1)S(1)}, u32[]{:S(2)}, u32[]{:S(2)}) collective-permute-start(bf16[1568,256]{1,0:T(8,128)(2,1)S(1)} %bitcast.65), channel_id=1, source_target_pairs={{0,6},{1,7},{2,0},{3,1},{4,2},{5,3},{6,4},{7,5},{8,14},{9,15},{10,... | collective-permute-start | bytes 2408456 | tf_op jit(solution)/shard_map/ppermute | solution.py:657
  172.0 4.5 collective-permute-start.20
  179.2 38.8 %collective-permute-start.26 = (bf16[1568,256]{1,0:T(8,128)(2,1)S(1)}, bf16[1568,256]{1,0:T(8,128)(2,1)S(1)}, u32[]{:S(2)}, u32[]{:S(2)}) collective-permute-start(bf16[1568,256]{1,0:T(8,128)(2,1)S(1)} %bitcast.64), channel_id=1, source_target_pairs={{0,4},{1,5},{2,6},{3,7},{4,0},{5,1},{6,2},{7,3},{8,12},{9,13},{10,... | collective-permute-start | bytes 2408456 | tf_op jit(solution)/shard_map/ppermute | solution.py:657
  203.1 14.9 %collective-permute-start.25 = (f32[4,2,256]{2,1,0:T(2,128)S(1)}, f32[4,2,256]{2,1,0:T(2,128)S(1)}, u32[]{:S(2)}, u32[]{:S(2)}) collective-permute-start(f32[4,2,256]{2,1,0:T(2,128)S(1)} %add.212), channel_id=1, source_target_pairs={{0,4},{1,5},{2,6},{3,7},{4,0},{5,1},{6,2},{7,3},{8,12},{9,13},{10,... | collective-permute-start | bytes 24584 | tf_op jit(solution)/shard_map/ppermute | solution.py:687
  228.5 4.5 collective-permute-start.28
  246.3 20.3 %collective-permute-start.34 = (bf16[1568,256]{1,0:T(8,128)(2,1)S(1)}, bf16[1568,256]{1,0:T(8,128)(2,1)S(1)}, u32[]{:S(2)}, u32[]{:S(2)}) collective-permute-start(bf16[1568,256]{1,0:T(8,128)(2,1)S(1)} %pass.3.refs_7_), channel_id=1, source_target_pairs={{0,6},{1,7},{2,0},{3,1},{4,2},{5,3},{6,4},{7,5},{8,14},{9,15},{10,... | collective-permute-start | bytes 2408456 | tf_op jit(solution)/shard_map/ppermute | solution.py:657
  256.7 9.9 %collective-permute-start.33 = (f32[2,2,256]{2,1,0:T(2,128)S(1)}, f32[2,2,256]{2,1,0:T(2,128)S(1)}, u32[]{:S(2)}, u32[]{:S(2)}) collective-permute-start(f32[2,2,256]{2,1,0:T(2,128)S(1)} %add.218.refs_0_), channel_id=1, source_target_pairs={{0,16},{8,24},{16,0},{24,8},{1,17},{9,25},{17,1},{25,9},{2,18},{10... | collective-permute-start | bytes 12296 | tf_op jit(solution)/shard_map/ppermute | solution.py:663
  270.3 4.5 collective-permute-start.36
  274.9 19.8 %collective-permute-start.37 = (bf16[1568,256]{1,0:T(8,128)(2,1)S(1)}, bf16[1568,256]{1,0:T(8,128)(2,1)S(1)}, u32[]{:S(2)}, u32[]{:S(2)}) collective-permute-start(bf16[1568,256]{1,0:T(8,128)(2,1)S(1)} %pass.4.refs_10_), channel_id=1, source_target_pairs={{0,2},{1,3},{2,4},{3,5},{4,6},{5,7},{6,0},{7,1},{8,10},{9,11},{10,... | collective-permute-start | bytes 2408456 | tf_op jit(solution)/shard_map/ppermute | solution.py:657
  298.2 4.5 collective-permute-start.41
  304.7 12.7 %collective-permute-start.43 = (bf16[2,1568,256]{2,1,0:T(8,128)(2,1)S(1)}, bf16[2,1568,256]{2,1,0:T(8,128)(2,1)S(1)}, u32[]{:S(2)}, u32[]{:S(2)}) collective-permute-start(bf16[2,1568,256]{2,1,0:T(8,128)(2,1)S(1)} %first_grad.1.refs_1_), channel_id=1, source_target_pairs={{0,1},{1,0},{2,3},{3,2},{4,5},{5,4},{6,7},{7,6},{8,9},{9,8},{10,11... | collective-permute-start | bytes 4816904 | tf_op jit(solution)/shard_map/ppermute | solution.py:660
  304.7 38.4 %collective-permute-start.42 = (bf16[1568,256]{1,0:T(8,128)(2,1)S(1)}, bf16[1568,256]{1,0:T(8,128)(2,1)S(1)}, u32[]{:S(2)}, u32[]{:S(2)}) collective-permute-start(bf16[1568,256]{1,0:T(8,128)(2,1)S(1)} %pass.5.refs_7_), channel_id=1, source_target_pairs={{0,4},{1,5},{2,6},{3,7},{4,0},{5,1},{6,2},{7,3},{8,12},{9,13},{10,... | collective-permute-start | bytes 2408456 | tf_op jit(solution)/shard_map/ppermute | solution.py:657
  313.2 39.0 %collective-permute-start.52 = (bf16[4,256,256]{2,1,0:T(8,128)(2,1)S(1)}, bf16[4,256,256]{2,1,0:T(8,128)(2,1)S(1)}, u32[]{:S(2)}, u32[]{:S(2)}) collective-permute-start(bf16[4,256,256]{2,1,0:T(8,128)(2,1)S(1)} %pick.7), channel_id=1, source_target_pairs={{0,24},{8,16},{16,8},{24,0},{1,25},{9,17},{17,9},{25,1},{2,26},{10... | collective-permute-start | bytes 1572872 | tf_op jit(solution)/shard_map/ppermute | solution.py:663
  315.7 36.5 %collective-permute-start.51 = (bf16[4,256,256]{2,1,0:T(8,128)(2,1)S(1)}, bf16[4,256,256]{2,1,0:T(8,128)(2,1)S(1)}, u32[]{:S(2)}, u32[]{:S(2)}) collective-permute-start(bf16[4,256,256]{2,1,0:T(8,128)(2,1)S(1)} %pick.6), channel_id=1, source_target_pairs={{0,16},{8,24},{16,0},{24,8},{1,17},{9,25},{17,1},{25,9},{2,18},{10... | collective-permute-start | bytes 1572872 | tf_op jit(solution)/shard_map/ppermute | solution.py:663
  316.8 35.3 %collective-permute-start.50 = (bf16[4,256,256]{2,1,0:T(8,128)(2,1)S(1)}, bf16[4,256,256]{2,1,0:T(8,128)(2,1)S(1)}, u32[]{:S(2)}, u32[]{:S(2)}) collective-permute-start(bf16[4,256,256]{2,1,0:T(8,128)(2,1)S(1)} %pick.5), channel_id=1, source_target_pairs={{0,8},{8,0},{16,24},{24,16},{1,9},{9,1},{17,25},{25,17},{2,10},{10... | collective-permute-start | bytes 1572872 | tf_op jit(solution)/shard_map/ppermute | solution.py:663
  353.0 7.3 %collective-permute-start.53 = (bf16[256,256]{1,0:T(8,128)(2,1)S(1)}, bf16[256,256]{1,0:T(8,128)(2,1)S(1)}, u32[]{:S(2)}, u32[]{:S(2)}) collective-permute-start(bf16[256,256]{1,0:T(8,128)(2,1)S(1)} %get-tuple-element.93), channel_id=1, source_target_pairs={{0,6},{1,7},{2,0},{3,1},{4,2},{5,3},{6,4},{7,5},{8,14},{9,15},{10,... | collective-permute-start | bytes 393224 | tf_op jit(solution)/shard_map/ppermute | solution.py:657
  355.1 29.1 %collective-permute-start.54 = (bf16[256,256]{1,0:T(8,128)(2,1)S(1)}, bf16[256,256]{1,0:T(8,128)(2,1)S(1)}, u32[]{:S(2)}, u32[]{:S(2)}) collective-permute-start(bf16[256,256]{1,0:T(8,128)(2,1)S(1)} %get-tuple-element.94), channel_id=1, source_target_pairs={{0,4},{1,5},{2,6},{3,7},{4,0},{5,1},{6,2},{7,3},{8,12},{9,13},{10,... | collective-permute-start | bytes 393224 | tf_op jit(solution)/shard_map/ppermute | solution.py:657
  355.1 29.1 %collective-permute-start.55 = (bf16[256,256]{1,0:T(8,128)(2,1)S(1)}, bf16[256,256]{1,0:T(8,128)(2,1)S(1)}, u32[]{:S(2)}, u32[]{:S(2)}) collective-permute-start(bf16[256,256]{1,0:T(8,128)(2,1)S(1)} %get-tuple-element.95), channel_id=1, source_target_pairs={{0,2},{1,3},{2,4},{3,5},{4,6},{5,7},{6,0},{7,1},{8,10},{9,11},{10,... | collective-permute-start | bytes 393224 | tf_op jit(solution)/shard_map/ppermute | solution.py:657
  356.3 39.1 %collective-permute-start.48 = (bf16[4,304,256]{2,1,0:T(8,128)(2,1)S(1)}, bf16[4,304,256]{2,1,0:T(8,128)(2,1)S(1)}, u32[]{:S(2)}, u32[]{:S(2)}) collective-permute-start(bf16[4,304,256]{2,1,0:T(8,128)(2,1)S(1)} %pick_both.7), channel_id=1, source_target_pairs={{0,16},{8,24},{16,0},{24,8},{1,17},{9,25},{17,1},{25,9},{2,18},{10... | collective-permute-start | bytes 1867784 | tf_op jit(solution)/shard_map/ppermute | solution.py:663
  357.9 61.7 %collective-permute-start.45 = (bf16[1568,256]{1,0:T(8,128)(2,1)}, bf16[1568,256]{1,0:T(8,128)(2,1)}, u32[]{:S(2)}, u32[]{:S(2)}) collective-permute-start(bf16[1568,256]{1,0:T(8,128)(2,1)} %input_grad.4.refs_3_), channel_id=1, source_target_pairs={{0,4},{1,5},{2,6},{3,7},{4,0},{5,1},{6,2},{7,3},{8,12},{9,13},{10,... | collective-permute-start | bytes 2408456 | tf_op jit(solution)/shard_map/ppermute | solution.py:657
  384.3 6.2 %collective-permute-start.56 = (bf16[256,256]{1,0:T(8,128)(2,1)S(1)}, bf16[256,256]{1,0:T(8,128)(2,1)S(1)}, u32[]{:S(2)}, u32[]{:S(2)}) collective-permute-start(bf16[256,256]{1,0:T(8,128)(2,1)S(1)} %total.2.refs_1_), channel_id=1, source_target_pairs={{0,8},{8,0},{16,24},{24,16},{1,9},{9,1},{17,25},{25,17},{2,10},{10... | collective-permute-start | bytes 393224 | tf_op jit(solution)/shard_map/ppermute | solution.py:663
  385.9 5.9 %collective-permute-start.57 = (bf16[256,256]{1,0:T(8,128)(2,1)S(1)}, bf16[256,256]{1,0:T(8,128)(2,1)S(1)}, u32[]{:S(2)}, u32[]{:S(2)}) collective-permute-start(bf16[256,256]{1,0:T(8,128)(2,1)S(1)} %total.2.refs_1_), channel_id=1, source_target_pairs={{0,16},{8,24},{16,0},{24,8},{1,17},{9,25},{17,1},{25,9},{2,18},{10... | collective-permute-start | bytes 393224 | tf_op jit(solution)/shard_map/ppermute | solution.py:663
  387.4 7.4 %collective-permute-start.58 = (bf16[256,256]{1,0:T(8,128)(2,1)S(1)}, bf16[256,256]{1,0:T(8,128)(2,1)S(1)}, u32[]{:S(2)}, u32[]{:S(2)}) collective-permute-start(bf16[256,256]{1,0:T(8,128)(2,1)S(1)} %total.2.refs_1_), channel_id=1, source_target_pairs={{0,24},{8,16},{16,8},{24,0},{1,25},{9,17},{17,9},{25,1},{2,26},{10... | collective-permute-start | bytes 393224 | tf_op jit(solution)/shard_map/ppermute | solution.py:663
  391.2 17.3 %collective-permute-start.47 = (bf16[4,304,256]{2,1,0:T(8,128)(2,1)}, bf16[4,304,256]{2,1,0:T(8,128)(2,1)}, u32[]{:S(2)}, u32[]{:S(2)}) collective-permute-start(bf16[4,304,256]{2,1,0:T(8,128)(2,1)} %pick_both.6), channel_id=1, source_target_pairs={{0,8},{8,0},{16,24},{24,16},{1,9},{9,1},{17,25},{25,17},{2,10},{10... | collective-permute-start | bytes 1867784 | tf_op jit(solution)/shard_map/ppermute | solution.py:663
  392.4 27.2 %collective-permute-start.49 = (bf16[4,304,256]{2,1,0:T(8,128)(2,1)}, bf16[4,304,256]{2,1,0:T(8,128)(2,1)}, u32[]{:S(2)}, u32[]{:S(2)}) collective-permute-start(bf16[4,304,256]{2,1,0:T(8,128)(2,1)} %pick_both.4.refs_5_), channel_id=1, source_target_pairs={{0,24},{8,16},{16,8},{24,0},{1,25},{9,17},{17,9},{25,1},{2,26},{10... | collective-permute-start | bytes 1867784 | tf_op jit(solution)/shard_map/ppermute | solution.py:663
  395.5 41.3 %collective-permute-start.46 = (bf16[1568,256]{1,0:T(8,128)(2,1)}, bf16[1568,256]{1,0:T(8,128)(2,1)}, u32[]{:S(2)}, u32[]{:S(2)}) collective-permute-start(bf16[1568,256]{1,0:T(8,128)(2,1)} %input_grad.5.refs_5_), channel_id=1, source_target_pairs={{0,6},{1,7},{2,0},{3,1},{4,2},{5,3},{6,4},{7,5},{8,14},{9,15},{10,... | collective-permute-start | bytes 2408456 | tf_op jit(solution)/shard_map/ppermute | solution.py:657
  396.3 82.5 %collective-permute-start.44 = (bf16[1568,256]{1,0:T(8,128)(2,1)}, bf16[1568,256]{1,0:T(8,128)(2,1)}, u32[]{:S(2)}, u32[]{:S(2)}) collective-permute-start(bf16[1568,256]{1,0:T(8,128)(2,1)} %input_grad.6.refs_5_), channel_id=1, source_target_pairs={{0,2},{1,3},{2,4},{3,5},{4,6},{5,7},{6,0},{7,1},{8,10},{9,11},{10,... | collective-permute-start | bytes 2408456 | tf_op jit(solution)/shard_map/ppermute | solution.py:657
  421.3 20.3 %collective-permute-start.59 = (bf16[304,256]{1,0:T(8,128)(2,1)S(1)}, bf16[304,256]{1,0:T(8,128)(2,1)S(1)}, u32[]{:S(2)}, u32[]{:S(2)}) collective-permute-start(bf16[304,256]{1,0:T(8,128)(2,1)S(1)} %get-tuple-element.98), channel_id=1, source_target_pairs={{0,6},{1,7},{2,0},{3,1},{4,2},{5,3},{6,4},{7,5},{8,14},{9,15},{10,... | collective-permute-start | bytes 466952 | tf_op jit(solution)/shard_map/ppermute | solution.py:657
  424.0 24.3 %collective-permute-start.60 = (bf16[304,256]{1,0:T(8,128)(2,1)S(1)}, bf16[304,256]{1,0:T(8,128)(2,1)S(1)}, u32[]{:S(2)}, u32[]{:S(2)}) collective-permute-start(bf16[304,256]{1,0:T(8,128)(2,1)S(1)} %get-tuple-element.99), channel_id=1, source_target_pairs={{0,4},{1,5},{2,6},{3,7},{4,0},{5,1},{6,2},{7,3},{8,12},{9,13},{10,... | collective-permute-start | bytes 466952 | tf_op jit(solution)/shard_map/ppermute | solution.py:657
  424.0 24.3 %collective-permute-start.61 = (bf16[304,256]{1,0:T(8,128)(2,1)S(1)}, bf16[304,256]{1,0:T(8,128)(2,1)S(1)}, u32[]{:S(2)}, u32[]{:S(2)}) collective-permute-start(bf16[304,256]{1,0:T(8,128)(2,1)S(1)} %get-tuple-element.100), channel_id=1, source_target_pairs={{0,2},{1,3},{2,4},{3,5},{4,6},{5,7},{6,0},{7,1},{8,10},{9,11},{10,... | collective-permute-start | bytes 466952 | tf_op jit(solution)/shard_map/ppermute | solution.py:657
  448.4 6.4 %collective-permute-start.62 = (bf16[304,256]{1,0:T(8,128)(2,1)S(1)}, bf16[304,256]{1,0:T(8,128)(2,1)S(1)}, u32[]{:S(2)}, u32[]{:S(2)}) collective-permute-start(bf16[304,256]{1,0:T(8,128)(2,1)S(1)} %total.3.refs_1_), channel_id=1, source_target_pairs={{0,8},{8,0},{16,24},{24,16},{1,9},{9,1},{17,25},{25,17},{2,10},{10... | collective-permute-start | bytes 466952 | tf_op jit(solution)/shard_map/ppermute | solution.py:663
  450.0 8.6 %collective-permute-start.63 = (bf16[304,256]{1,0:T(8,128)(2,1)S(1)}, bf16[304,256]{1,0:T(8,128)(2,1)S(1)}, u32[]{:S(2)}, u32[]{:S(2)}) collective-permute-start(bf16[304,256]{1,0:T(8,128)(2,1)S(1)} %total.3.refs_1_), channel_id=1, source_target_pairs={{0,16},{8,24},{16,0},{24,8},{1,17},{9,25},{17,1},{25,9},{2,18},{10... | collective-permute-start | bytes 466952 | tf_op jit(solution)/shard_map/ppermute | solution.py:663
  451.5 7.1 %collective-permute-start.64 = (bf16[304,256]{1,0:T(8,128)(2,1)S(1)}, bf16[304,256]{1,0:T(8,128)(2,1)S(1)}, u32[]{:S(2)}, u32[]{:S(2)}) collective-permute-start(bf16[304,256]{1,0:T(8,128)(2,1)S(1)} %total.3.refs_1_), channel_id=1, source_target_pairs={{0,24},{8,16},{16,8},{24,0},{1,25},{9,17},{17,9},{25,1},{2,26},{10... | collective-permute-start | bytes 466952 | tf_op jit(solution)/shard_map/ppermute | solution.py:663
  464.9 16.2 %collective-permute-start.67 = (f32[8,128]{1,0:T(8,128)S(1)}, f32[8,128]{1,0:T(8,128)S(1)}, u32[]{:S(2)}, u32[]{:S(2)}) collective-permute-start(f32[8,128]{1,0:T(8,128)S(1)} %add.227), channel_id=1, source_target_pairs={{0,4},{1,5},{2,6},{3,7},{4,0},{5,1},{6,2},{7,3},{8,12},{9,13},{10,... | collective-permute-start | bytes 12296 | tf_op jit(solution)/shard_map/ppermute | solution.py:1116
  (62 other events, 437.3 us)

commit v3 on v2

--- a/solution.py
+++ b/solution.py
@@ -92,7 +92,9 @@
     def step(i, c):
         return body(pl.ds(pl.multiple_of(i * size, size), size), c)
 
-    return lax.fori_loop(0, rows // size, step, carry, unroll=7)
+    trips = rows // size
+    unroll = max(u for u in range(1, 9) if trips % u == 0)
+    return lax.fori_loop(0, trips, step, carry, unroll=unroll)
 
 
 def fold(x):
@@ -180,15 +182,14 @@
 
 def stack_kernel(lines, *refs):
     reduce_part, expand_part = refs[-2:]
-    cb = expand_part.shape[2]
     for d, ref in enumerate(refs[:-2]):
         reduce_part[0, d] = ref[:lines]
         expand_part[0, d] = ref[lines:]
 
 
 def pair_kernel(a, b, out):
-    out[0] = a[0]
-    out[1] = b[0]
+    out[0] = a[...].reshape(out.shape[1:])
+    out[1] = b[...].reshape(out.shape[1:])
 
 
 def spread_kernel(nz, sc, *refs):
@@ -243,23 +244,21 @@
     return group_row == group_col
 
 
-def cut_kernel(nz, d, sc, cot, out, sem):
-    images = out.shape[1]
+def cut_kernel(nz, d, low, sc, cot, out, sem):
+    spots, images = out.shape[:2]
     start = pl.multiple_of(lax.rem(sc[2] + d, nz) * images, images)
-    copy = pltpu.make_async_copy(cot.at[:, pl.ds(start, images)], out, sem)
+    copy = pltpu.make_async_copy(cot.at[low : low + spots, pl.ds(start, images)], out, sem)
     copy.start()
     copy.wait()
 
 
-def pick_kernel(k, sc, parts, out):
-    out[...] = parts[sc[0] ^ k]
-
-
-def pick_both_kernel(nz, k, sc, parts, taps, out):
-    q, cb = sc[0] ^ k, parts.shape[2]
+def pick_kernel(nz, k, sc, parts, *refs):
+    q, out = sc[0] ^ k, refs[-1]
+    cb = parts.shape[2]
     for d in range(nz):
         out[d, :cb] = parts[q, d]
-        out[d, cb:] = taps[q, source_at(sc, nz, d)]
+        for taps in refs[:-1]:
+            out[d, cb:] = taps[q, source_at(sc, nz, d)]
 
 
 def total_kernel(*refs):
@@ -391,32 +390,43 @@
         put_sums(sums, source_at(sc, nz, d), tiles(e.shape[1], body, no_sums(e.shape[2])))
 
 
-def up_kernel(nz, count, sc, e, tot, par, *refs):
-    xs, cots = refs[:nz], refs[nz : 2 * nz]
-    outs, (up, sums) = refs[2 * nz : 3 * nz], refs[3 * nz :]
-    for d in range(nz):
+def up_kernel(nz, count, pieces, earlier, sc, e, tot, par, *refs):
+    many = len(pieces)
+    xs, refs = refs[:many], refs[many:]
+    cots, refs = refs[: sum(pieces.values())], refs[sum(pieces.values()) + 2 * earlier :]
+    outs, (up, sums) = refs[:many], refs[many:]
+    used = 0
+    for j, d in enumerate(pieces):
         zs = source_at(sc, nz, d)
         t = tot[zs]
         center, inv = norm_rows(t[0:1], t[1:2], count)
         gain, shift = par[zs, 0:1], par[zs, 1:2]
-
-        def body(at, c):
-            hat = (e[d, at] - center) * inv
-            value, slope = gelu_both(hat * gain + shift + xs[d][at].astype(F32))
-            outs[d][at] = value.astype(BF)
-            u = cots[d][at].astype(F32) * slope
-            up[d, at] = u
-            return c[0] + fold(u), c[1] + fold(u * hat)
-
-        put_sums(sums, zs, tiles(e.shape[1], body, no_sums(e.shape[2])))
+        base = 0
+        pair = no_sums(e.shape[2])
+        for cot in cots[used : used + pieces[d]]:
+
+            def body(local, c):
+                size = local.size
+                at = pl.ds(pl.multiple_of(local.start + base, size), size)
+                hat = (e[d, at] - center) * inv
+                value, slope = gelu_both(hat * gain + shift + xs[j][at].astype(F32))
+                outs[j][at] = value.astype(BF)
+                u = cot[local].astype(F32) * slope
+                up[d, at] = u
+                return c[0] + fold(u), c[1] + fold(u * hat)
+
+            pair = tiles(cot.shape[0], body, pair)
+            base += cot.shape[0]
+        used += pieces[d]
+        put_sums(sums, zs, pair)
 
 
 def add_kernel(a, b, out):
     out[...] = a[...] + b[...]
 
 
-def pass_kernel(value, out):
-    out[...] = value[...]
+def pass_kernel(low, value, out):
+    out[...] = value[low : low + out.shape[0]]
 
 
 def expand_back_kernel(nz, count, sc, e, up, tot, tot_b, par, w, eg, own, other):
@@ -558,53 +568,43 @@
     return sum(x[:, j : j + 128] for j in range(0, x.shape[1], 128)) if x.shape[1] > 128 else x
 
 
-def expand_home_kernel(nz, sc, *refs):
-    parts, (grad, squares, whole) = refs[:NQ], refs[NQ:]
-    rows = grad.shape[0] // (2 * nz)
+def grads_kernel(nz, sc, *refs):
+    firsts, seconds, (mid, out) = refs[:NQ], refs[NQ : 2 * NQ], refs[2 * NQ : 2 * NQ + 2]
+    expand, reduce, taps, squares, first, second = refs[2 * NQ + 2 :]
+    cb, mb = reduce.shape[0], taps.shape[2]
     half = nz // 2
     for k in range(NQ):
-        whole[sc[0] ^ k] = parts[k][...]
+        first[sc[0] ^ k] = firsts[k][...]
+        second[sc[0] ^ k] = seconds[k][...]
     total = jnp.zeros((8, 128), F32)
     for q in range(NQ):
         for a in range(half):
-            g = whole[q, a * rows : (a + 1) * rows].astype(F32)
-            start = (((q % 2) * half + a) * 2 + q // 2) * rows
-            grad[start : start + rows] = g
-            total = total + lane_fold(square_sum(g * g))
-    squares[...] = total
-
-
-def reduce_home_kernel(nz, sc, *refs):
-    parts, (mid, out, before) = refs[:NQ], refs[NQ : NQ + 3]
-    grad, taps, squares, whole = refs[NQ + 3 :]
-    cb, mb = grad.shape[0], taps.shape[2]
-    half = nz // 2
-    for k in range(NQ):
-        whole[sc[0] ^ k] = parts[k][...]
-    total = before[...]
-    for q in range(NQ):
-        for a in range(half):
             start = (((q % 2) * half + a) * 2 + q // 2) * mb
-            grad[:, start : start + mb] = whole[q, :cb, a * mb : (a + 1) * mb].astype(F32)
-        block = whole[q, cb:].astype(F32)
+            piece = second[q, a * mb : (a + 1) * mb].astype(F32)
+            expand[start : start + mb] = piece
+            total = total + lane_fold(square_sum(piece * piece))
+            piece = first[q, :cb, a * mb : (a + 1) * mb]
+            reduce[:, start : start + mb] = piece.astype(F32)
+        block = first[q, cb:].astype(F32)
         for t in range(9):
             line, lane = tap_spot(t, mb)
             taps[t, q * 8 : (q + 1) * 8] = block[line : line + 8, lane : lane + mb]
-        full = whole[q].astype(F32)
+        full = first[q].astype(F32)
         total = total + lane_fold(square_sum(full * full))
     extra = jnp.sum(mid[...] * mid[...]) + jnp.sum(out[...] * out[...])
-    first = lax.broadcasted_iota(jnp.int32, (8, 128), 0) + lax.broadcasted_iota(
+    corner = lax.broadcasted_iota(jnp.int32, (8, 128), 0) + lax.broadcasted_iota(
         jnp.int32, (8, 128), 1
     )
-    total = total + jnp.where(first == 0, extra, 0.0)
+    total = total + jnp.where(corner == 0, extra, 0.0)
     squares[...] = jnp.broadcast_to(jnp.sum(total, keepdims=True), (8, 128))
 
 
-def place_kernel(nz, d, sc, block, *refs):
-    out, sem = refs[-2:]
-    images = block.shape[1]
+def place_kernel(nz, d, low, sc, block, *refs):
+    out, token, sem = refs[-3:]
+    token[...] = jnp.zeros_like(token)
+    spots, images = block.shape[:2]
     start = pl.multiple_of(lax.rem(sc[2] + d, nz) * images, images)
-    copy = pltpu.make_async_copy(block, out.at[:, pl.ds(start, images)], sem)
+    copy = pltpu.make_async_copy(block, out.at[low : low + spots, pl.ds(start, images)], sem)
     copy.start()
     copy.wait()
 
@@ -733,26 +733,27 @@
         pack,
         deps=crops[:1],
     )
-    bundles = [bundle] + [over_z(bundle, d) for d in range(1, nz)]
 
     lines = cb + tap_lines(mb) + 16
+    parts = [sds((1, nz, lines, QW), BF), sds((1, nz, cb, QW), BF)]
+
+    def pair(a, b, shape, *deps):
+        return call(pair_kernel, "pair", sds((2,) + shape, BF), a, b, specs=[VMEM] * 2, deps=deps)
+
     first_w, second_w = call(
         functools.partial(stack_kernel, lines),
         "stack",
-        [sds((1, nz, lines, QW), BF), sds((1, nz, cb, QW), BF)],
-        *bundles,
+        parts,
+        bundle,
+        *[over_z(bundle, d) for d in range(1, nz)],
         specs=[VMEM] * nz,
         deps=[crops[-1], pixels[1]],
     )
 
-    def pair(a, b):
-        shape = sds((2,) + a.shape[1:], BF)
-        return call(pair_kernel, "pair", shape, a, b, specs=[VMEM] * 2, deps=[pixels[-1]])
-
     first_x, second_y = over_dp(first_w, 1), over_dp(second_w, 2)
     first_y, second_x = (
-        over_dp(pair(first_w, first_x), 2),
-        over_dp(pair(second_w, second_y), 1),
+        over_dp(pair(first_w, first_x, first_w.shape[1:], pixels[-1]), 2),
+        over_dp(pair(second_w, second_y, second_w.shape[1:], pixels[-1]), 1),
     )
     reduce_q, expand_q, diag, mid_par, out_par = call(
         functools.partial(spread_kernel, nz),
@@ -776,18 +777,17 @@
 
     cot = cotangent.transpose(1, 2, 0, 3).reshape(SPOTS, n, cb)
 
-    def cut(d, *deps):
-        piece = call(
-            functools.partial(cut_kernel, nz, d),
+    def cut(d, low, high, *deps):
+        return call(
+            functools.partial(cut_kernel, nz, d, low),
             "cut",
-            sds((SPOTS, images, cb), BF),
+            sds((high - low, images, cb), BF),
             sc,
             cot,
             specs=[SMEM, ANY],
             scratch=[pltpu.SemaphoreType.DMA],
             deps=deps,
-        ).reshape(rows, cb)
-        return piece
+        ).reshape((high - low) * images, cb)
 
     def turn(d):
         return 0 if d == 1 else (1 if d == nz - 1 else 2)
@@ -808,13 +808,21 @@
     )
     rec1 = over_core(oth1)
     turns = [[d for d in range(1, nz) if turn(d) == t] for t in range(3)]
-    cots = [cut(0, diag)] + [None] * (nz - 1)
+    split = SPOTS // 2
+    cot_turns = [
+        [(d, 0, SPOTS) for d in turns[0]],
+        [(d, 0, SPOTS) for d in turns[1]],
+        [(d, 0, split) for d in turns[2]],
+        [(d, split, SPOTS) for d in turns[2]],
+    ]
+    cots = {0: [cut(0, 0, SPOTS, diag)]}
 
     def send_cots(t, *deps):
-        pieces = [cut(d, *deps) for d in turns[t]]
-        for d, piece in zip(turns[t], pieces):
-            cots[d] = over_z(piece, d)
-        return pieces, [cots[d] for d in turns[t]]
+        pieces = [cut(*spot, *deps) for spot in cot_turns[t]]
+        moved = [over_z(piece, spot[0]) for spot, piece in zip(cot_turns[t], pieces)]
+        for spot, piece in zip(cot_turns[t], moved):
+            cots.setdefault(spot[0], []).append(piece)
+        return pieces, moved
 
     sent, pins = send_cots(0, oth1)
     sums1 = call(first_sums_kernel, "first_sums", sum2_s, sc, own1, rec1, deps=sent)
@@ -835,6 +843,7 @@
     )
     tot2 = everywhere(sums2, *pins)
     sent, pins = send_cots(2, tot2)
+    sent_more, last_cots = send_cots(3, tot2)
     sa = call(
         functools.partial(second_act_kernel, count),
         "second_act",
@@ -843,7 +852,7 @@
         v2,
         tot2,
         mid_par,
-        deps=sent,
+        deps=sent + sent_more,
     )
     sa_rec = over_core(sa)
     e, sums3 = call(
@@ -856,54 +865,75 @@
         expand_q,
         limit=12,
     )
-    tot3 = everywhere(sums3)
-    res = call(
-        functools.partial(up_kernel, nz, count),
-        "up",
-        [sds((rows, cb), BF)] * nz + [sds((nz, rows, cb), F32), sumz_s],
-        sc,
-        e,
-        tot3,
-        out_par,
-        *pixels,
-        *cots,
-    )
-    values, up3, sums3b = res[:nz], res[nz], res[nz + 1]
-    part3b = over_all_z(sums3b)
-    tot3b = over_all_dp(part3b)
-    outs = list(values)
-
-    def later(value, *deps):
-        return call(
-            pass_kernel, "pass", sds(value.shape, value.dtype), value, specs=[VMEM], deps=deps
+    tot3 = everywhere(sums3, *pins)
+    def upward(ds, *earlier, deps=()):
+        many = len(ds)
+        pieces = {d: len(cots[d]) for d in ds}
+        at = 4 + many + sum(pieces.values())
+        res = call(
+            functools.partial(up_kernel, nz, count, pieces, len(earlier) // 2),
+            "up",
+            [sds((rows, cb), BF)] * many + [sds((nz, rows, cb), F32), sumz_s],
+            sc,
+            e,
+            tot3,
+            out_par,
+            *[pixels[d] for d in ds],
+            *[piece for d in ds for piece in cots[d]],
+            *earlier,
+            input_output_aliases={at: many, at + 1: many + 1} if earlier else {},
+            deps=deps,
         )
-
-    def place(blocks, *deps):
-        result = None
-        for d in range(nz):
+        return dict(zip(ds, res[:many])), res[many], res[many + 1]
+
+    early, up3, sums3b = upward(turns[0], deps=last_cots)
+    values, up3, sums3b = upward([d for d in range(nz) if d not in turns[0]], up3, sums3b)
+    values.update(early)
+    outs = [(0, 0, values[0])]
+
+    def send_outs(t, *deps):
+        pieces, moved = [], []
+        for d, low, high in cot_turns[t]:
+            piece = values[d]
+            if deps:
+                piece = call(
+                    functools.partial(pass_kernel, low * images),
+                    "pass",
+                    sds(((high - low) * images, cb), BF),
+                    piece,
+                    specs=[VMEM],
+                    deps=deps,
+                )
+            pieces.append(piece)
+            moved.append(over_z(piece, -d))
+            outs.append((d, low, moved[-1]))
+        return pieces, moved
+
+    sent, pins = send_outs(0)
+    tot3b = everywhere(sums3b, *pins)
+
+    def place(pieces, result=None, *deps):
+        for d, low, piece in pieces:
             extra = () if result is None else (result,)
-            result = call(
-                functools.partial(place_kernel, nz, d),
+            result, token = call(
+                functools.partial(place_kernel, nz, d, low),
                 "place",
-                sds((SPOTS, n, cb), BF),
+                [sds((SPOTS, n, cb), BF), sds((8, 128), F32)],
                 sc,
-                blocks[d].reshape(SPOTS, images, cb),
+                piece.reshape(-1, images, cb),
                 *extra,
                 specs=[SMEM, VMEM] + [ANY] * len(extra),
-                out_specs=ANY,
+                out_specs=[ANY, VMEM],
                 scratch=[pltpu.SemaphoreType.DMA],
                 input_output_aliases={2: 0} if extra else {},
                 deps=deps,
             )
+        return result, token
+
+    def to_images(result):
         return result.reshape(HW, HW, n, cb).transpose(2, 0, 1, 3)
 
-    def send_outs(t, *deps):
-        pieces = [later(values[d], *deps) for d in turns[t]]
-        for d, piece in zip(turns[t], pieces):
-            outs[d] = over_z(piece, -d)
-        return pieces, [outs[d] for d in turns[t]]
-
-    sent, pins = send_outs(0, part3b)
+    sent, pins = send_outs(1, tot3b)
     eg, own2, oth2 = call(
         functools.partial(expand_back_kernel, nz, count),
         "expand_back",
@@ -917,6 +947,59 @@
         expand_q,
         deps=sent,
     )
+    expand_parts = call(
+        functools.partial(expand_wgrad_kernel, nz),
+        "expand_wgrad",
+        sds((NQ, nz, QW, cb), BF),
+        sc,
+        sa,
+        sa_rec,
+        eg,
+        limit=12,
+    )
+
+    def pick(k, parts, *more, deps=()):
+        return call(
+            functools.partial(pick_kernel, nz, k),
+            "pick",
+            sds((nz, parts.shape[2] + sum(v.shape[2] for v in more), parts.shape[3]), BF),
+            sc,
+            parts,
+            *more,
+            deps=deps,
+        )
+
+    def gather_home(picks, deps=()):
+        shape = picks[0].shape[1:]
+        return call(
+            functools.partial(home_kernel, nz),
+            "home",
+            [sds(shape, F32)] + [sds(shape, BF)] * (nz - 1),
+            sc,
+            picks[0],
+            *[over_dp(picks[k], k) for k in range(1, NQ)],
+            deps=deps,
+        )
+
+    def total_of(pieces, deps=()):
+        low = call(
+            total_kernel,
+            "total",
+            sds(pieces[0].shape, BF),
+            pieces[0],
+            *[over_z(pieces[d], -d) for d in range(1, nz)],
+            specs=[VMEM] * nz,
+            deps=deps,
+        )
+        k = NQ
+        while k < nd:
+            low = (low.astype(F32) + over_dp(low, k).astype(F32)).astype(BF)
+            k *= 2
+        return low
+
+    def to_all_dp(low):
+        return [low] + [over_dp(low, k) for k in range(1, NQ)]
+
     rec2 = over_core(oth2)
     up2, sums2b = call(
         functools.partial(second_up_kernel, count),
@@ -928,10 +1011,14 @@
         v2,
         tot2,
         mid_par,
+        deps=[expand_parts],
     )
     mid2b = over_all_dp(sums2b, *pins)
     tot2b = over_all_z(mid2b)
-    sent, pins = send_outs(1, tot2b)
+    sent, pins = send_outs(2, tot2b)
+    expand_picks = [pick(k, expand_parts, deps=[mid2b]) for k in range(NQ)]
+    expand_pieces = gather_home(expand_picks)
+    pins.append(expand_pieces[0])
     cg, up1, sums1b = call(
         functools.partial(conv_back_kernel, count, images),
         "conv_back",
@@ -950,7 +1037,6 @@
         deps=sent,
     )
     tot1b = everywhere(sums1b, *pins)
-    sent, _ = send_outs(2, tot1b)
     fg = call(
         functools.partial(first_grad_kernel, count),
         "first_grad",
@@ -962,7 +1048,6 @@
         tot1,
         tot1b,
         mid_par,
-        deps=sent,
     )
     fg_rec = over_core(fg)
     def input_block(d, *deps):
@@ -978,17 +1063,18 @@
             deps=deps,
         )
 
-    expand_parts = call(
-        functools.partial(expand_wgrad_kernel, nz),
-        "expand_wgrad",
-        sds((NQ, nz, QW, cb), BF),
-        sc,
-        sa,
-        sa_rec,
-        eg,
+    first = input_block(2)
+    reduce_parts = call(
+        functools.partial(reduce_wgrad_kernel, nz),
+        "reduce_wgrad",
+        sds((NQ, nz, cb, QW), BF),
+        sc,
+        fg,
+        fg_rec,
+        *pixels,
         limit=12,
-    )
-    first = input_block(2)
+        deps=[first],
+    )
     conv_parts = call(
         functools.partial(conv_wgrad_kernel, images, mb),
         "conv_wgrad",
@@ -997,99 +1083,37 @@
         act,
         cg,
         scratch=[pad_s],
-        deps=[first],
-    )
-    reduce_parts = call(
-        functools.partial(reduce_wgrad_kernel, nz),
-        "reduce_wgrad",
-        sds((NQ, nz, cb, QW), BF),
-        sc,
-        fg,
-        fg_rec,
-        *pixels,
-        limit=12,
-        deps=[conv_parts],
-    )
+        deps=[reduce_parts],
+    )
+    expand_low = total_of(expand_pieces, [conv_parts])
+    _, pins = send_outs(3, expand_low)
+
+    def later(value, *deps):
+        shape = sds(value.shape, value.dtype)
+        body = functools.partial(pass_kernel, 0)
+        return call(body, "pass", shape, value, specs=[VMEM], deps=deps)
+
     reduce_picks = [
-        call(
-            functools.partial(pick_both_kernel, nz, k),
-            "pick_both",
-            sds((nz, cb + tap_lines(mb), QW), BF),
-            sc,
-            reduce_parts,
-            conv_parts,
-            deps=[outs[d] for d in turns[2]],
-        )
-        for k in range(NQ)
+        pick(k, reduce_parts, conv_parts, deps=[expand_low]) for k in range(NQ)
     ]
-    input_blocks = {2: first}
-    last = reduce_picks[-1]
-    for d in [d for d in range(1, nz) if d != 2] + [0]:
+    final = nz - 1
+    input_blocks = {2: later(first, expand_low)}
+    last = reduce_picks[1]
+    for d in list(range(3, nz)) + [1, 0]:
         last = input_block(d, last)
         input_blocks[d] = last
-    input_moved = [over_z(input_blocks[d], -d) if d else input_blocks[0] for d in range(nz)]
-
-    def low_sum(mine, others):
-        total = mine.astype(F32)
-        for value in others:
-            total = total + value.astype(F32)
-        return total
-
-    def picks(parts, *deps):
-        return [
-            call(
-                functools.partial(pick_kernel, k),
-                "pick",
-                sds(parts.shape[1:], BF),
-                sc,
-                parts,
-                deps=deps,
-            )
-            for k in range(NQ)
-        ]
-
-    def home(parts, deps, pins):
-        shape = parts[0].shape[1:]
-        pieces = call(
-            functools.partial(home_kernel, nz),
-            "home",
-            [sds(shape, F32)] + [sds(shape, BF)] * (nz - 1),
-            sc,
-            parts[0],
-            *[over_dp(parts[k], k) for k in range(1, NQ)],
-            deps=deps,
-        )
-        low = call(
-            total_kernel,
-            "total",
-            sds(shape, BF),
-            pieces[0],
-            *[over_z(pieces[d], -d) for d in range(1, nz)],
-            specs=[VMEM] * nz,
-            deps=pins,
-        )
-        k = NQ
-        while k < nd:
-            low = low_sum(low, [over_dp(low, k)]).astype(BF)
-            k *= 2
-        return [low] + [over_dp(low, k) for k in range(1, NQ)]
-
-    expand_pieces = home(picks(expand_parts, mid2b), [last], [])
-    expand_wgrad, squares = call(
-        functools.partial(expand_home_kernel, nz),
-        "expand_home",
-        [sds((MID, cb), F32), sds((8, 128), F32)],
-        sc,
-        *expand_pieces,
-        scratch=[pltpu.VMEM((NQ, QW, cb), BF)],
-    )
-    reduce_pieces = home(
-        reduce_picks,
-        [input_moved[2], last, squares],
-        [input_moved[d] for d in range(1, nz) if d not in (2, nz - 1)],
-    )
-    input_grad = place(input_moved)
-    output = place(outs, last)
+    output, token = place(outs)
+    pieces = gather_home(reduce_picks, [last, token])
+
+    expand_home = to_all_dp(later(expand_low, pieces[0]))
+    moved = [(0, 0, input_blocks[0])]
+    moved += [(d, 0, over_z(input_blocks[d], -d)) for d in range(2, final)]
+    placed, token = place(moved)
+    reduce_low = total_of(pieces, [token])
+    reduce_home = to_all_dp(reduce_low)
+    second = later(input_blocks[1], reduce_low)
+    second_moved = over_z(second, -1)
+    placed, _ = place([(1, 0, second_moved)], placed)
 
     def my_mid(total):
         lanes = lax.dynamic_slice_in_dim(total.transpose(1, 0, 2).reshape(2, 2 * QW), z * mb, mb, 1)
@@ -1099,22 +1123,39 @@
     mine3 = lax.dynamic_index_in_dim(tot3b, z, 0, keepdims=False)
     out_grads = jnp.stack([mine3[1], mine3[0]])
 
-    reduce_wgrad, tap_grad, total_sq = call(
-        functools.partial(reduce_home_kernel, nz),
-        "reduce_home",
-        [sds((cb, MID), F32), sds((9, GW, mb), F32), sds((8, 128), F32)],
-        sc,
-        *reduce_pieces,
+    expand_wgrad, reduce_wgrad, tap_grad, total_sq = call(
+        functools.partial(grads_kernel, nz),
+        "grads",
+        [
+            sds((MID, cb), F32),
+            sds((cb, MID), F32),
+            sds((9, GW, mb), F32),
+            sds((8, 128), F32),
+        ],
+        sc,
+        *reduce_home,
+        *expand_home,
         mid_grads,
         out_grads,
-        squares,
-        scratch=[pltpu.VMEM((NQ, cb + tap_lines(mb), QW), BF)],
+        scratch=[
+            pltpu.VMEM((NQ, cb + tap_lines(mb), QW), BF),
+            pltpu.VMEM((NQ, QW, cb), BF),
+        ],
+        deps=[second],
     )
     group_wgrad = tap_grad.reshape(group_weight.shape)
-    k = 1
-    while k < ng:
-        total_sq = total_sq + lax.ppermute(total_sq, "group", [(a, a ^ k) for a in range(ng)])
-        k *= 2
+    total_sq = call(
+        add_kernel,
+        "add",
+        sds((8, 128), F32),
+        total_sq,
+        over_core(total_sq),
+        specs=[VMEM] * 2,
+        deps=[second_moved],
+    )
+    total_sq = over_all_z(total_sq)
+    moved = over_z(later(input_blocks[final], total_sq), -final)
+    input_grad, _ = place([(final, 0, moved)], placed)
     grad_norm = jnp.sqrt(total_sq[0, 0])
     clip_scale = jnp.minimum(1.0, clip_norm / (grad_norm + 1e-06))
     reduce_out = adam_step(
@@ -1144,8 +1185,8 @@
     mid_out = adam_step(mid_norms, mid_grads * clip_scale, mid_first, mid_second, 0.5, 0.0)
     out_out = adam_step(out_norms, out_grads * clip_scale, out_first, out_second, 0.5, 0.0)
     return (
-        output,
-        input_grad,
+        to_images(output),
+        to_images(input_grad),
         grad_norm,
         *reduce_out,
         *group_out,

time: 499 us -> 474 us (0.950); the launches traced: 493 us -> 474 us
  waiting for transfers between devices: 251 us -> 227 us
  starting transfers between devices: 107 us -> 117 us
    ppermute x28, waiting for transfers between devices: 58.8 us -> 37.9 us  [over_dp(): return lax.ppermute(value, 'dp', [(a, a ^ k) for a in range(nd)])]
    ppermute x21 -> x23, starting transfers between devices: 52 us -> 65.5 us  [over_z(): return lax.ppermute(value, 'group', pairs)]
    ppermute x21 -> x23, waiting for transfers between devices: 137 us -> 141 us  [over_z(): return lax.ppermute(value, 'group', pairs)]
    unnamed x85 -> x47, local copies, waits for them, and re-layouts: 11 us -> 8 us
    ppermute x12 -> x14, waiting for transfers between devices: 48.1 us -> 45.9 us  [over_all_z(): lax.ppermute(value, 'group', [(a, a ^ k) for a in range(ng)])]
    pallas_call x59 -> x68, Pallas kernels: 109 us -> 107 us  [call(): pl.pallas_call(inner, in_specs=(specs or [SMEM] + [VMEM] * (used - 1)) +...]
    ppermute x12 -> x14, starting transfers between devices: 11.4 us -> 12.3 us  [over_all_z(): lax.ppermute(value, 'group', [(a, a ^ k) for a in range(ng)])]
  transfers between devices with their start and end apart: 68 -> 70, of which waited for: 45 -> 44; matrix products, arithmetic and copies ran while one was open for 0% -> 2% of each run, Pallas kernels for 17% -> 18%
where the time goes in v3:
time: 474 us
  waiting for transfers between devices  227 us (48%)
  starting transfers between devices  117 us (25%)
  Pallas kernels  107 us (23%)
  local copies, waits for them, and re-layouts  10.5 us (2%)
  other arithmetic  9.24 us (2%)
    ppermute x23, waiting for transfers between devices, over_z(): return lax.ppermute(value, 'group', pairs)  141 us
    pallas_call x68, Pallas kernels, call(): pl.pallas_call(inner, in_specs=(specs or [SMEM] + [VMEM] * (used - 1)) +...  107 us
    ppermute x23, starting transfers between devices, over_z(): return lax.ppermute(value, 'group', pairs)  65.5 us
    ppermute x14, waiting for transfers between devices, over_all_z(): lax.ppermute(value, 'group', [(a, a ^ k) for a in range(ng)])  45.9 us
    ppermute x28, starting transfers between devices, over_dp(): return lax.ppermute(value, 'dp', [(a, a ^ k) for a in range(nd)])  38.5 us
    ppermute x28, waiting for transfers between devices, over_dp(): return lax.ppermute(value, 'dp', [(a, a ^ k) for a in range(nd)])  37.9 us
    ppermute x14, starting transfers between devices, over_all_z(): lax.ppermute(value, 'group', [(a, a ^ k) for a in range(ng)])  12.3 us
  transfers between devices with their start and end apart: 70, of which 44 were waited for; matrix products, arithmetic and copies ran while one was open for 2% of the time, Pallas kernels for 18%

profile of v3, /device:TPU:0, one launch (start us, length us, event | category | flops | bytes accessed | tf_op | source)
XLA Modules:
  0.0 474.3 jit_solution(11642059282012616809)
XLA Ops:
  1.6 2.5 copy-done
  5.1 3.1 collective-permute-start
  13.5 2.8 collective-permute-start.5
  16.4 2.5 copy-done.1
  22.4 13.0 %collective-permute-done.3.refs_1_ = bf16[576,256]{1,0:T(8,128)(2,1)S(1)} collective-permute-done((bf16[576,256]{1,0:T(8,128)(2,1)S(1)}, bf16[576,256]{1,0:T(8,128)(2,1)S(1)}, u32[]{:S(2)}, u32[]{:S(2)}) %collective-permute-start.3) | collective-permute-done | bytes 294944 | tf_op jit(solution)/shard_map/ppermute | solution.py:657
  35.4 11.8 %collective-permute-done.4.refs_2_ = bf16[576,256]{1,0:T(8,128)(2,1)S(1)} collective-permute-done((bf16[576,256]{1,0:T(8,128)(2,1)S(1)}, bf16[576,256]{1,0:T(8,128)(2,1)S(1)}, u32[]{:S(2)}, u32[]{:S(2)}) %collective-permute-start.4) | collective-permute-done | bytes 294944 | tf_op jit(solution)/shard_map/ppermute | solution.py:657
  50.4 13.9 %collective-permute-done.2.refs_2_.refs_4_.refs_6_ = bf16[1568,256]{1,0:T(8,128)(2,1)S(1)} collective-permute-done((bf16[1568,256]{1,0:T(8,128)(2,1)S(1)}, bf16[1568,256]{1,0:T(8,128)(2,1)S(1)}, u32[]{:S(2)}, u32[]{:S(2)}) %collective-permute-start.2) | collective-permute-done | bytes 802848 | tf_op jit(solution)/shard_map/ppermute | solution.py:657
  67.6 16.1 %collective-permute-start.1 = (bf16[1568,256]{1,0:T(8,128)(2,1)S(1)}, bf16[1568,256]{1,0:T(8,128)(2,1)S(1)}, u32[]{:S(2)}, u32[]{:S(2)}) collective-permute-start(bf16[1568,256]{1,0:T(8,128)(2,1)S(1)} %bitcast.73), channel_id=1, source_target_pairs={{0,4},{1,5},{2,6},{3,7},{4,0},{5,1},{6,2},{7,3},{8,12},{9,13},{10,... | collective-permute-start | bytes 2408456 | tf_op jit(solution)/shard_map/ppermute | solution.py:657
  83.7 7.2 %collective-permute-done.9.refs_6_ = bf16[2,4,256,256]{3,2,1,0:T(8,128)(2,1)S(1)} collective-permute-done((bf16[2,4,256,256]{3,2,1,0:T(8,128)(2,1)S(1)}, bf16[2,4,256,256]{3,2,1,0:T(8,128)(2,1)S(1)}, u32[]{:S(2)}, u32[]{:S(2)}) %collective-permute-start.9) | collective-permute-done | bytes 1048608 | tf_op jit(solution)/shard_map/ppermute | solution.py:663
  90.9 4.2 collective-permute-done.7.refs_3_
  96.3 14.7 %collective-permute-done.1.refs_3_.refs_5_ = bf16[1568,256]{1,0:T(8,128)(2,1)S(1)} collective-permute-done((bf16[1568,256]{1,0:T(8,128)(2,1)S(1)}, bf16[1568,256]{1,0:T(8,128)(2,1)S(1)}, u32[]{:S(2)}, u32[]{:S(2)}) %collective-permute-start.1) | collective-permute-done | bytes 802848 | tf_op jit(solution)/shard_map/ppermute | solution.py:657
  111.0 4.1 reduce.1
  115.9 4.3 collective-permute-start.13
  126.5 15.0 %collective-permute-done.13.refs_2_.refs_5_ = bf16[1568,256]{1,0:T(8,128)(2,1)S(1)} collective-permute-done((bf16[1568,256]{1,0:T(8,128)(2,1)S(1)}, bf16[1568,256]{1,0:T(8,128)(2,1)S(1)}, u32[]{:S(2)}, u32[]{:S(2)}) %collective-permute-start.13) | collective-permute-done | bytes 802848 | tf_op jit(solution)/shard_map/ppermute | solution.py:657
  141.6 3.6 collective-permute-done.14
  145.4 4.2 collective-permute-done.15
  152.4 8.8 %conv.1 = (bf16[2,1568,256]{2,1,0:T(8,128)(2,1)S(1)}, f32[2,1568,256]{2,1,0:T(8,128)S(1)}, f32[2,2,256]{2,1,0:T(2,128)S(1)}) custom-call(s32[3]{0:T(128)S(1)} %pad_add_fusion.refs_0_, f32[2,1568,256]{2,1,0:T(8,128)S(1)} %get-tuple-element.83.refs_1_.refs_7_.refs_2_, bf16[2,1568,256]{2,1,0:T(8,128)(2,1)S(1)} %collective-permute-done.10.refs_2_.refs_8_.refs_3_, ...), custom_call_target="tpu_custom_call" | custom-call | flops 1024 | bytes 1024 | tf_op jit(solution)/shard_map/conv/pallas_call | solution.py:72
  169.8 3.3 collective-permute-done.19
  173.6 4.0 collective-permute-done.20
  181.5 2.4 collective-permute-start.27
  184.4 8.6 %expand.1 = (f32[4,1568,256]{2,1,0:T(8,128)S(1)}, f32[4,2,256]{2,1,0:T(2,128)S(1)}) custom-call(s32[3]{0:T(128)S(1)} %pad_add_fusion.refs_0_, bf16[2,1568,256]{2,1,0:T(8,128)(2,1)S(1)} %second_act.1.refs_1_, bf16[2,1568,256]{2,1,0:T(8,128)(2,1)S(1)} %collective-permute-done.21.refs_2_, bf16[4,4,256,256]{3,2,1,0:T(8,128)(2,1)S(1)} %get-tuple-element.82.refs_9_.refs_3_.refs_6_), custom_call_target="tpu_custom_call" | custom-call | flops 1024 | bytes 1024 | tf_op jit(solution)/shard_map/expand/pallas_call | solution.py:72
  198.2 12.1 %collective-permute-done.24.refs_2_.refs_8_ = bf16[768,256]{1,0:T(8,128)(2,1)S(1)} collective-permute-done((bf16[768,256]{1,0:T(8,128)(2,1)S(1)}, bf16[768,256]{1,0:T(8,128)(2,1)S(1)}, u32[]{:S(2)}, u32[]{:S(2)}) %collective-permute-start.24) | collective-permute-done | bytes 393248 | tf_op jit(solution)/shard_map/ppermute | solution.py:657
  210.4 6.8 %collective-permute-done.25 = f32[4,2,256]{2,1,0:T(2,128)S(1)} collective-permute-done((f32[4,2,256]{2,1,0:T(2,128)S(1)}, f32[4,2,256]{2,1,0:T(2,128)S(1)}, u32[]{:S(2)}, u32[]{:S(2)}) %collective-permute-start.25) | collective-permute-done | bytes 8224 | tf_op jit(solution)/shard_map/ppermute | solution.py:687
  217.2 4.5 collective-permute-done.26
  226.7 5.1 %up.3 = (bf16[1568,256]{1,0:T(8,128)(2,1)S(1)}, bf16[1568,256]{1,0:T(8,128)(2,1)S(1)}, bf16[1568,256]{1,0:T(8,128)(2,1)S(1)}, f32[4,1568,256]{2,1,0:T(8,128)S(1)}, f32[4,2,256]{2,1,0:T(2,128)S(1)}) custom-call(s32[3]{0:T(128)S(1)} %pad_add_fusion.refs_0_, ...), custom_call_target="tpu_custom_call", output_to_operand_aliasing={{3}: (11, {}), {4}: (12, {})} | custom-call | flops 1024 | bytes 1024 | tf_op jit(solution)/shard_map/up/pallas_call | solution.py:72
  241.4 3.6 collective-permute-done.31
  247.2 2.5 collective-permute-done.32
  249.7 5.9 %expand_back.1 = (bf16[4,1568,256]{2,1,0:T(8,128)(2,1)S(1)}, f32[2,1568,256]{2,1,0:T(8,128)S(1)}, bf16[2,1568,256]{2,1,0:T(8,128)(2,1)S(1)}) custom-call(s32[3]{0:T(128)S(1)} %pad_add_fusion.refs_0_, f32[4,1568,256]{2,1,0:T(8,128)S(1)} %get-tuple-element.87.refs_1_, f32[4,1568,256]{2,1,0:T(8,128)S(1)} %get-tuple-element.92.refs_2_.refs_3_, ...), custom_call_target="tpu_custom_call" | custom-call | flops 1024 | bytes 1024 | tf_op jit(solution)/shard_map/expand_back/pallas_call | solution.py:72
  255.7 13.8 %collective-permute-start.36 = (bf16[1568,256]{1,0:T(8,128)(2,1)S(1)}, bf16[1568,256]{1,0:T(8,128)(2,1)S(1)}, u32[]{:S(2)}, u32[]{:S(2)}) collective-permute-start(bf16[1568,256]{1,0:T(8,128)(2,1)S(1)} %pass.7.refs_7_), channel_id=1, source_target_pairs={{0,2},{1,3},{2,4},{3,5},{4,6},{5,7},{6,0},{7,1},{8,10},{9,11},{10,... | collective-permute-start | bytes 2408456 | tf_op jit(solution)/shard_map/ppermute | solution.py:657
  269.5 4.5 expand_wgrad.1.refs_6_.refs_1_
  274.1 3.4 second_up.1
  282.7 7.5 %collective-permute-done.36.refs_2_ = bf16[1568,256]{1,0:T(8,128)(2,1)S(1)} collective-permute-done((bf16[1568,256]{1,0:T(8,128)(2,1)S(1)}, bf16[1568,256]{1,0:T(8,128)(2,1)S(1)}, u32[]{:S(2)}, u32[]{:S(2)}) %collective-permute-start.36) | collective-permute-done | bytes 802848 | tf_op jit(solution)/shard_map/ppermute | solution.py:657
  291.3 2.5 collective-permute-start.39
  295.5 3.6 collective-permute-done.43
  299.4 4.2 collective-permute-done.44
  304.0 10.1 %conv_back.1 = (bf16[2,1568,256]{2,1,0:T(8,128)(2,1)S(1)}, f32[2,1568,256]{2,1,0:T(8,128)S(1)}, f32[2,2,256]{2,1,0:T(2,128)S(1)}) custom-call(s32[3]{0:T(128)S(1)} %pad_add_fusion.refs_0_, f32[2,1568,256]{2,1,0:T(8,128)S(1)} %get-tuple-element.105.refs_1_, f32[2,1568,256]{2,1,0:T(8,128)S(1)} %get-tuple-element.85.refs_1_.refs_3_.refs_2_, ...), custom_call_target="tpu_custom_call" | custom-call | flops 1024 | bytes 1024 | tf_op jit(solution)/shard_map/conv_back/pallas_call | solution.py:72
  325.1 2.6 collective-permute-start.49
  337.6 4.6 reduce_wgrad.1.refs_3_.refs_1_
  342.2 5.1 %conv_wgrad.1.refs_4_.refs_2_ = bf16[4,4,48,256]{3,2,1,0:T(8,128)(2,1)S(1)} custom-call(s32[3]{0:T(128)S(1)} %pad_add_fusion.refs_0_, bf16[2,1568,256]{2,1,0:T(8,128)(2,1)S(1)} %copy-done.6, bf16[2,1568,256]{2,1,0:T(8,128)(2,1)S(1)} %get-tuple-element.106.refs_2_, bf16[4,4,256,256]{3,2,1,0:T(8,128)(2,1)S(1)} %reduce_wgrad.1.refs_3_.refs_1_), custom_call_target="tpu_custom_call" | custom-call | flops 1024 | bytes 1024 | tf_op jit(solution)/shard_map/conv_wgrad/pallas_call | solution.py:72
  350.1 2.5 collective-permute-start.54
  369.5 33.1 %collective-permute-done.51 = bf16[800,256]{1,0:T(8,128)(2,1)S(1)} collective-permute-done((bf16[800,256]{1,0:T(8,128)(2,1)S(1)}, bf16[800,256]{1,0:T(8,128)(2,1)S(1)}, u32[]{:S(2)}, u32[]{:S(2)}) %collective-permute-start.51) | collective-permute-done | bytes 409632 | tf_op jit(solution)/shard_map/ppermute | solution.py:657
  404.8 2.7 collective-permute-start.55
  412.0 8.6 %collective-permute-done.56.refs_2_ = bf16[304,256]{1,0:T(8,128)(2,1)S(1)} collective-permute-done((bf16[304,256]{1,0:T(8,128)(2,1)S(1)}, bf16[304,256]{1,0:T(8,128)(2,1)S(1)}, u32[]{:S(2)}, u32[]{:S(2)}) %collective-permute-start.56) | collective-permute-done | bytes 155680 | tf_op jit(solution)/shard_map/ppermute | solution.py:657
  435.4 2.3 collective-permute-done.61.refs_4_
  444.5 2.6 collective-permute-start.68
  454.4 4.5 fusion.11
  458.9 2.5 fusion.15
  461.4 9.5 %collective-permute-done.69 = bf16[1568,256]{1,0:T(8,128)(2,1)S(1)} collective-permute-done((bf16[1568,256]{1,0:T(8,128)(2,1)S(1)}, bf16[1568,256]{1,0:T(8,128)(2,1)S(1)}, u32[]{:S(2)}, u32[]{:S(2)}) %collective-permute-start.69) | collective-permute-done | bytes 802848 | tf_op jit(solution)/shard_map/ppermute | solution.py:657
  (246 shorter events, 149.8 us)
Async XLA Ops:
  5.1 42.1 %collective-permute-start = (bf16[1568,256]{1,0:T(8,128)(2,1)S(1)}, bf16[1568,256]{1,0:T(8,128)(2,1)S(1)}, u32[]{:S(2)}, u32[]{:S(2)}) collective-permute-start(bf16[1568,256]{1,0:T(8,128)(2,1)S(1)} %bitcast.61), channel_id=1, source_target_pairs={{0,2},{1,3},{2,4},{3,5},{4,6},{5,7},{6,0},{7,1},{8,10},{9,11},{10,... | collective-permute-start | bytes 2408456 | tf_op jit(solution)/shard_map/ppermute | solution.py:657
  10.8 24.6 %collective-permute-start.3 = (bf16[576,256]{1,0:T(8,128)(2,1)S(1)}, bf16[576,256]{1,0:T(8,128)(2,1)S(1)}, u32[]{:S(2)}, u32[]{:S(2)}) collective-permute-start(bf16[576,256]{1,0:T(8,128)(2,1)S(1)} %bundle.1.refs_0_), channel_id=1, source_target_pairs={{0,2},{1,3},{2,4},{3,5},{4,6},{5,7},{6,0},{7,1},{8,10},{9,11},{10,... | collective-permute-start | bytes 884744 | tf_op jit(solution)/shard_map/ppermute | solution.py:657
  12.4 34.8 %collective-permute-start.4 = (bf16[576,256]{1,0:T(8,128)(2,1)S(1)}, bf16[576,256]{1,0:T(8,128)(2,1)S(1)}, u32[]{:S(2)}, u32[]{:S(2)}) collective-permute-start(bf16[576,256]{1,0:T(8,128)(2,1)S(1)} %bundle.1.refs_0_), channel_id=1, source_target_pairs={{0,4},{1,5},{2,6},{3,7},{4,0},{5,1},{6,2},{7,3},{8,12},{9,13},{10,... | collective-permute-start | bytes 884744 | tf_op jit(solution)/shard_map/ppermute | solution.py:657
  13.5 33.7 %collective-permute-start.5 = (bf16[576,256]{1,0:T(8,128)(2,1)S(1)}, bf16[576,256]{1,0:T(8,128)(2,1)S(1)}, u32[]{:S(2)}, u32[]{:S(2)}) collective-permute-start(bf16[576,256]{1,0:T(8,128)(2,1)S(1)} %bundle.1.refs_0_), channel_id=1, source_target_pairs={{0,6},{1,7},{2,0},{3,1},{4,2},{5,3},{6,4},{7,5},{8,14},{9,15},{10,... | collective-permute-start | bytes 884744 | tf_op jit(solution)/shard_map/ppermute | solution.py:657
  19.9 44.4 %collective-permute-start.2 = (bf16[1568,256]{1,0:T(8,128)(2,1)S(1)}, bf16[1568,256]{1,0:T(8,128)(2,1)S(1)}, u32[]{:S(2)}, u32[]{:S(2)}) collective-permute-start(bf16[1568,256]{1,0:T(8,128)(2,1)S(1)} %bitcast.74), channel_id=1, source_target_pairs={{0,6},{1,7},{2,0},{3,1},{4,2},{5,3},{6,4},{7,5},{8,14},{9,15},{10,... | collective-permute-start | bytes 2408456 | tf_op jit(solution)/shard_map/ppermute | solution.py:657
  47.3 16.9 %collective-permute-start.6 = (bf16[1,4,320,256]{3,2,1,0:T(8,128)(2,1)S(1)}, bf16[1,4,320,256]{3,2,1,0:T(8,128)(2,1)S(1)}, u32[]{:S(2)}, u32[]{:S(2)}) collective-permute-start(bf16[1,4,320,256]{3,2,1,0:T(8,128)(2,1)S(1)} %get-tuple-element.76.refs_0_.refs_1_), channel_id=1, source_target_pairs={{0,8},{8,0},{16,24},{24,16},{1,9},{9,1},{17,25},{25,17},{2,10},{10... | collective-permute-start | bytes 1966088 | tf_op jit(solution)/shard_map/ppermute | solution.py:663
  48.9 17.1 %collective-permute-start.8 = (bf16[1,4,256,256]{3,2,1,0:T(8,128)(2,1)S(1)}, bf16[1,4,256,256]{3,2,1,0:T(8,128)(2,1)S(1)}, u32[]{:S(2)}, u32[]{:S(2)}) collective-permute-start(bf16[1,4,256,256]{3,2,1,0:T(8,128)(2,1)S(1)} %get-tuple-element.77.refs_0_.refs_4_), channel_id=1, source_target_pairs={{0,16},{8,24},{16,0},{24,8},{1,17},{9,25},{17,1},{25,9},{2,18},{10... | collective-permute-start | bytes 1572872 | tf_op jit(solution)/shard_map/ppermute | solution.py:663
  64.4 30.8 %collective-permute-start.7 = (bf16[2,4,320,256]{3,2,1,0:T(8,128)(2,1)S(1)}, bf16[2,4,320,256]{3,2,1,0:T(8,128)(2,1)S(1)}, u32[]{:S(2)}, u32[]{:S(2)}) collective-permute-start(bf16[2,4,320,256]{3,2,1,0:T(8,128)(2,1)S(1)} %pair.2), channel_id=1, source_target_pairs={{0,16},{8,24},{16,0},{24,8},{1,17},{9,25},{17,1},{25,9},{2,18},{10... | collective-permute-start | bytes 3932168 | tf_op jit(solution)/shard_map/ppermute | solution.py:663
  66.0 24.9 %collective-permute-start.9 = (bf16[2,4,256,256]{3,2,1,0:T(8,128)(2,1)S(1)}, bf16[2,4,256,256]{3,2,1,0:T(8,128)(2,1)S(1)}, u32[]{:S(2)}, u32[]{:S(2)}) collective-permute-start(bf16[2,4,256,256]{3,2,1,0:T(8,128)(2,1)S(1)} %pair.3), channel_id=1, source_target_pairs={{0,8},{8,0},{16,24},{24,16},{1,9},{9,1},{17,25},{25,17},{2,10},{10... | collective-permute-start | bytes 3145736 | tf_op jit(solution)/shard_map/ppermute | solution.py:663
  67.6 43.4 %collective-permute-start.1 = (bf16[1568,256]{1,0:T(8,128)(2,1)S(1)}, bf16[1568,256]{1,0:T(8,128)(2,1)S(1)}, u32[]{:S(2)}, u32[]{:S(2)}) collective-permute-start(bf16[1568,256]{1,0:T(8,128)(2,1)S(1)} %bitcast.73), channel_id=1, source_target_pairs={{0,4},{1,5},{2,6},{3,7},{4,0},{5,1},{6,2},{7,3},{8,12},{9,13},{10,... | collective-permute-start | bytes 2408456 | tf_op jit(solution)/shard_map/ppermute | solution.py:657
  115.1 5.1 %collective-permute-start.10 = (bf16[2,1568,256]{2,1,0:T(8,128)(2,1)S(1)}, bf16[2,1568,256]{2,1,0:T(8,128)(2,1)S(1)}, u32[]{:S(2)}, u32[]{:S(2)}) collective-permute-start(bf16[2,1568,256]{2,1,0:T(8,128)(2,1)S(1)} %get-tuple-element.84.refs_2_), channel_id=1, source_target_pairs={{0,1},{1,0},{2,3},{3,2},{4,5},{5,4},{6,7},{7,6},{8,9},{9,8},{10,11... | collective-permute-start | bytes 4816904 | tf_op jit(solution)/shard_map/ppermute | solution.py:660
  115.9 25.7 %collective-permute-start.13 = (bf16[1568,256]{1,0:T(8,128)(2,1)S(1)}, bf16[1568,256]{1,0:T(8,128)(2,1)S(1)}, u32[]{:S(2)}, u32[]{:S(2)}) collective-permute-start(bf16[1568,256]{1,0:T(8,128)(2,1)S(1)} %bitcast.70), channel_id=1, source_target_pairs={{0,2},{1,3},{2,4},{3,5},{4,6},{5,7},{6,0},{7,1},{8,10},{9,11},{10,... | collective-permute-start | bytes 2408456 | tf_op jit(solution)/shard_map/ppermute | solution.py:657
  125.0 16.5 %collective-permute-start.12 = (f32[2,2,256]{2,1,0:T(2,128)S(1)}, f32[2,2,256]{2,1,0:T(2,128)S(1)}, u32[]{:S(2)}, u32[]{:S(2)}) collective-permute-start(f32[2,2,256]{2,1,0:T(2,128)S(1)} %add.198.refs_0_), channel_id=1, source_target_pairs={{0,16},{8,24},{16,0},{24,8},{1,17},{9,25},{17,1},{25,9},{2,18},{10... | collective-permute-start | bytes 12296 | tf_op jit(solution)/shard_map/ppermute | solution.py:663
  150.3 19.2 %collective-permute-start.18 = (bf16[1568,256]{1,0:T(8,128)(2,1)S(1)}, bf16[1568,256]{1,0:T(8,128)(2,1)S(1)}, u32[]{:S(2)}, u32[]{:S(2)}) collective-permute-start(bf16[1568,256]{1,0:T(8,128)(2,1)S(1)} %bitcast.65), channel_id=1, source_target_pairs={{0,6},{1,7},{2,0},{3,1},{4,2},{5,3},{6,4},{7,5},{8,14},{9,15},{10,... | collective-permute-start | bytes 2408456 | tf_op jit(solution)/shard_map/ppermute | solution.py:657
  180.9 29.4 %collective-permute-start.24 = (bf16[768,256]{1,0:T(8,128)(2,1)S(1)}, bf16[768,256]{1,0:T(8,128)(2,1)S(1)}, u32[]{:S(2)}, u32[]{:S(2)}) collective-permute-start(bf16[768,256]{1,0:T(8,128)(2,1)S(1)} %bitcast.80), channel_id=1, source_target_pairs={{0,4},{1,5},{2,6},{3,7},{4,0},{5,1},{6,2},{7,3},{8,12},{9,13},{10,... | collective-permute-start | bytes 1179656 | tf_op jit(solution)/shard_map/ppermute | solution.py:657
  181.5 40.3 %collective-permute-start.27 = (bf16[800,256]{1,0:T(8,128)(2,1)S(1)}, bf16[800,256]{1,0:T(8,128)(2,1)S(1)}, u32[]{:S(2)}, u32[]{:S(2)}) collective-permute-start(bf16[800,256]{1,0:T(8,128)(2,1)S(1)} %bitcast.78), channel_id=1, source_target_pairs={{0,4},{1,5},{2,6},{3,7},{4,0},{5,1},{6,2},{7,3},{8,12},{9,13},{10,... | collective-permute-start | bytes 1228808 | tf_op jit(solution)/shard_map/ppermute | solution.py:657
  196.7 13.6 %collective-permute-start.23 = (f32[4,2,256]{2,1,0:T(2,128)S(1)}, f32[4,2,256]{2,1,0:T(2,128)S(1)}, u32[]{:S(2)}, u32[]{:S(2)}) collective-permute-start(f32[4,2,256]{2,1,0:T(2,128)S(1)} %add.204.refs_0_), channel_id=1, source_target_pairs={{0,16},{8,24},{16,0},{24,8},{1,17},{9,25},{17,1},{25,9},{2,18},{10... | collective-permute-start | bytes 24584 | tf_op jit(solution)/shard_map/ppermute | solution.py:663
  210.4 6.8 %collective-permute-start.25 = (f32[4,2,256]{2,1,0:T(2,128)S(1)}, f32[4,2,256]{2,1,0:T(2,128)S(1)}, u32[]{:S(2)}, u32[]{:S(2)}) collective-permute-start(f32[4,2,256]{2,1,0:T(2,128)S(1)} %add.303), channel_id=1, source_target_pairs={{0,2},{1,3},{2,0},{3,1},{4,6},{5,7},{6,4},{7,5},{8,10},{9,11},{10,... | collective-permute-start | bytes 24584 | tf_op jit(solution)/shard_map/ppermute | solution.py:687
  217.2 4.5 collective-permute-start.26
  223.9 17.6 %collective-permute-start.30 = (bf16[1568,256]{1,0:T(8,128)(2,1)S(1)}, bf16[1568,256]{1,0:T(8,128)(2,1)S(1)}, u32[]{:S(2)}, u32[]{:S(2)}) collective-permute-start(bf16[1568,256]{1,0:T(8,128)(2,1)S(1)} %get-tuple-element.94), channel_id=1, source_target_pairs={{0,6},{1,7},{2,0},{3,1},{4,2},{5,3},{6,4},{7,5},{8,14},{9,15},{10,... | collective-permute-start | bytes 2408456 | tf_op jit(solution)/shard_map/ppermute | solution.py:657
  255.6 18.4 %collective-permute-start.33 = (bf16[2,1568,256]{2,1,0:T(8,128)(2,1)S(1)}, bf16[2,1568,256]{2,1,0:T(8,128)(2,1)S(1)}, u32[]{:S(2)}, u32[]{:S(2)}) collective-permute-start(bf16[2,1568,256]{2,1,0:T(8,128)(2,1)S(1)} %get-tuple-element.98), channel_id=1, source_target_pairs={{0,1},{1,0},{2,3},{3,2},{4,5},{5,4},{6,7},{7,6},{8,9},{9,8},{10,11... | collective-permute-start | bytes 4816904 | tf_op jit(solution)/shard_map/ppermute | solution.py:660
  255.7 34.4 %collective-permute-start.36 = (bf16[1568,256]{1,0:T(8,128)(2,1)S(1)}, bf16[1568,256]{1,0:T(8,128)(2,1)S(1)}, u32[]{:S(2)}, u32[]{:S(2)}) collective-permute-start(bf16[1568,256]{1,0:T(8,128)(2,1)S(1)} %pass.7.refs_7_), channel_id=1, source_target_pairs={{0,2},{1,3},{2,4},{3,5},{4,6},{5,7},{6,0},{7,1},{8,10},{9,11},{10,... | collective-permute-start | bytes 2408456 | tf_op jit(solution)/shard_map/ppermute | solution.py:657
  281.1 9.0 %collective-permute-start.35 = (f32[2,2,256]{2,1,0:T(2,128)S(1)}, f32[2,2,256]{2,1,0:T(2,128)S(1)}, u32[]{:S(2)}, u32[]{:S(2)}) collective-permute-start(f32[2,2,256]{2,1,0:T(2,128)S(1)} %add.210.refs_0_), channel_id=1, source_target_pairs={{0,16},{8,24},{16,0},{24,8},{1,17},{9,25},{17,1},{25,9},{2,18},{10... | collective-permute-start | bytes 12296 | tf_op jit(solution)/shard_map/ppermute | solution.py:663
  291.3 28.6 %collective-permute-start.39 = (bf16[4,256,256]{2,1,0:T(8,128)(2,1)S(1)}, bf16[4,256,256]{2,1,0:T(8,128)(2,1)S(1)}, u32[]{:S(2)}, u32[]{:S(2)}) collective-permute-start(bf16[4,256,256]{2,1,0:T(8,128)(2,1)S(1)} %pick.11), channel_id=1, source_target_pairs={{0,24},{8,16},{16,8},{24,0},{1,25},{9,17},{17,9},{25,1},{2,26},{10... | collective-permute-start | bytes 1572872 | tf_op jit(solution)/shard_map/ppermute | solution.py:663
  293.8 26.1 %collective-permute-start.38 = (bf16[4,256,256]{2,1,0:T(8,128)(2,1)S(1)}, bf16[4,256,256]{2,1,0:T(8,128)(2,1)S(1)}, u32[]{:S(2)}, u32[]{:S(2)}) collective-permute-start(bf16[4,256,256]{2,1,0:T(8,128)(2,1)S(1)} %pick.10), channel_id=1, source_target_pairs={{0,16},{8,24},{16,0},{24,8},{1,17},{9,25},{17,1},{25,9},{2,18},{10... | collective-permute-start | bytes 1572872 | tf_op jit(solution)/shard_map/ppermute | solution.py:663
  294.9 25.1 %collective-permute-start.37 = (bf16[4,256,256]{2,1,0:T(8,128)(2,1)S(1)}, bf16[4,256,256]{2,1,0:T(8,128)(2,1)S(1)}, u32[]{:S(2)}, u32[]{:S(2)}) collective-permute-start(bf16[4,256,256]{2,1,0:T(8,128)(2,1)S(1)} %pick.9), channel_id=1, source_target_pairs={{0,8},{8,0},{16,24},{24,16},{1,9},{9,1},{17,25},{25,17},{2,10},{10... | collective-permute-start | bytes 1572872 | tf_op jit(solution)/shard_map/ppermute | solution.py:663
  303.7 17.8 %collective-permute-start.47 = (bf16[768,256]{1,0:T(8,128)(2,1)S(1)}, bf16[768,256]{1,0:T(8,128)(2,1)S(1)}, u32[]{:S(2)}, u32[]{:S(2)}) collective-permute-start(bf16[768,256]{1,0:T(8,128)(2,1)S(1)} %pass.8.refs_10_), channel_id=1, source_target_pairs={{0,4},{1,5},{2,6},{3,7},{4,0},{5,1},{6,2},{7,3},{8,12},{9,13},{10,... | collective-permute-start | bytes 1179656 | tf_op jit(solution)/shard_map/ppermute | solution.py:657
  331.2 4.8 %collective-permute-start.50 = (bf16[2,1568,256]{2,1,0:T(8,128)(2,1)S(1)}, bf16[2,1568,256]{2,1,0:T(8,128)(2,1)S(1)}, u32[]{:S(2)}, u32[]{:S(2)}) collective-permute-start(bf16[2,1568,256]{2,1,0:T(8,128)(2,1)S(1)} %first_grad.1.refs_1_), channel_id=1, source_target_pairs={{0,1},{1,0},{2,3},{3,2},{4,5},{5,4},{6,7},{7,6},{8,9},{9,8},{10,11... | collective-permute-start | bytes 4816904 | tf_op jit(solution)/shard_map/ppermute | solution.py:660
  331.2 16.1 %collective-permute-start.40 = (bf16[256,256]{1,0:T(8,128)(2,1)S(1)}, bf16[256,256]{1,0:T(8,128)(2,1)S(1)}, u32[]{:S(2)}, u32[]{:S(2)}) collective-permute-start(bf16[256,256]{1,0:T(8,128)(2,1)S(1)} %get-tuple-element.101), channel_id=1, source_target_pairs={{0,6},{1,7},{2,0},{3,1},{4,2},{5,3},{6,4},{7,5},{8,14},{9,15},{10,... | collective-permute-start | bytes 393224 | tf_op jit(solution)/shard_map/ppermute | solution.py:657
  333.4 14.0 %collective-permute-start.41 = (bf16[256,256]{1,0:T(8,128)(2,1)S(1)}, bf16[256,256]{1,0:T(8,128)(2,1)S(1)}, u32[]{:S(2)}, u32[]{:S(2)}) collective-permute-start(bf16[256,256]{1,0:T(8,128)(2,1)S(1)} %get-tuple-element.102), channel_id=1, source_target_pairs={{0,4},{1,5},{2,6},{3,7},{4,0},{5,1},{6,2},{7,3},{8,12},{9,13},{10,... | collective-permute-start | bytes 393224 | tf_op jit(solution)/shard_map/ppermute | solution.py:657
  334.8 12.6 %collective-permute-start.42 = (bf16[256,256]{1,0:T(8,128)(2,1)S(1)}, bf16[256,256]{1,0:T(8,128)(2,1)S(1)}, u32[]{:S(2)}, u32[]{:S(2)}) collective-permute-start(bf16[256,256]{1,0:T(8,128)(2,1)S(1)} %get-tuple-element.103), channel_id=1, source_target_pairs={{0,2},{1,3},{2,4},{3,5},{4,6},{5,7},{6,0},{7,1},{8,10},{9,11},{10,... | collective-permute-start | bytes 393224 | tf_op jit(solution)/shard_map/ppermute | solution.py:657
  347.5 62.9 %collective-permute-start.58 = (bf16[1568,256]{1,0:T(8,128)(2,1)S(1)}, bf16[1568,256]{1,0:T(8,128)(2,1)S(1)}, u32[]{:S(2)}, u32[]{:S(2)}) collective-permute-start(bf16[1568,256]{1,0:T(8,128)(2,1)S(1)} %pass.10), channel_id=1, source_target_pairs={{0,4},{1,5},{2,6},{3,7},{4,0},{5,1},{6,2},{7,3},{8,12},{9,13},{10,... | collective-permute-start | bytes 2408456 | tf_op jit(solution)/shard_map/ppermute | solution.py:657
  350.1 53.8 %collective-permute-start.54 = (bf16[4,304,256]{2,1,0:T(8,128)(2,1)S(1)}, bf16[4,304,256]{2,1,0:T(8,128)(2,1)S(1)}, u32[]{:S(2)}, u32[]{:S(2)}) collective-permute-start(bf16[4,304,256]{2,1,0:T(8,128)(2,1)S(1)} %pick.15), channel_id=1, source_target_pairs={{0,24},{8,16},{16,8},{24,0},{1,25},{9,17},{17,9},{25,1},{2,26},{10... | collective-permute-start | bytes 1867784 | tf_op jit(solution)/shard_map/ppermute | solution.py:663
  352.6 51.4 %collective-permute-start.53 = (bf16[4,304,256]{2,1,0:T(8,128)(2,1)S(1)}, bf16[4,304,256]{2,1,0:T(8,128)(2,1)S(1)}, u32[]{:S(2)}, u32[]{:S(2)}) collective-permute-start(bf16[4,304,256]{2,1,0:T(8,128)(2,1)S(1)} %pick.14), channel_id=1, source_target_pairs={{0,16},{8,24},{16,0},{24,8},{1,17},{9,25},{17,1},{25,9},{2,18},{10... | collective-permute-start | bytes 1867784 | tf_op jit(solution)/shard_map/ppermute | solution.py:663
  353.7 50.2 %collective-permute-start.52 = (bf16[4,304,256]{2,1,0:T(8,128)(2,1)S(1)}, bf16[4,304,256]{2,1,0:T(8,128)(2,1)S(1)}, u32[]{:S(2)}, u32[]{:S(2)}) collective-permute-start(bf16[4,304,256]{2,1,0:T(8,128)(2,1)S(1)} %pick.12.refs_5_), channel_id=1, source_target_pairs={{0,8},{8,0},{16,24},{24,16},{1,9},{9,1},{17,25},{25,17},{2,10},{10... | collective-permute-start | bytes 1867784 | tf_op jit(solution)/shard_map/ppermute | solution.py:663
  354.4 48.3 %collective-permute-start.51 = (bf16[800,256]{1,0:T(8,128)(2,1)S(1)}, bf16[800,256]{1,0:T(8,128)(2,1)S(1)}, u32[]{:S(2)}, u32[]{:S(2)}) collective-permute-start(bf16[800,256]{1,0:T(8,128)(2,1)S(1)} %pass.9), channel_id=1, source_target_pairs={{0,4},{1,5},{2,6},{3,7},{4,0},{5,1},{6,2},{7,3},{8,12},{9,13},{10,... | collective-permute-start | bytes 1228808 | tf_op jit(solution)/shard_map/ppermute | solution.py:657
  404.8 7.2 %collective-permute-start.55 = (bf16[304,256]{1,0:T(8,128)(2,1)S(1)}, bf16[304,256]{1,0:T(8,128)(2,1)S(1)}, u32[]{:S(2)}, u32[]{:S(2)}) collective-permute-start(bf16[304,256]{1,0:T(8,128)(2,1)S(1)} %get-tuple-element.117), channel_id=1, source_target_pairs={{0,6},{1,7},{2,0},{3,1},{4,2},{5,3},{6,4},{7,5},{8,14},{9,15},{10,... | collective-permute-start | bytes 466952 | tf_op jit(solution)/shard_map/ppermute | solution.py:657
  407.5 13.1 %collective-permute-start.56 = (bf16[304,256]{1,0:T(8,128)(2,1)S(1)}, bf16[304,256]{1,0:T(8,128)(2,1)S(1)}, u32[]{:S(2)}, u32[]{:S(2)}) collective-permute-start(bf16[304,256]{1,0:T(8,128)(2,1)S(1)} %get-tuple-element.118), channel_id=1, source_target_pairs={{0,4},{1,5},{2,6},{3,7},{4,0},{5,1},{6,2},{7,3},{8,12},{9,13},{10,... | collective-permute-start | bytes 466952 | tf_op jit(solution)/shard_map/ppermute | solution.py:657
  407.5 13.1 %collective-permute-start.57 = (bf16[304,256]{1,0:T(8,128)(2,1)S(1)}, bf16[304,256]{1,0:T(8,128)(2,1)S(1)}, u32[]{:S(2)}, u32[]{:S(2)}) collective-permute-start(bf16[304,256]{1,0:T(8,128)(2,1)S(1)} %get-tuple-element.119), channel_id=1, source_target_pairs={{0,2},{1,3},{2,4},{3,5},{4,6},{5,7},{6,0},{7,1},{8,10},{9,11},{10,... | collective-permute-start | bytes 466952 | tf_op jit(solution)/shard_map/ppermute | solution.py:657
  420.7 20.1 %collective-permute-start.66 = (bf16[1568,256]{1,0:T(8,128)(2,1)S(1)}, bf16[1568,256]{1,0:T(8,128)(2,1)S(1)}, u32[]{:S(2)}, u32[]{:S(2)}) collective-permute-start(bf16[1568,256]{1,0:T(8,128)(2,1)S(1)} %pass.12.refs_11_), channel_id=1, source_target_pairs={{0,6},{1,7},{2,0},{3,1},{4,2},{5,3},{6,4},{7,5},{8,14},{9,15},{10,... | collective-permute-start | bytes 2408456 | tf_op jit(solution)/shard_map/ppermute | solution.py:657
  422.2 6.4 %collective-permute-start.62 = (bf16[256,256]{1,0:T(8,128)(2,1)S(1)}, bf16[256,256]{1,0:T(8,128)(2,1)S(1)}, u32[]{:S(2)}, u32[]{:S(2)}) collective-permute-start(bf16[256,256]{1,0:T(8,128)(2,1)S(1)} %pass.11.refs_5_), channel_id=1, source_target_pairs={{0,8},{8,0},{16,24},{24,16},{1,9},{9,1},{17,25},{25,17},{2,10},{10... | collective-permute-start | bytes 393224 | tf_op jit(solution)/shard_map/ppermute | solution.py:663
  423.7 7.8 %collective-permute-start.63 = (bf16[256,256]{1,0:T(8,128)(2,1)S(1)}, bf16[256,256]{1,0:T(8,128)(2,1)S(1)}, u32[]{:S(2)}, u32[]{:S(2)}) collective-permute-start(bf16[256,256]{1,0:T(8,128)(2,1)S(1)} %pass.11.refs_5_), channel_id=1, source_target_pairs={{0,16},{8,24},{16,0},{24,8},{1,17},{9,25},{17,1},{25,9},{2,18},{10... | collective-permute-start | bytes 393224 | tf_op jit(solution)/shard_map/ppermute | solution.py:663
  425.3 7.4 %collective-permute-start.64 = (bf16[256,256]{1,0:T(8,128)(2,1)S(1)}, bf16[256,256]{1,0:T(8,128)(2,1)S(1)}, u32[]{:S(2)}, u32[]{:S(2)}) collective-permute-start(bf16[256,256]{1,0:T(8,128)(2,1)S(1)} %pass.11.refs_5_), channel_id=1, source_target_pairs={{0,24},{8,16},{16,8},{24,0},{1,25},{9,17},{17,9},{25,1},{2,26},{10... | collective-permute-start | bytes 393224 | tf_op jit(solution)/shard_map/ppermute | solution.py:663
  425.7 8.8 %collective-permute-start.59 = (bf16[304,256]{1,0:T(8,128)(2,1)S(1)}, bf16[304,256]{1,0:T(8,128)(2,1)S(1)}, u32[]{:S(2)}, u32[]{:S(2)}) collective-permute-start(bf16[304,256]{1,0:T(8,128)(2,1)S(1)} %total.3.refs_1_), channel_id=1, source_target_pairs={{0,8},{8,0},{16,24},{24,16},{1,9},{9,1},{17,25},{25,17},{2,10},{10... | collective-permute-start | bytes 466952 | tf_op jit(solution)/shard_map/ppermute | solution.py:663
  428.5 6.9 %collective-permute-start.60 = (bf16[304,256]{1,0:T(8,128)(2,1)S(1)}, bf16[304,256]{1,0:T(8,128)(2,1)S(1)}, u32[]{:S(2)}, u32[]{:S(2)}) collective-permute-start(bf16[304,256]{1,0:T(8,128)(2,1)S(1)} %total.3.refs_1_), channel_id=1, source_target_pairs={{0,16},{8,24},{16,0},{24,8},{1,17},{9,25},{17,1},{25,9},{2,18},{10... | collective-permute-start | bytes 466952 | tf_op jit(solution)/shard_map/ppermute | solution.py:663
  431.5 6.1 %collective-permute-start.61 = (bf16[304,256]{1,0:T(8,128)(2,1)S(1)}, bf16[304,256]{1,0:T(8,128)(2,1)S(1)}, u32[]{:S(2)}, u32[]{:S(2)}) collective-permute-start(bf16[304,256]{1,0:T(8,128)(2,1)S(1)} %total.3.refs_1_), channel_id=1, source_target_pairs={{0,24},{8,16},{16,8},{24,0},{1,25},{9,17},{17,9},{25,1},{2,26},{10... | collective-permute-start | bytes 466952 | tf_op jit(solution)/shard_map/ppermute | solution.py:663
  444.5 4.6 collective-permute-start.68
  450.5 20.4 %collective-permute-start.69 = (bf16[1568,256]{1,0:T(8,128)(2,1)S(1)}, bf16[1568,256]{1,0:T(8,128)(2,1)S(1)}, u32[]{:S(2)}, u32[]{:S(2)}) collective-permute-start(bf16[1568,256]{1,0:T(8,128)(2,1)S(1)} %pass.13), channel_id=1, source_target_pairs={{0,2},{1,3},{2,4},{3,5},{4,6},{5,7},{6,0},{7,1},{8,10},{9,11},{10,... | collective-permute-start | bytes 2408456 | tf_op jit(solution)/shard_map/ppermute | solution.py:657
  (45 other events, 291.8 us)

commit v4 on v3

--- a/solution.py
+++ b/solution.py
@@ -662,6 +662,10 @@
     def over_dp(value, k):
         return lax.ppermute(value, "dp", [(a, a ^ k) for a in range(nd)])
 
+    def pinned_add(a, b, pins):
+        shape = sds(a.shape, F32)
+        return call(add_kernel, "add", shape, a, b, specs=[VMEM] * 2, deps=pins)
+
     def over_all_dp(value, *pins):
         k = 1
         while k < nd:
@@ -670,26 +674,22 @@
             if k < nd or not pins:
                 value = value + other
             else:
-                value = call(
-                    add_kernel,
-                    "add",
-                    sds(value.shape, F32),
-                    value,
-                    other,
-                    specs=[VMEM] * 2,
-                    deps=pins,
-                )
+                value = pinned_add(value, other, pins)
         return value
 
-    def over_all_z(value):
+    def over_all_z(value, *pins):
         k = 2
         while k < ng:
-            value = value + lax.ppermute(value, "group", [(a, a ^ k) for a in range(ng)])
+            other = lax.ppermute(value, "group", [(a, a ^ k) for a in range(ng)])
             k *= 2
+            if k < ng or not pins:
+                value = value + other
+            else:
+                value = pinned_add(value, other, pins)
         return value
 
     def everywhere(value, *pins):
-        return over_all_z(over_all_dp(value, *pins))
+        return over_all_z(over_all_dp(value), *pins)
 
     src = source.transpose(1, 2, 0, 3)
     crops = []
@@ -1013,12 +1013,10 @@
         mid_par,
         deps=[expand_parts],
     )
-    mid2b = over_all_dp(sums2b, *pins)
-    tot2b = over_all_z(mid2b)
+    mid2b = over_all_dp(sums2b)
+    tot2b = over_all_z(mid2b, *pins)
     sent, pins = send_outs(2, tot2b)
     expand_picks = [pick(k, expand_parts, deps=[mid2b]) for k in range(NQ)]
-    expand_pieces = gather_home(expand_picks)
-    pins.append(expand_pieces[0])
     cg, up1, sums1b = call(
         functools.partial(conv_back_kernel, count, images),
         "conv_back",
@@ -1036,7 +1034,9 @@
         scratch=[pad_s, pltpu.VMEM((HW * images, QW), F32)],
         deps=sent,
     )
-    tot1b = everywhere(sums1b, *pins)
+    expand_pieces = gather_home(expand_picks, [sums1b])
+    expand_low = total_of(expand_pieces)
+    tot1b = over_all_z(over_all_dp(sums1b, expand_pieces[0]), *pins, expand_low)
     fg = call(
         functools.partial(first_grad_kernel, count),
         "first_grad",
@@ -1085,31 +1085,30 @@
         scratch=[pad_s],
         deps=[reduce_parts],
     )
-    expand_low = total_of(expand_pieces, [conv_parts])
-    _, pins = send_outs(3, expand_low)
+    _, pins = send_outs(3, tot1b)
 
     def later(value, *deps):
         shape = sds(value.shape, value.dtype)
         body = functools.partial(pass_kernel, 0)
         return call(body, "pass", shape, value, specs=[VMEM], deps=deps)
 
+    expand_home = to_all_dp(expand_low)
     reduce_picks = [
-        pick(k, reduce_parts, conv_parts, deps=[expand_low]) for k in range(NQ)
+        pick(k, reduce_parts, conv_parts, deps=expand_home[1:]) for k in range(NQ)
     ]
     final = nz - 1
-    input_blocks = {2: later(first, expand_low)}
+    input_blocks = {2: first}
     last = reduce_picks[1]
     for d in list(range(3, nz)) + [1, 0]:
         last = input_block(d, last)
         input_blocks[d] = last
-    output, token = place(outs)
+    output, token = place([v for v in outs if v[1] == 0])
     pieces = gather_home(reduce_picks, [last, token])
-
-    expand_home = to_all_dp(later(expand_low, pieces[0]))
+    output, _ = place([v for v in outs if v[1] > 0], output)
     moved = [(0, 0, input_blocks[0])]
     moved += [(d, 0, over_z(input_blocks[d], -d)) for d in range(2, final)]
     placed, token = place(moved)
-    reduce_low = total_of(pieces, [token])
+    reduce_low = total_of(pieces, [token] + pins)
     reduce_home = to_all_dp(reduce_low)
     second = later(input_blocks[1], reduce_low)
     second_moved = over_z(second, -1)
@@ -1144,17 +1143,8 @@
         deps=[second],
     )
     group_wgrad = tap_grad.reshape(group_weight.shape)
-    total_sq = call(
-        add_kernel,
-        "add",
-        sds((8, 128), F32),
-        total_sq,
-        over_core(total_sq),
-        specs=[VMEM] * 2,
-        deps=[second_moved],
-    )
-    total_sq = over_all_z(total_sq)
-    moved = over_z(later(input_blocks[final], total_sq), -final)
+    total_sq = over_all_z(total_sq + over_core(total_sq), second_moved)
+    moved = over_z(later(input_blocks[final], second_moved), -final)
     input_grad, _ = place([(final, 0, moved)], placed)
     grad_norm = jnp.sqrt(total_sq[0, 0])
     clip_scale = jnp.minimum(1.0, clip_norm / (grad_norm + 1e-06))

time: 474 us -> 452 us (0.954)
  waiting for transfers between devices: 227 us -> 196 us
    ppermute x23, waiting for transfers between devices: 141 us -> 92.7 us  [over_z(): return lax.ppermute(value, 'group', pairs)]
    ppermute x28, waiting for transfers between devices: 37.9 us -> 54.5 us  [over_dp(): return lax.ppermute(value, 'dp', [(a, a ^ k) for a in range(nd)])]
    ppermute x14, starting transfers between devices: 12.3 us -> 18.4 us  [over_all_z(): other = lax.ppermute(value, 'group', [(a, a ^ k) for a in range(ng)])]
    pallas_call x68 -> x67, Pallas kernels: 107 us -> 107 us  [call(): pl.pallas_call(inner, in_specs=(specs or [SMEM] + [VMEM] * (used - 1)) +...]
  transfers between devices with their start and end apart: 70 -> 70, of which waited for: 44 -> 41; matrix products, arithmetic and copies ran while one was open for 2% -> 3% of each run, Pallas kernels for 18% -> 19%
where the time goes in v4:
time: 452 us
  waiting for transfers between devices  196 us (43%)
  starting transfers between devices  121 us (27%)
  Pallas kernels  107 us (24%)
  local copies, waits for them, and re-layouts  13 us (3%)
  other arithmetic  10 us (2%)
    pallas_call x67, Pallas kernels, call(): pl.pallas_call(inner, in_specs=(specs or [SMEM] + [VMEM] * (used - 1)) +...  107 us
    ppermute x23, waiting for transfers between devices, over_z(): return lax.ppermute(value, 'group', pairs)  92.7 us
    ppermute x23, starting transfers between devices, over_z(): return lax.ppermute(value, 'group', pairs)  63.7 us
    ppermute x28, waiting for transfers between devices, over_dp(): return lax.ppermute(value, 'dp', [(a, a ^ k) for a in range(nd)])  54.5 us
    ppermute x14, waiting for transfers between devices, over_all_z(): other = lax.ppermute(value, 'group', [(a, a ^ k) for a in range(ng)])  47.5 us
    ppermute x28, starting transfers between devices, over_dp(): return lax.ppermute(value, 'dp', [(a, a ^ k) for a in range(nd)])  38.8 us
    ppermute x14, starting transfers between devices, over_all_z(): other = lax.ppermute(value, 'group', [(a, a ^ k) for a in range(ng)])  18.4 us
    unnamed x83, local copies, waits for them, and re-layouts  9.08 us
  transfers between devices with their start and end apart: 70, of which 41 were waited for; matrix products, arithmetic and copies ran while one was open for 3% of the time, Pallas kernels for 19%

profile of v4, /device:TPU:0, one launch (start us, length us, event | category | flops | bytes accessed | tf_op | source)
XLA Modules:
  0.0 451.8 jit_solution(16719051453866906541)
XLA Ops:
  1.6 2.5 copy-done
  5.1 3.1 collective-permute-start
  13.5 2.8 collective-permute-start.5
  16.4 2.5 copy-done.1
  22.4 13.0 %collective-permute-done.3.refs_1_ = bf16[576,256]{1,0:T(8,128)(2,1)S(1)} collective-permute-done((bf16[576,256]{1,0:T(8,128)(2,1)S(1)}, bf16[576,256]{1,0:T(8,128)(2,1)S(1)}, u32[]{:S(2)}, u32[]{:S(2)}) %collective-permute-start.3) | collective-permute-done | bytes 294944 | tf_op jit(solution)/shard_map/ppermute | solution.py:657
  35.4 11.8 %collective-permute-done.4.refs_2_ = bf16[576,256]{1,0:T(8,128)(2,1)S(1)} collective-permute-done((bf16[576,256]{1,0:T(8,128)(2,1)S(1)}, bf16[576,256]{1,0:T(8,128)(2,1)S(1)}, u32[]{:S(2)}, u32[]{:S(2)}) %collective-permute-start.4) | collective-permute-done | bytes 294944 | tf_op jit(solution)/shard_map/ppermute | solution.py:657
  50.4 13.9 %collective-permute-done.2.refs_2_.refs_4_.refs_6_ = bf16[1568,256]{1,0:T(8,128)(2,1)S(1)} collective-permute-done((bf16[1568,256]{1,0:T(8,128)(2,1)S(1)}, bf16[1568,256]{1,0:T(8,128)(2,1)S(1)}, u32[]{:S(2)}, u32[]{:S(2)}) %collective-permute-start.2) | collective-permute-done | bytes 802848 | tf_op jit(solution)/shard_map/ppermute | solution.py:657
  67.6 16.1 %collective-permute-start.1 = (bf16[1568,256]{1,0:T(8,128)(2,1)S(1)}, bf16[1568,256]{1,0:T(8,128)(2,1)S(1)}, u32[]{:S(2)}, u32[]{:S(2)}) collective-permute-start(bf16[1568,256]{1,0:T(8,128)(2,1)S(1)} %bitcast.73), channel_id=1, source_target_pairs={{0,4},{1,5},{2,6},{3,7},{4,0},{5,1},{6,2},{7,3},{8,12},{9,13},{10,... | collective-permute-start | bytes 2408456 | tf_op jit(solution)/shard_map/ppermute | solution.py:657
  83.7 7.2 %collective-permute-done.9.refs_6_ = bf16[2,4,256,256]{3,2,1,0:T(8,128)(2,1)S(1)} collective-permute-done((bf16[2,4,256,256]{3,2,1,0:T(8,128)(2,1)S(1)}, bf16[2,4,256,256]{3,2,1,0:T(8,128)(2,1)S(1)}, u32[]{:S(2)}, u32[]{:S(2)}) %collective-permute-start.9) | collective-permute-done | bytes 1048608 | tf_op jit(solution)/shard_map/ppermute | solution.py:663
  90.9 4.2 collective-permute-done.7.refs_3_
  96.3 14.7 %collective-permute-done.1.refs_3_.refs_5_ = bf16[1568,256]{1,0:T(8,128)(2,1)S(1)} collective-permute-done((bf16[1568,256]{1,0:T(8,128)(2,1)S(1)}, bf16[1568,256]{1,0:T(8,128)(2,1)S(1)}, u32[]{:S(2)}, u32[]{:S(2)}) %collective-permute-start.1) | collective-permute-done | bytes 802848 | tf_op jit(solution)/shard_map/ppermute | solution.py:657
  111.0 4.1 reduce.1
  115.8 4.3 collective-permute-start.15
  128.6 2.7 collective-permute-start.13
  131.3 6.7 %collective-permute-done.13 = f32[2,2,256]{2,1,0:T(2,128)S(1)} collective-permute-done((f32[2,2,256]{2,1,0:T(2,128)S(1)}, f32[2,2,256]{2,1,0:T(2,128)S(1)}, u32[]{:S(2)}, u32[]{:S(2)}) %collective-permute-start.13) | collective-permute-done | bytes 4128 | tf_op jit(solution)/shard_map/ppermute | solution.py:683
  138.0 4.1 collective-permute-start.14
  144.4 4.4 collective-permute-start.20
  148.8 8.7 %conv.1 = (bf16[2,1568,256]{2,1,0:T(8,128)(2,1)S(1)}, f32[2,1568,256]{2,1,0:T(8,128)S(1)}, f32[2,2,256]{2,1,0:T(2,128)S(1)}) custom-call(s32[3]{0:T(128)S(1)} %pad_add_fusion.refs_0_, f32[2,1568,256]{2,1,0:T(8,128)S(1)} %get-tuple-element.83.refs_1_.refs_7_.refs_2_, bf16[2,1568,256]{2,1,0:T(8,128)(2,1)S(1)} %collective-permute-done.10.refs_2_.refs_8_.refs_3_, ...), custom_call_target="tpu_custom_call" | custom-call | flops 1024 | bytes 1024 | tf_op jit(solution)/shard_map/conv/pallas_call | solution.py:72
  166.0 3.6 collective-permute-done.18
  169.6 4.5 collective-permute-done.19.refs_1_
  177.5 2.9 collective-permute-start.26
  180.8 8.6 %expand.1 = (f32[4,1568,256]{2,1,0:T(8,128)S(1)}, f32[4,2,256]{2,1,0:T(2,128)S(1)}) custom-call(s32[3]{0:T(128)S(1)} %pad_add_fusion.refs_0_, bf16[2,1568,256]{2,1,0:T(8,128)(2,1)S(1)} %second_act.1.refs_1_, bf16[2,1568,256]{2,1,0:T(8,128)(2,1)S(1)} %collective-permute-done.21.refs_2_, bf16[4,4,256,256]{3,2,1,0:T(8,128)(2,1)S(1)} %get-tuple-element.82.refs_9_.refs_3_.refs_6_), custom_call_target="tpu_custom_call" | custom-call | flops 1024 | bytes 1024 | tf_op jit(solution)/shard_map/expand/pallas_call | solution.py:72
  196.8 4.4 collective-permute-done.24
  201.3 14.2 %collective-permute-done.26.refs_2_.refs_8_ = bf16[768,256]{1,0:T(8,128)(2,1)S(1)} collective-permute-done((bf16[768,256]{1,0:T(8,128)(2,1)S(1)}, bf16[768,256]{1,0:T(8,128)(2,1)S(1)}, u32[]{:S(2)}, u32[]{:S(2)}) %collective-permute-start.26) | collective-permute-done | bytes 393248 | tf_op jit(solution)/shard_map/ppermute | solution.py:657
  219.3 5.1 %up.3 = (bf16[1568,256]{1,0:T(8,128)(2,1)S(1)}, bf16[1568,256]{1,0:T(8,128)(2,1)S(1)}, bf16[1568,256]{1,0:T(8,128)(2,1)S(1)}, f32[4,1568,256]{2,1,0:T(8,128)S(1)}, f32[4,2,256]{2,1,0:T(2,128)S(1)}) custom-call(s32[3]{0:T(128)S(1)} %pad_add_fusion.refs_0_, ...), custom_call_target="tpu_custom_call", output_to_operand_aliasing={{3}: (11, {}), {4}: (12, {})} | custom-call | flops 1024 | bytes 1024 | tf_op jit(solution)/shard_map/up/pallas_call | solution.py:72
  233.0 4.8 %collective-permute-done.30 = f32[4,2,256]{2,1,0:T(2,128)S(1)} collective-permute-done((f32[4,2,256]{2,1,0:T(2,128)S(1)}, f32[4,2,256]{2,1,0:T(2,128)S(1)}, u32[]{:S(2)}, u32[]{:S(2)}) %collective-permute-start.30) | collective-permute-done | bytes 8224 | tf_op jit(solution)/shard_map/ppermute | solution.py:683
  237.8 4.5 %collective-permute-done.31.refs_1_ = f32[4,2,256]{2,1,0:T(2,128)S(1)} collective-permute-done((f32[4,2,256]{2,1,0:T(2,128)S(1)}, f32[4,2,256]{2,1,0:T(2,128)S(1)}, u32[]{:S(2)}, u32[]{:S(2)}) %collective-permute-start.31) | collective-permute-done | bytes 8224 | tf_op jit(solution)/shard_map/ppermute | solution.py:683
  242.4 5.9 %expand_back.1 = (bf16[4,1568,256]{2,1,0:T(8,128)(2,1)S(1)}, f32[2,1568,256]{2,1,0:T(8,128)S(1)}, bf16[2,1568,256]{2,1,0:T(8,128)(2,1)S(1)}) custom-call(s32[3]{0:T(128)S(1)} %pad_add_fusion.refs_0_, f32[4,1568,256]{2,1,0:T(8,128)S(1)} %get-tuple-element.87.refs_1_, f32[4,1568,256]{2,1,0:T(8,128)S(1)} %get-tuple-element.92.refs_2_.refs_3_, ...), custom_call_target="tpu_custom_call" | custom-call | flops 1024 | bytes 1024 | tf_op jit(solution)/shard_map/expand_back/pallas_call | solution.py:72
  248.4 13.1 %collective-permute-start.38 = (bf16[1568,256]{1,0:T(8,128)(2,1)S(1)}, bf16[1568,256]{1,0:T(8,128)(2,1)S(1)}, u32[]{:S(2)}, u32[]{:S(2)}) collective-permute-start(bf16[1568,256]{1,0:T(8,128)(2,1)S(1)} %pass.5.refs_7_), channel_id=1, source_target_pairs={{0,2},{1,3},{2,4},{3,5},{4,6},{5,7},{6,0},{7,1},{8,10},{9,11},{10,... | collective-permute-start | bytes 2408456 | tf_op jit(solution)/shard_map/ppermute | solution.py:657
  261.5 4.5 %expand_wgrad.1.refs_6_.refs_1_ = bf16[4,4,256,256]{3,2,1,0:T(8,128)(2,1)S(1)} custom-call(s32[3]{0:T(128)S(1)} %pad_add_fusion.refs_0_, bf16[2,1568,256]{2,1,0:T(8,128)(2,1)S(1)} %second_act.1.refs_1_, bf16[2,1568,256]{2,1,0:T(8,128)(2,1)S(1)} %copy-done.4, bf16[4,1568,256]{2,1,0:T(8,128)(2,1)S(1)} %get-tuple-element.98.refs_3_), custom_call_target="tpu_custom_call" | custom-call | flops 1024 | bytes 1024 | tf_op jit(solution)/shard_map/expand_wgrad/pallas_call | solution.py:72
  266.1 3.4 second_up.1
  277.9 2.5 collective-permute-start.43
  282.2 3.5 collective-permute-done.36
  288.2 6.2 %collective-permute-done.37.refs_1_ = f32[2,2,256]{2,1,0:T(2,128)S(1)} collective-permute-done((f32[2,2,256]{2,1,0:T(2,128)S(1)}, f32[2,2,256]{2,1,0:T(2,128)S(1)}, u32[]{:S(2)}, u32[]{:S(2)}) %collective-permute-start.37) | collective-permute-done | bytes 4128 | tf_op jit(solution)/shard_map/ppermute | solution.py:683
  295.1 10.1 %conv_back.1 = (bf16[2,1568,256]{2,1,0:T(8,128)(2,1)S(1)}, f32[2,1568,256]{2,1,0:T(8,128)S(1)}, f32[2,2,256]{2,1,0:T(2,128)S(1)}) custom-call(s32[3]{0:T(128)S(1)} %pad_add_fusion.refs_0_, f32[2,1568,256]{2,1,0:T(8,128)S(1)} %get-tuple-element.99.refs_1_, f32[2,1568,256]{2,1,0:T(8,128)S(1)} %get-tuple-element.85.refs_1_.refs_3_.refs_2_, ...), custom_call_target="tpu_custom_call" | custom-call | flops 1024 | bytes 1024 | tf_op jit(solution)/shard_map/conv_back/pallas_call | solution.py:72
  306.1 2.6 collective-permute-start.47
  335.5 4.6 %reduce_wgrad.1.refs_3_.refs_1_ = bf16[4,4,256,256]{3,2,1,0:T(8,128)(2,1)S(1)} custom-call(s32[3]{0:T(128)S(1)} %pad_add_fusion.refs_0_, bf16[2,1568,256]{2,1,0:T(8,128)(2,1)S(1)} %first_grad.1.refs_1_, bf16[2,1568,256]{2,1,0:T(8,128)(2,1)S(1)} %collective-permute-done.51.refs_2_, bf16[1568,256]{1,0:T(8,128)(2,1)S(1)} %bitcast.60, ...), custom_call_target="tpu_custom_call" | custom-call | flops 1024 | bytes 1024 | tf_op jit(solution)/shard_map/reduce_wgrad/pallas_call | solution.py:72
  340.1 5.1 %conv_wgrad.1.refs_2_ = bf16[4,4,48,256]{3,2,1,0:T(8,128)(2,1)S(1)} custom-call(s32[3]{0:T(128)S(1)} %pad_add_fusion.refs_0_, bf16[2,1568,256]{2,1,0:T(8,128)(2,1)S(1)} %copy-done.8, bf16[2,1568,256]{2,1,0:T(8,128)(2,1)S(1)} %get-tuple-element.114.refs_2_, bf16[4,4,256,256]{3,2,1,0:T(8,128)(2,1)S(1)} %reduce_wgrad.1.refs_3_.refs_1_), custom_call_target="tpu_custom_call" | custom-call | flops 1024 | bytes 1024 | tf_op jit(solution)/shard_map/conv_wgrad/pallas_call | solution.py:72
  345.8 2.5 collective-permute-start.57
  364.8 11.0 %collective-permute-done.56.refs_3_ = bf16[4,304,256]{2,1,0:T(8,128)(2,1)S(1)} collective-permute-done((bf16[4,304,256]{2,1,0:T(8,128)(2,1)S(1)}, bf16[4,304,256]{2,1,0:T(8,128)(2,1)S(1)}, u32[]{:S(2)}, u32[]{:S(2)}) %collective-permute-start.56) | collective-permute-done | bytes 622624 | tf_op jit(solution)/shard_map/ppermute | solution.py:663
  384.0 12.6 %collective-permute-done.50.refs_5_ = bf16[800,256]{1,0:T(8,128)(2,1)S(1)} collective-permute-done((bf16[800,256]{1,0:T(8,128)(2,1)S(1)}, bf16[800,256]{1,0:T(8,128)(2,1)S(1)}, u32[]{:S(2)}, u32[]{:S(2)}) %collective-permute-start.50) | collective-permute-done | bytes 409632 | tf_op jit(solution)/shard_map/ppermute | solution.py:657
  396.6 5.7 %collective-permute-done.59.refs_2_ = bf16[304,256]{1,0:T(8,128)(2,1)S(1)} collective-permute-done((bf16[304,256]{1,0:T(8,128)(2,1)S(1)}, bf16[304,256]{1,0:T(8,128)(2,1)S(1)}, u32[]{:S(2)}, u32[]{:S(2)}) %collective-permute-start.59) | collective-permute-done | bytes 155680 | tf_op jit(solution)/shard_map/ppermute | solution.py:657
  407.5 2.8 collective-permute-done.64.refs_2_
  410.2 3.8 collective-permute-done.65.refs_3_
  419.0 2.6 collective-permute-done.68
  421.6 2.8 collective-permute-start.69
  435.6 2.5 fusion.11
  441.5 6.9 %collective-permute-done.63 = bf16[1568,256]{1,0:T(8,128)(2,1)S(1)} collective-permute-done((bf16[1568,256]{1,0:T(8,128)(2,1)S(1)}, bf16[1568,256]{1,0:T(8,128)(2,1)S(1)}, u32[]{:S(2)}, u32[]{:S(2)}) %collective-permute-start.63) | collective-permute-done | bytes 802848 | tf_op jit(solution)/shard_map/ppermute | solution.py:657
  (280 shorter events, 153.4 us)
Async XLA Ops:
  5.1 42.1 %collective-permute-start = (bf16[1568,256]{1,0:T(8,128)(2,1)S(1)}, bf16[1568,256]{1,0:T(8,128)(2,1)S(1)}, u32[]{:S(2)}, u32[]{:S(2)}) collective-permute-start(bf16[1568,256]{1,0:T(8,128)(2,1)S(1)} %bitcast.62), channel_id=1, source_target_pairs={{0,2},{1,3},{2,4},{3,5},{4,6},{5,7},{6,0},{7,1},{8,10},{9,11},{10,... | collective-permute-start | bytes 2408456 | tf_op jit(solution)/shard_map/ppermute | solution.py:657
  10.8 24.6 %collective-permute-start.3 = (bf16[576,256]{1,0:T(8,128)(2,1)S(1)}, bf16[576,256]{1,0:T(8,128)(2,1)S(1)}, u32[]{:S(2)}, u32[]{:S(2)}) collective-permute-start(bf16[576,256]{1,0:T(8,128)(2,1)S(1)} %bundle.1.refs_0_), channel_id=1, source_target_pairs={{0,2},{1,3},{2,4},{3,5},{4,6},{5,7},{6,0},{7,1},{8,10},{9,11},{10,... | collective-permute-start | bytes 884744 | tf_op jit(solution)/shard_map/ppermute | solution.py:657
  12.4 34.8 %collective-permute-start.4 = (bf16[576,256]{1,0:T(8,128)(2,1)S(1)}, bf16[576,256]{1,0:T(8,128)(2,1)S(1)}, u32[]{:S(2)}, u32[]{:S(2)}) collective-permute-start(bf16[576,256]{1,0:T(8,128)(2,1)S(1)} %bundle.1.refs_0_), channel_id=1, source_target_pairs={{0,4},{1,5},{2,6},{3,7},{4,0},{5,1},{6,2},{7,3},{8,12},{9,13},{10,... | collective-permute-start | bytes 884744 | tf_op jit(solution)/shard_map/ppermute | solution.py:657
  13.5 33.7 %collective-permute-start.5 = (bf16[576,256]{1,0:T(8,128)(2,1)S(1)}, bf16[576,256]{1,0:T(8,128)(2,1)S(1)}, u32[]{:S(2)}, u32[]{:S(2)}) collective-permute-start(bf16[576,256]{1,0:T(8,128)(2,1)S(1)} %bundle.1.refs_0_), channel_id=1, source_target_pairs={{0,6},{1,7},{2,0},{3,1},{4,2},{5,3},{6,4},{7,5},{8,14},{9,15},{10,... | collective-permute-start | bytes 884744 | tf_op jit(solution)/shard_map/ppermute | solution.py:657
  19.9 44.4 %collective-permute-start.2 = (bf16[1568,256]{1,0:T(8,128)(2,1)S(1)}, bf16[1568,256]{1,0:T(8,128)(2,1)S(1)}, u32[]{:S(2)}, u32[]{:S(2)}) collective-permute-start(bf16[1568,256]{1,0:T(8,128)(2,1)S(1)} %bitcast.74), channel_id=1, source_target_pairs={{0,6},{1,7},{2,0},{3,1},{4,2},{5,3},{6,4},{7,5},{8,14},{9,15},{10,... | collective-permute-start | bytes 2408456 | tf_op jit(solution)/shard_map/ppermute | solution.py:657
  47.3 16.9 %collective-permute-start.6 = (bf16[1,4,320,256]{3,2,1,0:T(8,128)(2,1)S(1)}, bf16[1,4,320,256]{3,2,1,0:T(8,128)(2,1)S(1)}, u32[]{:S(2)}, u32[]{:S(2)}) collective-permute-start(bf16[1,4,320,256]{3,2,1,0:T(8,128)(2,1)S(1)} %get-tuple-element.76.refs_0_.refs_1_), channel_id=1, source_target_pairs={{0,8},{8,0},{16,24},{24,16},{1,9},{9,1},{17,25},{25,17},{2,10},{10... | collective-permute-start | bytes 1966088 | tf_op jit(solution)/shard_map/ppermute | solution.py:663
  48.9 17.1 %collective-permute-start.8 = (bf16[1,4,256,256]{3,2,1,0:T(8,128)(2,1)S(1)}, bf16[1,4,256,256]{3,2,1,0:T(8,128)(2,1)S(1)}, u32[]{:S(2)}, u32[]{:S(2)}) collective-permute-start(bf16[1,4,256,256]{3,2,1,0:T(8,128)(2,1)S(1)} %get-tuple-element.77.refs_0_.refs_4_), channel_id=1, source_target_pairs={{0,16},{8,24},{16,0},{24,8},{1,17},{9,25},{17,1},{25,9},{2,18},{10... | collective-permute-start | bytes 1572872 | tf_op jit(solution)/shard_map/ppermute | solution.py:663
  64.4 30.8 %collective-permute-start.7 = (bf16[2,4,320,256]{3,2,1,0:T(8,128)(2,1)S(1)}, bf16[2,4,320,256]{3,2,1,0:T(8,128)(2,1)S(1)}, u32[]{:S(2)}, u32[]{:S(2)}) collective-permute-start(bf16[2,4,320,256]{3,2,1,0:T(8,128)(2,1)S(1)} %pair.2), channel_id=1, source_target_pairs={{0,16},{8,24},{16,0},{24,8},{1,17},{9,25},{17,1},{25,9},{2,18},{10... | collective-permute-start | bytes 3932168 | tf_op jit(solution)/shard_map/ppermute | solution.py:663
  66.0 24.9 %collective-permute-start.9 = (bf16[2,4,256,256]{3,2,1,0:T(8,128)(2,1)S(1)}, bf16[2,4,256,256]{3,2,1,0:T(8,128)(2,1)S(1)}, u32[]{:S(2)}, u32[]{:S(2)}) collective-permute-start(bf16[2,4,256,256]{3,2,1,0:T(8,128)(2,1)S(1)} %pair.3), channel_id=1, source_target_pairs={{0,8},{8,0},{16,24},{24,16},{1,9},{9,1},{17,25},{25,17},{2,10},{10... | collective-permute-start | bytes 3145736 | tf_op jit(solution)/shard_map/ppermute | solution.py:663
  67.6 43.4 %collective-permute-start.1 = (bf16[1568,256]{1,0:T(8,128)(2,1)S(1)}, bf16[1568,256]{1,0:T(8,128)(2,1)S(1)}, u32[]{:S(2)}, u32[]{:S(2)}) collective-permute-start(bf16[1568,256]{1,0:T(8,128)(2,1)S(1)} %bitcast.73), channel_id=1, source_target_pairs={{0,4},{1,5},{2,6},{3,7},{4,0},{5,1},{6,2},{7,3},{8,12},{9,13},{10,... | collective-permute-start | bytes 2408456 | tf_op jit(solution)/shard_map/ppermute | solution.py:657
  115.1 5.1 %collective-permute-start.10 = (bf16[2,1568,256]{2,1,0:T(8,128)(2,1)S(1)}, bf16[2,1568,256]{2,1,0:T(8,128)(2,1)S(1)}, u32[]{:S(2)}, u32[]{:S(2)}) collective-permute-start(bf16[2,1568,256]{2,1,0:T(8,128)(2,1)S(1)} %get-tuple-element.84.refs_2_), channel_id=1, source_target_pairs={{0,1},{1,0},{2,3},{3,2},{4,5},{5,4},{6,7},{7,6},{8,9},{9,8},{10,11... | collective-permute-start | bytes 4816904 | tf_op jit(solution)/shard_map/ppermute | solution.py:660
  115.8 26.3 %collective-permute-start.15 = (bf16[1568,256]{1,0:T(8,128)(2,1)S(1)}, bf16[1568,256]{1,0:T(8,128)(2,1)S(1)}, u32[]{:S(2)}, u32[]{:S(2)}) collective-permute-start(bf16[1568,256]{1,0:T(8,128)(2,1)S(1)} %bitcast.70), channel_id=1, source_target_pairs={{0,2},{1,3},{2,4},{3,5},{4,6},{5,7},{6,0},{7,1},{8,10},{9,11},{10,... | collective-permute-start | bytes 2408456 | tf_op jit(solution)/shard_map/ppermute | solution.py:657
  128.6 9.5 %collective-permute-start.13 = (f32[2,2,256]{2,1,0:T(2,128)S(1)}, f32[2,2,256]{2,1,0:T(2,128)S(1)}, u32[]{:S(2)}, u32[]{:S(2)}) collective-permute-start(f32[2,2,256]{2,1,0:T(2,128)S(1)} %add.197), channel_id=1, source_target_pairs={{0,2},{1,3},{2,0},{3,1},{4,6},{5,7},{6,4},{7,5},{8,10},{9,11},{10,... | collective-permute-start | bytes 12296 | tf_op jit(solution)/shard_map/ppermute | solution.py:683
  138.0 5.7 %collective-permute-start.14 = (f32[2,2,256]{2,1,0:T(2,128)S(1)}, f32[2,2,256]{2,1,0:T(2,128)S(1)}, u32[]{:S(2)}, u32[]{:S(2)}) collective-permute-start(f32[2,2,256]{2,1,0:T(2,128)S(1)} %add.198.refs_0_), channel_id=1, source_target_pairs={{0,4},{1,5},{2,6},{3,7},{4,0},{5,1},{6,2},{7,3},{8,12},{9,13},{10,... | collective-permute-start | bytes 12296 | tf_op jit(solution)/shard_map/ppermute | solution.py:683
  144.4 29.7 %collective-permute-start.20 = (bf16[1568,256]{1,0:T(8,128)(2,1)S(1)}, bf16[1568,256]{1,0:T(8,128)(2,1)S(1)}, u32[]{:S(2)}, u32[]{:S(2)}) collective-permute-start(bf16[1568,256]{1,0:T(8,128)(2,1)S(1)} %bitcast.66), channel_id=1, source_target_pairs={{0,6},{1,7},{2,0},{3,1},{4,2},{5,3},{6,4},{7,5},{8,14},{9,15},{10,... | collective-permute-start | bytes 2408456 | tf_op jit(solution)/shard_map/ppermute | solution.py:657
  177.4 38.2 %collective-permute-start.27 = (bf16[800,256]{1,0:T(8,128)(2,1)S(1)}, bf16[800,256]{1,0:T(8,128)(2,1)S(1)}, u32[]{:S(2)}, u32[]{:S(2)}) collective-permute-start(bf16[800,256]{1,0:T(8,128)(2,1)S(1)} %bitcast.78), channel_id=1, source_target_pairs={{0,4},{1,5},{2,6},{3,7},{4,0},{5,1},{6,2},{7,3},{8,12},{9,13},{10,... | collective-permute-start | bytes 1228808 | tf_op jit(solution)/shard_map/ppermute | solution.py:657
  177.5 38.0 %collective-permute-start.26 = (bf16[768,256]{1,0:T(8,128)(2,1)S(1)}, bf16[768,256]{1,0:T(8,128)(2,1)S(1)}, u32[]{:S(2)}, u32[]{:S(2)}) collective-permute-start(bf16[768,256]{1,0:T(8,128)(2,1)S(1)} %bitcast.81), channel_id=1, source_target_pairs={{0,4},{1,5},{2,6},{3,7},{4,0},{5,1},{6,2},{7,3},{8,12},{9,13},{10,... | collective-permute-start | bytes 1179656 | tf_op jit(solution)/shard_map/ppermute | solution.py:657
  201.3 14.3 %collective-permute-start.25 = (f32[4,2,256]{2,1,0:T(2,128)S(1)}, f32[4,2,256]{2,1,0:T(2,128)S(1)}, u32[]{:S(2)}, u32[]{:S(2)}) collective-permute-start(f32[4,2,256]{2,1,0:T(2,128)S(1)} %add.204.refs_0_), channel_id=1, source_target_pairs={{0,4},{1,5},{2,6},{3,7},{4,0},{5,1},{6,2},{7,3},{8,12},{9,13},{10,... | collective-permute-start | bytes 24584 | tf_op jit(solution)/shard_map/ppermute | solution.py:683
  217.7 24.7 %collective-permute-start.32 = (bf16[1568,256]{1,0:T(8,128)(2,1)S(1)}, bf16[1568,256]{1,0:T(8,128)(2,1)S(1)}, u32[]{:S(2)}, u32[]{:S(2)}) collective-permute-start(bf16[1568,256]{1,0:T(8,128)(2,1)S(1)} %get-tuple-element.94), channel_id=1, source_target_pairs={{0,6},{1,7},{2,0},{3,1},{4,2},{5,3},{6,4},{7,5},{8,14},{9,15},{10,... | collective-permute-start | bytes 2408456 | tf_op jit(solution)/shard_map/ppermute | solution.py:657
  231.8 6.0 %collective-permute-start.30 = (f32[4,2,256]{2,1,0:T(2,128)S(1)}, f32[4,2,256]{2,1,0:T(2,128)S(1)}, u32[]{:S(2)}, u32[]{:S(2)}) collective-permute-start(f32[4,2,256]{2,1,0:T(2,128)S(1)} %add.206), channel_id=1, source_target_pairs={{0,2},{1,3},{2,0},{3,1},{4,6},{5,7},{6,4},{7,5},{8,10},{9,11},{10,... | collective-permute-start | bytes 24584 | tf_op jit(solution)/shard_map/ppermute | solution.py:683
  237.8 4.5 %collective-permute-start.31 = (f32[4,2,256]{2,1,0:T(2,128)S(1)}, f32[4,2,256]{2,1,0:T(2,128)S(1)}, u32[]{:S(2)}, u32[]{:S(2)}) collective-permute-start(f32[4,2,256]{2,1,0:T(2,128)S(1)} %add.207.refs_0_), channel_id=1, source_target_pairs={{0,4},{1,5},{2,6},{3,7},{4,0},{5,1},{6,2},{7,3},{8,12},{9,13},{10,... | collective-permute-start | bytes 24584 | tf_op jit(solution)/shard_map/ppermute | solution.py:683
  248.3 17.8 %collective-permute-start.33 = (bf16[2,1568,256]{2,1,0:T(8,128)(2,1)S(1)}, bf16[2,1568,256]{2,1,0:T(8,128)(2,1)S(1)}, u32[]{:S(2)}, u32[]{:S(2)}) collective-permute-start(bf16[2,1568,256]{2,1,0:T(8,128)(2,1)S(1)} %get-tuple-element.97), channel_id=1, source_target_pairs={{0,1},{1,0},{2,3},{3,2},{4,5},{5,4},{6,7},{7,6},{8,9},{9,8},{10,11... | collective-permute-start | bytes 4816904 | tf_op jit(solution)/shard_map/ppermute | solution.py:660
  248.4 39.9 %collective-permute-start.38 = (bf16[1568,256]{1,0:T(8,128)(2,1)S(1)}, bf16[1568,256]{1,0:T(8,128)(2,1)S(1)}, u32[]{:S(2)}, u32[]{:S(2)}) collective-permute-start(bf16[1568,256]{1,0:T(8,128)(2,1)S(1)} %pass.5.refs_7_), channel_id=1, source_target_pairs={{0,2},{1,3},{2,4},{3,5},{4,6},{5,7},{6,0},{7,1},{8,10},{9,11},{10,... | collective-permute-start | bytes 2408456 | tf_op jit(solution)/shard_map/ppermute | solution.py:657
  277.9 27.4 %collective-permute-start.43 = (bf16[4,256,256]{2,1,0:T(8,128)(2,1)S(1)}, bf16[4,256,256]{2,1,0:T(8,128)(2,1)S(1)}, u32[]{:S(2)}, u32[]{:S(2)}) collective-permute-start(bf16[4,256,256]{2,1,0:T(8,128)(2,1)S(1)} %pick.11), channel_id=1, source_target_pairs={{0,24},{8,16},{16,8},{24,0},{1,25},{9,17},{17,9},{25,1},{2,26},{10... | collective-permute-start | bytes 1572872 | tf_op jit(solution)/shard_map/ppermute | solution.py:663
  280.5 24.9 %collective-permute-start.42 = (bf16[4,256,256]{2,1,0:T(8,128)(2,1)S(1)}, bf16[4,256,256]{2,1,0:T(8,128)(2,1)S(1)}, u32[]{:S(2)}, u32[]{:S(2)}) collective-permute-start(bf16[4,256,256]{2,1,0:T(8,128)(2,1)S(1)} %pick.10), channel_id=1, source_target_pairs={{0,16},{8,24},{16,0},{24,8},{1,17},{9,25},{17,1},{25,9},{2,18},{10... | collective-permute-start | bytes 1572872 | tf_op jit(solution)/shard_map/ppermute | solution.py:663
  281.5 23.8 %collective-permute-start.41 = (bf16[4,256,256]{2,1,0:T(8,128)(2,1)S(1)}, bf16[4,256,256]{2,1,0:T(8,128)(2,1)S(1)}, u32[]{:S(2)}, u32[]{:S(2)}) collective-permute-start(bf16[4,256,256]{2,1,0:T(8,128)(2,1)S(1)} %pick.9), channel_id=1, source_target_pairs={{0,8},{8,0},{16,24},{24,16},{1,9},{9,1},{17,25},{25,17},{2,10},{10... | collective-permute-start | bytes 1572872 | tf_op jit(solution)/shard_map/ppermute | solution.py:663
  285.8 8.7 %collective-permute-start.37 = (f32[2,2,256]{2,1,0:T(2,128)S(1)}, f32[2,2,256]{2,1,0:T(2,128)S(1)}, u32[]{:S(2)}, u32[]{:S(2)}) collective-permute-start(f32[2,2,256]{2,1,0:T(2,128)S(1)} %add.210.refs_0_), channel_id=1, source_target_pairs={{0,4},{1,5},{2,6},{3,7},{4,0},{5,1},{6,2},{7,3},{8,12},{9,13},{10,... | collective-permute-start | bytes 12296 | tf_op jit(solution)/shard_map/ppermute | solution.py:683
  294.5 29.6 %collective-permute-start.46 = (bf16[768,256]{1,0:T(8,128)(2,1)S(1)}, bf16[768,256]{1,0:T(8,128)(2,1)S(1)}, u32[]{:S(2)}, u32[]{:S(2)}) collective-permute-start(bf16[768,256]{1,0:T(8,128)(2,1)S(1)} %pass.6.refs_10_), channel_id=1, source_target_pairs={{0,4},{1,5},{2,6},{3,7},{4,0},{5,1},{6,2},{7,3},{8,12},{9,13},{10,... | collective-permute-start | bytes 1179656 | tf_op jit(solution)/shard_map/ppermute | solution.py:657
  306.1 17.9 %collective-permute-start.47 = (bf16[256,256]{1,0:T(8,128)(2,1)S(1)}, bf16[256,256]{1,0:T(8,128)(2,1)S(1)}, u32[]{:S(2)}, u32[]{:S(2)}) collective-permute-start(bf16[256,256]{1,0:T(8,128)(2,1)S(1)} %get-tuple-element.103), channel_id=1, source_target_pairs={{0,6},{1,7},{2,0},{3,1},{4,2},{5,3},{6,4},{7,5},{8,14},{9,15},{10,... | collective-permute-start | bytes 393224 | tf_op jit(solution)/shard_map/ppermute | solution.py:657
  308.8 15.2 %collective-permute-start.48 = (bf16[256,256]{1,0:T(8,128)(2,1)S(1)}, bf16[256,256]{1,0:T(8,128)(2,1)S(1)}, u32[]{:S(2)}, u32[]{:S(2)}) collective-permute-start(bf16[256,256]{1,0:T(8,128)(2,1)S(1)} %get-tuple-element.104), channel_id=1, source_target_pairs={{0,4},{1,5},{2,6},{3,7},{4,0},{5,1},{6,2},{7,3},{8,12},{9,13},{10,... | collective-permute-start | bytes 393224 | tf_op jit(solution)/shard_map/ppermute | solution.py:657
  310.8 13.2 %collective-permute-start.49 = (bf16[256,256]{1,0:T(8,128)(2,1)S(1)}, bf16[256,256]{1,0:T(8,128)(2,1)S(1)}, u32[]{:S(2)}, u32[]{:S(2)}) collective-permute-start(bf16[256,256]{1,0:T(8,128)(2,1)S(1)} %get-tuple-element.105), channel_id=1, source_target_pairs={{0,2},{1,3},{2,4},{3,5},{4,6},{5,7},{6,0},{7,1},{8,10},{9,11},{10,... | collective-permute-start | bytes 393224 | tf_op jit(solution)/shard_map/ppermute | solution.py:657
  328.1 17.1 %collective-permute-start.52 = (bf16[256,256]{1,0:T(8,128)(2,1)S(1)}, bf16[256,256]{1,0:T(8,128)(2,1)S(1)}, u32[]{:S(2)}, u32[]{:S(2)}) collective-permute-start(bf16[256,256]{1,0:T(8,128)(2,1)S(1)} %total.2.refs_3_.refs_5_), channel_id=1, source_target_pairs={{0,8},{8,0},{16,24},{24,16},{1,9},{9,1},{17,25},{25,17},{2,10},{10... | collective-permute-start | bytes 393224 | tf_op jit(solution)/shard_map/ppermute | solution.py:663
  329.7 15.5 %collective-permute-start.53 = (bf16[256,256]{1,0:T(8,128)(2,1)S(1)}, bf16[256,256]{1,0:T(8,128)(2,1)S(1)}, u32[]{:S(2)}, u32[]{:S(2)}) collective-permute-start(bf16[256,256]{1,0:T(8,128)(2,1)S(1)} %total.2.refs_3_.refs_5_), channel_id=1, source_target_pairs={{0,16},{8,24},{16,0},{24,8},{1,17},{9,25},{17,1},{25,9},{2,18},{10... | collective-permute-start | bytes 393224 | tf_op jit(solution)/shard_map/ppermute | solution.py:663
  331.2 14.0 %collective-permute-start.54 = (bf16[256,256]{1,0:T(8,128)(2,1)S(1)}, bf16[256,256]{1,0:T(8,128)(2,1)S(1)}, u32[]{:S(2)}, u32[]{:S(2)}) collective-permute-start(bf16[256,256]{1,0:T(8,128)(2,1)S(1)} %total.2.refs_3_.refs_5_), channel_id=1, source_target_pairs={{0,24},{8,16},{16,8},{24,0},{1,25},{9,17},{17,9},{25,1},{2,26},{10... | collective-permute-start | bytes 393224 | tf_op jit(solution)/shard_map/ppermute | solution.py:663
  333.4 49.1 %collective-permute-start.61 = (bf16[1568,256]{1,0:T(8,128)(2,1)S(1)}, bf16[1568,256]{1,0:T(8,128)(2,1)S(1)}, u32[]{:S(2)}, u32[]{:S(2)}) collective-permute-start(bf16[1568,256]{1,0:T(8,128)(2,1)S(1)} %input_grad.4.refs_7_), channel_id=1, source_target_pairs={{0,4},{1,5},{2,6},{3,7},{4,0},{5,1},{6,2},{7,3},{8,12},{9,13},{10,... | collective-permute-start | bytes 2408456 | tf_op jit(solution)/shard_map/ppermute | solution.py:657
  345.8 19.0 %collective-permute-start.57 = (bf16[4,304,256]{2,1,0:T(8,128)(2,1)S(1)}, bf16[4,304,256]{2,1,0:T(8,128)(2,1)S(1)}, u32[]{:S(2)}, u32[]{:S(2)}) collective-permute-start(bf16[4,304,256]{2,1,0:T(8,128)(2,1)S(1)} %pick.15), channel_id=1, source_target_pairs={{0,24},{8,16},{16,8},{24,0},{1,25},{9,17},{17,9},{25,1},{2,26},{10... | collective-permute-start | bytes 1867784 | tf_op jit(solution)/shard_map/ppermute | solution.py:663
  349.0 26.9 %collective-permute-start.56 = (bf16[4,304,256]{2,1,0:T(8,128)(2,1)S(1)}, bf16[4,304,256]{2,1,0:T(8,128)(2,1)S(1)}, u32[]{:S(2)}, u32[]{:S(2)}) collective-permute-start(bf16[4,304,256]{2,1,0:T(8,128)(2,1)S(1)} %pick.14), channel_id=1, source_target_pairs={{0,16},{8,24},{16,0},{24,8},{1,17},{9,25},{17,1},{25,9},{2,18},{10... | collective-permute-start | bytes 1867784 | tf_op jit(solution)/shard_map/ppermute | solution.py:663
  350.1 25.8 %collective-permute-start.55 = (bf16[4,304,256]{2,1,0:T(8,128)(2,1)S(1)}, bf16[4,304,256]{2,1,0:T(8,128)(2,1)S(1)}, u32[]{:S(2)}, u32[]{:S(2)}) collective-permute-start(bf16[4,304,256]{2,1,0:T(8,128)(2,1)S(1)} %pick.12.refs_5_), channel_id=1, source_target_pairs={{0,8},{8,0},{16,24},{24,16},{1,9},{9,1},{17,25},{25,17},{2,10},{10... | collective-permute-start | bytes 1867784 | tf_op jit(solution)/shard_map/ppermute | solution.py:663
  350.8 45.8 %collective-permute-start.50 = (bf16[800,256]{1,0:T(8,128)(2,1)S(1)}, bf16[800,256]{1,0:T(8,128)(2,1)S(1)}, u32[]{:S(2)}, u32[]{:S(2)}) collective-permute-start(bf16[800,256]{1,0:T(8,128)(2,1)S(1)} %pass.7), channel_id=1, source_target_pairs={{0,4},{1,5},{2,6},{3,7},{4,0},{5,1},{6,2},{7,3},{8,12},{9,13},{10,... | collective-permute-start | bytes 1228808 | tf_op jit(solution)/shard_map/ppermute | solution.py:657
  376.7 19.8 %collective-permute-start.58 = (bf16[304,256]{1,0:T(8,128)(2,1)S(1)}, bf16[304,256]{1,0:T(8,128)(2,1)S(1)}, u32[]{:S(2)}, u32[]{:S(2)}) collective-permute-start(bf16[304,256]{1,0:T(8,128)(2,1)S(1)} %get-tuple-element.117), channel_id=1, source_target_pairs={{0,6},{1,7},{2,0},{3,1},{4,2},{5,3},{6,4},{7,5},{8,14},{9,15},{10,... | collective-permute-start | bytes 466952 | tf_op jit(solution)/shard_map/ppermute | solution.py:657
  378.6 23.8 %collective-permute-start.59 = (bf16[304,256]{1,0:T(8,128)(2,1)S(1)}, bf16[304,256]{1,0:T(8,128)(2,1)S(1)}, u32[]{:S(2)}, u32[]{:S(2)}) collective-permute-start(bf16[304,256]{1,0:T(8,128)(2,1)S(1)} %get-tuple-element.118), channel_id=1, source_target_pairs={{0,4},{1,5},{2,6},{3,7},{4,0},{5,1},{6,2},{7,3},{8,12},{9,13},{10,... | collective-permute-start | bytes 466952 | tf_op jit(solution)/shard_map/ppermute | solution.py:657
  380.3 22.0 %collective-permute-start.60 = (bf16[304,256]{1,0:T(8,128)(2,1)S(1)}, bf16[304,256]{1,0:T(8,128)(2,1)S(1)}, u32[]{:S(2)}, u32[]{:S(2)}) collective-permute-start(bf16[304,256]{1,0:T(8,128)(2,1)S(1)} %get-tuple-element.119), channel_id=1, source_target_pairs={{0,2},{1,3},{2,4},{3,5},{4,6},{5,7},{6,0},{7,1},{8,10},{9,11},{10,... | collective-permute-start | bytes 466952 | tf_op jit(solution)/shard_map/ppermute | solution.py:657
  402.5 23.9 %collective-permute-start.62 = (bf16[1568,256]{1,0:T(8,128)(2,1)S(1)}, bf16[1568,256]{1,0:T(8,128)(2,1)S(1)}, u32[]{:S(2)}, u32[]{:S(2)}) collective-permute-start(bf16[1568,256]{1,0:T(8,128)(2,1)S(1)} %pass.8.refs_11_), channel_id=1, source_target_pairs={{0,6},{1,7},{2,0},{3,1},{4,2},{5,3},{6,4},{7,5},{8,14},{9,15},{10,... | collective-permute-start | bytes 2408456 | tf_op jit(solution)/shard_map/ppermute | solution.py:657
  404.0 6.3 %collective-permute-start.64 = (bf16[304,256]{1,0:T(8,128)(2,1)S(1)}, bf16[304,256]{1,0:T(8,128)(2,1)S(1)}, u32[]{:S(2)}, u32[]{:S(2)}) collective-permute-start(bf16[304,256]{1,0:T(8,128)(2,1)S(1)} %total.3.refs_1_), channel_id=1, source_target_pairs={{0,8},{8,0},{16,24},{24,16},{1,9},{9,1},{17,25},{25,17},{2,10},{10... | collective-permute-start | bytes 466952 | tf_op jit(solution)/shard_map/ppermute | solution.py:663
  405.4 8.6 %collective-permute-start.65 = (bf16[304,256]{1,0:T(8,128)(2,1)S(1)}, bf16[304,256]{1,0:T(8,128)(2,1)S(1)}, u32[]{:S(2)}, u32[]{:S(2)}) collective-permute-start(bf16[304,256]{1,0:T(8,128)(2,1)S(1)} %total.3.refs_1_), channel_id=1, source_target_pairs={{0,16},{8,24},{16,0},{24,8},{1,17},{9,25},{17,1},{25,9},{2,18},{10... | collective-permute-start | bytes 466952 | tf_op jit(solution)/shard_map/ppermute | solution.py:663
  407.0 7.0 %collective-permute-start.66 = (bf16[304,256]{1,0:T(8,128)(2,1)S(1)}, bf16[304,256]{1,0:T(8,128)(2,1)S(1)}, u32[]{:S(2)}, u32[]{:S(2)}) collective-permute-start(bf16[304,256]{1,0:T(8,128)(2,1)S(1)} %total.3.refs_1_), channel_id=1, source_target_pairs={{0,24},{8,16},{16,8},{24,0},{1,25},{9,17},{17,9},{25,1},{2,26},{10... | collective-permute-start | bytes 466952 | tf_op jit(solution)/shard_map/ppermute | solution.py:663
  421.6 4.8 %collective-permute-start.69 = (f32[8,128]{1,0:T(8,128)S(1)}, f32[8,128]{1,0:T(8,128)S(1)}, u32[]{:S(2)}, u32[]{:S(2)}) collective-permute-start(f32[8,128]{1,0:T(8,128)S(1)} %add.216.refs_0_), channel_id=1, source_target_pairs={{0,4},{1,5},{2,6},{3,7},{4,0},{5,1},{6,2},{7,3},{8,12},{9,13},{10,... | collective-permute-start | bytes 12296 | tf_op jit(solution)/shard_map/ppermute | solution.py:683
  427.9 20.5 %collective-permute-start.63 = (bf16[1568,256]{1,0:T(8,128)(2,1)S(1)}, bf16[1568,256]{1,0:T(8,128)(2,1)S(1)}, u32[]{:S(2)}, u32[]{:S(2)}) collective-permute-start(bf16[1568,256]{1,0:T(8,128)(2,1)S(1)} %pass.9), channel_id=1, source_target_pairs={{0,2},{1,3},{2,4},{3,5},{4,6},{5,7},{6,0},{7,1},{8,10},{9,11},{10,... | collective-permute-start | bytes 2408456 | tf_op jit(solution)/shard_map/ppermute | solution.py:657
  (63 other events, 510.3 us)

commit v5 on v4

--- a/solution.py
+++ b/solution.py
@@ -809,11 +809,17 @@
     rec1 = over_core(oth1)
     turns = [[d for d in range(1, nz) if turn(d) == t] for t in range(3)]
     split = SPOTS // 2
-    cot_turns = [
+    out_turns = [
         [(d, 0, SPOTS) for d in turns[0]],
         [(d, 0, SPOTS) for d in turns[1]],
         [(d, 0, split) for d in turns[2]],
         [(d, split, SPOTS) for d in turns[2]],
+    ]
+    cot_turns = [
+        [(d, 0, SPOTS) for d in turns[0]],
+        [(d, 0, SPOTS) for d in turns[1]] + [(d, 0, 10) for d in turns[2]],
+        [(d, 10, 30) for d in turns[2]],
+        [(d, 30, SPOTS) for d in turns[2]],
     ]
     cots = {0: [cut(0, 0, SPOTS, diag)]}
 
@@ -893,7 +899,7 @@
 
     def send_outs(t, *deps):
         pieces, moved = [], []
-        for d, low, high in cot_turns[t]:
+        for d, low, high in out_turns[t]:
             piece = values[d]
             if deps:
                 piece = call(

time: 452 us -> 444 us (0.982)
  waiting for transfers between devices: 196 us -> 188 us
    ppermute x23 -> x24, waiting for transfers between devices: 92.7 us -> 79.7 us  [over_z(): return lax.ppermute(value, 'group', pairs)]
    ppermute x14, waiting for transfers between devices: 47.5 us -> 53.9 us  [over_all_z(): other = lax.ppermute(value, 'group', [(a, a ^ k) for a in range(ng)])]
    ppermute x23 -> x24, starting transfers between devices: 63.7 us -> 67.1 us  [over_z(): return lax.ppermute(value, 'group', pairs)]
    unnamed x83 -> x61, local copies, waits for them, and re-layouts: 9.08 us -> 7.87 us
    pallas_call x67 -> x68, Pallas kernels: 107 us -> 108 us  [call(): pl.pallas_call(inner, in_specs=(specs or [SMEM] + [VMEM] * (used - 1)) +...]
  transfers between devices with their start and end apart: 70 -> 71, of which waited for: 41 -> 41; matrix products, arithmetic and copies ran while one was open for 3% -> 2% of each run, Pallas kernels for 19% -> 20%
where the time goes in v5:
time: 444 us
  waiting for transfers between devices  188 us (42%)
  starting transfers between devices  125 us (28%)
  Pallas kernels  108 us (24%)
  local copies, waits for them, and re-layouts  10.4 us (2%)
  other arithmetic  8.46 us (2%)
    pallas_call x68, Pallas kernels, call(): pl.pallas_call(inner, in_specs=(specs or [SMEM] + [VMEM] * (used - 1)) +...  108 us
    ppermute x24, waiting for transfers between devices, over_z(): return lax.ppermute(value, 'group', pairs)  79.7 us
    ppermute x24, starting transfers between devices, over_z(): return lax.ppermute(value, 'group', pairs)  67.1 us
    ppermute x14, waiting for transfers between devices, over_all_z(): other = lax.ppermute(value, 'group', [(a, a ^ k) for a in range(ng)])  53.9 us
    ppermute x28, waiting for transfers between devices, over_dp(): return lax.ppermute(value, 'dp', [(a, a ^ k) for a in range(nd)])  53.4 us
    ppermute x28, starting transfers between devices, over_dp(): return lax.ppermute(value, 'dp', [(a, a ^ k) for a in range(nd)])  39 us
    ppermute x14, starting transfers between devices, over_all_z(): other = lax.ppermute(value, 'group', [(a, a ^ k) for a in range(ng)])  18.9 us
  transfers between devices with their start and end apart: 71, of which 41 were waited for; matrix products, arithmetic and copies ran while one was open for 2% of the time, Pallas kernels for 20%

profile of v5, /device:TPU:0, one launch (start us, length us, event | category | flops | bytes accessed | tf_op | source)
XLA Modules:
  0.0 444.3 jit_solution(10954393085871688764)
XLA Ops:
  1.6 2.5 copy-done.1
  5.1 3.1 collective-permute-start
  13.5 2.8 collective-permute-start.5
  22.4 13.0 %collective-permute-done.3.refs_1_ = bf16[576,256]{1,0:T(8,128)(2,1)S(1)} collective-permute-done((bf16[576,256]{1,0:T(8,128)(2,1)S(1)}, bf16[576,256]{1,0:T(8,128)(2,1)S(1)}, u32[]{:S(2)}, u32[]{:S(2)}) %collective-permute-start.3) | collective-permute-done | bytes 294944 | tf_op jit(solution)/shard_map/ppermute | solution.py:657
  35.4 11.8 %collective-permute-done.4.refs_2_ = bf16[576,256]{1,0:T(8,128)(2,1)S(1)} collective-permute-done((bf16[576,256]{1,0:T(8,128)(2,1)S(1)}, bf16[576,256]{1,0:T(8,128)(2,1)S(1)}, u32[]{:S(2)}, u32[]{:S(2)}) %collective-permute-start.4) | collective-permute-done | bytes 294944 | tf_op jit(solution)/shard_map/ppermute | solution.py:657
  50.4 13.9 %collective-permute-done.2.refs_2_.refs_4_.refs_6_ = bf16[1568,256]{1,0:T(8,128)(2,1)S(1)} collective-permute-done((bf16[1568,256]{1,0:T(8,128)(2,1)S(1)}, bf16[1568,256]{1,0:T(8,128)(2,1)S(1)}, u32[]{:S(2)}, u32[]{:S(2)}) %collective-permute-start.2) | collective-permute-done | bytes 802848 | tf_op jit(solution)/shard_map/ppermute | solution.py:657
  67.6 16.1 %collective-permute-start.1 = (bf16[1568,256]{1,0:T(8,128)(2,1)S(1)}, bf16[1568,256]{1,0:T(8,128)(2,1)S(1)}, u32[]{:S(2)}, u32[]{:S(2)}) collective-permute-start(bf16[1568,256]{1,0:T(8,128)(2,1)S(1)} %bitcast.75), channel_id=1, source_target_pairs={{0,4},{1,5},{2,6},{3,7},{4,0},{5,1},{6,2},{7,3},{8,12},{9,13},{10,... | collective-permute-start | bytes 2408456 | tf_op jit(solution)/shard_map/ppermute | solution.py:657
  83.7 7.2 %collective-permute-done.9.refs_6_ = bf16[2,4,256,256]{3,2,1,0:T(8,128)(2,1)S(1)} collective-permute-done((bf16[2,4,256,256]{3,2,1,0:T(8,128)(2,1)S(1)}, bf16[2,4,256,256]{3,2,1,0:T(8,128)(2,1)S(1)}, u32[]{:S(2)}, u32[]{:S(2)}) %collective-permute-start.9) | collective-permute-done | bytes 1048608 | tf_op jit(solution)/shard_map/ppermute | solution.py:663
  90.9 4.2 collective-permute-done.7.refs_3_
  96.3 14.7 %collective-permute-done.1.refs_3_.refs_5_ = bf16[1568,256]{1,0:T(8,128)(2,1)S(1)} collective-permute-done((bf16[1568,256]{1,0:T(8,128)(2,1)S(1)}, bf16[1568,256]{1,0:T(8,128)(2,1)S(1)}, u32[]{:S(2)}, u32[]{:S(2)}) %collective-permute-start.1) | collective-permute-done | bytes 802848 | tf_op jit(solution)/shard_map/ppermute | solution.py:657
  111.0 4.1 reduce.1
  115.8 4.3 collective-permute-start.15
  128.6 2.7 collective-permute-start.13
  131.3 6.7 %collective-permute-done.13 = f32[2,2,256]{2,1,0:T(2,128)S(1)} collective-permute-done((f32[2,2,256]{2,1,0:T(2,128)S(1)}, f32[2,2,256]{2,1,0:T(2,128)S(1)}, u32[]{:S(2)}, u32[]{:S(2)}) %collective-permute-start.13) | collective-permute-done | bytes 4128 | tf_op jit(solution)/shard_map/ppermute | solution.py:683
  138.0 4.1 collective-permute-start.14
  144.4 4.4 collective-permute-start.20
  149.5 8.7 %conv.1 = (bf16[2,1568,256]{2,1,0:T(8,128)(2,1)S(1)}, f32[2,1568,256]{2,1,0:T(8,128)S(1)}, f32[2,2,256]{2,1,0:T(2,128)S(1)}) custom-call(s32[3]{0:T(128)S(1)} %pad_add_fusion.refs_0_, f32[2,1568,256]{2,1,0:T(8,128)S(1)} %get-tuple-element.83.refs_1_.refs_7_.refs_2_, bf16[2,1568,256]{2,1,0:T(8,128)(2,1)S(1)} %collective-permute-done.10.refs_2_.refs_8_.refs_3_, ...), custom_call_target="tpu_custom_call" | custom-call | flops 1024 | bytes 1024 | tf_op jit(solution)/shard_map/conv/pallas_call | solution.py:72
  166.4 2.8 collective-permute-done.18
  169.2 2.9 collective-permute-start.19
  177.0 3.0 collective-permute-start.27
  180.5 8.6 %expand.1 = (f32[4,1568,256]{2,1,0:T(8,128)S(1)}, f32[4,2,256]{2,1,0:T(2,128)S(1)}) custom-call(s32[3]{0:T(128)S(1)} %pad_add_fusion.refs_0_, bf16[2,1568,256]{2,1,0:T(8,128)(2,1)S(1)} %second_act.1.refs_1_, bf16[2,1568,256]{2,1,0:T(8,128)(2,1)S(1)} %collective-permute-done.22.refs_2_, bf16[4,4,256,256]{3,2,1,0:T(8,128)(2,1)S(1)} %get-tuple-element.82.refs_9_.refs_3_.refs_6_), custom_call_target="tpu_custom_call" | custom-call | flops 1024 | bytes 1024 | tf_op jit(solution)/shard_map/expand/pallas_call | solution.py:72
  198.1 4.5 %collective-permute-done.25 = f32[4,2,256]{2,1,0:T(2,128)S(1)} collective-permute-done((f32[4,2,256]{2,1,0:T(2,128)S(1)}, f32[4,2,256]{2,1,0:T(2,128)S(1)}, u32[]{:S(2)}, u32[]{:S(2)}) %collective-permute-start.25) | collective-permute-done | bytes 8224 | tf_op jit(solution)/shard_map/ppermute | solution.py:683
  203.0 6.0 %collective-permute-done.26.refs_1_ = f32[4,2,256]{2,1,0:T(2,128)S(1)} collective-permute-done((f32[4,2,256]{2,1,0:T(2,128)S(1)}, f32[4,2,256]{2,1,0:T(2,128)S(1)}, u32[]{:S(2)}, u32[]{:S(2)}) %collective-permute-start.26) | collective-permute-done | bytes 8224 | tf_op jit(solution)/shard_map/ppermute | solution.py:683
  213.9 5.3 %up.3 = (bf16[1568,256]{1,0:T(8,128)(2,1)S(1)}, bf16[1568,256]{1,0:T(8,128)(2,1)S(1)}, bf16[1568,256]{1,0:T(8,128)(2,1)S(1)}, f32[4,1568,256]{2,1,0:T(8,128)S(1)}, f32[4,2,256]{2,1,0:T(2,128)S(1)}) custom-call(s32[3]{0:T(128)S(1)} %pad_add_fusion.refs_0_, ...), custom_call_target="tpu_custom_call", output_to_operand_aliasing={{3}: (12, {}), {4}: (13, {})} | custom-call | flops 1024 | bytes 1024 | tf_op jit(solution)/shard_map/up/pallas_call | solution.py:72
  226.6 4.4 collective-permute-done.31
  231.7 3.8 collective-permute-done.32.refs_1_
  235.6 5.9 %expand_back.1 = (bf16[4,1568,256]{2,1,0:T(8,128)(2,1)S(1)}, f32[2,1568,256]{2,1,0:T(8,128)S(1)}, bf16[2,1568,256]{2,1,0:T(8,128)(2,1)S(1)}) custom-call(s32[3]{0:T(128)S(1)} %pad_add_fusion.refs_0_, f32[4,1568,256]{2,1,0:T(8,128)S(1)} %get-tuple-element.87.refs_1_, f32[4,1568,256]{2,1,0:T(8,128)S(1)} %get-tuple-element.92.refs_2_.refs_3_, ...), custom_call_target="tpu_custom_call" | custom-call | flops 1024 | bytes 1024 | tf_op jit(solution)/shard_map/expand_back/pallas_call | solution.py:72
  241.6 14.6 %collective-permute-start.39 = (bf16[1568,256]{1,0:T(8,128)(2,1)S(1)}, bf16[1568,256]{1,0:T(8,128)(2,1)S(1)}, u32[]{:S(2)}, u32[]{:S(2)}) collective-permute-start(bf16[1568,256]{1,0:T(8,128)(2,1)S(1)} %pass.5.refs_7_), channel_id=1, source_target_pairs={{0,2},{1,3},{2,4},{3,5},{4,6},{5,7},{6,0},{7,1},{8,10},{9,11},{10,... | collective-permute-start | bytes 2408456 | tf_op jit(solution)/shard_map/ppermute | solution.py:657
  256.1 4.6 %expand_wgrad.1.refs_6_.refs_1_ = bf16[4,4,256,256]{3,2,1,0:T(8,128)(2,1)S(1)} custom-call(s32[3]{0:T(128)S(1)} %pad_add_fusion.refs_0_, bf16[2,1568,256]{2,1,0:T(8,128)(2,1)S(1)} %second_act.1.refs_1_, bf16[2,1568,256]{2,1,0:T(8,128)(2,1)S(1)} %copy-done.4, bf16[4,1568,256]{2,1,0:T(8,128)(2,1)S(1)} %get-tuple-element.98.refs_3_), custom_call_target="tpu_custom_call" | custom-call | flops 1024 | bytes 1024 | tf_op jit(solution)/shard_map/expand_wgrad/pallas_call | solution.py:72
  260.7 3.3 second_up.1
  272.5 2.5 collective-permute-start.44
  276.7 3.6 collective-permute-done.37
  282.7 5.2 %collective-permute-done.38.refs_1_ = f32[2,2,256]{2,1,0:T(2,128)S(1)} collective-permute-done((f32[2,2,256]{2,1,0:T(2,128)S(1)}, f32[2,2,256]{2,1,0:T(2,128)S(1)}, u32[]{:S(2)}, u32[]{:S(2)}) %collective-permute-start.38) | collective-permute-done | bytes 4128 | tf_op jit(solution)/shard_map/ppermute | solution.py:683
  288.6 10.1 %conv_back.1 = (bf16[2,1568,256]{2,1,0:T(8,128)(2,1)S(1)}, f32[2,1568,256]{2,1,0:T(8,128)S(1)}, f32[2,2,256]{2,1,0:T(2,128)S(1)}) custom-call(s32[3]{0:T(128)S(1)} %pad_add_fusion.refs_0_, f32[2,1568,256]{2,1,0:T(8,128)S(1)} %get-tuple-element.99.refs_1_, f32[2,1568,256]{2,1,0:T(8,128)S(1)} %get-tuple-element.85.refs_1_.refs_3_.refs_2_, ...), custom_call_target="tpu_custom_call" | custom-call | flops 1024 | bytes 1024 | tf_op jit(solution)/shard_map/conv_back/pallas_call | solution.py:72
  299.9 2.8 collective-permute-start.49
  311.8 3.6 collective-permute-done.45
  316.0 4.0 collective-permute-done.46.refs_1_
  327.3 4.6 %reduce_wgrad.1.refs_3_.refs_1_ = bf16[4,4,256,256]{3,2,1,0:T(8,128)(2,1)S(1)} custom-call(s32[3]{0:T(128)S(1)} %pad_add_fusion.refs_0_, bf16[2,1568,256]{2,1,0:T(8,128)(2,1)S(1)} %first_grad.1.refs_1_, bf16[2,1568,256]{2,1,0:T(8,128)(2,1)S(1)} %collective-permute-done.52.refs_2_, bf16[1568,256]{1,0:T(8,128)(2,1)S(1)} %bitcast.62, ...), custom_call_target="tpu_custom_call" | custom-call | flops 1024 | bytes 1024 | tf_op jit(solution)/shard_map/reduce_wgrad/pallas_call | solution.py:72
  331.9 5.1 %conv_wgrad.1.refs_2_ = bf16[4,4,48,256]{3,2,1,0:T(8,128)(2,1)S(1)} custom-call(s32[3]{0:T(128)S(1)} %pad_add_fusion.refs_0_, bf16[2,1568,256]{2,1,0:T(8,128)(2,1)S(1)} %copy-done.6, bf16[2,1568,256]{2,1,0:T(8,128)(2,1)S(1)} %get-tuple-element.114.refs_2_, bf16[4,4,256,256]{3,2,1,0:T(8,128)(2,1)S(1)} %reduce_wgrad.1.refs_3_.refs_1_), custom_call_target="tpu_custom_call" | custom-call | flops 1024 | bytes 1024 | tf_op jit(solution)/shard_map/conv_wgrad/pallas_call | solution.py:72
  337.7 2.5 collective-permute-start.58
  342.6 2.6 collective-permute-start.51
  358.2 9.4 %collective-permute-done.57.refs_3_ = bf16[4,304,256]{2,1,0:T(8,128)(2,1)S(1)} collective-permute-done((bf16[4,304,256]{2,1,0:T(8,128)(2,1)S(1)}, bf16[4,304,256]{2,1,0:T(8,128)(2,1)S(1)}, u32[]{:S(2)}, u32[]{:S(2)}) %collective-permute-start.57) | collective-permute-done | bytes 622624 | tf_op jit(solution)/shard_map/ppermute | solution.py:663
  376.9 11.7 %collective-permute-done.51.refs_5_ = bf16[800,256]{1,0:T(8,128)(2,1)S(1)} collective-permute-done((bf16[800,256]{1,0:T(8,128)(2,1)S(1)}, bf16[800,256]{1,0:T(8,128)(2,1)S(1)}, u32[]{:S(2)}, u32[]{:S(2)}) %collective-permute-start.51) | collective-permute-done | bytes 409632 | tf_op jit(solution)/shard_map/ppermute | solution.py:657
  388.6 6.6 %collective-permute-done.60.refs_2_ = bf16[304,256]{1,0:T(8,128)(2,1)S(1)} collective-permute-done((bf16[304,256]{1,0:T(8,128)(2,1)S(1)}, bf16[304,256]{1,0:T(8,128)(2,1)S(1)}, u32[]{:S(2)}, u32[]{:S(2)}) %collective-permute-start.60) | collective-permute-done | bytes 155680 | tf_op jit(solution)/shard_map/ppermute | solution.py:657
  399.1 3.3 collective-permute-done.65.refs_2_
  402.4 3.7 collective-permute-done.66.refs_3_
  410.9 4.4 collective-permute-done.69
  433.0 7.9 %collective-permute-done.64 = bf16[1568,256]{1,0:T(8,128)(2,1)S(1)} collective-permute-done((bf16[1568,256]{1,0:T(8,128)(2,1)S(1)}, bf16[1568,256]{1,0:T(8,128)(2,1)S(1)}, u32[]{:S(2)}, u32[]{:S(2)}) %collective-permute-start.64) | collective-permute-done | bytes 802848 | tf_op jit(solution)/shard_map/ppermute | solution.py:657
  (261 shorter events, 152.8 us)
Async XLA Ops:
  5.1 42.1 %collective-permute-start = (bf16[1568,256]{1,0:T(8,128)(2,1)S(1)}, bf16[1568,256]{1,0:T(8,128)(2,1)S(1)}, u32[]{:S(2)}, u32[]{:S(2)}) collective-permute-start(bf16[1568,256]{1,0:T(8,128)(2,1)S(1)} %bitcast.64), channel_id=1, source_target_pairs={{0,2},{1,3},{2,4},{3,5},{4,6},{5,7},{6,0},{7,1},{8,10},{9,11},{10,... | collective-permute-start | bytes 2408456 | tf_op jit(solution)/shard_map/ppermute | solution.py:657
  10.8 24.6 %collective-permute-start.3 = (bf16[576,256]{1,0:T(8,128)(2,1)S(1)}, bf16[576,256]{1,0:T(8,128)(2,1)S(1)}, u32[]{:S(2)}, u32[]{:S(2)}) collective-permute-start(bf16[576,256]{1,0:T(8,128)(2,1)S(1)} %bundle.1.refs_0_), channel_id=1, source_target_pairs={{0,2},{1,3},{2,4},{3,5},{4,6},{5,7},{6,0},{7,1},{8,10},{9,11},{10,... | collective-permute-start | bytes 884744 | tf_op jit(solution)/shard_map/ppermute | solution.py:657
  12.4 34.8 %collective-permute-start.4 = (bf16[576,256]{1,0:T(8,128)(2,1)S(1)}, bf16[576,256]{1,0:T(8,128)(2,1)S(1)}, u32[]{:S(2)}, u32[]{:S(2)}) collective-permute-start(bf16[576,256]{1,0:T(8,128)(2,1)S(1)} %bundle.1.refs_0_), channel_id=1, source_target_pairs={{0,4},{1,5},{2,6},{3,7},{4,0},{5,1},{6,2},{7,3},{8,12},{9,13},{10,... | collective-permute-start | bytes 884744 | tf_op jit(solution)/shard_map/ppermute | solution.py:657
  13.5 33.7 %collective-permute-start.5 = (bf16[576,256]{1,0:T(8,128)(2,1)S(1)}, bf16[576,256]{1,0:T(8,128)(2,1)S(1)}, u32[]{:S(2)}, u32[]{:S(2)}) collective-permute-start(bf16[576,256]{1,0:T(8,128)(2,1)S(1)} %bundle.1.refs_0_), channel_id=1, source_target_pairs={{0,6},{1,7},{2,0},{3,1},{4,2},{5,3},{6,4},{7,5},{8,14},{9,15},{10,... | collective-permute-start | bytes 884744 | tf_op jit(solution)/shard_map/ppermute | solution.py:657
  19.9 44.4 %collective-permute-start.2 = (bf16[1568,256]{1,0:T(8,128)(2,1)S(1)}, bf16[1568,256]{1,0:T(8,128)(2,1)S(1)}, u32[]{:S(2)}, u32[]{:S(2)}) collective-permute-start(bf16[1568,256]{1,0:T(8,128)(2,1)S(1)} %bitcast.76), channel_id=1, source_target_pairs={{0,6},{1,7},{2,0},{3,1},{4,2},{5,3},{6,4},{7,5},{8,14},{9,15},{10,... | collective-permute-start | bytes 2408456 | tf_op jit(solution)/shard_map/ppermute | solution.py:657
  47.3 16.9 %collective-permute-start.6 = (bf16[1,4,320,256]{3,2,1,0:T(8,128)(2,1)S(1)}, bf16[1,4,320,256]{3,2,1,0:T(8,128)(2,1)S(1)}, u32[]{:S(2)}, u32[]{:S(2)}) collective-permute-start(bf16[1,4,320,256]{3,2,1,0:T(8,128)(2,1)S(1)} %get-tuple-element.76.refs_0_.refs_1_), channel_id=1, source_target_pairs={{0,8},{8,0},{16,24},{24,16},{1,9},{9,1},{17,25},{25,17},{2,10},{10... | collective-permute-start | bytes 1966088 | tf_op jit(solution)/shard_map/ppermute | solution.py:663
  48.9 17.1 %collective-permute-start.8 = (bf16[1,4,256,256]{3,2,1,0:T(8,128)(2,1)S(1)}, bf16[1,4,256,256]{3,2,1,0:T(8,128)(2,1)S(1)}, u32[]{:S(2)}, u32[]{:S(2)}) collective-permute-start(bf16[1,4,256,256]{3,2,1,0:T(8,128)(2,1)S(1)} %get-tuple-element.77.refs_0_.refs_4_), channel_id=1, source_target_pairs={{0,16},{8,24},{16,0},{24,8},{1,17},{9,25},{17,1},{25,9},{2,18},{10... | collective-permute-start | bytes 1572872 | tf_op jit(solution)/shard_map/ppermute | solution.py:663
  64.4 30.8 %collective-permute-start.7 = (bf16[2,4,320,256]{3,2,1,0:T(8,128)(2,1)S(1)}, bf16[2,4,320,256]{3,2,1,0:T(8,128)(2,1)S(1)}, u32[]{:S(2)}, u32[]{:S(2)}) collective-permute-start(bf16[2,4,320,256]{3,2,1,0:T(8,128)(2,1)S(1)} %pair.2), channel_id=1, source_target_pairs={{0,16},{8,24},{16,0},{24,8},{1,17},{9,25},{17,1},{25,9},{2,18},{10... | collective-permute-start | bytes 3932168 | tf_op jit(solution)/shard_map/ppermute | solution.py:663
  66.0 24.9 %collective-permute-start.9 = (bf16[2,4,256,256]{3,2,1,0:T(8,128)(2,1)S(1)}, bf16[2,4,256,256]{3,2,1,0:T(8,128)(2,1)S(1)}, u32[]{:S(2)}, u32[]{:S(2)}) collective-permute-start(bf16[2,4,256,256]{3,2,1,0:T(8,128)(2,1)S(1)} %pair.3), channel_id=1, source_target_pairs={{0,8},{8,0},{16,24},{24,16},{1,9},{9,1},{17,25},{25,17},{2,10},{10... | collective-permute-start | bytes 3145736 | tf_op jit(solution)/shard_map/ppermute | solution.py:663
  67.6 43.4 %collective-permute-start.1 = (bf16[1568,256]{1,0:T(8,128)(2,1)S(1)}, bf16[1568,256]{1,0:T(8,128)(2,1)S(1)}, u32[]{:S(2)}, u32[]{:S(2)}) collective-permute-start(bf16[1568,256]{1,0:T(8,128)(2,1)S(1)} %bitcast.75), channel_id=1, source_target_pairs={{0,4},{1,5},{2,6},{3,7},{4,0},{5,1},{6,2},{7,3},{8,12},{9,13},{10,... | collective-permute-start | bytes 2408456 | tf_op jit(solution)/shard_map/ppermute | solution.py:657
  115.1 5.0 %collective-permute-start.10 = (bf16[2,1568,256]{2,1,0:T(8,128)(2,1)S(1)}, bf16[2,1568,256]{2,1,0:T(8,128)(2,1)S(1)}, u32[]{:S(2)}, u32[]{:S(2)}) collective-permute-start(bf16[2,1568,256]{2,1,0:T(8,128)(2,1)S(1)} %get-tuple-element.84.refs_2_), channel_id=1, source_target_pairs={{0,1},{1,0},{2,3},{3,2},{4,5},{5,4},{6,7},{7,6},{8,9},{9,8},{10,11... | collective-permute-start | bytes 4816904 | tf_op jit(solution)/shard_map/ppermute | solution.py:660
  115.8 26.3 %collective-permute-start.15 = (bf16[1568,256]{1,0:T(8,128)(2,1)S(1)}, bf16[1568,256]{1,0:T(8,128)(2,1)S(1)}, u32[]{:S(2)}, u32[]{:S(2)}) collective-permute-start(bf16[1568,256]{1,0:T(8,128)(2,1)S(1)} %bitcast.72), channel_id=1, source_target_pairs={{0,2},{1,3},{2,4},{3,5},{4,6},{5,7},{6,0},{7,1},{8,10},{9,11},{10,... | collective-permute-start | bytes 2408456 | tf_op jit(solution)/shard_map/ppermute | solution.py:657
  128.6 9.5 %collective-permute-start.13 = (f32[2,2,256]{2,1,0:T(2,128)S(1)}, f32[2,2,256]{2,1,0:T(2,128)S(1)}, u32[]{:S(2)}, u32[]{:S(2)}) collective-permute-start(f32[2,2,256]{2,1,0:T(2,128)S(1)} %add.197), channel_id=1, source_target_pairs={{0,2},{1,3},{2,0},{3,1},{4,6},{5,7},{6,4},{7,5},{8,10},{9,11},{10,... | collective-permute-start | bytes 12296 | tf_op jit(solution)/shard_map/ppermute | solution.py:683
  138.0 5.7 %collective-permute-start.14 = (f32[2,2,256]{2,1,0:T(2,128)S(1)}, f32[2,2,256]{2,1,0:T(2,128)S(1)}, u32[]{:S(2)}, u32[]{:S(2)}) collective-permute-start(f32[2,2,256]{2,1,0:T(2,128)S(1)} %add.198.refs_0_), channel_id=1, source_target_pairs={{0,4},{1,5},{2,6},{3,7},{4,0},{5,1},{6,2},{7,3},{8,12},{9,13},{10,... | collective-permute-start | bytes 12296 | tf_op jit(solution)/shard_map/ppermute | solution.py:683
  144.4 29.3 %collective-permute-start.20 = (bf16[1568,256]{1,0:T(8,128)(2,1)S(1)}, bf16[1568,256]{1,0:T(8,128)(2,1)S(1)}, u32[]{:S(2)}, u32[]{:S(2)}) collective-permute-start(bf16[1568,256]{1,0:T(8,128)(2,1)S(1)} %bitcast.68), channel_id=1, source_target_pairs={{0,6},{1,7},{2,0},{3,1},{4,2},{5,3},{6,4},{7,5},{8,14},{9,15},{10,... | collective-permute-start | bytes 2408456 | tf_op jit(solution)/shard_map/ppermute | solution.py:657
  149.4 24.3 %collective-permute-start.21 = (bf16[320,256]{1,0:T(8,128)(2,1)S(1)}, bf16[320,256]{1,0:T(8,128)(2,1)S(1)}, u32[]{:S(2)}, u32[]{:S(2)}) collective-permute-start(bf16[320,256]{1,0:T(8,128)(2,1)S(1)} %bitcast.88), channel_id=1, source_target_pairs={{0,4},{1,5},{2,6},{3,7},{4,0},{5,1},{6,2},{7,3},{8,12},{9,13},{10,... | collective-permute-start | bytes 491528 | tf_op jit(solution)/shard_map/ppermute | solution.py:657
  177.0 26.0 %collective-permute-start.27 = (bf16[640,256]{1,0:T(8,128)(2,1)S(1)}, bf16[640,256]{1,0:T(8,128)(2,1)S(1)}, u32[]{:S(2)}, u32[]{:S(2)}) collective-permute-start(bf16[640,256]{1,0:T(8,128)(2,1)S(1)} %bitcast.82), channel_id=1, source_target_pairs={{0,4},{1,5},{2,6},{3,7},{4,0},{5,1},{6,2},{7,3},{8,12},{9,13},{10,... | collective-permute-start | bytes 983048 | tf_op jit(solution)/shard_map/ppermute | solution.py:657
  180.0 29.1 %collective-permute-start.28 = (bf16[608,256]{1,0:T(8,128)(2,1)S(1)}, bf16[608,256]{1,0:T(8,128)(2,1)S(1)}, u32[]{:S(2)}, u32[]{:S(2)}) collective-permute-start(bf16[608,256]{1,0:T(8,128)(2,1)S(1)} %bitcast.84), channel_id=1, source_target_pairs={{0,4},{1,5},{2,6},{3,7},{4,0},{5,1},{6,2},{7,3},{8,12},{9,13},{10,... | collective-permute-start | bytes 933896 | tf_op jit(solution)/shard_map/ppermute | solution.py:657
  196.4 6.2 %collective-permute-start.25 = (f32[4,2,256]{2,1,0:T(2,128)S(1)}, f32[4,2,256]{2,1,0:T(2,128)S(1)}, u32[]{:S(2)}, u32[]{:S(2)}) collective-permute-start(f32[4,2,256]{2,1,0:T(2,128)S(1)} %add.203), channel_id=1, source_target_pairs={{0,2},{1,3},{2,0},{3,1},{4,6},{5,7},{6,4},{7,5},{8,10},{9,11},{10,... | collective-permute-start | bytes 24584 | tf_op jit(solution)/shard_map/ppermute | solution.py:683
  202.6 6.4 %collective-permute-start.26 = (f32[4,2,256]{2,1,0:T(2,128)S(1)}, f32[4,2,256]{2,1,0:T(2,128)S(1)}, u32[]{:S(2)}, u32[]{:S(2)}) collective-permute-start(f32[4,2,256]{2,1,0:T(2,128)S(1)} %add.204.refs_0_), channel_id=1, source_target_pairs={{0,4},{1,5},{2,6},{3,7},{4,0},{5,1},{6,2},{7,3},{8,12},{9,13},{10,... | collective-permute-start | bytes 24584 | tf_op jit(solution)/shard_map/ppermute | solution.py:683
  211.1 24.4 %collective-permute-start.33 = (bf16[1568,256]{1,0:T(8,128)(2,1)S(1)}, bf16[1568,256]{1,0:T(8,128)(2,1)S(1)}, u32[]{:S(2)}, u32[]{:S(2)}) collective-permute-start(bf16[1568,256]{1,0:T(8,128)(2,1)S(1)} %get-tuple-element.94), channel_id=1, source_target_pairs={{0,6},{1,7},{2,0},{3,1},{4,2},{5,3},{6,4},{7,5},{8,14},{9,15},{10,... | collective-permute-start | bytes 2408456 | tf_op jit(solution)/shard_map/ppermute | solution.py:657
  241.5 19.2 %collective-permute-start.34 = (bf16[2,1568,256]{2,1,0:T(8,128)(2,1)S(1)}, bf16[2,1568,256]{2,1,0:T(8,128)(2,1)S(1)}, u32[]{:S(2)}, u32[]{:S(2)}) collective-permute-start(bf16[2,1568,256]{2,1,0:T(8,128)(2,1)S(1)} %get-tuple-element.97), channel_id=1, source_target_pairs={{0,1},{1,0},{2,3},{3,2},{4,5},{5,4},{6,7},{7,6},{8,9},{9,8},{10,11... | collective-permute-start | bytes 4816904 | tf_op jit(solution)/shard_map/ppermute | solution.py:660
  241.6 41.2 %collective-permute-start.39 = (bf16[1568,256]{1,0:T(8,128)(2,1)S(1)}, bf16[1568,256]{1,0:T(8,128)(2,1)S(1)}, u32[]{:S(2)}, u32[]{:S(2)}) collective-permute-start(bf16[1568,256]{1,0:T(8,128)(2,1)S(1)} %pass.5.refs_7_), channel_id=1, source_target_pairs={{0,2},{1,3},{2,4},{3,5},{4,6},{5,7},{6,0},{7,1},{8,10},{9,11},{10,... | collective-permute-start | bytes 2408456 | tf_op jit(solution)/shard_map/ppermute | solution.py:657
  272.5 26.3 %collective-permute-start.44 = (bf16[4,256,256]{2,1,0:T(8,128)(2,1)S(1)}, bf16[4,256,256]{2,1,0:T(8,128)(2,1)S(1)}, u32[]{:S(2)}, u32[]{:S(2)}) collective-permute-start(bf16[4,256,256]{2,1,0:T(8,128)(2,1)S(1)} %pick.11), channel_id=1, source_target_pairs={{0,24},{8,16},{16,8},{24,0},{1,25},{9,17},{17,9},{25,1},{2,26},{10... | collective-permute-start | bytes 1572872 | tf_op jit(solution)/shard_map/ppermute | solution.py:663
  275.0 23.8 %collective-permute-start.43 = (bf16[4,256,256]{2,1,0:T(8,128)(2,1)S(1)}, bf16[4,256,256]{2,1,0:T(8,128)(2,1)S(1)}, u32[]{:S(2)}, u32[]{:S(2)}) collective-permute-start(bf16[4,256,256]{2,1,0:T(8,128)(2,1)S(1)} %pick.10), channel_id=1, source_target_pairs={{0,16},{8,24},{16,0},{24,8},{1,17},{9,25},{17,1},{25,9},{2,18},{10... | collective-permute-start | bytes 1572872 | tf_op jit(solution)/shard_map/ppermute | solution.py:663
  276.1 22.7 %collective-permute-start.42 = (bf16[4,256,256]{2,1,0:T(8,128)(2,1)S(1)}, bf16[4,256,256]{2,1,0:T(8,128)(2,1)S(1)}, u32[]{:S(2)}, u32[]{:S(2)}) collective-permute-start(bf16[4,256,256]{2,1,0:T(8,128)(2,1)S(1)} %pick.9), channel_id=1, source_target_pairs={{0,8},{8,0},{16,24},{24,16},{1,9},{9,1},{17,25},{25,17},{2,10},{10... | collective-permute-start | bytes 1572872 | tf_op jit(solution)/shard_map/ppermute | solution.py:663
  280.3 7.6 %collective-permute-start.38 = (f32[2,2,256]{2,1,0:T(2,128)S(1)}, f32[2,2,256]{2,1,0:T(2,128)S(1)}, u32[]{:S(2)}, u32[]{:S(2)}) collective-permute-start(f32[2,2,256]{2,1,0:T(2,128)S(1)} %add.210.refs_0_), channel_id=1, source_target_pairs={{0,4},{1,5},{2,6},{3,7},{4,0},{5,1},{6,2},{7,3},{8,12},{9,13},{10,... | collective-permute-start | bytes 12296 | tf_op jit(solution)/shard_map/ppermute | solution.py:683
  287.9 28.0 %collective-permute-start.47 = (bf16[768,256]{1,0:T(8,128)(2,1)S(1)}, bf16[768,256]{1,0:T(8,128)(2,1)S(1)}, u32[]{:S(2)}, u32[]{:S(2)}) collective-permute-start(bf16[768,256]{1,0:T(8,128)(2,1)S(1)} %pass.6.refs_10_), channel_id=1, source_target_pairs={{0,4},{1,5},{2,6},{3,7},{4,0},{5,1},{6,2},{7,3},{8,12},{9,13},{10,... | collective-permute-start | bytes 1179656 | tf_op jit(solution)/shard_map/ppermute | solution.py:657
  299.6 16.3 %collective-permute-start.48 = (bf16[256,256]{1,0:T(8,128)(2,1)S(1)}, bf16[256,256]{1,0:T(8,128)(2,1)S(1)}, u32[]{:S(2)}, u32[]{:S(2)}) collective-permute-start(bf16[256,256]{1,0:T(8,128)(2,1)S(1)} %get-tuple-element.103), channel_id=1, source_target_pairs={{0,6},{1,7},{2,0},{3,1},{4,2},{5,3},{6,4},{7,5},{8,14},{9,15},{10,... | collective-permute-start | bytes 393224 | tf_op jit(solution)/shard_map/ppermute | solution.py:657
  299.9 16.0 %collective-permute-start.49 = (bf16[256,256]{1,0:T(8,128)(2,1)S(1)}, bf16[256,256]{1,0:T(8,128)(2,1)S(1)}, u32[]{:S(2)}, u32[]{:S(2)}) collective-permute-start(bf16[256,256]{1,0:T(8,128)(2,1)S(1)} %get-tuple-element.104), channel_id=1, source_target_pairs={{0,4},{1,5},{2,6},{3,7},{4,0},{5,1},{6,2},{7,3},{8,12},{9,13},{10,... | collective-permute-start | bytes 393224 | tf_op jit(solution)/shard_map/ppermute | solution.py:657
  302.7 13.2 %collective-permute-start.50 = (bf16[256,256]{1,0:T(8,128)(2,1)S(1)}, bf16[256,256]{1,0:T(8,128)(2,1)S(1)}, u32[]{:S(2)}, u32[]{:S(2)}) collective-permute-start(bf16[256,256]{1,0:T(8,128)(2,1)S(1)} %get-tuple-element.105), channel_id=1, source_target_pairs={{0,2},{1,3},{2,4},{3,5},{4,6},{5,7},{6,0},{7,1},{8,10},{9,11},{10,... | collective-permute-start | bytes 393224 | tf_op jit(solution)/shard_map/ppermute | solution.py:657
  321.6 15.4 %collective-permute-start.53 = (bf16[256,256]{1,0:T(8,128)(2,1)S(1)}, bf16[256,256]{1,0:T(8,128)(2,1)S(1)}, u32[]{:S(2)}, u32[]{:S(2)}) collective-permute-start(bf16[256,256]{1,0:T(8,128)(2,1)S(1)} %total.2.refs_3_.refs_5_), channel_id=1, source_target_pairs={{0,8},{8,0},{16,24},{24,16},{1,9},{9,1},{17,25},{25,17},{2,10},{10... | collective-permute-start | bytes 393224 | tf_op jit(solution)/shard_map/ppermute | solution.py:663
  323.2 13.9 %collective-permute-start.54 = (bf16[256,256]{1,0:T(8,128)(2,1)S(1)}, bf16[256,256]{1,0:T(8,128)(2,1)S(1)}, u32[]{:S(2)}, u32[]{:S(2)}) collective-permute-start(bf16[256,256]{1,0:T(8,128)(2,1)S(1)} %total.2.refs_3_.refs_5_), channel_id=1, source_target_pairs={{0,16},{8,24},{16,0},{24,8},{1,17},{9,25},{17,1},{25,9},{2,18},{10... | collective-permute-start | bytes 393224 | tf_op jit(solution)/shard_map/ppermute | solution.py:663
  324.7 12.4 %collective-permute-start.55 = (bf16[256,256]{1,0:T(8,128)(2,1)S(1)}, bf16[256,256]{1,0:T(8,128)(2,1)S(1)}, u32[]{:S(2)}, u32[]{:S(2)}) collective-permute-start(bf16[256,256]{1,0:T(8,128)(2,1)S(1)} %total.2.refs_3_.refs_5_), channel_id=1, source_target_pairs={{0,24},{8,16},{16,8},{24,0},{1,25},{9,17},{17,9},{25,1},{2,26},{10... | collective-permute-start | bytes 393224 | tf_op jit(solution)/shard_map/ppermute | solution.py:663
  326.9 48.6 %collective-permute-start.62 = (bf16[1568,256]{1,0:T(8,128)(2,1)S(1)}, bf16[1568,256]{1,0:T(8,128)(2,1)S(1)}, u32[]{:S(2)}, u32[]{:S(2)}) collective-permute-start(bf16[1568,256]{1,0:T(8,128)(2,1)S(1)} %input_grad.4.refs_7_), channel_id=1, source_target_pairs={{0,4},{1,5},{2,6},{3,7},{4,0},{5,1},{6,2},{7,3},{8,12},{9,13},{10,... | collective-permute-start | bytes 2408456 | tf_op jit(solution)/shard_map/ppermute | solution.py:657
  337.7 20.6 %collective-permute-start.58 = (bf16[4,304,256]{2,1,0:T(8,128)(2,1)S(1)}, bf16[4,304,256]{2,1,0:T(8,128)(2,1)S(1)}, u32[]{:S(2)}, u32[]{:S(2)}) collective-permute-start(bf16[4,304,256]{2,1,0:T(8,128)(2,1)S(1)} %pick.15), channel_id=1, source_target_pairs={{0,24},{8,16},{16,8},{24,0},{1,25},{9,17},{17,9},{25,1},{2,26},{10... | collective-permute-start | bytes 1867784 | tf_op jit(solution)/shard_map/ppermute | solution.py:663
  340.8 26.9 %collective-permute-start.57 = (bf16[4,304,256]{2,1,0:T(8,128)(2,1)S(1)}, bf16[4,304,256]{2,1,0:T(8,128)(2,1)S(1)}, u32[]{:S(2)}, u32[]{:S(2)}) collective-permute-start(bf16[4,304,256]{2,1,0:T(8,128)(2,1)S(1)} %pick.14), channel_id=1, source_target_pairs={{0,16},{8,24},{16,0},{24,8},{1,17},{9,25},{17,1},{25,9},{2,18},{10... | collective-permute-start | bytes 1867784 | tf_op jit(solution)/shard_map/ppermute | solution.py:663
  342.0 25.8 %collective-permute-start.56 = (bf16[4,304,256]{2,1,0:T(8,128)(2,1)S(1)}, bf16[4,304,256]{2,1,0:T(8,128)(2,1)S(1)}, u32[]{:S(2)}, u32[]{:S(2)}) collective-permute-start(bf16[4,304,256]{2,1,0:T(8,128)(2,1)S(1)} %pick.12.refs_5_), channel_id=1, source_target_pairs={{0,8},{8,0},{16,24},{24,16},{1,9},{9,1},{17,25},{25,17},{2,10},{10... | collective-permute-start | bytes 1867784 | tf_op jit(solution)/shard_map/ppermute | solution.py:663
  342.6 46.1 %collective-permute-start.51 = (bf16[800,256]{1,0:T(8,128)(2,1)S(1)}, bf16[800,256]{1,0:T(8,128)(2,1)S(1)}, u32[]{:S(2)}, u32[]{:S(2)}) collective-permute-start(bf16[800,256]{1,0:T(8,128)(2,1)S(1)} %pass.7), channel_id=1, source_target_pairs={{0,4},{1,5},{2,6},{3,7},{4,0},{5,1},{6,2},{7,3},{8,12},{9,13},{10,... | collective-permute-start | bytes 1228808 | tf_op jit(solution)/shard_map/ppermute | solution.py:657
  368.6 20.0 %collective-permute-start.59 = (bf16[304,256]{1,0:T(8,128)(2,1)S(1)}, bf16[304,256]{1,0:T(8,128)(2,1)S(1)}, u32[]{:S(2)}, u32[]{:S(2)}) collective-permute-start(bf16[304,256]{1,0:T(8,128)(2,1)S(1)} %get-tuple-element.117), channel_id=1, source_target_pairs={{0,6},{1,7},{2,0},{3,1},{4,2},{5,3},{6,4},{7,5},{8,14},{9,15},{10,... | collective-permute-start | bytes 466952 | tf_op jit(solution)/shard_map/ppermute | solution.py:657
  370.6 24.6 %collective-permute-start.60 = (bf16[304,256]{1,0:T(8,128)(2,1)S(1)}, bf16[304,256]{1,0:T(8,128)(2,1)S(1)}, u32[]{:S(2)}, u32[]{:S(2)}) collective-permute-start(bf16[304,256]{1,0:T(8,128)(2,1)S(1)} %get-tuple-element.118), channel_id=1, source_target_pairs={{0,4},{1,5},{2,6},{3,7},{4,0},{5,1},{6,2},{7,3},{8,12},{9,13},{10,... | collective-permute-start | bytes 466952 | tf_op jit(solution)/shard_map/ppermute | solution.py:657
  372.2 23.1 %collective-permute-start.61 = (bf16[304,256]{1,0:T(8,128)(2,1)S(1)}, bf16[304,256]{1,0:T(8,128)(2,1)S(1)}, u32[]{:S(2)}, u32[]{:S(2)}) collective-permute-start(bf16[304,256]{1,0:T(8,128)(2,1)S(1)} %get-tuple-element.119), channel_id=1, source_target_pairs={{0,2},{1,3},{2,4},{3,5},{4,6},{5,7},{6,0},{7,1},{8,10},{9,11},{10,... | collective-permute-start | bytes 466952 | tf_op jit(solution)/shard_map/ppermute | solution.py:657
  395.4 24.5 %collective-permute-start.63 = (bf16[1568,256]{1,0:T(8,128)(2,1)S(1)}, bf16[1568,256]{1,0:T(8,128)(2,1)S(1)}, u32[]{:S(2)}, u32[]{:S(2)}) collective-permute-start(bf16[1568,256]{1,0:T(8,128)(2,1)S(1)} %pass.8.refs_11_), channel_id=1, source_target_pairs={{0,6},{1,7},{2,0},{3,1},{4,2},{5,3},{6,4},{7,5},{8,14},{9,15},{10,... | collective-permute-start | bytes 2408456 | tf_op jit(solution)/shard_map/ppermute | solution.py:657
  395.5 6.9 %collective-permute-start.65 = (bf16[304,256]{1,0:T(8,128)(2,1)S(1)}, bf16[304,256]{1,0:T(8,128)(2,1)S(1)}, u32[]{:S(2)}, u32[]{:S(2)}) collective-permute-start(bf16[304,256]{1,0:T(8,128)(2,1)S(1)} %total.3.refs_1_), channel_id=1, source_target_pairs={{0,8},{8,0},{16,24},{24,16},{1,9},{9,1},{17,25},{25,17},{2,10},{10... | collective-permute-start | bytes 466952 | tf_op jit(solution)/shard_map/ppermute | solution.py:663
  397.1 9.0 %collective-permute-start.66 = (bf16[304,256]{1,0:T(8,128)(2,1)S(1)}, bf16[304,256]{1,0:T(8,128)(2,1)S(1)}, u32[]{:S(2)}, u32[]{:S(2)}) collective-permute-start(bf16[304,256]{1,0:T(8,128)(2,1)S(1)} %total.3.refs_1_), channel_id=1, source_target_pairs={{0,16},{8,24},{16,0},{24,8},{1,17},{9,25},{17,1},{25,9},{2,18},{10... | collective-permute-start | bytes 466952 | tf_op jit(solution)/shard_map/ppermute | solution.py:663
  398.6 7.5 %collective-permute-start.67 = (bf16[304,256]{1,0:T(8,128)(2,1)S(1)}, bf16[304,256]{1,0:T(8,128)(2,1)S(1)}, u32[]{:S(2)}, u32[]{:S(2)}) collective-permute-start(bf16[304,256]{1,0:T(8,128)(2,1)S(1)} %total.3.refs_1_), channel_id=1, source_target_pairs={{0,24},{8,16},{16,8},{24,0},{1,25},{9,17},{17,9},{25,1},{2,26},{10... | collective-permute-start | bytes 466952 | tf_op jit(solution)/shard_map/ppermute | solution.py:663
  409.2 6.1 %collective-permute-start.69 = (f32[8,128]{1,0:T(8,128)S(1)}, f32[8,128]{1,0:T(8,128)S(1)}, u32[]{:S(2)}, u32[]{:S(2)}) collective-permute-start(f32[8,128]{1,0:T(8,128)S(1)} %add.215), channel_id=1, source_target_pairs={{0,2},{1,3},{2,0},{3,1},{4,6},{5,7},{6,4},{7,5},{8,10},{9,11},{10,... | collective-permute-start | bytes 12296 | tf_op jit(solution)/shard_map/ppermute | solution.py:683
  421.3 19.7 %collective-permute-start.64 = (bf16[1568,256]{1,0:T(8,128)(2,1)S(1)}, bf16[1568,256]{1,0:T(8,128)(2,1)S(1)}, u32[]{:S(2)}, u32[]{:S(2)}) collective-permute-start(bf16[1568,256]{1,0:T(8,128)(2,1)S(1)} %pass.9), channel_id=1, source_target_pairs={{0,2},{1,3},{2,4},{3,5},{4,6},{5,7},{6,0},{7,1},{8,10},{9,11},{10,... | collective-permute-start | bytes 2408456 | tf_op jit(solution)/shard_map/ppermute | solution.py:657
  (53 other events, 329.7 us)

commit v6 on v5

--- a/solution.py
+++ b/solution.py
@@ -429,7 +429,7 @@
     out[...] = value[low : low + out.shape[0]]
 
 
-def expand_back_kernel(nz, count, sc, e, up, tot, tot_b, par, w, eg, own, other):
+def expand_back_kernel(nz, count, sc, e, up, tot, tot_b, par, w, eg, own, *others):
     for d in range(nz):
         zs = source_at(sc, nz, d)
         t, b = tot[zs], tot_b[zs]
@@ -444,18 +444,21 @@
         tiles(e.shape[1], body, 0)
     grads = lanes_of([eg.at[d] for d in range(nz)])
     for h in range(2):
-        for index, out in ((own_at(sc, h), own), (other_at(sc, h), other)):
-            out[h] = dot_t(grads, lanes_of([w.at[index, d] for d in range(nz)])).astype(out.dtype)
-
-
-def second_up_kernel(count, sc, own, rec, v2, tot, par, up, sums):
+        weights = lanes_of([w.at[other_at(sc, h), d] for d in range(nz)])
+        others[h][...] = dot_t(grads, weights).astype(BF)
+    for h in range(2):
+        own[h] = dot_t(grads, lanes_of([w.at[own_at(sc, h), d] for d in range(nz)]))
+
+
+def second_up_kernel(count, sc, own, rec0, rec1, v2, tot, par, up, sums):
     for h in range(2):
         center, inv = norm_rows(tot[h, 0:1], tot[h, 1:2], count)
         gain, shift = par[h, 2:3], par[h, 3:4]
 
         def body(at, c):
             hat = (v2[h, at] - center) * inv
-            u = (own[h, at] + rec[h, at].astype(F32)) * gelu_both(hat * gain + shift)[1]
+            received = (rec0, rec1)[h][at].astype(F32)
+            u = (own[h, at] + received) * gelu_both(hat * gain + shift)[1]
             up[h, at] = u
             return c[0] + fold(u), c[1] + fold(u * hat)
 
@@ -940,10 +943,10 @@
         return result.reshape(HW, HW, n, cb).transpose(2, 0, 1, 3)
 
     sent, pins = send_outs(1, tot3b)
-    eg, own2, oth2 = call(
+    eg, own2, *oth2 = call(
         functools.partial(expand_back_kernel, nz, count),
         "expand_back",
-        [sds((nz, rows, cb), BF), half_f, half_b],
+        [sds((nz, rows, cb), BF), half_f] + [sds((rows, QW), BF)] * 2,
         sc,
         e,
         up3,
@@ -1006,14 +1009,14 @@
     def to_all_dp(low):
         return [low] + [over_dp(low, k) for k in range(1, NQ)]
 
-    rec2 = over_core(oth2)
+    rec2 = [over_core(v) for v in oth2]
     up2, sums2b = call(
         functools.partial(second_up_kernel, count),
         "second_up",
         [half_f, sum2_s],
         sc,
         own2,
-        rec2,
+        *rec2,
         v2,
         tot2,
         mid_par,

time: 444 us -> 439 us (0.989); the launches traced: 444 us -> 433 us
  starting transfers between devices: 125 us -> 113 us
    ppermute x24, starting transfers between devices: 67.1 us -> 54.6 us  [over_z(): return lax.ppermute(value, 'group', pairs)]
  transfers between devices with their start and end apart: 71 -> 72, of which waited for: 41 -> 41; matrix products, arithmetic and copies ran while one was open for 2% -> 2% of each run, Pallas kernels for 20% -> 20%
where the time goes in v6:
time: 439 us; the launch traced here: 433 us
  waiting for transfers between devices  189 us (43%)
  starting transfers between devices  113 us (26%)
  Pallas kernels  108 us (25%)
  local copies, waits for them, and re-layouts  11.1 us (3%)
  other arithmetic  7.25 us (2%)
    pallas_call x68, Pallas kernels, call(): pl.pallas_call(inner, in_specs=(specs or [SMEM] + [VMEM] * (used - 1)) +...  108 us
    ppermute x24, waiting for transfers between devices, over_z(): return lax.ppermute(value, 'group', pairs)  80.8 us
    ppermute x24, starting transfers between devices, over_z(): return lax.ppermute(value, 'group', pairs)  54.6 us
    ppermute x28, waiting for transfers between devices, over_dp(): return lax.ppermute(value, 'dp', [(a, a ^ k) for a in range(nd)])  53.5 us
    ppermute x14, waiting for transfers between devices, over_all_z(): other = lax.ppermute(value, 'group', [(a, a ^ k) for a in range(ng)])  53.1 us
    ppermute x28, starting transfers between devices, over_dp(): return lax.ppermute(value, 'dp', [(a, a ^ k) for a in range(nd)])  39 us
    ppermute x14, starting transfers between devices, over_all_z(): other = lax.ppermute(value, 'group', [(a, a ^ k) for a in range(ng)])  18.9 us
  transfers between devices with their start and end apart: 72, of which 41 were waited for; matrix products, arithmetic and copies ran while one was open for 2% of the time, Pallas kernels for 20%

profile of v6, /device:TPU:0, one launch (start us, length us, event | category | flops | bytes accessed | tf_op | source)
XLA Modules:
  0.0 432.6 jit_solution(12458040433347928137)
XLA Ops:
  1.6 2.5 copy-done.1
  5.1 3.1 collective-permute-start
  13.5 2.8 collective-permute-start.5
  16.4 2.5 copy-done.2
  22.4 13.0 %collective-permute-done.3.refs_1_ = bf16[576,256]{1,0:T(8,128)(2,1)S(1)} collective-permute-done((bf16[576,256]{1,0:T(8,128)(2,1)S(1)}, bf16[576,256]{1,0:T(8,128)(2,1)S(1)}, u32[]{:S(2)}, u32[]{:S(2)}) %collective-permute-start.3) | collective-permute-done | bytes 294944 | tf_op jit(solution)/shard_map/ppermute | solution.py:660
  35.4 11.8 %collective-permute-done.4.refs_2_ = bf16[576,256]{1,0:T(8,128)(2,1)S(1)} collective-permute-done((bf16[576,256]{1,0:T(8,128)(2,1)S(1)}, bf16[576,256]{1,0:T(8,128)(2,1)S(1)}, u32[]{:S(2)}, u32[]{:S(2)}) %collective-permute-start.4) | collective-permute-done | bytes 294944 | tf_op jit(solution)/shard_map/ppermute | solution.py:660
  50.4 13.9 %collective-permute-done.2.refs_2_.refs_4_.refs_6_ = bf16[1568,256]{1,0:T(8,128)(2,1)S(1)} collective-permute-done((bf16[1568,256]{1,0:T(8,128)(2,1)S(1)}, bf16[1568,256]{1,0:T(8,128)(2,1)S(1)}, u32[]{:S(2)}, u32[]{:S(2)}) %collective-permute-start.2) | collective-permute-done | bytes 802848 | tf_op jit(solution)/shard_map/ppermute | solution.py:660
  67.6 16.1 %collective-permute-start.1 = (bf16[1568,256]{1,0:T(8,128)(2,1)S(1)}, bf16[1568,256]{1,0:T(8,128)(2,1)S(1)}, u32[]{:S(2)}, u32[]{:S(2)}) collective-permute-start(bf16[1568,256]{1,0:T(8,128)(2,1)S(1)} %bitcast.75), channel_id=1, source_target_pairs={{0,4},{1,5},{2,6},{3,7},{4,0},{5,1},{6,2},{7,3},{8,12},{9,13},{10,... | collective-permute-start | bytes 2408456 | tf_op jit(solution)/shard_map/ppermute | solution.py:660
  83.7 7.2 %collective-permute-done.9.refs_6_ = bf16[2,4,256,256]{3,2,1,0:T(8,128)(2,1)S(1)} collective-permute-done((bf16[2,4,256,256]{3,2,1,0:T(8,128)(2,1)S(1)}, bf16[2,4,256,256]{3,2,1,0:T(8,128)(2,1)S(1)}, u32[]{:S(2)}, u32[]{:S(2)}) %collective-permute-start.9) | collective-permute-done | bytes 1048608 | tf_op jit(solution)/shard_map/ppermute | solution.py:666
  90.9 4.2 collective-permute-done.7.refs_3_
  96.3 14.7 %collective-permute-done.1.refs_3_.refs_5_ = bf16[1568,256]{1,0:T(8,128)(2,1)S(1)} collective-permute-done((bf16[1568,256]{1,0:T(8,128)(2,1)S(1)}, bf16[1568,256]{1,0:T(8,128)(2,1)S(1)}, u32[]{:S(2)}, u32[]{:S(2)}) %collective-permute-start.1) | collective-permute-done | bytes 802848 | tf_op jit(solution)/shard_map/ppermute | solution.py:660
  111.0 4.1 reduce.1
  115.9 4.3 collective-permute-start.15
  128.6 2.7 collective-permute-start.13
  131.4 6.7 %collective-permute-done.13 = f32[2,2,256]{2,1,0:T(2,128)S(1)} collective-permute-done((f32[2,2,256]{2,1,0:T(2,128)S(1)}, f32[2,2,256]{2,1,0:T(2,128)S(1)}, u32[]{:S(2)}, u32[]{:S(2)}) %collective-permute-start.13) | collective-permute-done | bytes 4128 | tf_op jit(solution)/shard_map/ppermute | solution.py:686
  138.1 4.1 collective-permute-start.14
  144.4 4.3 collective-permute-start.20
  149.4 8.8 %conv.1 = (bf16[2,1568,256]{2,1,0:T(8,128)(2,1)S(1)}, f32[2,1568,256]{2,1,0:T(8,128)S(1)}, f32[2,2,256]{2,1,0:T(2,128)S(1)}) custom-call(s32[3]{0:T(128)S(1)} %pad_add_fusion.refs_0_, f32[2,1568,256]{2,1,0:T(8,128)S(1)} %get-tuple-element.84.refs_1_.refs_7_.refs_2_, bf16[2,1568,256]{2,1,0:T(8,128)(2,1)S(1)} %collective-permute-done.10.refs_2_.refs_8_.refs_3_, ...), custom_call_target="tpu_custom_call" | custom-call | flops 1024 | bytes 1024 | tf_op jit(solution)/shard_map/conv/pallas_call | solution.py:72
  166.3 2.8 collective-permute-done.18
  169.1 2.9 collective-permute-start.19
  177.0 3.0 collective-permute-start.27
  180.4 8.6 %expand.1 = (f32[4,1568,256]{2,1,0:T(8,128)S(1)}, f32[4,2,256]{2,1,0:T(2,128)S(1)}) custom-call(s32[3]{0:T(128)S(1)} %pad_add_fusion.refs_0_, bf16[2,1568,256]{2,1,0:T(8,128)(2,1)S(1)} %second_act.1.refs_1_, bf16[2,1568,256]{2,1,0:T(8,128)(2,1)S(1)} %collective-permute-done.22.refs_2_, bf16[4,4,256,256]{3,2,1,0:T(8,128)(2,1)S(1)} %get-tuple-element.83.refs_9_.refs_3_.refs_6_), custom_call_target="tpu_custom_call" | custom-call | flops 1024 | bytes 1024 | tf_op jit(solution)/shard_map/expand/pallas_call | solution.py:72
  198.0 4.5 %collective-permute-done.25 = f32[4,2,256]{2,1,0:T(2,128)S(1)} collective-permute-done((f32[4,2,256]{2,1,0:T(2,128)S(1)}, f32[4,2,256]{2,1,0:T(2,128)S(1)}, u32[]{:S(2)}, u32[]{:S(2)}) %collective-permute-start.25) | collective-permute-done | bytes 8224 | tf_op jit(solution)/shard_map/ppermute | solution.py:686
  202.9 6.0 %collective-permute-done.26.refs_1_ = f32[4,2,256]{2,1,0:T(2,128)S(1)} collective-permute-done((f32[4,2,256]{2,1,0:T(2,128)S(1)}, f32[4,2,256]{2,1,0:T(2,128)S(1)}, u32[]{:S(2)}, u32[]{:S(2)}) %collective-permute-start.26) | collective-permute-done | bytes 8224 | tf_op jit(solution)/shard_map/ppermute | solution.py:686
  214.0 5.3 %up.3 = (bf16[1568,256]{1,0:T(8,128)(2,1)S(1)}, bf16[1568,256]{1,0:T(8,128)(2,1)S(1)}, bf16[1568,256]{1,0:T(8,128)(2,1)S(1)}, f32[4,1568,256]{2,1,0:T(8,128)S(1)}, f32[4,2,256]{2,1,0:T(2,128)S(1)}) custom-call(s32[3]{0:T(128)S(1)} %pad_add_fusion.refs_0_, ...), custom_call_target="tpu_custom_call", output_to_operand_aliasing={{3}: (12, {}), {4}: (13, {})} | custom-call | flops 1024 | bytes 1024 | tf_op jit(solution)/shard_map/up/pallas_call | solution.py:72
  226.7 4.4 %collective-permute-done.31 = f32[4,2,256]{2,1,0:T(2,128)S(1)} collective-permute-done((f32[4,2,256]{2,1,0:T(2,128)S(1)}, f32[4,2,256]{2,1,0:T(2,128)S(1)}, u32[]{:S(2)}, u32[]{:S(2)}) %collective-permute-start.31) | collective-permute-done | bytes 8224 | tf_op jit(solution)/shard_map/ppermute | solution.py:686
  231.9 3.8 collective-permute-done.32.refs_1_
  235.8 5.8 %expand_back.1 = (bf16[4,1568,256]{2,1,0:T(8,128)(2,1)S(1)}, f32[2,1568,256]{2,1,0:T(8,128)S(1)}, bf16[1568,256]{1,0:T(8,128)(2,1)S(1)}, bf16[1568,256]{1,0:T(8,128)(2,1)S(1)}) custom-call(s32[3]{0:T(128)S(1)} %pad_add_fusion.refs_0_, f32[4,1568,256]{2,1,0:T(8,128)S(1)} %get-tuple-element.88.refs_1_, f32[4,1568,256]{2,1,0:T(8,128)S(1)} %get-tuple-element.93.refs_2_.refs_3_, ...), custom_call_target="tpu_custom_call" | custom-call | flops 1024 | bytes 1024 | tf_op jit(solution)/shard_map/expand_back/pallas_call | solution.py:72
  244.1 4.5 %expand_wgrad.1.refs_7_.refs_1_ = bf16[4,4,256,256]{3,2,1,0:T(8,128)(2,1)S(1)} custom-call(s32[3]{0:T(128)S(1)} %pad_add_fusion.refs_0_, bf16[2,1568,256]{2,1,0:T(8,128)(2,1)S(1)} %second_act.1.refs_1_, bf16[2,1568,256]{2,1,0:T(8,128)(2,1)S(1)} %copy-done.4, bf16[4,1568,256]{2,1,0:T(8,128)(2,1)S(1)} %get-tuple-element.100.refs_3_), custom_call_target="tpu_custom_call" | custom-call | flops 1024 | bytes 1024 | tf_op jit(solution)/shard_map/expand_wgrad/pallas_call | solution.py:72
  248.7 3.3 second_up.1
  260.4 2.5 collective-permute-start.45
  264.6 3.6 collective-permute-done.38
  270.7 5.0 %collective-permute-done.39.refs_1_ = f32[2,2,256]{2,1,0:T(2,128)S(1)} collective-permute-done((f32[2,2,256]{2,1,0:T(2,128)S(1)}, f32[2,2,256]{2,1,0:T(2,128)S(1)}, u32[]{:S(2)}, u32[]{:S(2)}) %collective-permute-start.39) | collective-permute-done | bytes 4128 | tf_op jit(solution)/shard_map/ppermute | solution.py:686
  276.4 10.1 %conv_back.1 = (bf16[2,1568,256]{2,1,0:T(8,128)(2,1)S(1)}, f32[2,1568,256]{2,1,0:T(8,128)S(1)}, f32[2,2,256]{2,1,0:T(2,128)S(1)}) custom-call(s32[3]{0:T(128)S(1)} %pad_add_fusion.refs_0_, f32[2,1568,256]{2,1,0:T(8,128)S(1)} %get-tuple-element.101.refs_1_, f32[2,1568,256]{2,1,0:T(8,128)S(1)} %get-tuple-element.86.refs_1_.refs_4_.refs_2_, ...), custom_call_target="tpu_custom_call" | custom-call | flops 1024 | bytes 1024 | tf_op jit(solution)/shard_map/conv_back/pallas_call | solution.py:72
  287.6 2.8 collective-permute-start.50
  299.6 3.6 collective-permute-done.46
  303.7 4.0 collective-permute-done.47.refs_1_
  315.3 4.6 %reduce_wgrad.1.refs_3_.refs_1_ = bf16[4,4,256,256]{3,2,1,0:T(8,128)(2,1)S(1)} custom-call(s32[3]{0:T(128)S(1)} %pad_add_fusion.refs_0_, bf16[2,1568,256]{2,1,0:T(8,128)(2,1)S(1)} %first_grad.1.refs_1_, bf16[2,1568,256]{2,1,0:T(8,128)(2,1)S(1)} %collective-permute-done.53.refs_2_, bf16[1568,256]{1,0:T(8,128)(2,1)S(1)} %bitcast.62, ...), custom_call_target="tpu_custom_call" | custom-call | flops 1024 | bytes 1024 | tf_op jit(solution)/shard_map/reduce_wgrad/pallas_call | solution.py:72
  319.9 5.1 %conv_wgrad.1.refs_2_ = bf16[4,4,48,256]{3,2,1,0:T(8,128)(2,1)S(1)} custom-call(s32[3]{0:T(128)S(1)} %pad_add_fusion.refs_0_, bf16[2,1568,256]{2,1,0:T(8,128)(2,1)S(1)} %copy-done.6, bf16[2,1568,256]{2,1,0:T(8,128)(2,1)S(1)} %get-tuple-element.116.refs_2_, bf16[4,4,256,256]{3,2,1,0:T(8,128)(2,1)S(1)} %reduce_wgrad.1.refs_3_.refs_1_), custom_call_target="tpu_custom_call" | custom-call | flops 1024 | bytes 1024 | tf_op jit(solution)/shard_map/conv_wgrad/pallas_call | solution.py:72
  325.6 2.5 collective-permute-start.59
  330.5 2.6 collective-permute-start.52
  346.1 9.6 %collective-permute-done.58.refs_3_ = bf16[4,304,256]{2,1,0:T(8,128)(2,1)S(1)} collective-permute-done((bf16[4,304,256]{2,1,0:T(8,128)(2,1)S(1)}, bf16[4,304,256]{2,1,0:T(8,128)(2,1)S(1)}, u32[]{:S(2)}, u32[]{:S(2)}) %collective-permute-start.58) | collective-permute-done | bytes 622624 | tf_op jit(solution)/shard_map/ppermute | solution.py:666
  364.9 11.7 %collective-permute-done.52.refs_5_ = bf16[800,256]{1,0:T(8,128)(2,1)S(1)} collective-permute-done((bf16[800,256]{1,0:T(8,128)(2,1)S(1)}, bf16[800,256]{1,0:T(8,128)(2,1)S(1)}, u32[]{:S(2)}, u32[]{:S(2)}) %collective-permute-start.52) | collective-permute-done | bytes 409632 | tf_op jit(solution)/shard_map/ppermute | solution.py:660
  376.6 6.6 %collective-permute-done.61.refs_2_ = bf16[304,256]{1,0:T(8,128)(2,1)S(1)} collective-permute-done((bf16[304,256]{1,0:T(8,128)(2,1)S(1)}, bf16[304,256]{1,0:T(8,128)(2,1)S(1)}, u32[]{:S(2)}, u32[]{:S(2)}) %collective-permute-start.61) | collective-permute-done | bytes 155680 | tf_op jit(solution)/shard_map/ppermute | solution.py:660
  387.1 3.3 collective-permute-done.66.refs_2_
  390.4 3.7 collective-permute-done.67.refs_3_
  399.6 3.8 collective-permute-done.70
  419.8 9.1 %collective-permute-done.65 = bf16[1568,256]{1,0:T(8,128)(2,1)S(1)} collective-permute-done((bf16[1568,256]{1,0:T(8,128)(2,1)S(1)}, bf16[1568,256]{1,0:T(8,128)(2,1)S(1)}, u32[]{:S(2)}, u32[]{:S(2)}) %collective-permute-start.65) | collective-permute-done | bytes 802848 | tf_op jit(solution)/shard_map/ppermute | solution.py:660
  (265 shorter events, 152.6 us)
Async XLA Ops:
  5.1 42.1 %collective-permute-start = (bf16[1568,256]{1,0:T(8,128)(2,1)S(1)}, bf16[1568,256]{1,0:T(8,128)(2,1)S(1)}, u32[]{:S(2)}, u32[]{:S(2)}) collective-permute-start(bf16[1568,256]{1,0:T(8,128)(2,1)S(1)} %bitcast.64), channel_id=1, source_target_pairs={{0,2},{1,3},{2,4},{3,5},{4,6},{5,7},{6,0},{7,1},{8,10},{9,11},{10,... | collective-permute-start | bytes 2408456 | tf_op jit(solution)/shard_map/ppermute | solution.py:660
  10.8 24.6 %collective-permute-start.3 = (bf16[576,256]{1,0:T(8,128)(2,1)S(1)}, bf16[576,256]{1,0:T(8,128)(2,1)S(1)}, u32[]{:S(2)}, u32[]{:S(2)}) collective-permute-start(bf16[576,256]{1,0:T(8,128)(2,1)S(1)} %bundle.1.refs_0_), channel_id=1, source_target_pairs={{0,2},{1,3},{2,4},{3,5},{4,6},{5,7},{6,0},{7,1},{8,10},{9,11},{10,... | collective-permute-start | bytes 884744 | tf_op jit(solution)/shard_map/ppermute | solution.py:660
  12.4 34.8 %collective-permute-start.4 = (bf16[576,256]{1,0:T(8,128)(2,1)S(1)}, bf16[576,256]{1,0:T(8,128)(2,1)S(1)}, u32[]{:S(2)}, u32[]{:S(2)}) collective-permute-start(bf16[576,256]{1,0:T(8,128)(2,1)S(1)} %bundle.1.refs_0_), channel_id=1, source_target_pairs={{0,4},{1,5},{2,6},{3,7},{4,0},{5,1},{6,2},{7,3},{8,12},{9,13},{10,... | collective-permute-start | bytes 884744 | tf_op jit(solution)/shard_map/ppermute | solution.py:660
  13.5 33.7 %collective-permute-start.5 = (bf16[576,256]{1,0:T(8,128)(2,1)S(1)}, bf16[576,256]{1,0:T(8,128)(2,1)S(1)}, u32[]{:S(2)}, u32[]{:S(2)}) collective-permute-start(bf16[576,256]{1,0:T(8,128)(2,1)S(1)} %bundle.1.refs_0_), channel_id=1, source_target_pairs={{0,6},{1,7},{2,0},{3,1},{4,2},{5,3},{6,4},{7,5},{8,14},{9,15},{10,... | collective-permute-start | bytes 884744 | tf_op jit(solution)/shard_map/ppermute | solution.py:660
  19.9 44.4 %collective-permute-start.2 = (bf16[1568,256]{1,0:T(8,128)(2,1)S(1)}, bf16[1568,256]{1,0:T(8,128)(2,1)S(1)}, u32[]{:S(2)}, u32[]{:S(2)}) collective-permute-start(bf16[1568,256]{1,0:T(8,128)(2,1)S(1)} %bitcast.76), channel_id=1, source_target_pairs={{0,6},{1,7},{2,0},{3,1},{4,2},{5,3},{6,4},{7,5},{8,14},{9,15},{10,... | collective-permute-start | bytes 2408456 | tf_op jit(solution)/shard_map/ppermute | solution.py:660
  47.3 16.9 %collective-permute-start.6 = (bf16[1,4,320,256]{3,2,1,0:T(8,128)(2,1)S(1)}, bf16[1,4,320,256]{3,2,1,0:T(8,128)(2,1)S(1)}, u32[]{:S(2)}, u32[]{:S(2)}) collective-permute-start(bf16[1,4,320,256]{3,2,1,0:T(8,128)(2,1)S(1)} %get-tuple-element.77.refs_0_.refs_1_), channel_id=1, source_target_pairs={{0,8},{8,0},{16,24},{24,16},{1,9},{9,1},{17,25},{25,17},{2,10},{10... | collective-permute-start | bytes 1966088 | tf_op jit(solution)/shard_map/ppermute | solution.py:666
  48.9 17.1 %collective-permute-start.8 = (bf16[1,4,256,256]{3,2,1,0:T(8,128)(2,1)S(1)}, bf16[1,4,256,256]{3,2,1,0:T(8,128)(2,1)S(1)}, u32[]{:S(2)}, u32[]{:S(2)}) collective-permute-start(bf16[1,4,256,256]{3,2,1,0:T(8,128)(2,1)S(1)} %get-tuple-element.78.refs_0_.refs_4_), channel_id=1, source_target_pairs={{0,16},{8,24},{16,0},{24,8},{1,17},{9,25},{17,1},{25,9},{2,18},{10... | collective-permute-start | bytes 1572872 | tf_op jit(solution)/shard_map/ppermute | solution.py:666
  64.4 30.8 %collective-permute-start.7 = (bf16[2,4,320,256]{3,2,1,0:T(8,128)(2,1)S(1)}, bf16[2,4,320,256]{3,2,1,0:T(8,128)(2,1)S(1)}, u32[]{:S(2)}, u32[]{:S(2)}) collective-permute-start(bf16[2,4,320,256]{3,2,1,0:T(8,128)(2,1)S(1)} %pair.2), channel_id=1, source_target_pairs={{0,16},{8,24},{16,0},{24,8},{1,17},{9,25},{17,1},{25,9},{2,18},{10... | collective-permute-start | bytes 3932168 | tf_op jit(solution)/shard_map/ppermute | solution.py:666
  66.0 24.9 %collective-permute-start.9 = (bf16[2,4,256,256]{3,2,1,0:T(8,128)(2,1)S(1)}, bf16[2,4,256,256]{3,2,1,0:T(8,128)(2,1)S(1)}, u32[]{:S(2)}, u32[]{:S(2)}) collective-permute-start(bf16[2,4,256,256]{3,2,1,0:T(8,128)(2,1)S(1)} %pair.3), channel_id=1, source_target_pairs={{0,8},{8,0},{16,24},{24,16},{1,9},{9,1},{17,25},{25,17},{2,10},{10... | collective-permute-start | bytes 3145736 | tf_op jit(solution)/shard_map/ppermute | solution.py:666
  67.6 43.4 %collective-permute-start.1 = (bf16[1568,256]{1,0:T(8,128)(2,1)S(1)}, bf16[1568,256]{1,0:T(8,128)(2,1)S(1)}, u32[]{:S(2)}, u32[]{:S(2)}) collective-permute-start(bf16[1568,256]{1,0:T(8,128)(2,1)S(1)} %bitcast.75), channel_id=1, source_target_pairs={{0,4},{1,5},{2,6},{3,7},{4,0},{5,1},{6,2},{7,3},{8,12},{9,13},{10,... | collective-permute-start | bytes 2408456 | tf_op jit(solution)/shard_map/ppermute | solution.py:660
  115.9 26.3 %collective-permute-start.15 = (bf16[1568,256]{1,0:T(8,128)(2,1)S(1)}, bf16[1568,256]{1,0:T(8,128)(2,1)S(1)}, u32[]{:S(2)}, u32[]{:S(2)}) collective-permute-start(bf16[1568,256]{1,0:T(8,128)(2,1)S(1)} %bitcast.72), channel_id=1, source_target_pairs={{0,2},{1,3},{2,4},{3,5},{4,6},{5,7},{6,0},{7,1},{8,10},{9,11},{10,... | collective-permute-start | bytes 2408456 | tf_op jit(solution)/shard_map/ppermute | solution.py:660
  128.6 9.4 %collective-permute-start.13 = (f32[2,2,256]{2,1,0:T(2,128)S(1)}, f32[2,2,256]{2,1,0:T(2,128)S(1)}, u32[]{:S(2)}, u32[]{:S(2)}) collective-permute-start(f32[2,2,256]{2,1,0:T(2,128)S(1)} %add.197), channel_id=1, source_target_pairs={{0,2},{1,3},{2,0},{3,1},{4,6},{5,7},{6,4},{7,5},{8,10},{9,11},{10,... | collective-permute-start | bytes 12296 | tf_op jit(solution)/shard_map/ppermute | solution.py:686
  138.1 5.7 %collective-permute-start.14 = (f32[2,2,256]{2,1,0:T(2,128)S(1)}, f32[2,2,256]{2,1,0:T(2,128)S(1)}, u32[]{:S(2)}, u32[]{:S(2)}) collective-permute-start(f32[2,2,256]{2,1,0:T(2,128)S(1)} %add.198.refs_0_), channel_id=1, source_target_pairs={{0,4},{1,5},{2,6},{3,7},{4,0},{5,1},{6,2},{7,3},{8,12},{9,13},{10,... | collective-permute-start | bytes 12296 | tf_op jit(solution)/shard_map/ppermute | solution.py:686
  144.4 29.2 %collective-permute-start.20 = (bf16[1568,256]{1,0:T(8,128)(2,1)S(1)}, bf16[1568,256]{1,0:T(8,128)(2,1)S(1)}, u32[]{:S(2)}, u32[]{:S(2)}) collective-permute-start(bf16[1568,256]{1,0:T(8,128)(2,1)S(1)} %bitcast.68), channel_id=1, source_target_pairs={{0,6},{1,7},{2,0},{3,1},{4,2},{5,3},{6,4},{7,5},{8,14},{9,15},{10,... | collective-permute-start | bytes 2408456 | tf_op jit(solution)/shard_map/ppermute | solution.py:660
  149.3 24.3 %collective-permute-start.21 = (bf16[320,256]{1,0:T(8,128)(2,1)S(1)}, bf16[320,256]{1,0:T(8,128)(2,1)S(1)}, u32[]{:S(2)}, u32[]{:S(2)}) collective-permute-start(bf16[320,256]{1,0:T(8,128)(2,1)S(1)} %bitcast.88), channel_id=1, source_target_pairs={{0,4},{1,5},{2,6},{3,7},{4,0},{5,1},{6,2},{7,3},{8,12},{9,13},{10,... | collective-permute-start | bytes 491528 | tf_op jit(solution)/shard_map/ppermute | solution.py:660
  177.0 26.0 %collective-permute-start.27 = (bf16[640,256]{1,0:T(8,128)(2,1)S(1)}, bf16[640,256]{1,0:T(8,128)(2,1)S(1)}, u32[]{:S(2)}, u32[]{:S(2)}) collective-permute-start(bf16[640,256]{1,0:T(8,128)(2,1)S(1)} %bitcast.82), channel_id=1, source_target_pairs={{0,4},{1,5},{2,6},{3,7},{4,0},{5,1},{6,2},{7,3},{8,12},{9,13},{10,... | collective-permute-start | bytes 983048 | tf_op jit(solution)/shard_map/ppermute | solution.py:660
  179.9 29.1 %collective-permute-start.28 = (bf16[608,256]{1,0:T(8,128)(2,1)S(1)}, bf16[608,256]{1,0:T(8,128)(2,1)S(1)}, u32[]{:S(2)}, u32[]{:S(2)}) collective-permute-start(bf16[608,256]{1,0:T(8,128)(2,1)S(1)} %bitcast.84), channel_id=1, source_target_pairs={{0,4},{1,5},{2,6},{3,7},{4,0},{5,1},{6,2},{7,3},{8,12},{9,13},{10,... | collective-permute-start | bytes 933896 | tf_op jit(solution)/shard_map/ppermute | solution.py:660
  196.4 6.2 %collective-permute-start.25 = (f32[4,2,256]{2,1,0:T(2,128)S(1)}, f32[4,2,256]{2,1,0:T(2,128)S(1)}, u32[]{:S(2)}, u32[]{:S(2)}) collective-permute-start(f32[4,2,256]{2,1,0:T(2,128)S(1)} %add.203), channel_id=1, source_target_pairs={{0,2},{1,3},{2,0},{3,1},{4,6},{5,7},{6,4},{7,5},{8,10},{9,11},{10,... | collective-permute-start | bytes 24584 | tf_op jit(solution)/shard_map/ppermute | solution.py:686
  202.6 6.4 %collective-permute-start.26 = (f32[4,2,256]{2,1,0:T(2,128)S(1)}, f32[4,2,256]{2,1,0:T(2,128)S(1)}, u32[]{:S(2)}, u32[]{:S(2)}) collective-permute-start(f32[4,2,256]{2,1,0:T(2,128)S(1)} %add.204.refs_0_), channel_id=1, source_target_pairs={{0,4},{1,5},{2,6},{3,7},{4,0},{5,1},{6,2},{7,3},{8,12},{9,13},{10,... | collective-permute-start | bytes 24584 | tf_op jit(solution)/shard_map/ppermute | solution.py:686
  211.1 24.6 %collective-permute-start.33 = (bf16[1568,256]{1,0:T(8,128)(2,1)S(1)}, bf16[1568,256]{1,0:T(8,128)(2,1)S(1)}, u32[]{:S(2)}, u32[]{:S(2)}) collective-permute-start(bf16[1568,256]{1,0:T(8,128)(2,1)S(1)} %get-tuple-element.95), channel_id=1, source_target_pairs={{0,6},{1,7},{2,0},{3,1},{4,2},{5,3},{6,4},{7,5},{8,14},{9,15},{10,... | collective-permute-start | bytes 2408456 | tf_op jit(solution)/shard_map/ppermute | solution.py:660
  241.6 7.0 %collective-permute-start.34 = (bf16[1568,256]{1,0:T(8,128)(2,1)S(1)}, bf16[1568,256]{1,0:T(8,128)(2,1)S(1)}, u32[]{:S(2)}, u32[]{:S(2)}) collective-permute-start(bf16[1568,256]{1,0:T(8,128)(2,1)S(1)} %get-tuple-element.98), channel_id=1, source_target_pairs={{0,1},{1,0},{2,3},{3,2},{4,5},{5,4},{6,7},{7,6},{8,9},{9,8},{10,11... | collective-permute-start | bytes 2408456 | tf_op jit(solution)/shard_map/ppermute | solution.py:663
  241.7 7.0 %collective-permute-start.35 = (bf16[1568,256]{1,0:T(8,128)(2,1)S(1)}, bf16[1568,256]{1,0:T(8,128)(2,1)S(1)}, u32[]{:S(2)}, u32[]{:S(2)}) collective-permute-start(bf16[1568,256]{1,0:T(8,128)(2,1)S(1)} %get-tuple-element.99), channel_id=1, source_target_pairs={{0,1},{1,0},{2,3},{3,2},{4,5},{5,4},{6,7},{7,6},{8,9},{9,8},{10,11... | collective-permute-start | bytes 2408456 | tf_op jit(solution)/shard_map/ppermute | solution.py:663
  242.2 28.5 %collective-permute-start.40 = (bf16[1568,256]{1,0:T(8,128)(2,1)S(1)}, bf16[1568,256]{1,0:T(8,128)(2,1)S(1)}, u32[]{:S(2)}, u32[]{:S(2)}) collective-permute-start(bf16[1568,256]{1,0:T(8,128)(2,1)S(1)} %pass.5.refs_7_), channel_id=1, source_target_pairs={{0,2},{1,3},{2,4},{3,5},{4,6},{5,7},{6,0},{7,1},{8,10},{9,11},{10,... | collective-permute-start | bytes 2408456 | tf_op jit(solution)/shard_map/ppermute | solution.py:660
  260.4 26.2 %collective-permute-start.45 = (bf16[4,256,256]{2,1,0:T(8,128)(2,1)S(1)}, bf16[4,256,256]{2,1,0:T(8,128)(2,1)S(1)}, u32[]{:S(2)}, u32[]{:S(2)}) collective-permute-start(bf16[4,256,256]{2,1,0:T(8,128)(2,1)S(1)} %pick.11), channel_id=1, source_target_pairs={{0,24},{8,16},{16,8},{24,0},{1,25},{9,17},{17,9},{25,1},{2,26},{10... | collective-permute-start | bytes 1572872 | tf_op jit(solution)/shard_map/ppermute | solution.py:666
  262.9 23.7 %collective-permute-start.44 = (bf16[4,256,256]{2,1,0:T(8,128)(2,1)S(1)}, bf16[4,256,256]{2,1,0:T(8,128)(2,1)S(1)}, u32[]{:S(2)}, u32[]{:S(2)}) collective-permute-start(bf16[4,256,256]{2,1,0:T(8,128)(2,1)S(1)} %pick.10), channel_id=1, source_target_pairs={{0,16},{8,24},{16,0},{24,8},{1,17},{9,25},{17,1},{25,9},{2,18},{10... | collective-permute-start | bytes 1572872 | tf_op jit(solution)/shard_map/ppermute | solution.py:666
  264.0 22.6 %collective-permute-start.43 = (bf16[4,256,256]{2,1,0:T(8,128)(2,1)S(1)}, bf16[4,256,256]{2,1,0:T(8,128)(2,1)S(1)}, u32[]{:S(2)}, u32[]{:S(2)}) collective-permute-start(bf16[4,256,256]{2,1,0:T(8,128)(2,1)S(1)} %pick.9), channel_id=1, source_target_pairs={{0,8},{8,0},{16,24},{24,16},{1,9},{9,1},{17,25},{25,17},{2,10},{10... | collective-permute-start | bytes 1572872 | tf_op jit(solution)/shard_map/ppermute | solution.py:666
  268.2 7.5 %collective-permute-start.39 = (f32[2,2,256]{2,1,0:T(2,128)S(1)}, f32[2,2,256]{2,1,0:T(2,128)S(1)}, u32[]{:S(2)}, u32[]{:S(2)}) collective-permute-start(f32[2,2,256]{2,1,0:T(2,128)S(1)} %add.210.refs_0_), channel_id=1, source_target_pairs={{0,4},{1,5},{2,6},{3,7},{4,0},{5,1},{6,2},{7,3},{8,12},{9,13},{10,... | collective-permute-start | bytes 12296 | tf_op jit(solution)/shard_map/ppermute | solution.py:686
  275.8 28.0 %collective-permute-start.48 = (bf16[768,256]{1,0:T(8,128)(2,1)S(1)}, bf16[768,256]{1,0:T(8,128)(2,1)S(1)}, u32[]{:S(2)}, u32[]{:S(2)}) collective-permute-start(bf16[768,256]{1,0:T(8,128)(2,1)S(1)} %pass.6.refs_10_), channel_id=1, source_target_pairs={{0,4},{1,5},{2,6},{3,7},{4,0},{5,1},{6,2},{7,3},{8,12},{9,13},{10,... | collective-permute-start | bytes 1179656 | tf_op jit(solution)/shard_map/ppermute | solution.py:660
  287.4 16.2 %collective-permute-start.49 = (bf16[256,256]{1,0:T(8,128)(2,1)S(1)}, bf16[256,256]{1,0:T(8,128)(2,1)S(1)}, u32[]{:S(2)}, u32[]{:S(2)}) collective-permute-start(bf16[256,256]{1,0:T(8,128)(2,1)S(1)} %get-tuple-element.105), channel_id=1, source_target_pairs={{0,6},{1,7},{2,0},{3,1},{4,2},{5,3},{6,4},{7,5},{8,14},{9,15},{10,... | collective-permute-start | bytes 393224 | tf_op jit(solution)/shard_map/ppermute | solution.py:660
  287.6 16.0 %collective-permute-start.50 = (bf16[256,256]{1,0:T(8,128)(2,1)S(1)}, bf16[256,256]{1,0:T(8,128)(2,1)S(1)}, u32[]{:S(2)}, u32[]{:S(2)}) collective-permute-start(bf16[256,256]{1,0:T(8,128)(2,1)S(1)} %get-tuple-element.106), channel_id=1, source_target_pairs={{0,4},{1,5},{2,6},{3,7},{4,0},{5,1},{6,2},{7,3},{8,12},{9,13},{10,... | collective-permute-start | bytes 393224 | tf_op jit(solution)/shard_map/ppermute | solution.py:660
  290.4 13.2 %collective-permute-start.51 = (bf16[256,256]{1,0:T(8,128)(2,1)S(1)}, bf16[256,256]{1,0:T(8,128)(2,1)S(1)}, u32[]{:S(2)}, u32[]{:S(2)}) collective-permute-start(bf16[256,256]{1,0:T(8,128)(2,1)S(1)} %get-tuple-element.107), channel_id=1, source_target_pairs={{0,2},{1,3},{2,4},{3,5},{4,6},{5,7},{6,0},{7,1},{8,10},{9,11},{10,... | collective-permute-start | bytes 393224 | tf_op jit(solution)/shard_map/ppermute | solution.py:660
  309.6 15.4 %collective-permute-start.54 = (bf16[256,256]{1,0:T(8,128)(2,1)S(1)}, bf16[256,256]{1,0:T(8,128)(2,1)S(1)}, u32[]{:S(2)}, u32[]{:S(2)}) collective-permute-start(bf16[256,256]{1,0:T(8,128)(2,1)S(1)} %total.2.refs_3_.refs_5_), channel_id=1, source_target_pairs={{0,8},{8,0},{16,24},{24,16},{1,9},{9,1},{17,25},{25,17},{2,10},{10... | collective-permute-start | bytes 393224 | tf_op jit(solution)/shard_map/ppermute | solution.py:666
  311.2 13.8 %collective-permute-start.55 = (bf16[256,256]{1,0:T(8,128)(2,1)S(1)}, bf16[256,256]{1,0:T(8,128)(2,1)S(1)}, u32[]{:S(2)}, u32[]{:S(2)}) collective-permute-start(bf16[256,256]{1,0:T(8,128)(2,1)S(1)} %total.2.refs_3_.refs_5_), channel_id=1, source_target_pairs={{0,16},{8,24},{16,0},{24,8},{1,17},{9,25},{17,1},{25,9},{2,18},{10... | collective-permute-start | bytes 393224 | tf_op jit(solution)/shard_map/ppermute | solution.py:666
  312.7 12.3 %collective-permute-start.56 = (bf16[256,256]{1,0:T(8,128)(2,1)S(1)}, bf16[256,256]{1,0:T(8,128)(2,1)S(1)}, u32[]{:S(2)}, u32[]{:S(2)}) collective-permute-start(bf16[256,256]{1,0:T(8,128)(2,1)S(1)} %total.2.refs_3_.refs_5_), channel_id=1, source_target_pairs={{0,24},{8,16},{16,8},{24,0},{1,25},{9,17},{17,9},{25,1},{2,26},{10... | collective-permute-start | bytes 393224 | tf_op jit(solution)/shard_map/ppermute | solution.py:666
  314.9 48.6 %collective-permute-start.63 = (bf16[1568,256]{1,0:T(8,128)(2,1)S(1)}, bf16[1568,256]{1,0:T(8,128)(2,1)S(1)}, u32[]{:S(2)}, u32[]{:S(2)}) collective-permute-start(bf16[1568,256]{1,0:T(8,128)(2,1)S(1)} %input_grad.4.refs_7_), channel_id=1, source_target_pairs={{0,4},{1,5},{2,6},{3,7},{4,0},{5,1},{6,2},{7,3},{8,12},{9,13},{10,... | collective-permute-start | bytes 2408456 | tf_op jit(solution)/shard_map/ppermute | solution.py:660
  325.6 20.4 %collective-permute-start.59 = (bf16[4,304,256]{2,1,0:T(8,128)(2,1)S(1)}, bf16[4,304,256]{2,1,0:T(8,128)(2,1)S(1)}, u32[]{:S(2)}, u32[]{:S(2)}) collective-permute-start(bf16[4,304,256]{2,1,0:T(8,128)(2,1)S(1)} %pick.15), channel_id=1, source_target_pairs={{0,24},{8,16},{16,8},{24,0},{1,25},{9,17},{17,9},{25,1},{2,26},{10... | collective-permute-start | bytes 1867784 | tf_op jit(solution)/shard_map/ppermute | solution.py:666
  328.7 26.9 %collective-permute-start.58 = (bf16[4,304,256]{2,1,0:T(8,128)(2,1)S(1)}, bf16[4,304,256]{2,1,0:T(8,128)(2,1)S(1)}, u32[]{:S(2)}, u32[]{:S(2)}) collective-permute-start(bf16[4,304,256]{2,1,0:T(8,128)(2,1)S(1)} %pick.14), channel_id=1, source_target_pairs={{0,16},{8,24},{16,0},{24,8},{1,17},{9,25},{17,1},{25,9},{2,18},{10... | collective-permute-start | bytes 1867784 | tf_op jit(solution)/shard_map/ppermute | solution.py:666
  329.9 25.8 %collective-permute-start.57 = (bf16[4,304,256]{2,1,0:T(8,128)(2,1)S(1)}, bf16[4,304,256]{2,1,0:T(8,128)(2,1)S(1)}, u32[]{:S(2)}, u32[]{:S(2)}) collective-permute-start(bf16[4,304,256]{2,1,0:T(8,128)(2,1)S(1)} %pick.12.refs_5_), channel_id=1, source_target_pairs={{0,8},{8,0},{16,24},{24,16},{1,9},{9,1},{17,25},{25,17},{2,10},{10... | collective-permute-start | bytes 1867784 | tf_op jit(solution)/shard_map/ppermute | solution.py:666
  330.5 46.1 %collective-permute-start.52 = (bf16[800,256]{1,0:T(8,128)(2,1)S(1)}, bf16[800,256]{1,0:T(8,128)(2,1)S(1)}, u32[]{:S(2)}, u32[]{:S(2)}) collective-permute-start(bf16[800,256]{1,0:T(8,128)(2,1)S(1)} %pass.7), channel_id=1, source_target_pairs={{0,4},{1,5},{2,6},{3,7},{4,0},{5,1},{6,2},{7,3},{8,12},{9,13},{10,... | collective-permute-start | bytes 1228808 | tf_op jit(solution)/shard_map/ppermute | solution.py:660
  356.6 20.1 %collective-permute-start.60 = (bf16[304,256]{1,0:T(8,128)(2,1)S(1)}, bf16[304,256]{1,0:T(8,128)(2,1)S(1)}, u32[]{:S(2)}, u32[]{:S(2)}) collective-permute-start(bf16[304,256]{1,0:T(8,128)(2,1)S(1)} %get-tuple-element.119), channel_id=1, source_target_pairs={{0,6},{1,7},{2,0},{3,1},{4,2},{5,3},{6,4},{7,5},{8,14},{9,15},{10,... | collective-permute-start | bytes 466952 | tf_op jit(solution)/shard_map/ppermute | solution.py:660
  358.8 24.4 %collective-permute-start.61 = (bf16[304,256]{1,0:T(8,128)(2,1)S(1)}, bf16[304,256]{1,0:T(8,128)(2,1)S(1)}, u32[]{:S(2)}, u32[]{:S(2)}) collective-permute-start(bf16[304,256]{1,0:T(8,128)(2,1)S(1)} %get-tuple-element.120), channel_id=1, source_target_pairs={{0,4},{1,5},{2,6},{3,7},{4,0},{5,1},{6,2},{7,3},{8,12},{9,13},{10,... | collective-permute-start | bytes 466952 | tf_op jit(solution)/shard_map/ppermute | solution.py:660
  360.4 22.8 %collective-permute-start.62 = (bf16[304,256]{1,0:T(8,128)(2,1)S(1)}, bf16[304,256]{1,0:T(8,128)(2,1)S(1)}, u32[]{:S(2)}, u32[]{:S(2)}) collective-permute-start(bf16[304,256]{1,0:T(8,128)(2,1)S(1)} %get-tuple-element.121), channel_id=1, source_target_pairs={{0,2},{1,3},{2,4},{3,5},{4,6},{5,7},{6,0},{7,1},{8,10},{9,11},{10,... | collective-permute-start | bytes 466952 | tf_op jit(solution)/shard_map/ppermute | solution.py:660
  383.4 24.5 %collective-permute-start.64 = (bf16[1568,256]{1,0:T(8,128)(2,1)S(1)}, bf16[1568,256]{1,0:T(8,128)(2,1)S(1)}, u32[]{:S(2)}, u32[]{:S(2)}) collective-permute-start(bf16[1568,256]{1,0:T(8,128)(2,1)S(1)} %pass.8.refs_11_), channel_id=1, source_target_pairs={{0,6},{1,7},{2,0},{3,1},{4,2},{5,3},{6,4},{7,5},{8,14},{9,15},{10,... | collective-permute-start | bytes 2408456 | tf_op jit(solution)/shard_map/ppermute | solution.py:660
  383.5 6.9 %collective-permute-start.66 = (bf16[304,256]{1,0:T(8,128)(2,1)S(1)}, bf16[304,256]{1,0:T(8,128)(2,1)S(1)}, u32[]{:S(2)}, u32[]{:S(2)}) collective-permute-start(bf16[304,256]{1,0:T(8,128)(2,1)S(1)} %total.3.refs_1_), channel_id=1, source_target_pairs={{0,8},{8,0},{16,24},{24,16},{1,9},{9,1},{17,25},{25,17},{2,10},{10... | collective-permute-start | bytes 466952 | tf_op jit(solution)/shard_map/ppermute | solution.py:666
  385.1 9.0 %collective-permute-start.67 = (bf16[304,256]{1,0:T(8,128)(2,1)S(1)}, bf16[304,256]{1,0:T(8,128)(2,1)S(1)}, u32[]{:S(2)}, u32[]{:S(2)}) collective-permute-start(bf16[304,256]{1,0:T(8,128)(2,1)S(1)} %total.3.refs_1_), channel_id=1, source_target_pairs={{0,16},{8,24},{16,0},{24,8},{1,17},{9,25},{17,1},{25,9},{2,18},{10... | collective-permute-start | bytes 466952 | tf_op jit(solution)/shard_map/ppermute | solution.py:666
  386.6 7.5 %collective-permute-start.68 = (bf16[304,256]{1,0:T(8,128)(2,1)S(1)}, bf16[304,256]{1,0:T(8,128)(2,1)S(1)}, u32[]{:S(2)}, u32[]{:S(2)}) collective-permute-start(bf16[304,256]{1,0:T(8,128)(2,1)S(1)} %total.3.refs_1_), channel_id=1, source_target_pairs={{0,24},{8,16},{16,8},{24,0},{1,25},{9,17},{17,9},{25,1},{2,26},{10... | collective-permute-start | bytes 466952 | tf_op jit(solution)/shard_map/ppermute | solution.py:666
  397.9 5.5 %collective-permute-start.70 = (f32[8,128]{1,0:T(8,128)S(1)}, f32[8,128]{1,0:T(8,128)S(1)}, u32[]{:S(2)}, u32[]{:S(2)}) collective-permute-start(f32[8,128]{1,0:T(8,128)S(1)} %add.215), channel_id=1, source_target_pairs={{0,2},{1,3},{2,0},{3,1},{4,6},{5,7},{6,4},{7,5},{8,10},{9,11},{10,... | collective-permute-start | bytes 12296 | tf_op jit(solution)/shard_map/ppermute | solution.py:686
  409.2 19.7 %collective-permute-start.65 = (bf16[1568,256]{1,0:T(8,128)(2,1)S(1)}, bf16[1568,256]{1,0:T(8,128)(2,1)S(1)}, u32[]{:S(2)}, u32[]{:S(2)}) collective-permute-start(bf16[1568,256]{1,0:T(8,128)(2,1)S(1)} %pass.9), channel_id=1, source_target_pairs={{0,2},{1,3},{2,4},{3,5},{4,6},{5,7},{6,0},{7,1},{8,10},{9,11},{10,... | collective-permute-start | bytes 2408456 | tf_op jit(solution)/shard_map/ppermute | solution.py:660
  (55 other events, 302.9 us)
